TPU v7x, 32 devices: a whole 2x2x4 slice. The times are simulated.
32 devices in a mesh: dp: 8 (over z, y), tok: 4 (over x, core).
Axes of the slice: x: 2, y: 2, z: 4, core: 2. Of those that a mesh axis runs over, the one named last changes fastest.
Arguments:
- images: bfloat16 [196, 128, 768], P('tok', 'dp'), may hold values from -6 to 6
- partner: int32 [128], replicated, may hold values from 0 to 127, as said below
- lam: float32 [128], replicated, may hold values from 0.2 to 0.8
- labels: int32 [128], replicated, may hold values from 0 to 999
- counts: int32 [8, 2], replicated, may hold values from 1 to 8
- class_weights: float32 [1000], replicated, may hold values from 0.5 to 2
- stem_w: float32 [768, 768], P(None, 'dp'), may hold values from -0.21875 to 0.21875
- stem_m: float32 [768, 768], P(None, 'dp'), may hold values from -0.00015258789 to 0.00015258789
- stem_v: float32 [768, 768], P(None, 'dp'), may hold values from 2.5950322e-11 to 4.1520515e-10
- tok_w: float32 [2, 2, 196, 384], P(None, None, None, 'tok'), may hold values from -0.4375 to 0.4375
- tok_m: float32 [2, 2, 196, 384], P(None, None, None, 'tok'), may hold values from -0.00021362305 to 0.00021362305
- tok_v: float32 [2, 2, 196, 384], P(None, None, None, 'tok'), may hold values from 5.1900644e-11 to 8.304103e-10
- chan_w: float32 [2, 2, 768, 3072], P(None, None, 'dp'), may hold values from -0.21875 to 0.21875
- chan_m: float32 [2, 2, 768, 3072], P(None, None, 'dp'), may hold values from -0.00015258789 to 0.00015258789
- chan_v: float32 [2, 2, 768, 3072], P(None, None, 'dp'), may hold values from 2.5950322e-11 to 4.1520515e-10
- head_w: float32 [768, 1000], P('dp'), may hold values from -0.21875 to 0.21875
- head_m: float32 [768, 1000], P('dp'), may hold values from -0.0024414062 to 0.0024414062
- head_v: float32 [768, 1000], P('dp'), may hold values from 7.8125e-09 to 1.25e-07
- vec_w: float32 [11, 768], replicated, may hold values from -1 to 2.3
- vec_m: float32 [11, 768], replicated, may hold values from -0.00061035156 to 0.00061035156
- vec_v: float32 [11, 768], replicated, may hold values from 4.1520515e-10 to 6.6432824e-09
- hb_w: float32 [1000], replicated, may hold values from -1.75 to 1.75
- hb_m: float32 [1000], replicated, may hold values from -0.0024414062 to 0.0024414062
- hb_v: float32 [1000], replicated, may hold values from 7.8125e-09 to 1.25e-07
Outputs:
- stem_new: float32 [768, 768], P(None, 'dp')
- stem_m_new: float32 [768, 768], P(None, 'dp')
- stem_v_new: float32 [768, 768], P(None, 'dp')
- tok_new: float32 [2, 2, 196, 384], P(None, None, None, 'tok')
- tok_m_new: float32 [2, 2, 196, 384], P(None, None, None, 'tok')
- tok_v_new: float32 [2, 2, 196, 384], P(None, None, None, 'tok')
- chan_new: float32 [2, 2, 768, 3072], P(None, None, 'dp')
- chan_m_new: float32 [2, 2, 768, 3072], P(None, None, 'dp')
- chan_v_new: float32 [2, 2, 768, 3072], P(None, None, 'dp')
- head_new: float32 [768, 1000], P('dp')
- head_m_new: float32 [768, 1000], P('dp')
- head_v_new: float32 [768, 1000], P('dp')
- vec_new: float32 [11, 768], replicated
- vec_m_new: float32 [11, 768], replicated
- vec_v_new: float32 [11, 768], replicated
- hb_new: float32 [1000], replicated
- hb_m_new: float32 [1000], replicated
- hb_v_new: float32 [1000], replicated
- stem_low: bfloat16 [768, 768], P(None, 'dp')
- tok_low: bfloat16 [2, 2, 196, 384], P(None, None, None, 'tok')
- chan_low: bfloat16 [2, 2, 768, 3072], P(None, None, 'dp')
- head_low: bfloat16 [768, 1000], P('dp')
- norms: float32 [22, 2], replicated
- loss_parts: float32 [2], replicated
Inputs may be any that keep to these rules, and one draw needn't show every extreme that they name: `partner`: with d = i // 16 the data index of image i and b = (i // 8) mod 2 its micro-batch, partner_i is an image of micro-batch b of data index (d + 8 / 2) mod 8, where 8 is the number of data indices; the partners of the 8 images of one micro-batch of one data index are all different.
All inputs are finite; a program needn't handle non-finite values.
Results may differ from a plain program's by a relative error of at most 0.023.
Values may be sent and summed in bfloat16 or wider, within the bound.
No kernel may reach another device: no remote copies, remote signals or barrier semaphores. Data moves between devices by JAX's collectives and lax.ppermute only.
A program may use at most 384 MiB of HBM per device.

v0:
```python
import jax
import jax.numpy as jnp
from jax import lax
from jax.sharding import PartitionSpec as P

S = 196
LAYERS = 2
MB = 2
STEP = 5
IMG_MB = 8
NV = 11


highest = lax.Precision.HIGHEST
beta_one = 0.9
beta_two = 0.999
epsilon = 1e-06
weight_decay = 0.01
learn_rate = 0.3


def from_behind(array, axis, by):
    length = lax.axis_size(axis)
    return lax.ppermute(array, axis, [(i, (i + by) % length) for i in range(length)])


def layer_norm(values, gain, shift):
    centre = values - jnp.mean(values, -1, keepdims=True)
    spread = jnp.mean(centre * centre, -1, keepdims=True)
    return centre * lax.rsqrt(spread + 1e-06) * gain + shift


def gelu_back(inputs, upstream):
    return jax.vjp(jax.nn.gelu, inputs)[1](upstream)[0]


def moments(weight, gradient, first, second, decay_rate):
    first_new = beta_one * first + (1 - beta_one) * gradient
    second_new = beta_two * second + (1 - beta_two) * gradient * gradient
    update = (
        first_new / (1 - beta_one**STEP) / (jnp.sqrt(second_new / (1 - beta_two**STEP)) + epsilon)
        + decay_rate * weight
    )
    return (first_new, second_new, update)


def row_squares(array, groups):
    flat = array.reshape(groups, -1)
    return jnp.sum(flat * flat, 1)


def renew(weight, update, weight_norm, update_norm, groups):
    trust = weight_norm / (update_norm + epsilon)
    return weight - learn_rate * (trust[:, None] * update.reshape(groups, -1)).reshape(weight.shape)


def fetch_partners(own_block, picks):
    half_axis = lax.axis_size("dp") // 2
    incoming = from_behind(own_block, "dp", half_axis)
    per_batch = own_block.shape[1]
    within = picks % per_batch
    pick = (within[:, None] == jnp.arange(per_batch, dtype=jnp.int32)[None, :]).astype(jnp.bfloat16)
    return jnp.einsum("kx,sxp->skp", pick, incoming, preferred_element_type=jnp.float32)


def layer_forward(state, token_in, token_out, channel_in, channel_out, gains):
    normed_one = layer_norm(state, gains[0], gains[1]).astype(jnp.bfloat16)
    rows_all = lax.all_gather(normed_one, "tok", axis=0, tiled=True)
    before = jnp.einsum("sj,sbc->jbc", token_in, rows_all, preferred_element_type=jnp.float32)
    hidden = jax.nn.gelu(before).astype(jnp.bfloat16)
    middle = state + lax.psum_scatter(
        jnp.einsum("sj,jbc->sbc", token_out, hidden, preferred_element_type=jnp.float32),
        "tok",
        scatter_dimension=0,
        tiled=True,
    )
    normed_two = layer_norm(middle, gains[2], gains[3]).astype(jnp.bfloat16)
    inner = jnp.einsum("sbc,cf->sbf", normed_two, channel_in, preferred_element_type=jnp.float32)
    active = jax.nn.gelu(inner).astype(jnp.bfloat16)
    result = middle + jnp.einsum(
        "sbf,cf->sbc", active, channel_out, preferred_element_type=jnp.float32
    )
    return (result, (state, rows_all, before, hidden, middle, normed_two, inner, active))


def layer_backward(gradient, saved, token_in, token_out, channel_in, channel_out, gains):
    state, rows_all, before, hidden, middle, normed_two, inner, active = saved
    grad_out = gradient.astype(jnp.bfloat16)
    grad_channel_out = jnp.einsum(
        "sbf,sbc->cf", active, grad_out, preferred_element_type=jnp.float32
    )
    grad_active = jnp.einsum(
        "sbc,cf->sbf", grad_out, channel_out, preferred_element_type=jnp.float32
    )
    grad_inner = gelu_back(inner, grad_active).astype(jnp.bfloat16)
    grad_channel_in = jnp.einsum(
        "sbc,sbf->cf", normed_two, grad_inner, preferred_element_type=jnp.float32
    )
    grad_normed_two = jnp.einsum(
        "sbf,cf->sbc", grad_inner, channel_in, preferred_element_type=jnp.float32
    )
    second_back = jax.vjp(layer_norm, middle, gains[2], gains[3])[1]
    grad_middle_norm, grad_gain_two, grad_shift_two = second_back(grad_normed_two)
    grad_middle = gradient + grad_middle_norm
    grad_token = grad_middle.astype(jnp.bfloat16)
    piece = lax.all_gather(grad_token, "tok", axis=0, tiled=True)
    rows = token_out
    hidden_sum = jnp.einsum("sj,sbc->jbc", rows, piece, preferred_element_type=jnp.float32)
    block_rows = jnp.einsum("sbc,jbc->sj", piece, hidden, preferred_element_type=jnp.float32)
    grad_before = gelu_back(before, hidden_sum).astype(jnp.bfloat16)
    grad_token_in = jnp.einsum(
        "sbc,jbc->sj", rows_all, grad_before, preferred_element_type=jnp.float32
    )
    rows = token_in
    grad_normed_one = lax.psum_scatter(
        jnp.einsum("sj,jbc->sbc", rows, grad_before, preferred_element_type=jnp.float32).astype(
            jnp.bfloat16
        ),
        "tok",
        scatter_dimension=0,
        tiled=True,
    ).astype(jnp.float32)
    first_back = jax.vjp(layer_norm, state, gains[0], gains[1])[1]
    grad_state_norm, grad_gain_one, grad_shift_one = first_back(grad_normed_one)
    token_grads = jnp.stack([grad_token_in, block_rows])
    channel_grads = jnp.stack([grad_channel_in, grad_channel_out])
    vector_grads = jnp.stack([grad_gain_one, grad_shift_one, grad_gain_two, grad_shift_two])
    return (grad_middle + grad_state_norm, token_grads, channel_grads, vector_grads)


def body(
    images,
    partner,
    lam,
    labels,
    counts,
    class_weights,
    stem_w,
    stem_m,
    stem_v,
    tok_w,
    tok_m,
    tok_v,
    chan_w,
    chan_m,
    chan_v,
    head_w,
    head_m,
    head_v,
    vec_w,
    vec_m,
    vec_v,
    hb_w,
    hb_m,
    hb_v,
):
    stem_all, chan_all, head_all = (
        lax.all_gather(stem_w.astype(jnp.bfloat16), "dp", axis=1, tiled=True),
        lax.all_gather(chan_w.astype(jnp.bfloat16), "dp", axis=2, tiled=True),
        lax.all_gather(head_w.astype(jnp.bfloat16), "dp", axis=0, tiled=True),
    )
    token_low = tok_w.astype(jnp.bfloat16)
    head_float = head_all.astype(jnp.float32)
    count_dp = lax.axis_size("dp")
    count_tok = lax.axis_size("tok")
    device_row = lax.axis_index("dp")
    token_row = lax.axis_index("tok")
    per_device = images.shape[1]
    per_tok = IMG_MB // count_tok
    classes = jnp.arange(hb_w.shape[0], dtype=jnp.int32)
    own_hot = (labels[:, None] == classes[None, :]).astype(jnp.float32)
    other_hot = (jnp.take(labels, partner)[:, None] == classes[None, :]).astype(jnp.float32)
    live = (
        (jnp.arange(IMG_MB, dtype=jnp.int32)[None, :] < counts.reshape(-1)[:, None])
        .astype(jnp.float32)
        .reshape(-1)
    )
    targets = lam[:, None] * own_hot + (1 - lam[:, None]) * other_hot
    weights = live * jnp.sum(targets * class_weights[None, :], 1)
    total = jnp.sum(weights)
    big_total = (
        jnp.zeros(stem_all.shape, jnp.float32),
        jnp.zeros(chan_all.shape, jnp.float32),
        jnp.zeros(head_all.shape, jnp.float32),
    )
    reduced = (
        jnp.zeros(stem_w.shape, jnp.float32),
        jnp.zeros(chan_w.shape, jnp.float32),
        jnp.zeros(head_w.shape, jnp.float32),
    )
    token_sum = jnp.zeros(token_low.shape, jnp.float32)
    vector_sum = jnp.zeros(vec_w.shape, jnp.float32)
    bias_sum = jnp.zeros(hb_w.shape, jnp.float32)
    loss_local = jnp.zeros((), jnp.float32)
    for batch in range(MB):
        own_block = images[:, batch * IMG_MB : (batch + 1) * IMG_MB]
        start = device_row * per_device + batch * IMG_MB
        picks = lax.dynamic_slice_in_dim(partner, start, IMG_MB, 0)
        other = fetch_partners(own_block, picks)
        own = own_block.astype(jnp.float32)
        share = lax.dynamic_slice_in_dim(lam, start, IMG_MB, 0)[None, :, None]
        mixed = (share * own + (1 - share) * other).astype(jnp.bfloat16)
        state = (
            jnp.einsum("sbp,pc->sbc", mixed, stem_all, preferred_element_type=jnp.float32)
            + vec_w[0]
        )
        saved_layers = []
        for layer in range(LAYERS):
            state, saved = layer_forward(
                state,
                token_low[layer, 0],
                token_low[layer, 1],
                chan_all[layer, 0],
                chan_all[layer, 1],
                vec_w[1 + 4 * layer : 5 + 4 * layer],
            )
            saved_layers.append(saved)
        final, final_back = jax.vjp(layer_norm, state, vec_w[NV - 2], vec_w[NV - 1])
        pooled = lax.psum_scatter(jnp.sum(final, 0), "tok", scatter_dimension=0, tiled=True) / S
        pooled_low = pooled.astype(jnp.bfloat16)
        logits = jnp.dot(pooled_low, head_all, preferred_element_type=jnp.float32) + hb_w
        first_row = start + token_row * per_tok
        target_rows = lax.dynamic_slice_in_dim(targets, first_row, per_tok, 0)
        weight_rows = lax.dynamic_slice_in_dim(weights, first_row, per_tok, 0)
        log_probs = jax.nn.log_softmax(logits, -1)
        loss_local = loss_local + jnp.sum(weight_rows * -jnp.sum(target_rows * log_probs, -1))
        grad_logits = (weight_rows / total)[:, None] * (
            jnp.exp(log_probs) * jnp.sum(target_rows, -1, keepdims=True) - target_rows
        )
        head_grad = jnp.dot(pooled_low.astype(jnp.float32).T, grad_logits, precision=highest)
        bias_sum = bias_sum + jnp.sum(grad_logits, 0)
        grad_pooled = jnp.dot(grad_logits, head_float.T, precision=highest) / S
        grad_pooled_all = lax.all_gather(grad_pooled, "tok", axis=0, tiled=True)
        grad_state, grad_gain_last, grad_shift_last = final_back(
            jnp.broadcast_to(grad_pooled_all[None], final.shape)
        )
        token_list = [None] * LAYERS
        channel_list = [None] * LAYERS
        vector_list = [None] * LAYERS
        for layer in reversed(range(LAYERS)):
            grad_state, token_list[layer], channel_list[layer], vector_list[layer] = layer_backward(
                grad_state,
                saved_layers[layer],
                token_low[layer, 0],
                token_low[layer, 1],
                chan_all[layer, 0],
                chan_all[layer, 1],
                vec_w[1 + 4 * layer : 5 + 4 * layer],
            )
        grad_low = grad_state.astype(jnp.bfloat16)
        stem_grad = jnp.einsum("sbp,sbc->pc", mixed, grad_low, preferred_element_type=jnp.float32)
        stem_bias = jnp.sum(grad_low.astype(jnp.float32), (0, 1))
        vector_sum = vector_sum + jnp.concatenate(
            [stem_bias[None]] + vector_list + [grad_gain_last[None], grad_shift_last[None]], 0
        )
        token_sum = token_sum + jnp.stack(token_list)
        batch_grads = (stem_grad, jnp.stack(channel_list), head_grad)
        big_total = jax.tree.map(jnp.add, big_total, batch_grads)
    reduced = (
        lax.psum_scatter(big_total[0], "dp", scatter_dimension=1, tiled=True),
        lax.psum_scatter(big_total[1], "dp", scatter_dimension=2, tiled=True),
        lax.psum_scatter(big_total[2], "dp", scatter_dimension=0, tiled=True),
    )
    token_grad, vector_part, bias_part, loss_part = lax.psum(
        (token_sum, vector_sum, bias_sum, loss_local), "dp"
    )
    stem_grad, chan_grad, head_grad, vector_grad, bias_grad, loss_total = (
        lax.psum(reduced[0].astype(jnp.bfloat16), "tok").astype(jnp.float32),
        lax.psum(reduced[1].astype(jnp.bfloat16), "tok").astype(jnp.float32),
        lax.psum(reduced[2].astype(jnp.bfloat16), "tok").astype(jnp.float32),
        lax.psum(vector_part.astype(jnp.bfloat16), "tok").astype(jnp.float32),
        lax.psum(bias_part.astype(jnp.bfloat16), "tok").astype(jnp.float32),
        lax.psum(loss_part.astype(jnp.bfloat16), "tok").astype(jnp.float32),
    )
    stem_first, stem_second, stem_update = moments(stem_w, stem_grad, stem_m, stem_v, weight_decay)
    tok_first, tok_second, tok_update = moments(tok_w, token_grad, tok_m, tok_v, weight_decay)
    chan_first, chan_second, chan_update = moments(chan_w, chan_grad, chan_m, chan_v, weight_decay)
    head_first, head_second, head_update = moments(head_w, head_grad, head_m, head_v, weight_decay)
    vec_first, vec_second, vec_update = moments(vec_w, vector_grad, vec_m, vec_v, 0.0)
    hb_first, hb_second, hb_update = moments(hb_w, bias_grad, hb_m, hb_v, 0.0)
    matrix_groups = 2 * LAYERS
    weight_squares = jnp.concatenate(
        [
            row_squares(stem_w, 1) / count_tok,
            row_squares(tok_w, matrix_groups) / count_dp,
            row_squares(chan_w, matrix_groups) / count_tok,
            row_squares(head_w, 1) / count_tok,
        ]
    )
    update_squares = jnp.concatenate(
        [
            row_squares(stem_update, 1) / count_tok,
            row_squares(tok_update, matrix_groups) / count_dp,
            row_squares(chan_update, matrix_groups) / count_tok,
            row_squares(head_update, 1) / count_tok,
        ]
    )
    weight_total, update_total = lax.psum((weight_squares, update_squares), ("dp", "tok"))
    weight_norms = jnp.sqrt(weight_total)
    update_norms = jnp.sqrt(update_total)
    stem_end = 1
    tok_end = 1 + matrix_groups
    chan_end = 1 + 2 * matrix_groups
    stem_new = renew(stem_w, stem_update, weight_norms[0:stem_end], update_norms[0:stem_end], 1)
    tok_new = renew(
        tok_w,
        tok_update,
        weight_norms[stem_end:tok_end],
        update_norms[stem_end:tok_end],
        matrix_groups,
    )
    chan_new = renew(
        chan_w,
        chan_update,
        weight_norms[tok_end:chan_end],
        update_norms[tok_end:chan_end],
        matrix_groups,
    )
    head_new = renew(head_w, head_update, weight_norms[chan_end:], update_norms[chan_end:], 1)
    vec_weight_norm = jnp.sqrt(row_squares(vec_w, NV))
    vec_update_norm = jnp.sqrt(row_squares(vec_update, NV))
    hb_weight_norm = jnp.sqrt(row_squares(hb_w, 1))
    hb_update_norm = jnp.sqrt(row_squares(hb_update, 1))
    vec_new = renew(vec_w, vec_update, vec_weight_norm, vec_update_norm, NV)
    hb_new = renew(hb_w, hb_update, hb_weight_norm, hb_update_norm, 1)
    norms = jnp.stack(
        [
            jnp.concatenate([weight_norms, vec_weight_norm, hb_weight_norm]),
            jnp.concatenate([update_norms, vec_update_norm, hb_update_norm]),
        ],
        1,
    )
    loss_parts = jnp.stack([loss_total, total])
    return (
        stem_new,
        stem_first,
        stem_second,
        tok_new,
        tok_first,
        tok_second,
        chan_new,
        chan_first,
        chan_second,
        head_new,
        head_first,
        head_second,
        vec_new,
        vec_first,
        vec_second,
        hb_new,
        hb_first,
        hb_second,
        stem_new.astype(jnp.bfloat16),
        tok_new.astype(jnp.bfloat16),
        chan_new.astype(jnp.bfloat16),
        head_new.astype(jnp.bfloat16),
        norms,
        loss_parts,
    )


def solution(mesh):
    in_specs = (
        P("tok", "dp", None),
        P(),
        P(),
        P(),
        P(),
        P(),
        P(None, "dp"),
        P(None, "dp"),
        P(None, "dp"),
        P(None, None, None, "tok"),
        P(None, None, None, "tok"),
        P(None, None, None, "tok"),
        P(None, None, "dp", None),
        P(None, None, "dp", None),
        P(None, None, "dp", None),
        P("dp", None),
        P("dp", None),
        P("dp", None),
        P(),
        P(),
        P(),
        P(),
        P(),
        P(),
    )
    out_specs = (
        P(None, "dp"),
        P(None, "dp"),
        P(None, "dp"),
        P(None, None, None, "tok"),
        P(None, None, None, "tok"),
        P(None, None, None, "tok"),
        P(None, None, "dp", None),
        P(None, None, "dp", None),
        P(None, None, "dp", None),
        P("dp", None),
        P("dp", None),
        P("dp", None),
        P(),
        P(),
        P(),
        P(),
        P(),
        P(),
        P(None, "dp"),
        P(None, None, None, "tok"),
        P(None, None, "dp", None),
        P("dp", None),
        P(),
        P(),
    )
    return jax.shard_map(body, mesh=mesh, in_specs=in_specs, out_specs=out_specs, check_vma=False)
```

profile of v0, /device:TPU:0, one launch (start us, length us, event | category | flops | bytes accessed | tf_op | source)
XLA Modules:
  0.0 2147.3 jit_solution(14826593055923351630)
XLA Ops:
  10.4 4.1 collective-permute-start.1
  15.4 44.2 %collective-permute-done.1 = bf16[49,8,768]{2,1,0:T(8,128)(2,1)} collective-permute-done((bf16[49,8,768]{2,1,0:T(8,128)(2,1)S(1)}, bf16[49,8,768]{2,1,0:T(8,128)(2,1)}, u32[]{:S(2)}, u32[]{:S(2)}) %collective-permute-start.1) | collective-permute-done | bytes 602144 | tf_op jit(solution)/shard_map/ppermute | solution.py:24
  61.2 10.6 collective-permute-done
  73.2 21.4 all-gather.14.cloned.1.call-done
  101.1 22.4 %all-gather.28.cloned.1.call-done = bf16[196,8,768]{2,1,0:T(8,128)(2,1)} async-done(((bf16[49,8,768]{2,1,0:T(8,128)(2,1)}), bf16[196,8,768]{2,1,0:T(8,128)(2,1)}) %all-gather.28.cloned.1.call-update) | async-done | bytes 2408464 | tf_op jit(solution)/shard_map/all_gather | solution.py:68
  131.8 18.2 all-gather.16.cloned.1.call-done
  158.6 4.7 convert_element_type.237
  163.9 37.1 %reduce-scatter.20.cloned.1.call-done = f32[49,8,768]{2,1,0:T(8,128)} async-done(((f32[196,8,768]{2,1,0:T(8,128)}), f32[49,8,768]{2,1,0:T(8,128)}) %reduce-scatter.20.cloned.1.call-update) | async-done | bytes 1204240 | tf_op jit(solution)/shard_map/reduce_scatter | solution.py:71
  203.8 48.3 %reduce-scatter.12.cloned.1.call-done = f32[49,8,768]{2,1,0:T(8,128)} async-done(((f32[196,8,768]{2,1,0:T(8,128)}), f32[49,8,768]{2,1,0:T(8,128)}) %reduce-scatter.12.cloned.1.call-update) | async-done | bytes 1204240 | tf_op jit(solution)/shard_map/reduce_scatter | solution.py:71
  253.9 362.6 %all-gather.18.cloned.1.call-done = bf16[2,2,768,3072]{3,2,1,0:T(8,128)(2,1)} async-done(((bf16[2,2,96,3072]{3,2,1,0:T(8,128)(2,1)}), bf16[2,2,768,3072]{3,2,1,0:T(8,128)(2,1)}) %all-gather.18.cloned.1.call-update) | async-done | bytes 18874384 | tf_op jit(solution)/shard_map/all_gather | solution.py:159
  616.5 5.0 fusion.31
  621.5 7.1 fusion.285
  631.9 5.2 fusion.284
  639.9 23.5 %all-gather.20.cloned.1.call-done = bf16[196,8,768]{2,1,0:T(8,128)(2,1)} async-done(((bf16[49,8,768]{2,1,0:T(8,128)(2,1)}), bf16[196,8,768]{2,1,0:T(8,128)(2,1)}) %all-gather.20.cloned.1.call-update) | async-done | bytes 2408464 | tf_op jit(solution)/shard_map/all_gather | solution.py:68
  671.7 18.3 all-gather.30.cloned.1.call-done
  704.8 36.2 %reduce-scatter.14.cloned.1.call-done = f32[49,8,768]{2,1,0:T(8,128)} async-done(((f32[196,8,768]{2,1,0:T(8,128)}), f32[49,8,768]{2,1,0:T(8,128)}) %reduce-scatter.14.cloned.1.call-update) | async-done | bytes 1204240 | tf_op jit(solution)/shard_map/reduce_scatter | solution.py:71
  742.8 4.5 fusion.39
  747.4 8.3 fusion.287
  755.7 36.4 %reduce-scatter.22.cloned.1.call-done = f32[49,8,768]{2,1,0:T(8,128)} async-done(((f32[196,8,768]{2,1,0:T(8,128)}), f32[49,8,768]{2,1,0:T(8,128)}) %reduce-scatter.22.cloned.1.call-update) | async-done | bytes 1204240 | tf_op jit(solution)/shard_map/reduce_scatter | solution.py:71
  794.3 4.4 fusion.37
  798.8 7.2 fusion.286
  807.0 11.7 all-reduce.4
  818.7 20.3 all-gather.22.cloned.1.call-done
  848.5 5.2 all-gather
  858.0 5.2 all-gather.1
  867.5 9.4 fusion.27
  877.0 4.7 fusion.248
  881.7 7.7 fusion.13
  889.4 4.9 multiply_reduce_fusion.3
  901.8 19.0 all-gather.32.cloned.1.call-done
  920.8 4.4 fusion.73
  929.0 17.7 all-gather.24.cloned.1.call-done
  946.8 4.4 fusion.59
  955.0 27.6 %reduce-scatter.24.cloned.1.call-done = bf16[49,8,768]{2,1,0:T(8,128)(2,1)} async-done(((bf16[196,8,768]{2,1,0:T(8,128)(2,1)}), bf16[49,8,768]{2,1,0:T(8,128)(2,1)}) %reduce-scatter.24.cloned.1.call-update) | async-done | bytes 602128 | tf_op jit(solution)/shard_map/reduce_scatter | solution.py:115
  987.3 6.9 fusion.20
  994.3 6.1 fusion.249
  1002.9 16.2 reduce-scatter.16.cloned.1.call-done
  1019.1 4.9 fusion.269
  1025.8 6.9 fusion.6
  1032.7 6.0 fusion.251
  1043.9 9.3 convolution_bitcast_fusion
  1053.3 6.9 convolution_bitcast_fusion.1
  1066.4 13.5 maximum_bitcast_fusion.3
  1088.8 9.0 convolution_bitcast_fusion.4
  1097.8 4.4 fusion.66
  1107.4 4.6 convolution_bitcast_fusion.5
  1112.0 10.5 maximum_bitcast_fusion.1
  1133.0 5.6 convolution_bitcast_fusion.2
  1138.7 5.4 convolution_bitcast_fusion.6
  1144.1 6.3 convolution_bitcast_fusion.3
  1158.3 7.7 reduce-scatter.26.cloned.1.call-done
  1175.9 4.8 convolution_bitcast_fusion.7
  1180.7 13.0 maximum_bitcast_fusion.2
  1193.7 10.7 maximum_bitcast_fusion
  1204.4 38.9 %maximum_add_fusion = f32[2,2,768,3072]{3,2,1,0:T(8,128)} fusion(f32[1,2,768,3072]{3,2,1,0:T(8,128)} %maximum_bitcast_fusion.1, f32[1,2,768,3072]{3,2,1,0:T(8,128)} %maximum_bitcast_fusion, f32[1,2,768,3072]{3,2,1,0:T(8,128)} %maximum_bitcast_fusion.3, f32[1,2,768,3072]{3,2,1,0:T(8,128)} %maximum_bitcast_fusion.2), kind=kLoop, calls=%fused_computation.1 | loop fusion | flops 28311552 | bytes 113246208 | tf_op jit(solution)/shard_map/add | solution.py:258
  1247.3 71.5 %all-reduce.10.cloned.1.call-done = f32[2,2,196,96]{2,3,1,0:T(8,128)} async-done(((f32[2,2,196,96]{2,3,1,0:T(8,128)}), f32[2,2,196,96]{2,3,1,0:T(8,128)}) %all-reduce.10.cloned.1.call-update) | async-done | bytes 301072 | tf_op jit(solution)/shard_map/psum | solution.py:264
  1320.9 70.6 %reduce-scatter.28.cloned.1.call-done = f32[768,96]{0,1:T(8,128)} async-done(((f32[768,768]{0,1:T(8,128)}), f32[768,96]{0,1:T(8,128)}) %reduce-scatter.28.cloned.1.call-update) | async-done | bytes 294928 | tf_op jit(solution)/shard_map/reduce_scatter | solution.py:260
  1393.2 606.3 %reduce-scatter.30.cloned.1.call-done = f32[2,2,96,3072]{3,2,1,0:T(8,128)} async-done(((f32[2,2,768,3072]{3,2,1,0:T(8,128)}), f32[2,2,96,3072]{3,2,1,0:T(8,128)}) %reduce-scatter.30.cloned.1.call-update) | async-done | bytes 4718608 | tf_op jit(solution)/shard_map/reduce_scatter | solution.py:261
  2004.4 35.7 %all-reduce.3 = (bf16[11,768]{1,0:T(8,128)(2,1)S(1)}, bf16[1000]{0:T(1024)(128)(2,1)S(1)}, bf16[]{:T(256)}) all-reduce(f32[11,768]{1,0:T(8,128)S(1)} %add.690, f32[1000]{0:T(1024)S(1)} %add.697, f32[]{:T(128)S(6)} %add.704), channel_id=1, replica_groups=mesh['dp'=8,'tok'=4] {'dp'}, use_global_device_ids=true, to_apply=%region_98.100 | all-reduce | flops 9449 | bytes 56694 | tf_op jit(solution)/shard_map/psum | solution.py:264
  2040.1 12.8 all-reduce.5
  2057.7 7.6 all-reduce.12.cloned.1.call-done
  2065.2 11.6 multiply_reduce_fusion
  2085.0 39.2 %all-reduce.2 = (f32[10]{0:T(128)S(1)}, f32[10]{0:T(128)S(1)}) all-reduce(f32[10]{0:T(128)S(1)} %pad_maximum_fusion.1, f32[10]{0:T(128)S(1)} %pad_maximum_fusion.2), channel_id=1, replica_groups=mesh['dp'=8,'tok'=4] {'dp','tok'}, use_global_device_ids=true, to_apply=%region_4.5 | all-reduce | flops 20 | bytes 160 | tf_op jit(solution)/shard_map/psum | solution.py:298
  2130.0 8.3 fusion.253
  (657 shorter events, 187.7 us)
Async XLA Ops:
  7.2 52.5 %copy-start.58 = (bf16[49,16,768]{2,1,0:T(8,128)(2,1)S(1)}, bf16[49,16,768]{2,1,0:T(8,128)(2,1)}, u32[]{:S(2)}) copy-start(bf16[49,16,768]{2,1,0:T(8,128)(2,1)} %param.25) | copy-start | bytes 3612676
  7.2 87.3 %all-gather.14.cloned.1.call-start = ((), (), s32[]{:S(2)}) async-start(), calls=%async_computation.11 | async-start | bytes 1327104 | tf_op jit(solution)/shard_map/all_gather | solution.py:158
  9.0 114.5 %all-gather.28.cloned.1.call-start = ((), (), s32[]{:S(2)}) async-start(), calls=%async_computation.22 | async-start | bytes 3010560 | tf_op jit(solution)/shard_map/all_gather | solution.py:68
  10.4 49.3 %collective-permute-start.1 = (bf16[49,8,768]{2,1,0:T(8,128)(2,1)S(1)}, bf16[49,8,768]{2,1,0:T(8,128)(2,1)}, u32[]{:S(2)}, u32[]{:S(2)}) collective-permute-start(bf16[49,8,768]{2,1,0:T(8,128)(2,1)S(1)} %get-tuple-element.159), channel_id=1, source_target_pairs={{0,16},{4,20},{8,24},{12,28},{16,0},{20,4},{24,8},{28,12},{1,17},{... | collective-permute-start | bytes 1806344 | tf_op jit(solution)/shard_map/ppermute | solution.py:24
  14.5 57.2 %collective-permute-start = (bf16[49,8,768]{2,1,0:T(8,128)(2,1)S(1)}, bf16[49,8,768]{2,1,0:T(8,128)(2,1)}, u32[]{:S(2)}, u32[]{:S(2)}) collective-permute-start(bf16[49,8,768]{2,1,0:T(8,128)(2,1)S(1)} %get-tuple-element.158), channel_id=1, source_target_pairs={{0,16},{4,20},{8,24},{12,28},{16,0},{20,4},{24,8},{28,12},{1,17},{... | collective-permute-start | bytes 1806344 | tf_op jit(solution)/shard_map/ppermute | solution.py:24
  15.4 83.3 %copy-start.125 = (f32[768]{0:T(1024)}, f32[768]{0:T(1024)S(1)}, u32[]{:S(2)}) copy-start(f32[768]{0:T(1024)S(1)} %get-tuple-element.84) | copy-start | bytes 9220
  15.4 613.5 %copy-start.154 = (f32[768]{0:T(1024)}, f32[768]{0:T(1024)S(1)}, u32[]{:S(2)}) copy-start(f32[768]{0:T(1024)S(1)} %get-tuple-element.81) | copy-start | bytes 9220
  15.4 778.9 %copy-start.156 = (f32[768]{0:T(1024)}, f32[768]{0:T(1024)S(1)}, u32[]{:S(2)}) copy-start(f32[768]{0:T(1024)S(1)} %get-tuple-element.77) | copy-start | bytes 9220
  61.1 35.6 %copy-start.77 = (bf16[49,8,768]{2,1,0:T(8,128)(2,1)}, bf16[49,8,768]{2,1,0:T(8,128)(2,1)S(1)}, u32[]{:S(2)}) copy-start(bf16[49,8,768]{2,1,0:T(8,128)(2,1)S(1)} %fusion.146) | copy-start | bytes 1806340
  96.7 104.2 %copy-start.1 = (f32[49,8,768]{2,1,0:T(8,128)}, f32[49,8,768]{2,1,0:T(8,128)S(1)}, u32[]{:S(2)}) copy-start(f32[49,8,768]{2,1,0:T(8,128)S(1)} %get-tuple-element.198) | copy-start | bytes 3612676
  97.5 154.5 %copy-start.3 = (f32[49,8,768]{2,1,0:T(8,128)}, f32[49,8,768]{2,1,0:T(8,128)S(1)}, u32[]{:S(2)}) copy-start(f32[49,8,768]{2,1,0:T(8,128)S(1)} %get-tuple-element.196) | copy-start | bytes 3612676
  100.2 49.8 %all-gather.16.cloned.1.call-start = ((), (), s32[]{:S(2)}) async-start(), calls=%async_computation.12 | async-start | bytes 3010560 | tf_op jit(solution)/shard_map/all_gather | solution.py:68
  101.0 100.0 %reduce-scatter.20.cloned.1.call-start = ((), (), s32[]{:S(2)}) async-start(), calls=%async_computation.23 | async-start | bytes 6021120 | tf_op jit(solution)/shard_map/reduce_scatter | solution.py:71
  101.1 850.1 %copy-start.48 = (bf16[2,2,196,96]{2,3,1,0:T(8,128)(2,1)}, bf16[2,2,196,96]{2,3,1,0:T(8,128)(2,1)S(1)}, u32[]{:S(2)}) copy-start(bf16[2,2,196,96]{2,3,1,0:T(8,128)(2,1)S(1)} %convert_element_type.234) | copy-start | bytes 451588
  131.8 120.3 %reduce-scatter.12.cloned.1.call-start = ((), (), s32[]{:S(2)}) async-start(), calls=%async_computation.13 | async-start | bytes 6021120 | tf_op jit(solution)/shard_map/reduce_scatter | solution.py:71
  158.6 458.0 %all-gather.18.cloned.1.call-start = ((), (), s32[]{:S(2)}) async-start(), calls=%async_computation.14 | async-start | bytes 21233664 | tf_op jit(solution)/shard_map/all_gather | solution.py:159
  163.4 500.1 %all-gather.20.cloned.1.call-start = ((), (), s32[]{:S(2)}) async-start(), calls=%async_computation.15 | async-start | bytes 3010560 | tf_op jit(solution)/shard_map/all_gather | solution.py:68
  202.5 816.6 %copy-start.91 = (f32[49,8]{1,0:T(8,128)}, f32[49,8]{1,0:T(8,128)S(1)}, u32[]{:S(2)}) copy-start(f32[49,8]{1,0:T(8,128)S(1)} %broadcast_multiply_fusion.3) | copy-start | bytes 4708
  253.6 375.4 %copy-start.12 = (f32[49,8,768]{2,1,0:T(8,128)}, f32[49,8,768]{2,1,0:T(8,128)S(1)}, u32[]{:S(2)}) copy-start(f32[49,8,768]{2,1,0:T(8,128)S(1)} %get-tuple-element.149) | copy-start | bytes 3612676
  253.6 787.1 %copy-start.85 = (f32[49,8]{1,0:T(8,128)}, f32[49,8]{1,0:T(8,128)S(1)}, u32[]{:S(2)}) copy-start(f32[49,8]{1,0:T(8,128)S(1)} %broadcast_multiply_fusion.8) | copy-start | bytes 4708
  253.8 367.6 %copy-start.111 = (f32[49,8]{1,0:T(8,128)}, f32[49,8]{1,0:T(8,128)S(1)}, u32[]{:S(2)}) copy-start(f32[49,8]{1,0:T(8,128)S(1)} %multiply_reduce_fusion.20) | copy-start | bytes 4708
  253.9 765.2 %copy-start.113 = (f32[49,8]{1,0:T(8,128)}, f32[49,8]{1,0:T(8,128)S(1)}, u32[]{:S(2)}) copy-start(f32[49,8]{1,0:T(8,128)S(1)} %fusion.217) | copy-start | bytes 4708
  253.9 786.8 %copy-start.103 = (f32[49,8]{1,0:T(8,128)}, f32[49,8]{1,0:T(8,128)S(1)}, u32[]{:S(2)}) copy-start(f32[49,8]{1,0:T(8,128)S(1)} %fusion.212) | copy-start | bytes 4708
  638.9 51.0 %all-gather.30.cloned.1.call-start = ((), (), s32[]{:S(2)}) async-start(), calls=%async_computation.24 | async-start | bytes 3010560 | tf_op jit(solution)/shard_map/all_gather | solution.py:68
  639.7 101.3 %reduce-scatter.14.cloned.1.call-start = ((), (), s32[]{:S(2)}) async-start(), calls=%async_computation.16 | async-start | bytes 6021120 | tf_op jit(solution)/shard_map/reduce_scatter | solution.py:71
  671.6 120.4 %reduce-scatter.22.cloned.1.call-start = ((), (), s32[]{:S(2)}) async-start(), calls=%async_computation.25 | async-start | bytes 6021120 | tf_op jit(solution)/shard_map/reduce_scatter | solution.py:71
  698.3 140.8 %all-gather.22.cloned.1.call-start = ((), (), s32[]{:S(2)}) async-start(), calls=%async_computation.17 | async-start | bytes 1769472 | tf_op jit(solution)/shard_map/all_gather | solution.py:160
  700.1 220.8 %all-gather.32.cloned.1.call-start = ((), (), s32[]{:S(2)}) async-start(), calls=%async_computation.26 | async-start | bytes 3010560 | tf_op jit(solution)/shard_map/all_gather | solution.py:106
  742.5 155.1 %copy-start.93 = (f32[49,8]{1,0:T(8,128)}, f32[49,8]{1,0:T(8,128)S(1)}, u32[]{:S(2)}) copy-start(f32[49,8]{1,0:T(8,128)S(1)} %broadcast_multiply_fusion.6) | copy-start | bytes 4708
  742.8 154.8 %copy-start.115 = (f32[49,8]{1,0:T(8,128)}, f32[49,8]{1,0:T(8,128)S(1)}, u32[]{:S(2)}) copy-start(f32[49,8]{1,0:T(8,128)S(1)} %fusion.214) | copy-start | bytes 4708
  755.7 141.9 %copy-start.69 = (f32[49,8]{1,0:T(8,128)}, f32[49,8]{1,0:T(8,128)S(1)}, u32[]{:S(2)}) copy-start(f32[49,8]{1,0:T(8,128)S(1)} %broadcast_multiply_fusion.5) | copy-start | bytes 4708
  794.0 100.4 %copy-start.121 = (f32[49,8]{1,0:T(8,128)}, f32[49,8]{1,0:T(8,128)S(1)}, u32[]{:S(2)}) copy-start(f32[49,8]{1,0:T(8,128)S(1)} %fusion.219) | copy-start | bytes 4708
  806.0 33.1 %copy-start.131 = (f32[1000]{0:T(1024)S(1)}, f32[1000]{0:T(1024)}, u32[]{:S(2)}) copy-start(f32[1000]{0:T(1024)} %param.46) | copy-start | bytes 12004
  806.3 91.3 %copy-start.83 = (f32[49,8]{1,0:T(8,128)}, f32[49,8]{1,0:T(8,128)S(1)}, u32[]{:S(2)}) copy-start(f32[49,8]{1,0:T(8,128)S(1)} %fusion.215) | copy-start | bytes 4708
  853.7 43.9 %copy-start.95 = (f32[8,768]{1,0:T(8,128)}, f32[8,768]{1,0:T(8,128)S(1)}, u32[]{:S(2)}) copy-start(f32[8,768]{1,0:T(8,128)S(1)} %reshape.541) | copy-start | bytes 73732
  855.3 42.3 %copy-start.105 = (f32[49,8]{1,0:T(8,128)}, f32[49,8]{1,0:T(8,128)S(1)}, u32[]{:S(2)}) copy-start(f32[49,8]{1,0:T(8,128)S(1)} %multiply_multiply_fusion.34) | copy-start | bytes 4708
  897.5 49.3 %all-gather.24.cloned.1.call-start = ((), (), s32[]{:S(2)}) async-start(), calls=%async_computation.18 | async-start | bytes 3010560 | tf_op jit(solution)/shard_map/all_gather | solution.py:106
  901.6 81.0 %reduce-scatter.24.cloned.1.call-start = ((), (), s32[]{:S(2)}) async-start(), calls=%async_computation.27 | async-start | bytes 3010560 | tf_op jit(solution)/shard_map/reduce_scatter | solution.py:115
  929.0 90.1 %reduce-scatter.16.cloned.1.call-start = ((), (), s32[]{:S(2)}) async-start(), calls=%async_computation.19 | async-start | bytes 3010560 | tf_op jit(solution)/shard_map/reduce_scatter | solution.py:115
  955.0 125.0 %all-gather.26.cloned.1.call-start = ((), (), s32[]{:S(2)}) async-start(), calls=%async_computation.20 | async-start | bytes 3010560 | tf_op jit(solution)/shard_map/all_gather | solution.py:106
  1043.8 54.0 %all-gather.34.cloned.1.call-start = ((), (), s32[]{:S(2)}) async-start(), calls=%async_computation.28 | async-start | bytes 3010560 | tf_op jit(solution)/shard_map/all_gather | solution.py:106
  1053.2 105.0 %reduce-scatter.18.cloned.1.call-start = ((), (), s32[]{:S(2)}) async-start(), calls=%async_computation.21 | async-start | bytes 3010560 | tf_op jit(solution)/shard_map/reduce_scatter | solution.py:115
  1087.5 78.5 %reduce-scatter.26.cloned.1.call-start = ((), (), s32[]{:S(2)}) async-start(), calls=%async_computation.29 | async-start | bytes 3010560 | tf_op jit(solution)/shard_map/reduce_scatter | solution.py:115
  1106.1 139.3 %reduce-scatter.32.cloned.1.call-start = ((), (), s32[]{:S(2)}) async-start(), calls=%async_computation.33 | async-start | bytes 3538944 | tf_op jit(solution)/shard_map/reduce_scatter | solution.py:262
  1122.5 196.3 %all-reduce.10.cloned.1.call-start = ((), (), s32[]{:S(2)}) async-start(), calls=%async_computation.31 | async-start | bytes 786432 | tf_op jit(solution)/shard_map/psum | solution.py:264
  1158.2 233.3 %reduce-scatter.28.cloned.1.call-start = ((), (), s32[]{:S(2)}) async-start(), calls=%async_computation.30 | async-start | bytes 2654208 | tf_op jit(solution)/shard_map/reduce_scatter | solution.py:260
  1174.6 824.8 %reduce-scatter.30.cloned.1.call-start = ((), (), s32[]{:S(2)}) async-start(), calls=%async_computation.32 | async-start | bytes 42467328 | tf_op jit(solution)/shard_map/reduce_scatter | solution.py:261
  1243.4 75.3 %copy-start.45 = (f32[2,2,196,96]{2,3,1,0:T(8,128)S(1)}, f32[2,2,196,96]{2,3,1,0:T(8,128)}, u32[]{:S(2)}) copy-start(f32[2,2,196,96]{2,3,1,0:T(8,128)} %param.34) | copy-start | bytes 903172
  1243.5 75.3 %copy-start.97 = (f32[2,2,196,96]{2,3,1,0:T(8,128)S(1)}, f32[2,2,196,96]{2,3,1,0:T(8,128)}, u32[]{:S(2)}) copy-start(f32[2,2,196,96]{2,3,1,0:T(8,128)} %param.35) | copy-start | bytes 903172
  1243.5 75.3 %copy-start.98 = (f32[2,2,196,96]{2,3,1,0:T(8,128)S(1)}, f32[2,2,196,96]{2,3,1,0:T(8,128)}, u32[]{:S(2)}) copy-start(f32[2,2,196,96]{2,3,1,0:T(8,128)} %param.36) | copy-start | bytes 903172
  1243.5 821.7 %all-reduce.12.cloned.1.call-start = ((), (), s32[]{:S(2)}) async-start(), calls=%async_computation.34 | async-start | bytes 5406720 | tf_op jit(solution)/shard_map/psum | solution.py:270
  1320.2 818.1 %copy-start.54 = (f32[2,2,196,96]{2,3,1,0:T(8,128)}, f32[2,2,196,96]{2,3,1,0:T(8,128)S(1)}, u32[]{:S(2)}) copy-start(f32[2,2,196,96]{2,3,1,0:T(8,128)S(1)} %get-tuple-element.130) | copy-start | bytes 903172
  1320.2 818.1 %copy-start.55 = (f32[2,2,196,96]{2,3,1,0:T(8,128)}, f32[2,2,196,96]{2,3,1,0:T(8,128)S(1)}, u32[]{:S(2)}) copy-start(f32[2,2,196,96]{2,3,1,0:T(8,128)S(1)} %get-tuple-element.131) | copy-start | bytes 903172
  2003.5 50.0 %copy-start.132 = (f32[1000]{0:T(1024)S(1)}, f32[1000]{0:T(1024)}, u32[]{:S(2)}) copy-start(f32[1000]{0:T(1024)} %param.46) | copy-start | bytes 12004
  2003.5 50.0 %copy-start.163 = (f32[1000]{0:T(1024)S(1)}, f32[1000]{0:T(1024)}, u32[]{:S(2)}) copy-start(f32[1000]{0:T(1024)} %param.47) | copy-start | bytes 12004
  2003.5 50.0 %copy-start.164 = (f32[1000]{0:T(1024)S(1)}, f32[1000]{0:T(1024)}, u32[]{:S(2)}) copy-start(f32[1000]{0:T(1024)} %param.48) | copy-start | bytes 12004
  2003.6 52.1 %copy-start.102 = (f32[11,768]{1,0:T(8,128)S(1)}, f32[11,768]{1,0:T(8,128)}, u32[]{:S(2)}) copy-start(f32[11,768]{1,0:T(8,128)} %param.43) | copy-start | bytes 101380
  2003.6 52.1 %copy-start.133 = (f32[11,768]{1,0:T(8,128)S(1)}, f32[11,768]{1,0:T(8,128)}, u32[]{:S(2)}) copy-start(f32[11,768]{1,0:T(8,128)} %param.44) | copy-start | bytes 101380
  2003.6 52.1 %copy-start.134 = (f32[11,768]{1,0:T(8,128)S(1)}, f32[11,768]{1,0:T(8,128)}, u32[]{:S(2)}) copy-start(f32[11,768]{1,0:T(8,128)} %param.45) | copy-start | bytes 101380
  2076.9 48.5 %copy-start.166 = (f32[11]{0:T(128)S(1)}, f32[11]{0:T(128)}, u32[]{:S(2)}) copy-start(f32[11]{0:T(128)} %get-tuple-element.182) | copy-start | bytes 136
  2078.9 59.4 %copy-start.56 = (f32[96,1000]{1,0:T(8,128)}, f32[96,1000]{1,0:T(8,128)S(1)}, u32[]{:S(2)}) copy-start(f32[96,1000]{1,0:T(8,128)S(1)} %get-tuple-element.134) | copy-start | bytes 1152004
  2078.9 59.4 %copy-start.57 = (f32[96,1000]{1,0:T(8,128)}, f32[96,1000]{1,0:T(8,128)S(1)}, u32[]{:S(2)}) copy-start(f32[96,1000]{1,0:T(8,128)S(1)} %get-tuple-element.135) | copy-start | bytes 1152004
  2081.6 57.8 %copy-start.67 = (f32[768,96]{0,1:T(8,128)}, f32[768,96]{0,1:T(8,128)S(1)}, u32[]{:S(2)}) copy-start(f32[768,96]{0,1:T(8,128)S(1)} %get-tuple-element.128) | copy-start | bytes 884740
  2081.6 57.8 %copy-start.68 = (f32[768,96]{0,1:T(8,128)}, f32[768,96]{0,1:T(8,128)S(1)}, u32[]{:S(2)}) copy-start(f32[768,96]{0,1:T(8,128)S(1)} %get-tuple-element.129) | copy-start | bytes 884740
  (158 other events, 904.8 us)
Sparse Core Ops, SparseCore 0:
  10.8 83.7 all-gather.13
  100.4 23.1 all-gather.27
  125.7 24.3 all-gather.15
  152.5 48.4 reduce-scatter.19
  203.5 48.4 reduce-scatter.11
  254.0 362.4 all-gather.17
  639.1 24.3 all-gather.19
  665.6 24.3 all-gather.29
  692.5 48.4 reduce-scatter.13
  743.6 48.4 reduce-scatter.21
  794.8 44.1 all-gather.21
  897.6 23.1 all-gather.31
  922.4 24.3 all-gather.23
  949.2 33.3 reduce-scatter.23
  985.7 33.3 reduce-scatter.15
  1043.9 24.3 all-gather.25
  1069.7 24.3 all-gather.33
  1096.5 33.3 reduce-scatter.17
  1132.6 33.3 reduce-scatter.25
  1170.0 74.2 reduce-scatter.31
  1248.3 70.4 all-reduce.9
  1323.3 68.2 reduce-scatter.27
  1395.9 603.5 reduce-scatter.29
  2003.7 61.4 all-reduce.11
where the time goes:
time: 2160 us; the launch traced here: 2150 us
  waiting for transfers between devices  1550 us (72%)
  matrix products  218 us (10%)
  other arithmetic  189 us (9%)
  blocking collectives  110 us (5%)
  local copies, waits for them, and re-layouts  52.2 us (2%)
  between operations  26.6 us (1%)
    reduce_scatter x1, waiting for transfers between devices, body(): lax.psum_scatter(big_total[1], 'dp', scatter_dimension=2, tiled=True)  606 us
    all_gather x1, waiting for transfers between devices, body(): lax.all_gather(chan_w.astype(jnp.bfloat16), 'dp', axis=2, tiled=True)  363 us
    reduce_scatter x4, waiting for transfers between devices, layer_forward(): lax.psum_scatter(jnp.einsum('sj,jbc->sbc', token_out, hidden, preferred_e...  158 us
    all_gather x4, waiting for transfers between devices, layer_forward(): rows_all = lax.all_gather(normed_one, 'tok', axis=0, tiled=True)  82.4 us
    psum x1, waiting for transfers between devices, body(): lax.psum((token_sum, vector_sum, bias_sum, loss_local), 'dp')  71.5 us
    reduce_scatter x1, waiting for transfers between devices, body(): lax.psum_scatter(big_total[0], 'dp', scatter_dimension=1, tiled=True)  70.6 us
    ppermute x2, waiting for transfers between devices, from_behind(): lax.ppermute(array, axis, [(i, (i + by) % length) for i in range(length)])  54.8 us
    reduce_scatter x4, waiting for transfers between devices, layer_backward(): lax.psum_scatter(jnp.einsum('sj,jbc->sbc', rows, grad_before, preferred_e...  51.5 us
  transfers between devices with their start and end apart: 26, of which 22 were waited for; matrix products, arithmetic and copies ran while one was open for 14% of the time, Pallas kernels for 0%

commit v1 on v0

v1 whole, which is shorter than its diff:
```python
import jax
import jax.numpy as jnp
from jax import lax
from jax.sharding import PartitionSpec as P

LAYERS = 2
STEP = 5
IMG_MB = 8
NV = 11
LANES = 128

highest = lax.Precision.HIGHEST
low = jnp.bfloat16
beta_one = 0.9
beta_two = 0.999
epsilon = 1e-06
weight_decay = 0.01
learn_rate = 0.3


def swap(array, axis, mask):
    count = lax.axis_size(axis)
    return lax.ppermute(array, axis, [(i, i ^ mask) for i in range(count)])


def dp_masks():
    masks = []
    mask = lax.axis_size("dp") // 2
    while mask > 1:
        masks.append(mask)
        mask //= 2
    return masks


def row_order():
    order = [0]
    for mask in dp_masks() + [1]:
        order = order + [r ^ mask for r in order]
    return order


def spread(piece, tok_first):
    for mask in dp_masks():
        piece = jnp.concatenate([piece, swap(piece, "dp", mask)], 0)
    if tok_first:
        second = swap(piece, "tok", 2)
        low_row, low_second = swap(piece, "dp", 1), swap(second, "dp", 1)
    else:
        low_row = swap(piece, "dp", 1)
        second, low_second = swap(piece, "tok", 2), swap(low_row, "tok", 2)
    near = [[piece, second], [low_row, low_second]]
    return [row + [swap(block, "tok", 1) for block in row] for row in near]


def joined(blocks):
    return jnp.concatenate([jnp.concatenate(row, 1) for row in blocks], 0)


def halves(array, axis):
    middle = array.shape[axis] // 2
    return (
        lax.slice_in_dim(array, 0, middle, axis=axis),
        lax.slice_in_dim(array, middle, 2 * middle, axis=axis),
    )


def fold(array, dimension, axis, mask):
    keep, send = halves(array, dimension)
    return keep.astype(jnp.float32) + swap(send.astype(low), axis, mask).astype(jnp.float32)


def collect(grad, tok_first):
    grad = fold(grad, 1, "tok", 1)
    if tok_first:
        grad = fold(fold(grad, 0, "dp", 1), 1, "tok", 2)
    else:
        grad = fold(fold(grad, 1, "tok", 2), 0, "dp", 1)
    for mask in reversed(dp_masks()):
        grad = fold(grad, 0, "dp", mask)
    own = grad.astype(low)
    far = swap(own, "tok", 2)
    return jnp.concatenate([own, far, swap(own, "tok", 1), swap(far, "tok", 1)], 1)


def ordered(array, axis, bits):
    row = lax.axis_index("tok")
    blocks = jnp.split(array, 4, axis)
    rel = [blocks[0], blocks[2], blocks[1], blocks[3]] if bits else blocks
    rel = [jnp.where((row & 1) == 1, rel[k ^ 1], rel[k]) for k in range(4)]
    rel = [jnp.where((row & 2) == 2, rel[k ^ 2], rel[k]) for k in range(4)]
    return jnp.concatenate(rel, axis)


def relative(array, axis):
    row = lax.axis_index("tok")
    rel = jnp.split(array, 4, axis)
    rel = [jnp.where((row & 1) == 1, rel[k ^ 1], rel[k]) for k in range(4)]
    rel = [jnp.where((row & 2) == 2, rel[k ^ 2], rel[k]) for k in range(4)]
    return jnp.concatenate([rel[0], rel[2], rel[1], rel[3]], axis)


def quarter(array, axis):
    size = array.shape[axis] // lax.axis_size("tok")
    return lax.dynamic_slice_in_dim(array, lax.axis_index("tok") * size, size, axis)


def layer_norm(values, gain, shift):
    centre = values - jnp.mean(values, -1, keepdims=True)
    spread_of = jnp.mean(centre * centre, -1, keepdims=True)
    return centre * lax.rsqrt(spread_of + 1e-06) * gain + shift


def gelu_back(inputs, upstream):
    return jax.vjp(jax.nn.gelu, inputs)[1](upstream)[0]


def moments(weight, gradient, first, second, decay_rate):
    first_new = beta_one * first + (1 - beta_one) * gradient
    second_new = beta_two * second + (1 - beta_two) * gradient * gradient
    update = (
        first_new / (1 - beta_one**STEP) / (jnp.sqrt(second_new / (1 - beta_two**STEP)) + epsilon)
        + decay_rate * weight
    )
    return (first_new, second_new, update)


def row_squares(array, groups):
    flat = array.reshape(groups, -1)
    return jnp.sum(flat * flat, 1)


def renew(weight, update, weight_norm, update_norm, groups):
    trust = weight_norm / (update_norm + epsilon)
    return weight - learn_rate * (trust[:, None] * update.reshape(groups, -1)).reshape(weight.shape)


def layer_forward(state, token_in, token_out, channel_in, channel_out, gains):
    normed_one = layer_norm(state, gains[0], gains[1]).astype(low)
    before = jnp.einsum("sj,bsc->bjc", token_in, normed_one, preferred_element_type=jnp.float32)
    hidden = jax.nn.gelu(before).astype(low)
    middle = state + jnp.einsum("sj,bjc->bsc", token_out, hidden, preferred_element_type=jnp.float32)
    normed_two = layer_norm(middle, gains[2], gains[3]).astype(low)
    inner = jnp.einsum("bsc,cf->bsf", normed_two, channel_in, preferred_element_type=jnp.float32)
    active = jax.nn.gelu(inner).astype(low)
    result = middle + jnp.einsum("bsf,cf->bsc", active, channel_out, preferred_element_type=jnp.float32)
    return (result, (state, normed_one, before, hidden, middle, normed_two, inner, active))


def layer_backward(gradient, saved, token_in, token_out, channel_in, channel_out, gains):
    state, normed_one, before, hidden, middle, normed_two, inner, active = saved
    grad_out = gradient.astype(low)
    grad_channel_out = jnp.einsum("bsf,bsc->cf", active, grad_out, preferred_element_type=jnp.float32)
    grad_active = jnp.einsum("bsc,cf->bsf", grad_out, channel_out, preferred_element_type=jnp.float32)
    grad_inner = gelu_back(inner, grad_active).astype(low)
    grad_channel_in = jnp.einsum("bsc,bsf->cf", normed_two, grad_inner, preferred_element_type=jnp.float32)
    grad_normed_two = jnp.einsum("bsf,cf->bsc", grad_inner, channel_in, preferred_element_type=jnp.float32)
    second_back = jax.vjp(layer_norm, middle, gains[2], gains[3])[1]
    grad_middle_norm, grad_gain_two, grad_shift_two = second_back(grad_normed_two)
    grad_middle = gradient + grad_middle_norm
    grad_token = grad_middle.astype(low)
    hidden_sum = jnp.einsum("sj,bsc->bjc", token_out, grad_token, preferred_element_type=jnp.float32)
    grad_token_out = jnp.einsum("bsc,bjc->sj", grad_token, hidden, preferred_element_type=jnp.float32)
    grad_before = gelu_back(before, hidden_sum).astype(low)
    grad_token_in = jnp.einsum("bsc,bjc->sj", normed_one, grad_before, preferred_element_type=jnp.float32)
    grad_normed_one = jnp.einsum("sj,bjc->bsc", token_in, grad_before, preferred_element_type=jnp.float32)
    first_back = jax.vjp(layer_norm, state, gains[0], gains[1])[1]
    grad_state_norm, grad_gain_one, grad_shift_one = first_back(grad_normed_one)
    token_grads = jnp.stack([grad_token_in, grad_token_out])
    vector_grads = jnp.stack([grad_gain_one, grad_shift_one, grad_gain_two, grad_shift_two])
    return (grad_middle + grad_state_norm, token_grads, grad_channel_in, grad_channel_out, vector_grads)


def body(
    images,
    partner,
    lam,
    labels,
    counts,
    class_weights,
    stem_w,
    stem_m,
    stem_v,
    tok_w,
    tok_m,
    tok_v,
    chan_w,
    chan_m,
    chan_v,
    head_w,
    head_m,
    head_v,
    vec_w,
    vec_m,
    vec_v,
    hb_w,
    hb_m,
    hb_v,
):
    count_dp = lax.axis_size("dp")
    count_tok = lax.axis_size("tok")
    device_row = lax.axis_index("dp")
    token_row = lax.axis_index("tok")
    patches = images.shape[0]
    all_patches = patches * count_tok
    per_device = images.shape[1]
    per_tok = per_device // count_tok
    classes_all = hb_w.shape[0]
    class_pad = -classes_all % (count_tok * LANES)
    width = vec_w.shape[1]

    incoming = swap(images, "dp", count_dp // 2)
    stem_piece = quarter(stem_w.astype(low).T, 1)
    stem_blocks = spread(stem_piece, False)
    chan_low = quarter(chan_w.astype(low), 3)
    chan_blocks = [
        [spread(chan_low[layer, way], way == 1) for way in range(2)] for layer in range(LAYERS)
    ]
    head_piece = quarter(jnp.pad(head_w.astype(low), ((0, 0), (0, class_pad))), 1)
    head_blocks = spread(head_piece, True)
    tok_low = tok_w.astype(low)
    tok_far = swap(tok_low, "tok", 2)
    tok_all = jnp.concatenate([tok_low, tok_far, swap(tok_low, "tok", 1), swap(tok_far, "tok", 1)], 3)

    start = device_row * per_device
    picks = lax.dynamic_slice_in_dim(partner, start, per_device, 0)
    share = lax.dynamic_slice_in_dim(lam, start, per_device, 0)
    place = picks % per_device
    pick = (place[:, None] == jnp.arange(per_device, dtype=jnp.int32)[None, :]).astype(low)
    other = jnp.einsum("kx,sxp->ksp", pick, incoming, preferred_element_type=jnp.float32)
    own = jnp.swapaxes(images, 0, 1).astype(jnp.float32)
    mixed_all = (share[:, None, None] * own + (1 - share)[:, None, None] * other).astype(low)
    groups = mixed_all.reshape(count_tok, per_tok, patches, -1)
    shares = [
        lax.dynamic_index_in_dim(groups, token_row ^ q, 0, keepdims=False) for q in range(count_tok)
    ]
    arrived = [shares[0]] + [swap(shares[q], "tok", q) for q in range(1, count_tok)]
    mixed = jnp.concatenate(arrived, 1)
    mixed = ordered(mixed, 1, False)

    order = row_order()
    rows = jnp.asarray(order, jnp.int32) ^ device_row
    vectors = vec_w.reshape(NV, count_dp, -1)[:, rows].reshape(NV, width)
    stem_all = ordered(joined(stem_blocks), 1, True)
    chan_all = [[joined(blocks) for blocks in pair] for pair in chan_blocks]
    head_all = joined(head_blocks)
    token_low = tok_all

    padded = classes_all + class_pad
    numbers = relative(jnp.arange(padded, dtype=jnp.int32), 0)
    bias = relative(jnp.pad(hb_w, (0, class_pad)), 0)
    own_hot = (labels[:, None] == jnp.arange(classes_all, dtype=jnp.int32)[None, :]).astype(jnp.float32)
    other_labels = jnp.take(labels, partner)
    own_weight = jnp.sum(own_hot * class_weights[None, :], 1)
    other_weight = jnp.take(own_weight, partner)
    live = (
        (jnp.arange(IMG_MB, dtype=jnp.int32)[None, :] < counts.reshape(-1)[:, None])
        .astype(jnp.float32)
        .reshape(-1)
    )
    weights = live * (lam * own_weight + (1 - lam) * other_weight)
    total = jnp.sum(weights)
    first_row = start + token_row * per_tok
    row_of = lambda array: lax.dynamic_slice_in_dim(array, first_row, per_tok, 0)
    lam_rows = row_of(lam)[:, None]
    targets = lam_rows * (row_of(labels)[:, None] == numbers[None, :]).astype(jnp.float32) + (
        1 - lam_rows
    ) * (row_of(other_labels)[:, None] == numbers[None, :]).astype(jnp.float32)
    weight_rows = row_of(weights)

    state = jnp.einsum("bsp,cp->bsc", mixed, stem_all, preferred_element_type=jnp.float32) + vectors[0]
    saved_layers = []
    for layer in range(LAYERS):
        state, saved = layer_forward(
            state,
            token_low[layer, 0],
            token_low[layer, 1],
            chan_all[layer][0],
            chan_all[layer][1],
            vectors[1 + 4 * layer : 5 + 4 * layer],
        )
        saved_layers.append(saved)
    final, final_back = jax.vjp(layer_norm, state, vectors[NV - 2], vectors[NV - 1])
    pooled_low = (jnp.sum(final, 1) / all_patches).astype(low)
    logits = jnp.dot(pooled_low, head_all, preferred_element_type=jnp.float32) + bias
    logits = jnp.where(numbers[None, :] < classes_all, logits, -jnp.inf)
    peak = jnp.max(logits, -1, keepdims=True)
    powers = jnp.exp(logits - peak)
    mass = jnp.sum(powers, -1, keepdims=True)
    log_probs = jnp.where(numbers[None, :] < classes_all, logits - peak - jnp.log(mass), 0.0)
    loss_local = jnp.sum(weight_rows * -jnp.sum(targets * log_probs, -1))
    grad_logits = (weight_rows / total)[:, None] * (
        powers / mass * jnp.sum(targets, -1, keepdims=True) - targets
    )
    head_grad = jnp.dot(pooled_low.astype(jnp.float32).T, grad_logits, precision=highest)
    grad_pooled = jnp.dot(grad_logits, head_all.astype(jnp.float32).T, precision=highest) / all_patches
    head_sum = collect(head_grad, True)
    grad_state, grad_gain_last, grad_shift_last = final_back(
        jnp.broadcast_to(grad_pooled[:, None], final.shape)
    )
    token_list = [None] * LAYERS
    channel_list = [None] * LAYERS
    vector_list = [None] * LAYERS
    for layer in reversed(range(LAYERS)):
        grad_state, token_list[layer], grad_in, grad_out, vector_list[layer] = layer_backward(
            grad_state,
            saved_layers[layer],
            token_low[layer, 0],
            token_low[layer, 1],
            chan_all[layer][0],
            chan_all[layer][1],
            vectors[1 + 4 * layer : 5 + 4 * layer],
        )
        channel_list[layer] = jnp.stack([collect(grad_in, False), collect(grad_out, True)])
    grad_low = grad_state.astype(low)
    stem_grad = jnp.einsum("bsc,bsp->cp", grad_low, mixed, preferred_element_type=jnp.float32)
    stem_bias = jnp.sum(grad_low.astype(jnp.float32), (0, 1))
    stem_sum = ordered(collect(relative(stem_grad, 1), False), 1, True).astype(jnp.float32).T
    vector_part = jnp.concatenate(
        [stem_bias[None]] + vector_list + [grad_gain_last[None], grad_shift_last[None]], 0
    )
    back_rows = jnp.argsort(rows)
    vector_part = vector_part.reshape(NV, count_dp, -1)[:, back_rows].reshape(NV, width)
    bias_part = ordered(jnp.sum(grad_logits, 0), 0, True)[:classes_all]
    token_part = fold(fold(jnp.stack(token_list), 3, "tok", 1), 3, "tok", 2)
    token_grad = lax.psum(token_part, "dp")
    vector_grad, bias_grad, loss_total = lax.psum((vector_part, bias_part, loss_local), ("dp", "tok"))
    chan_grad = ordered(jnp.stack(channel_list), 3, True).astype(jnp.float32)
    head_grad = ordered(head_sum, 1, True)[:, :classes_all].astype(jnp.float32)
    stem_grad = stem_sum
    stem_first, stem_second, stem_update = moments(stem_w, stem_grad, stem_m, stem_v, weight_decay)
    tok_first, tok_second, tok_update = moments(tok_w, token_grad, tok_m, tok_v, weight_decay)
    chan_first, chan_second, chan_update = moments(chan_w, chan_grad, chan_m, chan_v, weight_decay)
    head_first, head_second, head_update = moments(head_w, head_grad, head_m, head_v, weight_decay)
    vec_first, vec_second, vec_update = moments(vec_w, vector_grad, vec_m, vec_v, 0.0)
    hb_first, hb_second, hb_update = moments(hb_w, bias_grad, hb_m, hb_v, 0.0)
    matrix_groups = 2 * LAYERS
    weight_squares = jnp.concatenate(
        [
            row_squares(stem_w, 1) / count_tok,
            row_squares(tok_w, matrix_groups) / count_dp,
            row_squares(chan_w, matrix_groups) / count_tok,
            row_squares(head_w, 1) / count_tok,
        ]
    )
    update_squares = jnp.concatenate(
        [
            row_squares(stem_update, 1) / count_tok,
            row_squares(tok_update, matrix_groups) / count_dp,
            row_squares(chan_update, matrix_groups) / count_tok,
            row_squares(head_update, 1) / count_tok,
        ]
    )
    weight_total, update_total = lax.psum((weight_squares, update_squares), ("dp", "tok"))
    weight_norms = jnp.sqrt(weight_total)
    update_norms = jnp.sqrt(update_total)
    stem_end = 1
    tok_end = 1 + matrix_groups
    chan_end = 1 + 2 * matrix_groups
    stem_new = renew(stem_w, stem_update, weight_norms[0:stem_end], update_norms[0:stem_end], 1)
    tok_new = renew(
        tok_w,
        tok_update,
        weight_norms[stem_end:tok_end],
        update_norms[stem_end:tok_end],
        matrix_groups,
    )
    chan_new = renew(
        chan_w,
        chan_update,
        weight_norms[tok_end:chan_end],
        update_norms[tok_end:chan_end],
        matrix_groups,
    )
    head_new = renew(head_w, head_update, weight_norms[chan_end:], update_norms[chan_end:], 1)
    vec_weight_norm = jnp.sqrt(row_squares(vec_w, NV))
    vec_update_norm = jnp.sqrt(row_squares(vec_update, NV))
    hb_weight_norm = jnp.sqrt(row_squares(hb_w, 1))
    hb_update_norm = jnp.sqrt(row_squares(hb_update, 1))
    vec_new = renew(vec_w, vec_update, vec_weight_norm, vec_update_norm, NV)
    hb_new = renew(hb_w, hb_update, hb_weight_norm, hb_update_norm, 1)
    norms = jnp.stack(
        [
            jnp.concatenate([weight_norms, vec_weight_norm, hb_weight_norm]),
            jnp.concatenate([update_norms, vec_update_norm, hb_update_norm]),
        ],
        1,
    )
    loss_parts = jnp.stack([loss_total, total])
    return (
        stem_new,
        stem_first,
        stem_second,
        tok_new,
        tok_first,
        tok_second,
        chan_new,
        chan_first,
        chan_second,
        head_new,
        head_first,
        head_second,
        vec_new,
        vec_first,
        vec_second,
        hb_new,
        hb_first,
        hb_second,
        stem_new.astype(jnp.bfloat16),
        tok_new.astype(jnp.bfloat16),
        chan_new.astype(jnp.bfloat16),
        head_new.astype(jnp.bfloat16),
        norms,
        loss_parts,
    )


def solution(mesh):
    in_specs = (
        P("tok", "dp", None),
        P(),
        P(),
        P(),
        P(),
        P(),
        P(None, "dp"),
        P(None, "dp"),
        P(None, "dp"),
        P(None, None, None, "tok"),
        P(None, None, None, "tok"),
        P(None, None, None, "tok"),
        P(None, None, "dp", None),
        P(None, None, "dp", None),
        P(None, None, "dp", None),
        P("dp", None),
        P("dp", None),
        P("dp", None),
        P(),
        P(),
        P(),
        P(),
        P(),
        P(),
    )
    out_specs = (
        P(None, "dp"),
        P(None, "dp"),
        P(None, "dp"),
        P(None, None, None, "tok"),
        P(None, None, None, "tok"),
        P(None, None, None, "tok"),
        P(None, None, "dp", None),
        P(None, None, "dp", None),
        P(None, None, "dp", None),
        P("dp", None),
        P("dp", None),
        P("dp", None),
        P(),
        P(),
        P(),
        P(),
        P(),
        P(),
        P(None, "dp"),
        P(None, None, None, "tok"),
        P(None, None, "dp", None),
        P("dp", None),
        P(),
        P(),
    )
    return jax.shard_map(body, mesh=mesh, in_specs=in_specs, out_specs=out_specs, check_vma=False)
```

time: 2160 us -> 810 us (0.38)
  waiting for transfers between devices: 1550 us -> 286 us
  starting transfers between devices: 6.16 us -> 86.2 us
  other arithmetic: 189 us -> 109 us
  blocking collectives: 110 us -> 39.4 us
    reduce_scatter x11 -> x0, waiting for transfers between devices: 886 us -> none  [the longest x1 606 us: body(): lax.psum_scatter(big_total[1], 'dp', scatter_dimension=2, tiled=True)]
    all_gather x11 -> x0, waiting for transfers between devices: 523 us -> none  [the longest x1 363 us: body(): lax.all_gather(chan_w.astype(jnp.bfloat16), 'dp', axis=2, tiled=True)]
    ppermute x2 -> x111, waiting for transfers between devices: 54.8 us -> 226 us  [swap(): return lax.ppermute(array, axis, [(i, i ^ mask) for i in range(count)])]
    ppermute x2 -> x111, starting transfers between devices: 4.18 us -> 86.2 us  [swap(): return lax.ppermute(array, axis, [(i, i ^ mask) for i in range(count)])]
    psum x2 -> x0, blocking collectives: 48.4 us -> none  [the longest x1 35.7 us: body(): lax.psum((token_sum, vector_sum, bias_sum, loss_local), 'dp')]
    another operation x8 -> x10, other arithmetic: 47.7 us -> 1.04 us  [the longest x4 47.7 us: body(): batch_grads = (stem_grad, jnp.stack(channel_list), head_grad)]
    convert_element_type x15 -> x9, other arithmetic: 33.4 us -> 1.5 us  [the longest x1 1.02 us: body(): head_w.astype(low)]
    dot_general x8 -> x0, local copies, waits for them, and re-layouts: 22.5 us -> none  [the longest x4 14.9 us: layer_forward(): jnp.einsum('sj,jbc->sbc', token_out, hidden, preferred_element_type=jnp.f...]
  transfers between devices with their start and end apart: 26 -> 112, of which waited for: 22 -> 42; matrix products, arithmetic and copies ran while one was open for 14% -> 19% of each run, Pallas kernels for 0% -> 0%
where the time goes in v1:
time: 810 us; the launch traced here: 799 us
  waiting for transfers between devices  286 us (35%)
  matrix products  200 us (25%)
  other arithmetic  109 us (13%)
  starting transfers between devices  86.2 us (11%)
  local copies, waits for them, and re-layouts  54.8 us (7%)
  blocking collectives  39.4 us (5%)
  between operations  24.3 us (3%)
    ppermute x111, waiting for transfers between devices, swap(): return lax.ppermute(array, axis, [(i, i ^ mask) for i in range(count)])  226 us
    ppermute x111, starting transfers between devices, swap(): return lax.ppermute(array, axis, [(i, i ^ mask) for i in range(count)])  86.2 us
    dot_general x2, matrix products, layer_backward(): jnp.einsum('bsc,cf->bsf', grad_out, channel_out, preferred_element_type=j...  68.4 us
    psum x1, waiting for transfers between devices, body(): token_grad = lax.psum(token_part, 'dp')  59.7 us
    psum x1, blocking collectives, body(): lax.psum((weight_squares, update_squares), ('dp', 'tok'))  39.4 us
    add x26, other arithmetic, fold(): keep.astype(jnp.float32)  26.8 us
    dot_general x2, matrix products, layer_backward(): jnp.einsum('bsf,cf->bsc', grad_inner, channel_in, preferred_element_type=...  23 us
    slice x30, local copies, waits for them, and re-layouts, halves(): lax.slice_in_dim(array, middle, 2 * middle, axis=axis)  22.4 us
  transfers between devices with their start and end apart: 112, of which 42 were waited for; matrix products, arithmetic and copies ran while one was open for 19% of the time, Pallas kernels for 0%

profile of v1, /device:TPU:0, one launch (start us, length us, event | category | flops | bytes accessed | tf_op | source)
XLA Modules:
  0.0 799.0 jit_solution(4234657743656297336)
XLA Ops:
  9.1 2.6 collective-permute-start.13
  12.7 2.7 collective-permute-start.4
  18.2 2.7 collective-permute-start.34
  39.5 3.2 collective-permute-done.5
  42.7 4.8 collective-permute-start.25
  49.0 5.0 collective-permute-done.53
  55.8 5.4 collective-permute-done.43
  64.3 2.6 collective-permute-done.6
  70.5 8.8 %collective-permute-done.26 = bf16[192,768]{1,0:T(8,128)(2,1)S(1)} collective-permute-done((bf16[192,768]{1,0:T(8,128)(2,1)S(1)}, bf16[192,768]{1,0:T(8,128)(2,1)S(1)}, u32[]{:S(2)}, u32[]{:S(2)}) %collective-permute-start.26) | collective-permute-done | bytes 294944 | tf_op jit(solution)/shard_map/ppermute | solution.py:23
  80.9 4.7 collective-permute-done.17
  91.3 15.8 %collective-permute-done.44 = bf16[192,768]{1,0:T(8,128)(2,1)S(1)} collective-permute-done((bf16[192,768]{1,0:T(8,128)(2,1)S(1)}, bf16[192,768]{1,0:T(8,128)(2,1)S(1)}, u32[]{:S(2)}, u32[]{:S(2)}) %collective-permute-start.44) | collective-permute-done | bytes 294944 | tf_op jit(solution)/shard_map/ppermute | solution.py:23
  107.0 3.2 collective-permute-done.35
  114.7 7.3 maximum_maximum_fusion.1
  129.5 3.7 maximum_maximum_fusion
  133.3 6.7 collective-permute-done.21
  140.4 5.2 collective-permute-done.2
  155.4 2.8 collective-permute-done.27
  158.6 12.2 %collective-permute-done.18 = bf16[384,768]{1,0:T(8,128)(2,1)S(1)} collective-permute-done((bf16[384,768]{1,0:T(8,128)(2,1)}, bf16[384,768]{1,0:T(8,128)(2,1)S(1)}, u32[]{:S(2)}, u32[]{:S(2)}) %collective-permute-start.18) | collective-permute-done | bytes 589856 | tf_op jit(solution)/shard_map/ppermute | solution.py:23
  170.9 12.3 %collective-permute-done.22 = bf16[384,768]{1,0:T(8,128)(2,1)S(1)} collective-permute-done((bf16[384,768]{1,0:T(8,128)(2,1)}, bf16[384,768]{1,0:T(8,128)(2,1)S(1)}, u32[]{:S(2)}, u32[]{:S(2)}) %collective-permute-start.22) | collective-permute-done | bytes 589856 | tf_op jit(solution)/shard_map/ppermute | solution.py:23
  185.4 9.1 %fusion.82 = f32[4,196,3072]{2,1,0:T(8,128)} fusion(f32[4,196,768]{2,1,0:T(8,128)S(1)} %get-tuple-element.262, f32[768]{0:T(1024)S(1)} %add.503, f32[768]{0:T(1024)S(1)} %mul.940, f32[4,196]{1,0:T(4,128)S(1)} %fusion.90, f32[4,196]{1,0:T(4,128)S(1)} %broadcast_multiply_fusion.3, bf16[384,768]{1,0:T(8,128)(2,1)S(1)} %collective-permute-done.24, ...), kind=kOutput, calls=%fused_computation.355 | convolution fusion | flops 3749572608 | bytes 16773248 | tf_op jit(solution)/shard_map/bsc,cf->bsf/dot_general | solution.py:143
  194.6 5.2 collective-permute-done.39
  204.1 10.4 %fusion.131 = (f32[4,196]{1,0:T(4,128)S(1)}, f32[4,196,768]{2,1,0:T(8,128)S(1)}) fusion(f32[4,196,768]{2,1,0:T(8,128)S(1)} %get-tuple-element.262, bf16[384,768]{1,0:T(8,128)(2,1)} %copy-done.169, bf16[384,768]{1,0:T(8,128)(2,1)} %copy-done.167, bf16[384,768]{1,0:T(8,128)(2,1)S(1)} %collective-permute-done.31, ...), kind=kOutput, calls=%fused_computation.494 | convolution fusion | flops 3769441536 | bytes 19172416 | tf_op jit(solution)/shard_map/bsf,cf->bsc/dot_general | solution.py:145
  220.8 8.3 %collective-permute-done.36 = bf16[384,768]{1,0:T(8,128)(2,1)S(1)} collective-permute-done((bf16[384,768]{1,0:T(8,128)(2,1)S(1)}, bf16[384,768]{1,0:T(8,128)(2,1)S(1)}, u32[]{:S(2)}, u32[]{:S(2)}) %collective-permute-start.36) | collective-permute-done | bytes 589856 | tf_op jit(solution)/shard_map/ppermute | solution.py:23
  229.1 10.5 %collective-permute-done.40 = bf16[384,768]{1,0:T(8,128)(2,1)S(1)} collective-permute-done((bf16[384,768]{1,0:T(8,128)(2,1)}, bf16[384,768]{1,0:T(8,128)(2,1)S(1)}, u32[]{:S(2)}, u32[]{:S(2)}) %collective-permute-start.40) | collective-permute-done | bytes 589856 | tf_op jit(solution)/shard_map/ppermute | solution.py:23
  241.6 9.6 %fusion.83 = f32[4,196,3072]{2,1,0:T(8,128)} fusion(f32[4,196,768]{2,1,0:T(8,128)S(1)} %get-tuple-element.266, f32[768]{0:T(1024)S(1)} %add.518, f32[768]{0:T(1024)S(1)} %mul.961, f32[4,196]{1,0:T(4,128)S(1)} %fusion.92, f32[4,196]{1,0:T(4,128)S(1)} %broadcast_multiply_fusion.1, bf16[384,768]{1,0:T(8,128)(2,1)S(1)} %collective-permute-done.42, ...), kind=kOutput, calls=%fused_computation.356 | convolution fusion | flops 3749572608 | bytes 16773248 | tf_op jit(solution)/shard_map/bsc,cf->bsf/dot_general | solution.py:143
  251.3 11.0 %fusion.133 = (f32[4,196]{1,0:T(4,128)S(1)}, f32[4,196,768]{2,1,0:T(8,128)S(1)}) fusion(f32[4,196,768]{2,1,0:T(8,128)S(1)} %get-tuple-element.266, bf16[384,768]{1,0:T(8,128)(2,1)S(1)} %collective-permute-done.51, bf16[384,768]{1,0:T(8,128)(2,1)S(1)} %collective-permute-done.50, bf16[384,768]{1,0:T(8,128)(2,1)S(1)} %collective-permute-done.49, ...), kind=kOutput, calls=%fused_computation.496 | convolution fusion | flops 3769441536 | bytes 19172416 | tf_op jit(solution)/shard_map/bsf,cf->bsc/dot_general | solution.py:145
  270.6 10.2 %convolution_bitcast_fusion = f32[768,3072]{1,0:T(8,128)} fusion(f32[4,196]{1,0:T(4,128)S(1)} %negate_multiply_fusion.4, f32[4,196]{1,0:T(4,128)S(1)} %multiply_multiply_fusion.20, f32[4,196,768]{2,1,0:T(8,128)S(1)} %get-tuple-element.268, f32[4,196]{1,0:T(4,128)S(1)} %broadcast_multiply_fusion, f32[4,196]{1,0:T(4,128)S(1)} %fusion.93, f32[768]{0:T(1024)S(1)} %mul.971, ...), kind=kOutput, calls=%fused_computation.30 | convolution fusion | flops 3725869056 | bytes 21507328 | tf_op jit(solution)/shard_map/bsf,bsc->cf/dot_general | solution.py:152
  280.8 19.3 %fusion.13 = bf16[4,196,3072]{2,1,0:T(8,128)(2,1)} fusion(f32[4,196,3072]{2,1,0:T(8,128)} %fusion.83, f32[4,196]{1,0:T(4,128)S(1)} %negate_multiply_fusion.4, f32[4,196]{1,0:T(4,128)S(1)} %multiply_multiply_fusion.20, f32[4,196,768]{2,1,0:T(8,128)S(1)} %get-tuple-element.268, f32[4,196]{1,0:T(4,128)S(1)} %broadcast_multiply_fusion, ...), kind=kOutput, calls=%fused_computation.21 | convolution fusion | flops 3799547904 | bytes 21605632 | tf_op jit(solution)/shard_map/bsc,cf->bsf/dot_general | solution.py:153
  300.1 15.8 %fusion.106 = (f32[768]{0:T(1024)S(1)}, f32[4,196]{1,0:T(4,128)S(1)}, f32[4,196,768]{2,1,0:T(8,128)S(1)}) fusion(f32[768]{0:T(1024)S(1)} %mul.961, f32[4,196,768]{2,1,0:T(8,128)} %copy-done.5, f32[4,196]{1,0:T(4,128)S(1)} %broadcast_multiply_fusion.1, bf16[4,196,3072]{2,1,0:T(8,128)(2,1)} %fusion.13, bf16[384,768]{1,0:T(8,128)(2,1)} %copy-done.176, ...), kind=kOutput, calls=%fused_computation.481 | convolution fusion | flops 3749571072 | bytes 14364800 | tf_op jit(solution)/shard_map/bsf,cf->bsc/dot_general | solution.py:156
  321.2 4.0 fusion.28
  331.8 7.8 convolution_bitcast_fusion.2
  339.8 49.1 %fusion.6 = bf16[4,196,3072]{2,1,0:T(8,128)(2,1)} fusion(f32[4,196,3072]{2,1,0:T(8,128)} %fusion.82, bf16[4,196,768]{2,1,0:T(8,128)(2,1)S(1)} %fusion.50, bf16[384,768]{1,0:T(8,128)(2,1)S(1)} %copy-done.170, bf16[384,768]{1,0:T(8,128)(2,1)S(1)} %copy-done.168, bf16[384,768]{1,0:T(8,128)(2,1)S(1)} %copy-done.162, bf16[384,768]{1,0:T(8,128)(2,1)S(1)} %copy-done.148, ...), kind=kOutput, calls=%fused_computation.14 | convolution fusion | flops 3794731008 | bytes 20373504 | tf_op jit(solution)/shard_map/bsc,cf->bsf/dot_general | solution.py:153
  389.0 7.2 fusion.107
  399.0 4.3 convolution_bitcast_fusion.7
  403.4 4.0 fusion.21
  410.0 7.9 convolution_bitcast_fusion.3
  417.9 8.0 convolution_bitcast_fusion.1
  442.9 4.0 slice.636
  446.9 4.1 slice.638
  451.0 4.0 slice.637
  455.0 4.0 slice.635
  469.9 5.3 collective-permute-done.62
  476.6 59.7 %all-reduce.5.cloned.1.call-done = f32[2,2,196,96]{3,2,1,0:T(8,128)} async-done(((f32[2,2,196,96]{3,2,1,0:T(8,128)}), f32[2,2,196,96]{3,2,1,0:T(8,128)}) %all-reduce.5.cloned.1.call-update) | async-done | bytes 301072 | tf_op jit(solution)/shard_map/psum | solution.py:325
  561.9 2.6 multiply_reduce_fusion.18
  566.5 2.8 multiply_reduce_fusion.15
  570.6 3.9 slice_add_fusion
  577.3 3.9 slice_add_fusion.2
  582.8 2.9 slice_add_fusion.3
  588.4 2.5 slice_add_fusion.1
  591.6 13.2 %collective-permute-done.96 = bf16[384,1536]{1,0:T(8,128)(2,1)} collective-permute-done((bf16[384,1536]{1,0:T(8,128)(2,1)}, bf16[384,1536]{1,0:T(8,128)(2,1)}, u32[]{:S(2)}, u32[]{:S(2)}) %collective-permute-start.96) | collective-permute-done | bytes 1179680 | tf_op jit(solution)/shard_map/ppermute | solution.py:23
  608.1 21.1 %collective-permute-done.80 = bf16[384,1536]{1,0:T(8,128)(2,1)} collective-permute-done((bf16[384,1536]{1,0:T(8,128)(2,1)}, bf16[384,1536]{1,0:T(8,128)(2,1)}, u32[]{:S(2)}, u32[]{:S(2)}) %collective-permute-start.80) | collective-permute-done | bytes 1179680 | tf_op jit(solution)/shard_map/ppermute | solution.py:23
  635.9 5.4 collective-permute-done.88
  643.4 10.5 %collective-permute-done.97 = bf16[384,768]{1,0:T(8,128)(2,1)S(1)} collective-permute-done((bf16[384,768]{1,0:T(8,128)(2,1)S(1)}, bf16[384,768]{1,0:T(8,128)(2,1)S(1)}, u32[]{:S(2)}, u32[]{:S(2)}) %collective-permute-start.97) | collective-permute-done | bytes 589856 | tf_op jit(solution)/shard_map/ppermute | solution.py:23
  655.2 9.8 %collective-permute-done.81 = bf16[384,768]{1,0:T(8,128)(2,1)S(1)} collective-permute-done((bf16[384,768]{1,0:T(8,128)(2,1)S(1)}, bf16[384,768]{1,0:T(8,128)(2,1)S(1)}, u32[]{:S(2)}, u32[]{:S(2)}) %collective-permute-start.81) | collective-permute-done | bytes 589856 | tf_op jit(solution)/shard_map/ppermute | solution.py:23
  671.0 9.0 %collective-permute-done.82 = bf16[192,768]{1,0:T(8,128)(2,1)S(1)} collective-permute-done((bf16[192,768]{1,0:T(8,128)(2,1)S(1)}, bf16[192,768]{1,0:T(8,128)(2,1)S(1)}, u32[]{:S(2)}, u32[]{:S(2)}) %collective-permute-start.82) | collective-permute-done | bytes 294944 | tf_op jit(solution)/shard_map/ppermute | solution.py:23
  680.7 7.3 collective-permute-done.74
  688.2 4.1 collective-permute-done.90
  694.4 5.3 collective-permute-done.83
  699.8 3.0 collective-permute-done.75
  706.2 3.1 collective-permute-done.84
  713.1 2.9 collective-permute-done.92
  719.9 7.9 multiply_reduce_fusion
  728.1 39.4 %all-reduce.2 = (f32[10]{0:T(128)S(1)}, f32[10]{0:T(128)S(1)}, f32[11,768]{1,0:T(8,128)}, f32[1000]{0:T(1024)S(1)}, f32[1]{0:T(128)}) all-reduce(f32[10]{0:T(128)S(1)} %pad_maximum_fusion.27, f32[10]{0:T(128)S(1)} %pad_maximum_fusion.28, f32[11,768]{1,0:T(8,128)S(1)} %reshape.448, ...), channel_id=1, replica_groups=mesh['dp'=8,'tok'=4] {'dp','tok'}, use_global_device_ids=true, to_apply=%region_4.5 | all-reduce | flops 9469 | bytes 75752 | tf_op jit(solution)/shard_map/psum | solution.py:353
  783.6 8.3 %fusion.109 = (bf16[2,2,96,3072]{3,2,1,0:T(8,128)(2,1)}, f32[2,2,96,3072]{3,2,1,0:T(8,128)}) fusion(f32[2,2,96,3072]{3,2,1,0:T(8,128)} %param.37, f32[2,2,96,3072]{3,2,1,0:T(8,128)} %get-tuple-element.187, f32[2,2,96,3072]{3,2,1,0:T(8,128)} %get-tuple-element.186, f32[2,2]{1,0:T(2,128)S(1)} %div.349), kind=kLoop, calls=%fused_computation.484 | loop fusion | flops 11796480 | bytes 21233680 | tf_op jit(solution)/shard_map/convert_element_type | solution.py:410
  (866 shorter events, 211.2 us)
Async XLA Ops:
  7.3 529.1 %all-reduce.5.cloned.1.call-start = ((), (), s32[]{:S(2)}) async-start(), calls=%async_computation | async-start | bytes 819200 | tf_op jit(solution)/shard_map/psum | solution.py:325
  8.6 52.9 %collective-permute-start.14 = (bf16[2,2,196,96]{3,2,1,0:T(8,128)(2,1)S(1)}, bf16[2,2,196,96]{3,2,1,0:T(8,128)(2,1)S(1)}, u32[]{:S(2)}, u32[]{:S(2)}) collective-permute-start(bf16[2,2,196,96]{3,2,1,0:T(8,128)(2,1)S(1)} %convert_element_type.257), channel_id=1, source_target_pairs={{0,1},{1,0},{2,3},{3,2},{4,5},{5,4},{6,7},{7,6},{8,9},{9,8},{10,11... | collective-permute-start | bytes 451592 | tf_op jit(solution)/shard_map/ppermute | solution.py:23
  9.1 52.4 %collective-permute-start.13 = (bf16[2,2,196,96]{3,2,1,0:T(8,128)(2,1)S(1)}, bf16[2,2,196,96]{3,2,1,0:T(8,128)(2,1)}, u32[]{:S(2)}, u32[]{:S(2)}) collective-permute-start(bf16[2,2,196,96]{3,2,1,0:T(8,128)(2,1)S(1)} %convert_element_type.257), channel_id=1, source_target_pairs={{0,2},{1,3},{2,0},{3,1},{4,6},{5,7},{6,4},{7,5},{8,10},{9,11},{10,... | collective-permute-start | bytes 451592 | tf_op jit(solution)/shard_map/ppermute | solution.py:23
  12.7 24.7 %collective-permute-start.4 = (bf16[96,192]{1,0:T(8,128)(2,1)S(1)}, bf16[96,192]{1,0:T(8,128)(2,1)S(1)}, u32[]{:S(2)}, u32[]{:S(2)}) collective-permute-start(bf16[96,192]{1,0:T(8,128)(2,1)S(1)} %fusion.81), channel_id=1, source_target_pairs={{0,16},{4,20},{8,24},{12,28},{16,0},{20,4},{24,8},{28,12},{1,17},{... | collective-permute-start | bytes 110600 | tf_op jit(solution)/shard_map/ppermute | solution.py:23
  16.4 21.4 %collective-permute-start.52 = (bf16[96,256]{1,0:T(8,128)(2,1)S(1)}, bf16[96,256]{1,0:T(8,128)(2,1)S(1)}, u32[]{:S(2)}, u32[]{:S(2)}) collective-permute-start(bf16[96,256]{1,0:T(8,128)(2,1)S(1)} %pad_dynamic-slice_fusion), channel_id=1, source_target_pairs={{0,16},{4,20},{8,24},{12,28},{16,0},{20,4},{24,8},{28,12},{1,17},{... | collective-permute-start | bytes 147464 | tf_op jit(solution)/shard_map/ppermute | solution.py:23
  18.2 37.4 %collective-permute-start.34 = (bf16[96,768]{1,0:T(8,128)(2,1)S(1)}, bf16[96,768]{1,0:T(8,128)(2,1)S(1)}, u32[]{:S(2)}, u32[]{:S(2)}) collective-permute-start(bf16[96,768]{1,0:T(8,128)(2,1)S(1)} %get-tuple-element.223), channel_id=1, source_target_pairs={{0,16},{4,20},{8,24},{12,28},{16,0},{20,4},{24,8},{28,12},{1,17},{... | collective-permute-start | bytes 442376 | tf_op jit(solution)/shard_map/ppermute | solution.py:23
  61.5 17.8 %collective-permute-start.26 = (bf16[192,768]{1,0:T(8,128)(2,1)S(1)}, bf16[192,768]{1,0:T(8,128)(2,1)S(1)}, u32[]{:S(2)}, u32[]{:S(2)}) collective-permute-start(bf16[192,768]{1,0:T(8,128)(2,1)S(1)} %pad_maximum_fusion.11), channel_id=1, source_target_pairs={{0,8},{4,12},{8,0},{12,4},{16,24},{20,28},{24,16},{28,20},{1,9},{5... | collective-permute-start | bytes 884744 | tf_op jit(solution)/shard_map/ppermute | solution.py:23
  61.5 24.1 %collective-permute-start.17 = (bf16[192,768]{1,0:T(8,128)(2,1)S(1)}, bf16[192,768]{1,0:T(8,128)(2,1)S(1)}, u32[]{:S(2)}, u32[]{:S(2)}) collective-permute-start(bf16[192,768]{1,0:T(8,128)(2,1)S(1)} %pad_maximum_fusion.10), channel_id=1, source_target_pairs={{0,8},{4,12},{8,0},{12,4},{16,24},{20,28},{24,16},{28,20},{1,9},{5... | collective-permute-start | bytes 884744 | tf_op jit(solution)/shard_map/ppermute | solution.py:23
  63.6 60.3 %collective-permute-start = (bf16[49,16,768]{2,1,0:T(8,128)(2,1)S(1)}, bf16[49,16,768]{2,1,0:T(8,128)(2,1)S(1)}, u32[]{:S(2)}, u32[]{:S(2)}) collective-permute-start(bf16[49,16,768]{2,1,0:T(8,128)(2,1)S(1)} %copy-done.36), channel_id=1, source_target_pairs={{0,16},{4,20},{8,24},{12,28},{16,0},{20,4},{24,8},{28,12},{1,17},{... | collective-permute-start | bytes 3612680 | tf_op jit(solution)/shard_map/ppermute | solution.py:23
  66.9 40.1 %collective-permute-start.44 = (bf16[192,768]{1,0:T(8,128)(2,1)S(1)}, bf16[192,768]{1,0:T(8,128)(2,1)S(1)}, u32[]{:S(2)}, u32[]{:S(2)}) collective-permute-start(bf16[192,768]{1,0:T(8,128)(2,1)S(1)} %pad_maximum_fusion.13), channel_id=1, source_target_pairs={{0,8},{4,12},{8,0},{12,4},{16,24},{20,28},{24,16},{28,20},{1,9},{5... | collective-permute-start | bytes 884744 | tf_op jit(solution)/shard_map/ppermute | solution.py:23
  67.0 43.2 %collective-permute-start.35 = (bf16[192,768]{1,0:T(8,128)(2,1)S(1)}, bf16[192,768]{1,0:T(8,128)(2,1)S(1)}, u32[]{:S(2)}, u32[]{:S(2)}) collective-permute-start(bf16[192,768]{1,0:T(8,128)(2,1)S(1)} %pad_maximum_fusion.12), channel_id=1, source_target_pairs={{0,8},{4,12},{8,0},{12,4},{16,24},{20,28},{24,16},{28,20},{1,9},{5... | collective-permute-start | bytes 884744 | tf_op jit(solution)/shard_map/ppermute | solution.py:23
  87.7 24.3 %collective-permute-start.54 = (bf16[384,256]{1,0:T(8,128)(2,1)}, bf16[384,256]{1,0:T(8,128)(2,1)}, u32[]{:S(2)}, u32[]{:S(2)}) collective-permute-start(bf16[384,256]{1,0:T(8,128)(2,1)} %pad_maximum_fusion.18), channel_id=1, source_target_pairs={{0,2},{1,3},{2,0},{3,1},{4,6},{5,7},{6,4},{7,5},{8,10},{9,11},{10,... | collective-permute-start | bytes 589832 | tf_op jit(solution)/shard_map/ppermute | solution.py:23
  91.3 21.2 %collective-permute-start.11 = (bf16[384,192]{1,0:T(8,128)(2,1)S(1)}, bf16[384,192]{1,0:T(8,128)(2,1)S(1)}, u32[]{:S(2)}, u32[]{:S(2)}) collective-permute-start(bf16[384,192]{1,0:T(8,128)(2,1)S(1)} %collective-permute-done.9), channel_id=1, source_target_pairs={{0,1},{1,0},{2,3},{3,2},{4,5},{5,4},{6,7},{7,6},{8,9},{9,8},{10,11... | collective-permute-start | bytes 442376 | tf_op jit(solution)/shard_map/ppermute | solution.py:23
  112.0 13.5 %collective-permute-start.55 = (bf16[384,256]{1,0:T(8,128)(2,1)}, bf16[384,256]{1,0:T(8,128)(2,1)}, u32[]{:S(2)}, u32[]{:S(2)}) collective-permute-start(bf16[384,256]{1,0:T(8,128)(2,1)} %pad_maximum_fusion.18), channel_id=1, source_target_pairs={{0,1},{1,0},{2,3},{3,2},{4,5},{5,4},{6,7},{7,6},{8,9},{9,8},{10,11... | collective-permute-start | bytes 589832 | tf_op jit(solution)/shard_map/ppermute | solution.py:23
  114.1 13.6 %collective-permute-start.56 = (bf16[384,256]{1,0:T(8,128)(2,1)}, bf16[384,256]{1,0:T(8,128)(2,1)}, u32[]{:S(2)}, u32[]{:S(2)}) collective-permute-start(bf16[384,256]{1,0:T(8,128)(2,1)} %collective-permute-done.54), channel_id=1, source_target_pairs={{0,1},{1,0},{2,3},{3,2},{4,5},{5,4},{6,7},{7,6},{8,9},{9,8},{10,11... | collective-permute-start | bytes 589832 | tf_op jit(solution)/shard_map/ppermute | solution.py:23
  123.5 16.5 %collective-permute-start.21 = (bf16[384,768]{1,0:T(8,128)(2,1)}, bf16[384,768]{1,0:T(8,128)(2,1)}, u32[]{:S(2)}, u32[]{:S(2)}) collective-permute-start(bf16[384,768]{1,0:T(8,128)(2,1)} %pad_maximum_fusion.5), channel_id=1, source_target_pairs={{0,4},{4,0},{8,12},{12,8},{16,20},{20,16},{24,28},{28,24},{1,5},{5... | collective-permute-start | bytes 1769480 | tf_op jit(solution)/shard_map/ppermute | solution.py:23
  125.9 29.4 %collective-permute-start.30 = (bf16[384,768]{1,0:T(8,128)(2,1)S(1)}, bf16[384,768]{1,0:T(8,128)(2,1)S(1)}, u32[]{:S(2)}, u32[]{:S(2)}) collective-permute-start(bf16[384,768]{1,0:T(8,128)(2,1)S(1)} %copy-done.52), channel_id=1, source_target_pairs={{0,4},{4,0},{8,12},{12,8},{16,20},{20,16},{24,28},{28,24},{1,5},{5... | collective-permute-start | bytes 1769480 | tf_op jit(solution)/shard_map/ppermute | solution.py:23
  127.7 17.9 %collective-permute-start.2 = (bf16[4,49,768]{2,1,0:T(8,128)(2,1)S(1)}, bf16[4,49,768]{2,1,0:T(8,128)(2,1)S(1)}, u32[]{:S(2)}, u32[]{:S(2)}) collective-permute-start(bf16[4,49,768]{2,1,0:T(8,128)(2,1)S(1)} %bitcast.290), channel_id=1, source_target_pairs={{0,2},{1,3},{2,0},{3,1},{4,6},{5,7},{6,4},{7,5},{8,10},{9,11},{10,... | collective-permute-start | bytes 903176 | tf_op jit(solution)/shard_map/ppermute | solution.py:23
  129.4 16.5 %collective-permute-start.3 = (bf16[4,49,768]{2,1,0:T(8,128)(2,1)S(1)}, bf16[4,49,768]{2,1,0:T(8,128)(2,1)S(1)}, u32[]{:S(2)}, u32[]{:S(2)}) collective-permute-start(bf16[4,49,768]{2,1,0:T(8,128)(2,1)S(1)} %bitcast.289), channel_id=1, source_target_pairs={{0,1},{1,0},{2,3},{3,2},{4,5},{5,4},{6,7},{7,6},{8,9},{9,8},{10,11... | collective-permute-start | bytes 903176 | tf_op jit(solution)/shard_map/ppermute | solution.py:23
  140.0 18.2 %collective-permute-start.27 = (bf16[384,768]{1,0:T(8,128)(2,1)S(1)}, bf16[384,768]{1,0:T(8,128)(2,1)S(1)}, u32[]{:S(2)}, u32[]{:S(2)}) collective-permute-start(bf16[384,768]{1,0:T(8,128)(2,1)S(1)} %copy-done.52), channel_id=1, source_target_pairs={{0,2},{1,3},{2,0},{3,1},{4,6},{5,7},{6,4},{7,5},{8,10},{9,11},{10,... | collective-permute-start | bytes 1769480 | tf_op jit(solution)/shard_map/ppermute | solution.py:23
  140.3 43.4 %collective-permute-start.19 = (bf16[384,768]{1,0:T(8,128)(2,1)}, bf16[384,768]{1,0:T(8,128)(2,1)S(1)}, u32[]{:S(2)}, u32[]{:S(2)}) collective-permute-start(bf16[384,768]{1,0:T(8,128)(2,1)} %pad_maximum_fusion.5), channel_id=1, source_target_pairs={{0,1},{1,0},{2,3},{3,2},{4,5},{5,4},{6,7},{7,6},{8,9},{9,8},{10,11... | collective-permute-start | bytes 1769480 | tf_op jit(solution)/shard_map/ppermute | solution.py:23
  145.6 25.3 %collective-permute-start.18 = (bf16[384,768]{1,0:T(8,128)(2,1)}, bf16[384,768]{1,0:T(8,128)(2,1)S(1)}, u32[]{:S(2)}, u32[]{:S(2)}) collective-permute-start(bf16[384,768]{1,0:T(8,128)(2,1)} %pad_maximum_fusion.5), channel_id=1, source_target_pairs={{0,2},{1,3},{2,0},{3,1},{4,6},{5,7},{6,4},{7,5},{8,10},{9,11},{10,... | collective-permute-start | bytes 1769480 | tf_op jit(solution)/shard_map/ppermute | solution.py:23
  145.9 37.2 %collective-permute-start.22 = (bf16[384,768]{1,0:T(8,128)(2,1)}, bf16[384,768]{1,0:T(8,128)(2,1)S(1)}, u32[]{:S(2)}, u32[]{:S(2)}) collective-permute-start(bf16[384,768]{1,0:T(8,128)(2,1)} %collective-permute-done.21), channel_id=1, source_target_pairs={{0,2},{1,3},{2,0},{3,1},{4,6},{5,7},{6,4},{7,5},{8,10},{9,11},{10,... | collective-permute-start | bytes 1769480 | tf_op jit(solution)/shard_map/ppermute | solution.py:23
  155.3 29.5 %collective-permute-start.23 = (bf16[384,768]{1,0:T(8,128)(2,1)}, bf16[384,768]{1,0:T(8,128)(2,1)S(1)}, u32[]{:S(2)}, u32[]{:S(2)}) collective-permute-start(bf16[384,768]{1,0:T(8,128)(2,1)} %collective-permute-done.21), channel_id=1, source_target_pairs={{0,1},{1,0},{2,3},{3,2},{4,5},{5,4},{6,7},{7,6},{8,9},{9,8},{10,11... | collective-permute-start | bytes 1769480 | tf_op jit(solution)/shard_map/ppermute | solution.py:23
  158.2 26.1 %collective-permute-start.31 = (bf16[384,768]{1,0:T(8,128)(2,1)S(1)}, bf16[384,768]{1,0:T(8,128)(2,1)S(1)}, u32[]{:S(2)}, u32[]{:S(2)}) collective-permute-start(bf16[384,768]{1,0:T(8,128)(2,1)S(1)} %collective-permute-done.27), channel_id=1, source_target_pairs={{0,4},{4,0},{8,12},{12,8},{16,20},{20,16},{24,28},{28,24},{1,5},{5... | collective-permute-start | bytes 1769480 | tf_op jit(solution)/shard_map/ppermute | solution.py:23
  170.9 13.9 %collective-permute-start.20 = (bf16[384,768]{1,0:T(8,128)(2,1)S(1)}, bf16[384,768]{1,0:T(8,128)(2,1)S(1)}, u32[]{:S(2)}, u32[]{:S(2)}) collective-permute-start(bf16[384,768]{1,0:T(8,128)(2,1)S(1)} %collective-permute-done.18), channel_id=1, source_target_pairs={{0,1},{1,0},{2,3},{3,2},{4,5},{5,4},{6,7},{7,6},{8,9},{9,8},{10,11... | collective-permute-start | bytes 1769480 | tf_op jit(solution)/shard_map/ppermute | solution.py:23
  183.7 16.4 %collective-permute-start.28 = (bf16[384,768]{1,0:T(8,128)(2,1)S(1)}, bf16[384,768]{1,0:T(8,128)(2,1)S(1)}, u32[]{:S(2)}, u32[]{:S(2)}) collective-permute-start(bf16[384,768]{1,0:T(8,128)(2,1)S(1)} %copy-done.52), channel_id=1, source_target_pairs={{0,1},{1,0},{2,3},{3,2},{4,5},{5,4},{6,7},{7,6},{8,9},{9,8},{10,11... | collective-permute-start | bytes 1769480 | tf_op jit(solution)/shard_map/ppermute | solution.py:23
  184.3 15.4 %collective-permute-start.39 = (bf16[384,768]{1,0:T(8,128)(2,1)S(1)}, bf16[384,768]{1,0:T(8,128)(2,1)}, u32[]{:S(2)}, u32[]{:S(2)}) collective-permute-start(bf16[384,768]{1,0:T(8,128)(2,1)S(1)} %copy-done.51), channel_id=1, source_target_pairs={{0,4},{4,0},{8,12},{12,8},{16,20},{20,16},{24,28},{28,24},{1,5},{5... | collective-permute-start | bytes 1769480 | tf_op jit(solution)/shard_map/ppermute | solution.py:23
  184.8 16.1 %collective-permute-start.29 = (bf16[384,768]{1,0:T(8,128)(2,1)S(1)}, bf16[384,768]{1,0:T(8,128)(2,1)S(1)}, u32[]{:S(2)}, u32[]{:S(2)}) collective-permute-start(bf16[384,768]{1,0:T(8,128)(2,1)S(1)} %collective-permute-done.27), channel_id=1, source_target_pairs={{0,1},{1,0},{2,3},{3,2},{4,5},{5,4},{6,7},{7,6},{8,9},{9,8},{10,11... | collective-permute-start | bytes 1769480 | tf_op jit(solution)/shard_map/ppermute | solution.py:23
  184.8 16.1 %collective-permute-start.32 = (bf16[384,768]{1,0:T(8,128)(2,1)S(1)}, bf16[384,768]{1,0:T(8,128)(2,1)S(1)}, u32[]{:S(2)}, u32[]{:S(2)}) collective-permute-start(bf16[384,768]{1,0:T(8,128)(2,1)S(1)} %collective-permute-done.30), channel_id=1, source_target_pairs={{0,1},{1,0},{2,3},{3,2},{4,5},{5,4},{6,7},{7,6},{8,9},{9,8},{10,11... | collective-permute-start | bytes 1769480 | tf_op jit(solution)/shard_map/ppermute | solution.py:23
  185.3 17.0 %collective-permute-start.33 = (bf16[384,768]{1,0:T(8,128)(2,1)S(1)}, bf16[384,768]{1,0:T(8,128)(2,1)S(1)}, u32[]{:S(2)}, u32[]{:S(2)}) collective-permute-start(bf16[384,768]{1,0:T(8,128)(2,1)S(1)} %collective-permute-done.31), channel_id=1, source_target_pairs={{0,1},{1,0},{2,3},{3,2},{4,5},{5,4},{6,7},{7,6},{8,9},{9,8},{10,11... | collective-permute-start | bytes 1769480 | tf_op jit(solution)/shard_map/ppermute | solution.py:23
  199.7 19.3 %collective-permute-start.48 = (bf16[384,768]{1,0:T(8,128)(2,1)S(1)}, bf16[384,768]{1,0:T(8,128)(2,1)}, u32[]{:S(2)}, u32[]{:S(2)}) collective-permute-start(bf16[384,768]{1,0:T(8,128)(2,1)S(1)} %copy-done.50), channel_id=1, source_target_pairs={{0,4},{4,0},{8,12},{12,8},{16,20},{20,16},{24,28},{28,24},{1,5},{5... | collective-permute-start | bytes 1769480 | tf_op jit(solution)/shard_map/ppermute | solution.py:23
  200.2 18.9 %collective-permute-start.45 = (bf16[384,768]{1,0:T(8,128)(2,1)S(1)}, bf16[384,768]{1,0:T(8,128)(2,1)}, u32[]{:S(2)}, u32[]{:S(2)}) collective-permute-start(bf16[384,768]{1,0:T(8,128)(2,1)S(1)} %copy-done.50), channel_id=1, source_target_pairs={{0,2},{1,3},{2,0},{3,1},{4,6},{5,7},{6,4},{7,5},{8,10},{9,11},{10,... | collective-permute-start | bytes 1769480 | tf_op jit(solution)/shard_map/ppermute | solution.py:23
  200.9 39.2 %collective-permute-start.37 = (bf16[384,768]{1,0:T(8,128)(2,1)S(1)}, bf16[384,768]{1,0:T(8,128)(2,1)S(1)}, u32[]{:S(2)}, u32[]{:S(2)}) collective-permute-start(bf16[384,768]{1,0:T(8,128)(2,1)S(1)} %copy-done.51), channel_id=1, source_target_pairs={{0,1},{1,0},{2,3},{3,2},{4,5},{5,4},{6,7},{7,6},{8,9},{9,8},{10,11... | collective-permute-start | bytes 1769480 | tf_op jit(solution)/shard_map/ppermute | solution.py:23
  200.9 28.1 %collective-permute-start.36 = (bf16[384,768]{1,0:T(8,128)(2,1)S(1)}, bf16[384,768]{1,0:T(8,128)(2,1)S(1)}, u32[]{:S(2)}, u32[]{:S(2)}) collective-permute-start(bf16[384,768]{1,0:T(8,128)(2,1)S(1)} %copy-done.51), channel_id=1, source_target_pairs={{0,2},{1,3},{2,0},{3,1},{4,6},{5,7},{6,4},{7,5},{8,10},{9,11},{10,... | collective-permute-start | bytes 1769480 | tf_op jit(solution)/shard_map/ppermute | solution.py:23
  203.1 36.5 %collective-permute-start.40 = (bf16[384,768]{1,0:T(8,128)(2,1)}, bf16[384,768]{1,0:T(8,128)(2,1)S(1)}, u32[]{:S(2)}, u32[]{:S(2)}) collective-permute-start(bf16[384,768]{1,0:T(8,128)(2,1)} %collective-permute-done.39), channel_id=1, source_target_pairs={{0,2},{1,3},{2,0},{3,1},{4,6},{5,7},{6,4},{7,5},{8,10},{9,11},{10,... | collective-permute-start | bytes 1769480 | tf_op jit(solution)/shard_map/ppermute | solution.py:23
  219.0 21.8 %collective-permute-start.41 = (bf16[384,768]{1,0:T(8,128)(2,1)}, bf16[384,768]{1,0:T(8,128)(2,1)S(1)}, u32[]{:S(2)}, u32[]{:S(2)}) collective-permute-start(bf16[384,768]{1,0:T(8,128)(2,1)} %collective-permute-done.39), channel_id=1, source_target_pairs={{0,1},{1,0},{2,3},{3,2},{4,5},{5,4},{6,7},{7,6},{8,9},{9,8},{10,11... | collective-permute-start | bytes 1769480 | tf_op jit(solution)/shard_map/ppermute | solution.py:23
  219.1 21.6 %collective-permute-start.49 = (bf16[384,768]{1,0:T(8,128)(2,1)}, bf16[384,768]{1,0:T(8,128)(2,1)S(1)}, u32[]{:S(2)}, u32[]{:S(2)}) collective-permute-start(bf16[384,768]{1,0:T(8,128)(2,1)} %collective-permute-done.45), channel_id=1, source_target_pairs={{0,4},{4,0},{8,12},{12,8},{16,20},{20,16},{24,28},{28,24},{1,5},{5... | collective-permute-start | bytes 1769480 | tf_op jit(solution)/shard_map/ppermute | solution.py:23
  434.2 27.2 %collective-permute-start.61 = (bf16[768,384]{1,0:T(8,128)(2,1)}, bf16[768,384]{1,0:T(8,128)(2,1)}, u32[]{:S(2)}, u32[]{:S(2)}) collective-permute-start(bf16[768,384]{1,0:T(8,128)(2,1)} %pad_maximum_fusion.9), channel_id=1, source_target_pairs={{0,1},{1,0},{2,3},{3,2},{4,5},{5,4},{6,7},{7,6},{8,9},{9,8},{10,11... | collective-permute-start | bytes 1769480 | tf_op jit(solution)/shard_map/ppermute | solution.py:23
  435.5 29.5 %collective-permute-start.103 = (bf16[768,512]{1,0:T(8,128)(2,1)}, bf16[768,512]{1,0:T(8,128)(2,1)}, u32[]{:S(2)}, u32[]{:S(2)}) collective-permute-start(bf16[768,512]{1,0:T(8,128)(2,1)} %slice.643), channel_id=1, source_target_pairs={{0,1},{1,0},{2,3},{3,2},{4,5},{5,4},{6,7},{7,6},{8,9},{9,8},{10,11... | collective-permute-start | bytes 2359304 | tf_op jit(solution)/shard_map/ppermute | solution.py:23
  437.6 22.0 %collective-permute-start.70 = (bf16[2,2,196,96]{3,2,1,0:T(8,128)(2,1)S(1)}, bf16[2,2,196,96]{3,2,1,0:T(8,128)(2,1)}, u32[]{:S(2)}, u32[]{:S(2)}) collective-permute-start(bf16[2,2,196,96]{3,2,1,0:T(8,128)(2,1)S(1)} %slice.654), channel_id=1, source_target_pairs={{0,2},{1,3},{2,0},{3,1},{4,6},{5,7},{6,4},{7,5},{8,10},{9,11},{10,... | collective-permute-start | bytes 451592 | tf_op jit(solution)/shard_map/ppermute | solution.py:23
  459.1 111.5 %collective-permute-start.95 = (bf16[768,1536]{1,0:T(8,128)(2,1)}, bf16[768,1536]{1,0:T(8,128)(2,1)}, u32[]{:S(2)}, u32[]{:S(2)}) collective-permute-start(bf16[768,1536]{1,0:T(8,128)(2,1)} %slice.635), channel_id=1, source_target_pairs={{0,1},{1,0},{2,3},{3,2},{4,5},{5,4},{6,7},{7,6},{8,9},{9,8},{10,11... | collective-permute-start | bytes 7077896 | tf_op jit(solution)/shard_map/ppermute | solution.py:23
  459.1 118.3 %collective-permute-start.79 = (bf16[768,1536]{1,0:T(8,128)(2,1)}, bf16[768,1536]{1,0:T(8,128)(2,1)}, u32[]{:S(2)}, u32[]{:S(2)}) collective-permute-start(bf16[768,1536]{1,0:T(8,128)(2,1)} %slice.637), channel_id=1, source_target_pairs={{0,1},{1,0},{2,3},{3,2},{4,5},{5,4},{6,7},{7,6},{8,9},{9,8},{10,11... | collective-permute-start | bytes 7077896 | tf_op jit(solution)/shard_map/ppermute | solution.py:23
  459.6 123.2 %collective-permute-start.71 = (bf16[768,1536]{1,0:T(8,128)(2,1)}, bf16[768,1536]{1,0:T(8,128)(2,1)}, u32[]{:S(2)}, u32[]{:S(2)}) collective-permute-start(bf16[768,1536]{1,0:T(8,128)(2,1)} %slice.638), channel_id=1, source_target_pairs={{0,1},{1,0},{2,3},{3,2},{4,5},{5,4},{6,7},{7,6},{8,9},{9,8},{10,11... | collective-permute-start | bytes 7077896 | tf_op jit(solution)/shard_map/ppermute | solution.py:23
  468.3 72.0 %collective-permute-start.104 = (bf16[384,512]{1,0:T(8,128)(2,1)}, bf16[384,512]{1,0:T(8,128)(2,1)}, u32[]{:S(2)}, u32[]{:S(2)}) collective-permute-start(bf16[384,512]{1,0:T(8,128)(2,1)} %slice.648), channel_id=1, source_target_pairs={{0,4},{4,0},{8,12},{12,8},{16,20},{20,16},{24,28},{28,24},{1,5},{5... | collective-permute-start | bytes 1179656 | tf_op jit(solution)/shard_map/ppermute | solution.py:23
  475.3 62.7 %collective-permute-start.63 = (bf16[384,192]{1,0:T(8,128)(2,1)S(1)}, bf16[384,192]{1,0:T(8,128)(2,1)}, u32[]{:S(2)}, u32[]{:S(2)}) collective-permute-start(bf16[384,192]{1,0:T(8,128)(2,1)S(1)} %slice.656), channel_id=1, source_target_pairs={{0,4},{4,0},{8,12},{12,8},{16,20},{20,16},{24,28},{28,24},{1,5},{5... | collective-permute-start | bytes 442376 | tf_op jit(solution)/shard_map/ppermute | solution.py:23
  565.8 22.5 %collective-permute-start.87 = (bf16[768,1536]{1,0:T(8,128)(2,1)}, bf16[768,1536]{1,0:T(8,128)(2,1)}, u32[]{:S(2)}, u32[]{:S(2)}) collective-permute-start(bf16[768,1536]{1,0:T(8,128)(2,1)} %slice.636), channel_id=1, source_target_pairs={{0,1},{1,0},{2,3},{3,2},{4,5},{5,4},{6,7},{7,6},{8,9},{9,8},{10,11... | collective-permute-start | bytes 7077896 | tf_op jit(solution)/shard_map/ppermute | solution.py:23
  575.7 29.1 %collective-permute-start.96 = (bf16[384,1536]{1,0:T(8,128)(2,1)}, bf16[384,1536]{1,0:T(8,128)(2,1)}, u32[]{:S(2)}, u32[]{:S(2)}) collective-permute-start(bf16[384,1536]{1,0:T(8,128)(2,1)} %slice.639), channel_id=1, source_target_pairs={{0,4},{4,0},{8,12},{12,8},{16,20},{20,16},{24,28},{28,24},{1,5},{5... | collective-permute-start | bytes 3538952 | tf_op jit(solution)/shard_map/ppermute | solution.py:23
  582.4 46.7 %collective-permute-start.80 = (bf16[384,1536]{1,0:T(8,128)(2,1)}, bf16[384,1536]{1,0:T(8,128)(2,1)}, u32[]{:S(2)}, u32[]{:S(2)}) collective-permute-start(bf16[384,1536]{1,0:T(8,128)(2,1)} %slice.641), channel_id=1, source_target_pairs={{0,4},{4,0},{8,12},{12,8},{16,20},{20,16},{24,28},{28,24},{1,5},{5... | collective-permute-start | bytes 3538952 | tf_op jit(solution)/shard_map/ppermute | solution.py:23
  586.9 45.5 %collective-permute-start.72 = (bf16[768,768]{1,0:T(8,128)(2,1)}, bf16[768,768]{1,0:T(8,128)(2,1)}, u32[]{:S(2)}, u32[]{:S(2)}) collective-permute-start(bf16[768,768]{1,0:T(8,128)(2,1)} %slice.642), channel_id=1, source_target_pairs={{0,2},{1,3},{2,0},{3,1},{4,6},{5,7},{6,4},{7,5},{8,10},{9,11},{10,... | collective-permute-start | bytes 3538952 | tf_op jit(solution)/shard_map/ppermute | solution.py:23
  591.0 50.2 %collective-permute-start.88 = (bf16[768,768]{1,0:T(8,128)(2,1)S(1)}, bf16[768,768]{1,0:T(8,128)(2,1)S(1)}, u32[]{:S(2)}, u32[]{:S(2)}) collective-permute-start(bf16[768,768]{1,0:T(8,128)(2,1)S(1)} %slice.640), channel_id=1, source_target_pairs={{0,2},{1,3},{2,0},{3,1},{4,6},{5,7},{6,4},{7,5},{8,10},{9,11},{10,... | collective-permute-start | bytes 3538952 | tf_op jit(solution)/shard_map/ppermute | solution.py:23
  606.5 47.4 %collective-permute-start.97 = (bf16[384,768]{1,0:T(8,128)(2,1)S(1)}, bf16[384,768]{1,0:T(8,128)(2,1)S(1)}, u32[]{:S(2)}, u32[]{:S(2)}) collective-permute-start(bf16[384,768]{1,0:T(8,128)(2,1)S(1)} %slice.644), channel_id=1, source_target_pairs={{0,2},{1,3},{2,0},{3,1},{4,6},{5,7},{6,4},{7,5},{8,10},{9,11},{10,... | collective-permute-start | bytes 1769480 | tf_op jit(solution)/shard_map/ppermute | solution.py:23
  630.9 34.2 %collective-permute-start.81 = (bf16[384,768]{1,0:T(8,128)(2,1)S(1)}, bf16[384,768]{1,0:T(8,128)(2,1)S(1)}, u32[]{:S(2)}, u32[]{:S(2)}) collective-permute-start(bf16[384,768]{1,0:T(8,128)(2,1)S(1)} %slice.646), channel_id=1, source_target_pairs={{0,2},{1,3},{2,0},{3,1},{4,6},{5,7},{6,4},{7,5},{8,10},{9,11},{10,... | collective-permute-start | bytes 1769480 | tf_op jit(solution)/shard_map/ppermute | solution.py:23
  634.2 32.2 %collective-permute-start.73 = (bf16[384,768]{1,0:T(8,128)(2,1)S(1)}, bf16[384,768]{1,0:T(8,128)(2,1)S(1)}, u32[]{:S(2)}, u32[]{:S(2)}) collective-permute-start(bf16[384,768]{1,0:T(8,128)(2,1)S(1)} %slice.647), channel_id=1, source_target_pairs={{0,4},{4,0},{8,12},{12,8},{16,20},{20,16},{24,28},{28,24},{1,5},{5... | collective-permute-start | bytes 1769480 | tf_op jit(solution)/shard_map/ppermute | solution.py:23
  641.7 25.9 %collective-permute-start.89 = (bf16[384,768]{1,0:T(8,128)(2,1)S(1)}, bf16[384,768]{1,0:T(8,128)(2,1)S(1)}, u32[]{:S(2)}, u32[]{:S(2)}) collective-permute-start(bf16[384,768]{1,0:T(8,128)(2,1)S(1)} %slice.645), channel_id=1, source_target_pairs={{0,4},{4,0},{8,12},{12,8},{16,20},{20,16},{24,28},{28,24},{1,5},{5... | collective-permute-start | bytes 1769480 | tf_op jit(solution)/shard_map/ppermute | solution.py:23
  654.1 14.7 %collective-permute-start.98 = (bf16[192,768]{1,0:T(8,128)(2,1)S(1)}, bf16[192,768]{1,0:T(8,128)(2,1)S(1)}, u32[]{:S(2)}, u32[]{:S(2)}) collective-permute-start(bf16[192,768]{1,0:T(8,128)(2,1)S(1)} %slice.650), channel_id=1, source_target_pairs={{0,8},{4,12},{8,0},{12,4},{16,24},{20,28},{24,16},{28,20},{1,9},{5... | collective-permute-start | bytes 884744 | tf_op jit(solution)/shard_map/ppermute | solution.py:23
  665.2 14.8 %collective-permute-start.82 = (bf16[192,768]{1,0:T(8,128)(2,1)S(1)}, bf16[192,768]{1,0:T(8,128)(2,1)S(1)}, u32[]{:S(2)}, u32[]{:S(2)}) collective-permute-start(bf16[192,768]{1,0:T(8,128)(2,1)S(1)} %slice.652), channel_id=1, source_target_pairs={{0,8},{4,12},{8,0},{12,4},{16,24},{20,28},{24,16},{28,20},{1,9},{5... | collective-permute-start | bytes 884744 | tf_op jit(solution)/shard_map/ppermute | solution.py:23
  666.5 21.5 %collective-permute-start.74 = (bf16[192,768]{1,0:T(8,128)(2,1)S(1)}, bf16[192,768]{1,0:T(8,128)(2,1)S(1)}, u32[]{:S(2)}, u32[]{:S(2)}) collective-permute-start(bf16[192,768]{1,0:T(8,128)(2,1)S(1)} %slice.653), channel_id=1, source_target_pairs={{0,8},{4,12},{8,0},{12,4},{16,24},{20,28},{24,16},{28,20},{1,9},{5... | collective-permute-start | bytes 884744 | tf_op jit(solution)/shard_map/ppermute | solution.py:23
  667.7 24.7 %collective-permute-start.90 = (bf16[192,768]{1,0:T(8,128)(2,1)S(1)}, bf16[192,768]{1,0:T(8,128)(2,1)S(1)}, u32[]{:S(2)}, u32[]{:S(2)}) collective-permute-start(bf16[192,768]{1,0:T(8,128)(2,1)S(1)} %slice.651), channel_id=1, source_target_pairs={{0,8},{4,12},{8,0},{12,4},{16,24},{20,28},{24,16},{28,20},{1,9},{5... | collective-permute-start | bytes 884744 | tf_op jit(solution)/shard_map/ppermute | solution.py:23
  668.9 23.9 %collective-permute-start.99 = (bf16[96,768]{1,0:T(8,128)(2,1)S(1)}, bf16[96,768]{1,0:T(8,128)(2,1)S(1)}, u32[]{:S(2)}, u32[]{:S(2)}) collective-permute-start(bf16[96,768]{1,0:T(8,128)(2,1)S(1)} %slice.657), channel_id=1, source_target_pairs={{0,16},{4,20},{8,24},{12,28},{16,0},{20,4},{24,8},{28,12},{1,17},{... | collective-permute-start | bytes 442376 | tf_op jit(solution)/shard_map/ppermute | solution.py:23
  680.1 19.6 %collective-permute-start.83 = (bf16[96,768]{1,0:T(8,128)(2,1)S(1)}, bf16[96,768]{1,0:T(8,128)(2,1)S(1)}, u32[]{:S(2)}, u32[]{:S(2)}) collective-permute-start(bf16[96,768]{1,0:T(8,128)(2,1)S(1)} %slice.659), channel_id=1, source_target_pairs={{0,16},{4,20},{8,24},{12,28},{16,0},{20,4},{24,8},{28,12},{1,17},{... | collective-permute-start | bytes 442376 | tf_op jit(solution)/shard_map/ppermute | solution.py:23
  688.1 14.8 %collective-permute-start.75 = (bf16[96,768]{1,0:T(8,128)(2,1)S(1)}, bf16[96,768]{1,0:T(8,128)(2,1)S(1)}, u32[]{:S(2)}, u32[]{:S(2)}) collective-permute-start(bf16[96,768]{1,0:T(8,128)(2,1)S(1)} %slice.660), channel_id=1, source_target_pairs={{0,16},{4,20},{8,24},{12,28},{16,0},{20,4},{24,8},{28,12},{1,17},{... | collective-permute-start | bytes 442376 | tf_op jit(solution)/shard_map/ppermute | solution.py:23
  692.8 23.4 %collective-permute-start.101 = (bf16[96,768]{1,0:T(8,128)(2,1)S(1)}, bf16[96,768]{1,0:T(8,128)(2,1)S(1)}, u32[]{:S(2)}, u32[]{:S(2)}) collective-permute-start(bf16[96,768]{1,0:T(8,128)(2,1)S(1)} %fusion.68), channel_id=1, source_target_pairs={{0,1},{1,0},{2,3},{3,2},{4,5},{5,4},{6,7},{7,6},{8,9},{9,8},{10,11... | collective-permute-start | bytes 442376 | tf_op jit(solution)/shard_map/ppermute | solution.py:23
  692.9 19.5 %collective-permute-start.100 = (bf16[96,768]{1,0:T(8,128)(2,1)S(1)}, bf16[96,768]{1,0:T(8,128)(2,1)S(1)}, u32[]{:S(2)}, u32[]{:S(2)}) collective-permute-start(bf16[96,768]{1,0:T(8,128)(2,1)S(1)} %fusion.68), channel_id=1, source_target_pairs={{0,2},{1,3},{2,0},{3,1},{4,6},{5,7},{6,4},{7,5},{8,10},{9,11},{10,... | collective-permute-start | bytes 442376 | tf_op jit(solution)/shard_map/ppermute | solution.py:23
  (254 other events, 4682.0 us)
Sparse Core Ops, SparseCore 0:
  461.6 74.7 all-reduce.4

commit v2 on v1

v2 whole, which is shorter than its diff:
```python
import functools

import jax
import jax.numpy as jnp
from jax import lax
from jax.experimental import pallas as pl
from jax.experimental.pallas import tpu as pltpu
from jax.sharding import PartitionSpec as P

LAYERS = 2
STEP = 5
IMG_MB = 8
NV = 11
LANES = 128
SUBLANES = 8
FOLD_MAX = 1200000

low = jnp.bfloat16
beta_one = 0.9
beta_two = 0.999
epsilon = 1e-06
weight_decay = 0.01
learn_rate = 0.3
root = 0.7978845608028654
cubic = 0.044715
room = pltpu.CompilerParams(vmem_limit_bytes=44 * 1024 * 1024)
places = (0, 2, 1, 3)


def dot(left, right, contract=(1, 0)):
    return lax.dot_general(
        left, right, (((contract[0],), (contract[1],)), ((), ())), preferred_element_type=jnp.float32
    )


def gelu(values):
    return 0.5 * values * (1 + jnp.tanh(root * values * (1 + cubic * values * values)))


def gelu_both(values):
    square = values * values
    bend = jnp.tanh(root * values * (1 + cubic * square))
    half = 0.5 * (1 + bend)
    slope = half + 0.5 * values * (1 - bend * bend) * (root * (1 + 3 * cubic * square))
    return values * half, slope


def centred(values):
    centre = values - jnp.mean(values, -1, keepdims=True)
    inverse = lax.rsqrt(jnp.mean(centre * centre, -1, keepdims=True) + 1e-06)
    return centre * inverse, inverse


def centred_back(scaled, hat, inverse):
    return inverse * (
        scaled - jnp.mean(scaled, -1, keepdims=True) - hat * jnp.mean(scaled * hat, -1, keepdims=True)
    )


def whole(array):
    zeros = (0,) * array.ndim
    return pl.BlockSpec(array.shape, lambda *_: zeros)


def cost(flops, bytes_accessed, powers=0):
    return pl.CostEstimate(flops=flops, bytes_accessed=bytes_accessed, transcendentals=powers)


def token_forward_kernel(state, gains, token_in, token_out, middle, before):
    hat, _ = centred(state[...])
    normed = (hat * gains[0:1] + gains[1:2]).astype(low)
    pre = dot(token_in[...], normed)
    before[0] = pre.astype(low)
    middle[...] = state[...] + dot(token_out[...], gelu(pre).astype(low))


def token_forward(state, gains, token_in, token_out):
    hidden, rows = token_in.shape
    count, width = state.shape[0] // rows, state.shape[1]
    one = pl.BlockSpec((rows, width), lambda i: (i, 0))
    return pl.pallas_call(
        token_forward_kernel,
        grid=(count,),
        in_specs=[one, whole(gains), whole(token_in), whole(token_out)],
        out_specs=[one, pl.BlockSpec((1, hidden, width), lambda i: (i, 0, 0))],
        out_shape=[
            jax.ShapeDtypeStruct(state.shape, jnp.float32),
            jax.ShapeDtypeStruct((count, hidden, width), low),
        ],
        compiler_params=room,
        cost_estimate=cost(4 * count * rows * hidden * width, 10 * state.size, 0),
        name="token_forward",
    )(state, gains, token_in, token_out)


def hbm(arrays):
    return [pl.BlockSpec(memory_space=pl.ANY)] * len(arrays)


scalars = pl.BlockSpec(memory_space=pltpu.SMEM)


class Pieces:
    def __init__(self, first, second):
        self.arrays = [*first, *second]
        self.specs = hbm(self.arrays)
        self.width = 2 * second[0].shape[1]
        self.size = second[0].shape[2]
        self.sems = 4

    def copies(self, refs, held_in, held_out, sems, slot, place):
        half = self.width // 2
        out = []
        for side in range(2):
            rows = pl.ds(side * half, half)
            first = refs[place].at[side, pl.ds(0, half)]
            second = refs[4 + place // 2 * 2 + side].at[place % 2]
            out.append(pltpu.make_async_copy(first, held_in.at[slot, rows], sems.at[slot, side]))
            out.append(pltpu.make_async_copy(second, held_out.at[slot, rows], sems.at[slot, 2 + side]))
        return out


class Gathered:
    def __init__(self, array, shards, device):
        self.arrays = [shards, device, array]
        self.specs = [scalars, scalars] + hbm([array])
        self.blocks, self.rows, self.size = array.shape[0], array.shape[2] // 2, array.shape[3]
        self.width = self.blocks * self.rows
        self.sems = 2 * self.blocks

    def copies(self, refs, held_in, held_out, sems, slot, place):
        shards, device, array = refs
        quarter_at = device[0] ^ places[place]
        out = []
        for block in range(self.blocks):
            rows = pl.ds(block * self.rows, self.rows)
            for way, held in enumerate((held_in, held_out)):
                out.append(
                    pltpu.make_async_copy(
                        array.at[shards[block], quarter_at, pl.ds(way * self.rows, self.rows)],
                        held.at[slot, rows],
                        sems.at[slot, 2 * block + way],
                    )
                )
        return out


def channel_forward_kernel(source, middle, gains, *rest):
    refs = rest[: len(source.arrays)]
    result, inner, normed, held_in, held_out, sems = rest[-6:]
    step = pl.program_id(0)

    @pl.when(step == 0)
    def _():
        for q in range(4):
            for copy in source.copies(refs, held_in, held_out, sems, q, q):
                copy.start()
        hat, _ = centred(middle[...])
        normed[...] = (hat * gains[2:3] + gains[3:4]).astype(low)
        result[...] = middle[...]

    for q in range(4):

        @pl.when(step == q)
        def _(q=q):
            for copy in source.copies(refs, held_in, held_out, sems, q, q):
                copy.wait()
            product = dot(normed[...], held_in[q])
            inner[...] = product.astype(low)
            result[...] += dot(gelu(product).astype(low), held_out[q], (1, 1))


def channel_forward(middle, gains, source):
    rows, width = middle.shape
    size = source.size
    total = 4 * size
    return pl.pallas_call(
        functools.partial(channel_forward_kernel, source),
        grid=(4,),
        in_specs=[whole(middle), whole(gains)] + source.specs,
        out_specs=[whole(middle), pl.BlockSpec((rows, size), lambda i: (0, i))],
        out_shape=[
            jax.ShapeDtypeStruct(middle.shape, jnp.float32),
            jax.ShapeDtypeStruct((rows, total), low),
        ],
        scratch_shapes=[
            pltpu.VMEM(middle.shape, low),
            pltpu.VMEM((4, width, size), low),
            pltpu.VMEM((4, width, size), low),
            pltpu.SemaphoreType.DMA((4, source.sems)),
        ],
        compiler_params=room,
        cost_estimate=cost(4 * rows * width * total, 4 * width * total + 2 * rows * total),
        name="channel_forward",
    )(middle, gains, *source.arrays)


def channel_backward_kernel(source, last, gradient, middle, gains, inner, *rest):
    if last:
        before, rest = rest[0], rest[1:]
    refs = rest[: len(source.arrays)]
    grads, total, grad_vectors, grad_low, grad_turn, normed_turn, held_in, held_out, sems = rest[-9:]
    step = pl.program_id(0)
    first = 0 if last else 2

    @pl.when(step == 0)
    def _():
        for q in range(2):
            for copy in source.copies(refs, held_in, held_out, sems, q, first + q):
                copy.start()
        grad_low[...] = gradient[...].astype(low)
        grad_turn[...] = gradient[...].T.astype(low)
        hat, _ = centred(middle[...])
        normed_turn[...] = (hat * gains[2:3] + gains[3:4]).T.astype(low)
        total[...] = before[...] if last else jnp.zeros_like(total)

    for q in range(2):

        @pl.when(step == q)
        def _(q=q):
            for copy in source.copies(refs, held_in, held_out, sems, q, first + q):
                copy.wait()
            active, slope = gelu_both(inner[...].astype(jnp.float32))
            grads[1, 0] = dot(grad_turn[...], active.astype(low)).astype(low)
            grad_inner = (slope * dot(grad_low[...], held_out[q])).astype(low)
            grads[0, 0] = dot(normed_turn[...], grad_inner).astype(low)
            total[...] += dot(grad_inner, held_in[q], (1, 1))

    if last:

        @pl.when(step == 1)
        def _():
            hat, inverse = centred(middle[...])
            upstream = total[...]
            grad_vectors[0:1] = jnp.sum(upstream * hat, 0, keepdims=True)
            grad_vectors[1:2] = jnp.sum(upstream, 0, keepdims=True)
            total[...] = gradient[...] + centred_back(upstream * gains[2:3], hat, inverse)


def channel_backward(gradient, middle, gains, inner, source, before=None):
    rows, width = middle.shape
    size = source.size
    last = before is not None
    shift = 0 if last else 2
    carried = [before] if last else []
    total = 2 * size
    return pl.pallas_call(
        functools.partial(channel_backward_kernel, source, last),
        grid=(2,),
        in_specs=[whole(middle), whole(middle), whole(gains), pl.BlockSpec((rows, size), lambda i: (0, i + shift))]
        + [whole(array) for array in carried]
        + source.specs,
        out_specs=[
            pl.BlockSpec((2, 1, width, size), lambda i: (0, i, 0, 0)),
            whole(middle),
            pl.BlockSpec((2, width), lambda i: (0, 0)),
        ],
        out_shape=[
            jax.ShapeDtypeStruct((2, 2, width, size), low),
            jax.ShapeDtypeStruct(middle.shape, jnp.float32),
            jax.ShapeDtypeStruct((2, width), jnp.float32),
        ],
        scratch_shapes=[
            pltpu.VMEM((rows, width), low),
            pltpu.VMEM((width, rows), low),
            pltpu.VMEM((width, rows), low),
            pltpu.VMEM((2, width, size), low),
            pltpu.VMEM((2, width, size), low),
            pltpu.SemaphoreType.DMA((2, source.sems)),
        ],
        compiler_params=room,
        cost_estimate=cost(8 * rows * width * total, 8 * width * total + 2 * rows * total),
        name="channel_backward",
    )(gradient, middle, gains, inner, *carried, *source.arrays)


def step_kernel(device, weight, mean, power, near, far, *rest):
    apart, (mean_new, power_new, update, sums) = rest[:4], rest[-4:]
    way = pl.program_id(0)
    size = near.shape[2]
    weight_part, update_part = 0.0, 0.0
    for a in range(4):
        rel = device[0] ^ a
        lanes = slice(a * size, (a + 1) * size)
        values = [
            jnp.where(way == 0, one.astype(jnp.float32), two[...].astype(jnp.float32))
            for one, two in zip((near[0], far[0], near[1], far[1]), apart, strict=True)
        ]
        grad = jnp.where(
            rel < 2, jnp.where(rel == 0, values[0], values[1]), jnp.where(rel == 2, values[2], values[3])
        )
        value = weight[0, 0, :, lanes]
        mean_next, power_next, change = moments(
            value, grad, mean[0, 0, :, lanes], power[0, 0, :, lanes], weight_decay
        )
        mean_new[0, 0, :, lanes] = mean_next
        power_new[0, 0, :, lanes] = power_next
        update[0, 0, :, lanes] = change
        weight_part += jnp.sum(value * value)
        update_part += jnp.sum(change * change)
    sums[way, 0] = weight_part
    sums[way, 1] = update_part


def channel_step(layer, device, weight, mean, power, chain_in, chain_out, earlier):
    near, far = chain_in
    rows = near.shape[1]
    columns = weight.shape[3]
    block = pl.BlockSpec((1, 1, rows, columns), lambda w: (layer, w, 0, 0))
    shape = jax.ShapeDtypeStruct(weight.shape, jnp.float32)
    return pl.pallas_call(
        step_kernel,
        grid=(2,),
        in_specs=[scalars, block, block, block]
        + [whole(array) for array in (near, far, *chain_out)]
        + hbm(earlier),
        out_specs=[block, block, block, scalars],
        out_shape=[shape, shape, shape, jax.ShapeDtypeStruct((2, 2), jnp.float32)],
        input_output_aliases={10 + i: i for i in range(len(earlier))},
        compiler_params=room,
        cost_estimate=cost(40 * near.size, 104 * near.size),
        name="channel_step",
    )(device, weight, mean, power, near, far, *chain_out, *earlier)


def renew_kernel(trust, weight, update, fresh, fresh_low):
    value = weight[...] - learn_rate * (trust[pl.program_id(0), pl.program_id(1)] * update[...])
    fresh[...] = value
    fresh_low[...] = value.astype(low)


def channel_renew(trust, weight, update):
    layers, ways, rows, columns = weight.shape
    block = pl.BlockSpec((1, 1, rows, columns), lambda i, j: (i, j, 0, 0))
    return pl.pallas_call(
        renew_kernel,
        grid=(layers, ways),
        in_specs=[pl.BlockSpec(memory_space=pltpu.SMEM), block, block],
        out_specs=[block, block],
        out_shape=[jax.ShapeDtypeStruct(weight.shape, jnp.float32), jax.ShapeDtypeStruct(weight.shape, low)],
        compiler_params=room,
        cost_estimate=cost(3 * weight.size, 14 * weight.size),
        name="channel_renew",
    )(trust, weight, update)


def token_backward_kernel(gradient, state, gains, before, token_in, token_out_turn, *rest):
    grad_state, grad_vectors, grad_in, grad_out = rest[-4:]
    step = pl.program_id(0)
    token_grad = gradient[...].astype(low)
    hat, inverse = centred(state[...])
    normed = (hat * gains[0:1] + gains[1:2]).astype(low)
    hidden, slope = gelu_both(before[0].astype(jnp.float32))
    grad_before = (slope * dot(token_out_turn[...], token_grad)).astype(low)
    part_out = dot(token_grad, hidden.astype(low), (1, 1))
    part_in = dot(normed, grad_before, (1, 1))
    upstream = dot(token_in[...], grad_before)
    grad_state[...] = gradient[...] + centred_back(upstream * gains[0:1], hat, inverse)
    part_gain = jnp.sum(upstream * hat, 0, keepdims=True)
    part_shift = jnp.sum(upstream, 0, keepdims=True)

    @pl.when(step == 0)
    def _():
        grad_out[...] = part_out
        grad_in[...] = part_in
        grad_vectors[0:1] = part_gain
        grad_vectors[1:2] = part_shift

    @pl.when(step > 0)
    def _():
        grad_out[...] += part_out
        grad_in[...] += part_in
        grad_vectors[0:1] += part_gain
        grad_vectors[1:2] += part_shift


def token_backward(gradient, state, gains, before, token_in, token_out_turn, after=()):
    rows, hidden = token_in.shape
    count, width = state.shape[0] // rows, state.shape[1]
    one = pl.BlockSpec((rows, width), lambda i: (i, 0))
    still = lambda shape: pl.BlockSpec(shape, lambda i: (0, 0))
    return pl.pallas_call(
        token_backward_kernel,
        grid=(count,),
        in_specs=[
            one, one, whole(gains), pl.BlockSpec((1, hidden, width), lambda i: (i, 0, 0)),
            whole(token_in), whole(token_out_turn),
        ] + [pl.BlockSpec(memory_space=pl.ANY)] * len(after),
        out_specs=[one, still((2, width)), still((rows, hidden)), still((rows, hidden))],
        out_shape=[
            jax.ShapeDtypeStruct(state.shape, jnp.float32),
            jax.ShapeDtypeStruct((2, width), jnp.float32),
            jax.ShapeDtypeStruct((rows, hidden), jnp.float32),
            jax.ShapeDtypeStruct((rows, hidden), jnp.float32),
        ],
        compiler_params=room,
        cost_estimate=cost(8 * count * rows * hidden * width, 16 * state.size, 0),
        name="token_backward",
    )(gradient, state, gains, before, token_in, token_out_turn, *after)


def mix_kernel(place, share, device, own, incoming, *rest):
    outs, (own_wide, incoming_wide, joint) = rest[:-3], rest[-3:]
    patches, images, width = own.shape
    group = images // len(outs)
    for at in range(0, width, LANES):
        lanes = slice(at, at + LANES)
        own_wide[...] = own[:, :, lanes].astype(jnp.float32).reshape(own_wide.shape)
        incoming_wide[...] = incoming[:, :, lanes].astype(jnp.float32).reshape(own_wide.shape)
        for q, out in enumerate(outs):
            for i in range(group):
                image = (device[0] ^ q) * group + i
                first = own_wide[pl.ds(image, patches, stride=images), :]
                second = incoming_wide[pl.ds(place[image], patches, stride=images), :]
                joint[i * patches : (i + 1) * patches, :] = (
                    share[image] * first + (1 - share[image]) * second
                )
            out[:, lanes] = joint[...].astype(low)


def mix(place, share, device, own, incoming, groups):
    patches, images, width = own.shape
    rows = images // groups * patches
    scalar = pl.BlockSpec(memory_space=pltpu.SMEM)
    return pl.pallas_call(
        mix_kernel,
        in_specs=[scalar, scalar, scalar, pl.BlockSpec(), pl.BlockSpec()],
        out_shape=[jax.ShapeDtypeStruct((rows, width), low)] * groups,
        scratch_shapes=[
            pltpu.VMEM((patches * images, LANES), jnp.float32),
            pltpu.VMEM((patches * images, LANES), jnp.float32),
            pltpu.VMEM((rows, LANES), jnp.float32),
        ],
        compiler_params=room,
        cost_estimate=cost(4 * own.size, 6 * own.size),
        name="mix",
    )(place, share, device, own, incoming)


def stem_kernel(device, *rest):
    pieces, (weights, gains, mixed, state, joint, spare) = rest[:-6], rest[-6:]
    count = len(pieces) // 2
    odd, upper = (device[0] & 1) == 1, (device[0] & 2) == 2
    patches = pieces[0].shape[0] // 2
    rows = joint.shape[0] // (2 * 2)
    joint[...] = jnp.zeros_like(joint)
    for side in range(2):
        arrived = [ref[...].astype(jnp.float32) for ref in pieces[side * count : (side + 1) * count]]
        arrived = [jnp.where(odd, arrived[k ^ 1], arrived[k]) for k in range(count)]
        for k in range(count):
            spare[...] = jnp.where(upper, arrived[k ^ 2], arrived[k])
            for i in range(2):
                at = (side * 2 + i) * rows + k * patches
                joint[at : at + patches, :] = spare[i * patches : (i + 1) * patches, :]
    mixed[...] = joint[...].astype(low)
    state[...] = dot(mixed[...], weights[...], (1, 1)) + gains[0:1]


def stem(device, pieces, weights, gains, rows, after=()):
    width, pixels = weights.shape
    scalar = pl.BlockSpec(memory_space=pltpu.SMEM)
    return pl.pallas_call(
        stem_kernel,
        in_specs=[scalar] + [pl.BlockSpec()] * (len(pieces) + 2),
        out_shape=[
            jax.ShapeDtypeStruct((rows, pixels), low),
            jax.ShapeDtypeStruct((rows, width), jnp.float32),
        ],
        scratch_shapes=[
            pltpu.VMEM((rows, pixels), jnp.float32),
            pltpu.VMEM(pieces[0].shape, jnp.float32),
        ],
        compiler_params=room,
        cost_estimate=cost(2 * rows * width * pixels, 12 * rows * width),
        name="stem",
    )(device, *pieces, weights, gains)


def head_kernel(
    patches, device, state, gains, head, bias, numbers, labels, others, lam, weight, scale,
    gradient, grad_vectors, grads, grad_bias, loss, pooled, upstream,
):
    rows, width = state.shape
    count = lam.shape[0]
    each = rows // count
    live = lax.broadcasted_iota(jnp.int32, (each, 1), 0) < patches
    hat, inverse = centred(state[...])
    pooled[...] = jnp.zeros_like(pooled)
    sums = []
    for i in range(count):
        sums.append(jnp.sum(jnp.where(live, hat[i * each : (i + 1) * each], 0.0), 0, keepdims=True))
        pooled[i : i + 1] = sums[i] / patches * gains[0:1] + gains[1:2]
    pooled_low = pooled[...].astype(low)
    logits = dot(pooled_low, head[...])[:count] + bias[...]
    logits = jnp.where(numbers[...] >= 0, logits, -jnp.inf)
    peak = jnp.max(logits, -1, keepdims=True)
    powers = jnp.exp(logits - peak)
    mass = jnp.sum(powers, -1, keepdims=True)
    targets = jnp.where(numbers[...] == labels[...], lam[...], 0.0) + jnp.where(
        numbers[...] == others[...], 1 - lam[...], 0.0
    )
    log_probs = jnp.where(numbers[...] >= 0, logits - peak - jnp.log(mass), 0.0)
    losses = -jnp.sum(targets * log_probs, -1, keepdims=True)
    loss[...] = jnp.sum(weight[...] * losses, 0, keepdims=True)
    grad_logits = scale[...] * (powers / mass * jnp.sum(targets, -1, keepdims=True) - targets)
    grad_bias[...] = jnp.sum(grad_logits, 0, keepdims=True)
    pad = jnp.zeros((pooled.shape[0] - count, grad_logits.shape[1]), jnp.float32)
    grad_logits = jnp.concatenate([grad_logits, pad], 0)
    main = grad_logits.astype(low)
    rest = (grad_logits - main.astype(jnp.float32)).astype(low)
    size = main.shape[1] // 4
    for a in range(4):
        lanes = slice(a * size, (a + 1) * size)
        part = dot(pooled_low, main[:, lanes], (0, 0)) + dot(pooled_low, rest[:, lanes], (0, 0))
        rel = device[0] ^ a
        grads[(rel & 1) * 2 + (rel >> 1)] = part.astype(low)
    spread_back = (dot(main, head[...], (1, 1)) + dot(rest, head[...], (1, 1))) / patches
    upstream[...] = jnp.zeros_like(upstream)
    grad_gain = jnp.zeros((1, width), jnp.float32)
    for i in range(count):
        one = spread_back[i : i + 1]
        grad_gain = grad_gain + one * sums[i]
        upstream[i * each : (i + 1) * each] = jnp.where(live, one, 0.0)
    grad_vectors[0:1] = grad_gain
    grad_vectors[1:2] = jnp.sum(spread_back[:count], 0, keepdims=True) * patches
    gradient[...] = centred_back(upstream[...] * gains[0:1], hat, inverse)


def head_step(device, state, gains, weights, bias, numbers, labels, others, lam, weight, scale, patches):
    rows, width = state.shape
    columns = weights.shape[1]
    return pl.pallas_call(
        functools.partial(head_kernel, patches),
        in_specs=[scalars] + [pl.BlockSpec()] * 10,
        out_shape=[
            jax.ShapeDtypeStruct(state.shape, jnp.float32),
            jax.ShapeDtypeStruct((2, width), jnp.float32),
            jax.ShapeDtypeStruct((4, width, columns // 4), low),
            jax.ShapeDtypeStruct((1, columns), jnp.float32),
            jax.ShapeDtypeStruct((1, 1), jnp.float32),
        ],
        scratch_shapes=[
            pltpu.VMEM((16, width), jnp.float32),
            pltpu.VMEM(state.shape, jnp.float32),
        ],
        compiler_params=room,
        cost_estimate=cost(64 * width * columns, 8 * rows * width),
        name="head_step",
    )(device, state, gains, weights, bias, numbers, labels, others, lam, weight, scale)


def stem_backward_kernel(device, gradient, mixed, grads, shift):
    rounded = gradient[...].astype(low)
    shift[...] = jnp.sum(rounded.astype(jnp.float32), 0, keepdims=True)
    whole_grad = dot(gradient[...].T.astype(low), mixed[...]).astype(low)
    size = whole_grad.shape[1] // 4
    for a in range(4):
        rel = device[0] ^ a
        grads[(rel & 1) * 2 + (rel >> 1)] = whole_grad[:, a * size : (a + 1) * size]


def stem_backward(device, gradient, mixed):
    width, pixels = gradient.shape[1], mixed.shape[1]
    return pl.pallas_call(
        stem_backward_kernel,
        in_specs=[scalars] + [pl.BlockSpec()] * 2,
        out_shape=[
            jax.ShapeDtypeStruct((4, width, pixels // 4), low),
            jax.ShapeDtypeStruct((1, width), jnp.float32),
        ],
        compiler_params=room,
        cost_estimate=cost(2 * gradient.size * pixels, 8 * gradient.size),
        name="stem_backward",
    )(device, gradient, mixed)


def moved(values, source, way):
    spots = (lax.broadcasted_iota(jnp.int32, (values.shape[1],) * 2, 0) == source).astype(low)
    main = values.astype(low)
    rest = values - main.astype(jnp.float32)
    middle = rest.astype(low)
    rest = (rest - middle.astype(jnp.float32)).astype(low)
    return sum(dot(part, spots, (1, way)) for part in (main, middle, rest))


def vectors_kernel(vectors, source, out):
    out[...] = moved(vectors[...], source[...], 0)


def relative_vectors(vectors, source):
    return pl.pallas_call(
        vectors_kernel,
        out_shape=jax.ShapeDtypeStruct(vectors.shape, jnp.float32),
        compiler_params=room,
        name="relative_vectors",
    )(vectors, source)


def gather_small_kernel(source, *rest):
    parts, (bias, loss, out, joint) = rest[:-4], rest[-4:]
    joint[...] = jnp.zeros_like(joint)
    at = 0
    for part in parts:
        joint[at : at + part.shape[0]] = part[...]
        at += part.shape[0]
    out[...] = jnp.zeros_like(out)
    out[:, : joint.shape[1]] = moved(joint[...], source[...], 1)
    out[at : at + 1] = bias[...]
    out[at + 1 : at + 2, 0:1] = loss[...]


def gather_small(source, parts, bias, loss):
    return pl.pallas_call(
        gather_small_kernel,
        out_shape=jax.ShapeDtypeStruct((16, bias.shape[1]), jnp.float32),
        scratch_shapes=[pltpu.VMEM((16, parts[0].shape[1]), jnp.float32)],
        compiler_params=room,
        name="gather_small",
    )(source, *parts, bias, loss)


def swap(array, axis, mask):
    count = lax.axis_size(axis)
    return lax.ppermute(array, axis, [(i, i ^ mask) for i in range(count)])


def fence(*trees):
    return lax.optimization_barrier(trees)


def dp_masks():
    masks = []
    mask = lax.axis_size("dp") // 2
    while mask > 1:
        masks.append(mask)
        mask //= 2
    return masks


def row_order():
    order = [0]
    for mask in dp_masks() + [1]:
        order = order + [r ^ mask for r in order]
    return order


def packed(blocks):
    return jnp.concatenate(blocks, 0)


def unpacked(array, blocks):
    out = []
    at = 0
    for block in blocks:
        out.append(lax.slice_in_dim(array, at, at + block.shape[0], axis=0))
        at += block.shape[0]
    return out


def doubled(blocks, got):
    return [jnp.concatenate(pair, 0) for pair in zip(blocks, unpacked(got, blocks), strict=True)]


def added(keep, got):
    return (keep.astype(jnp.float32) + got.astype(jnp.float32)).astype(keep.dtype)


def cut_rows(array, half):
    middle = array.shape[-2] // 2
    return array[..., half * middle : (half + 1) * middle, :]


def folded(keep, got, kind):
    if kind == "rows":
        return [added(cut_rows(keep, half), cut_rows(got, half)) for half in range(2)]
    if kind == "blocks":
        return [added(keep[0], got[0]), added(keep[1], got[1])]
    if kind == "turned":
        return [jnp.stack([added(keep[0], got[1]), added(keep[1], got[0])])]
    return [added(keep, got)]


def fold_kernel(kinds, *refs):
    outs = list(refs[2 * len(kinds) :])
    for i, kind in enumerate(kinds):
        for value in folded(refs[2 * i][...], refs[2 * i + 1][...], kind):
            outs.pop(0)[...] = value


def fold_all(jobs):
    kinds = [kind for _, _, kind in jobs]
    arrays = [array for keep, got, _ in jobs for array in (keep, got)]
    shapes = [jax.eval_shape(functools.partial(folded, kind=kind), keep, got) for keep, got, kind in jobs]
    flat = [shape for group in shapes for shape in group]
    outs = pl.pallas_call(
        functools.partial(fold_kernel, kinds),
        out_shape=flat,
        compiler_params=room,
        cost_estimate=cost(sum(a.size for a in arrays), sum(4 * a.size for a in arrays)),
        name="fold_all",
    )(*arrays)
    out = []
    for group in shapes:
        out.append(outs[: len(group)])
        outs = outs[len(group) :]
    return out


def reduce_rows(keep, got):
    keep, send = yield keep, got, "rows"
    steps = [1] + dp_masks()[::-1]
    for mask in steps[:-1]:
        keep, send = yield keep, swap(send, "dp", mask), "rows"
    (keep,) = yield keep, swap(send, "dp", steps[-1]), "sum"
    (keep,) = yield keep, swap(keep, "tok", 2), "turned"
    near, far = yield keep, swap(keep, "tok", 1), "none"
    return near, far


def reduce_columns(keep, got):
    keep, send = yield keep, got, "blocks"
    keep, send = yield keep, swap(send, "tok", 2), "rows"
    steps = [1] + dp_masks()[::-1]
    for mask in steps[:-1]:
        keep, send = yield keep, swap(send, "dp", mask), "rows"
    (keep,) = yield keep, swap(send, "dp", steps[-1]), "sum"
    keep, others = yield keep, [swap(keep, "tok", q) for q in range(1, 4)], "none"
    return [keep, *others]


def reduce_cores(grads):
    keep, got = grads[:2], swap(grads[2:], "tok", 1)
    return (yield from reduce_columns(keep, got))


def reduce_tokens(array):
    axis = array.ndim - 1
    for mask in (1, 2):
        middle = array.shape[axis] // 2
        keep = lax.slice_in_dim(array, 0, middle, axis=axis)
        send = lax.slice_in_dim(array, middle, 2 * middle, axis=axis)
        (array,) = yield keep, swap(send, "tok", mask), "sum"
    for mask in [1] + dp_masks()[::-1]:
        (array,) = yield array, swap(array, "dp", mask), "sum"
    return array


def sum_over(array, steps):
    for axis, mask in steps:
        (array,) = yield array, swap(array, axis, mask), "sum"
    return array


class Chain:
    def __init__(self, moves):
        self.moves, self.result = moves, None
        self.state = next(moves)

    def push(self, state):
        try:
            self.state = self.moves.send(state)
        except StopIteration as end:
            self.state, self.result = None, end.value


def advance(chains, *others):
    chains = [chain for chain in chains if chain.state is not None]
    states, others = fence([chain.state[:2] for chain in chains], others)
    jobs = []
    for chain, (keep, got) in zip(chains, states, strict=True):
        kind = chain.state[2]
        small = keep.size <= FOLD_MAX if kind != "none" else False
        if kind in ("rows",) and keep.shape[-2] % 32:
            small = False
        if small:
            jobs.append((chain, keep, got, kind))
    results = dict(
        zip([id(job[0]) for job in jobs], fold_all([job[1:] for job in jobs]) if jobs else [], strict=True)
    )
    for chain, (keep, got) in zip(chains, states, strict=True):
        kind = chain.state[2]
        if id(chain) in results:
            chain.push(results[id(chain)])
        elif kind == "none":
            chain.push((keep, got))
        else:
            chain.push(folded(keep, got, kind))
    return others


def exchanged(blocks):
    row = lax.axis_index("tok")
    blocks = [jnp.where((row & 1) == 1, blocks[k ^ 1], blocks[k]) for k in range(4)]
    return [jnp.where((row & 2) == 2, blocks[k ^ 2], blocks[k]) for k in range(4)]


def ordered(blocks, axis):
    return jnp.concatenate(exchanged([blocks[0], blocks[2], blocks[1], blocks[3]]), axis)


def quarter(array, axis):
    size = array.shape[axis] // lax.axis_size("tok")
    return lax.dynamic_slice_in_dim(array, lax.axis_index("tok") * size, size, axis)


def moments(weight, gradient, first, second, decay_rate):
    first_new = beta_one * first + (1 - beta_one) * gradient
    second_new = beta_two * second + (1 - beta_two) * gradient * gradient
    update = (
        first_new / (1 - beta_one**STEP) / (jnp.sqrt(second_new / (1 - beta_two**STEP)) + epsilon)
        + decay_rate * weight
    )
    return (first_new, second_new, update)


def row_squares(array, groups):
    flat = array.reshape(groups, -1)
    return jnp.sum(flat * flat, 1)


def renew(weight, update, weight_norm, update_norm, groups):
    trust = weight_norm / (update_norm + epsilon)
    return weight - learn_rate * (trust[:, None] * update.reshape(groups, -1)).reshape(weight.shape)


def body(
    images,
    partner,
    lam,
    labels,
    counts,
    class_weights,
    stem_w,
    stem_m,
    stem_v,
    tok_w,
    tok_m,
    tok_v,
    chan_w,
    chan_m,
    chan_v,
    head_w,
    head_m,
    head_v,
    vec_w,
    vec_m,
    vec_v,
    hb_w,
    hb_m,
    hb_v,
):
    count_dp = lax.axis_size("dp")
    count_tok = lax.axis_size("tok")
    device_row = lax.axis_index("dp")
    token_row = lax.axis_index("tok")
    patches = images.shape[0]
    all_patches = patches * count_tok
    per_device = images.shape[1]
    per_tok = per_device // count_tok
    classes_all = hb_w.shape[0]
    class_pad = -classes_all % (count_tok * LANES)
    width = vec_w.shape[1]
    each = all_patches + -all_patches % SUBLANES

    masks = dp_masks()
    batches = per_device // IMG_MB
    start = device_row * per_device
    own_parts, owners, shares = [], [], []
    for batch in range(batches):
        at = start + batch * IMG_MB
        own_parts.append(images[:, batch * IMG_MB : (batch + 1) * IMG_MB])
        owners.append(lax.dynamic_slice_in_dim(partner, at, IMG_MB, 0) % IMG_MB)
        shares.append(lax.dynamic_slice_in_dim(lam, at, IMG_MB, 0))
    device = token_row.astype(jnp.int32)[None]

    def mixed_pieces(batch, incoming):
        sends = mix(owners[batch], shares[batch], device, own_parts[batch], incoming, count_tok)
        return [sends[0]] + [swap(sends[q], "tok", q) for q in range(1, count_tok)]

    chan_low = quarter(chan_w.astype(low), 3)
    shard, size = chan_low.shape[2:]
    order = row_order()
    rows = jnp.asarray(order, jnp.int32) ^ device_row
    column_source = (rows[:, None] * shard + jnp.arange(shard, dtype=jnp.int32)[None, :]).reshape(1, width)
    ends = jnp.concatenate([stem_w.astype(low).T, jnp.pad(head_w.astype(low), ((0, 0), (0, class_pad)))], 1)
    ends = lax.all_gather(ends, "dp")
    later = lax.all_gather(chan_low[1].reshape(2 * shard, size), ("dp", "tok"))
    later = later.reshape(count_dp, count_tok, 2 * shard, size)

    vectors = relative_vectors(vec_w, column_source)
    numbers = jnp.arange(classes_all + class_pad, dtype=jnp.int32)
    numbers = jnp.where(numbers < classes_all, numbers, -1)[None]
    bias = jnp.pad(hb_w, (0, class_pad))[None]
    own_hot = (labels[:, None] == jnp.arange(classes_all, dtype=jnp.int32)[None, :]).astype(jnp.float32)
    other_labels = jnp.take(labels, partner)
    own_weight = jnp.sum(own_hot * class_weights[None, :], 1)
    other_weight = jnp.take(own_weight, partner)
    live = (
        (jnp.arange(IMG_MB, dtype=jnp.int32)[None, :] < counts.reshape(-1)[:, None])
        .astype(jnp.float32)
        .reshape(-1)
    )
    weights = live * (lam * own_weight + (1 - lam) * other_weight)
    total = jnp.sum(weights)
    group = IMG_MB // count_tok

    def row_of(array):
        return jnp.concatenate(
            [
                lax.dynamic_slice_in_dim(array, start + batch * IMG_MB + token_row * group, group, 0)
                for batch in range(batches)
            ]
        )[:, None]

    image_rows = [row_of(array) for array in (labels, other_labels, lam, weights, weights / total)]

    blocks = [chan_low[0, 0], chan_low[0, 1]]
    tok_low = tok_w.astype(low)
    partner_mask = count_dp // 2
    incoming_one = swap(own_parts[0], "dp", partner_mask)
    for step, mask in enumerate(masks):
        got = swap(packed(blocks), "dp", mask)
        if step == 0:
            blocks, got, tok_far, own_parts[1] = fence(blocks, got, swap(tok_low, "tok", 2), own_parts[1])
            tok_half = jnp.concatenate([tok_low, tok_far], 3)
            tok_near = swap(tok_half, "tok", 1)
        elif step == 1:
            blocks, got, tok_near, incoming_one, own_parts[1], vectors, image_rows = fence(
                blocks, got, tok_near, incoming_one, own_parts[1], vectors, image_rows
            )
        else:
            blocks, got = fence(blocks, got)
        blocks = doubled(blocks, got)
    tok_all = jnp.concatenate([tok_half, tok_near], 3)
    tok_all = jnp.pad(tok_all, ((0, 0), (0, 0), (0, each - all_patches), (0, 0)))
    tok_turn = jnp.swapaxes(tok_all, 2, 3)

    incoming_two = swap(own_parts[1], "dp", partner_mask)
    first, second = blocks
    first_low, second_far = swap(first, "dp", 1), swap(second, "tok", 2)
    first, second, first_low, second_far, incoming_one = fence(first, second, first_low, second_far, incoming_one)
    pieces = mixed_pieces(0, incoming_one)
    firsts, seconds = jnp.stack([first, first_low]), jnp.stack([second, second_far])
    firsts_far, seconds_low = swap(firsts, "tok", 2), swap(seconds, "dp", 1)
    firsts, seconds, firsts_far, seconds_low, incoming_two, pieces, tok_all, tok_turn = fence(
        firsts, seconds, firsts_far, seconds_low, incoming_two, pieces, tok_all, tok_turn
    )
    more = mixed_pieces(1, incoming_two)
    source_zero = Pieces(
        [firsts, firsts_far, swap(firsts, "tok", 1), swap(firsts_far, "tok", 1)],
        [seconds, seconds_low, swap(seconds, "tok", 1), swap(seconds_low, "tok", 1)],
    )
    ends = jnp.take(ends, rows, axis=0).reshape(width, -1)
    stem_all, head_all = ends[:, : stem_w.shape[0]], ends[:, stem_w.shape[0] :]
    if shard % 16:
        later = jnp.take(later, rows, axis=0).reshape(width // 96, 96 // shard, count_tok, 2, shard, size)
        later = later.transpose(0, 2, 3, 1, 4, 5).reshape(width // 96, count_tok, 2 * 96, size)
        source_one = Gathered(later, jnp.arange(width // 96, dtype=jnp.int32), device)
    else:
        source_one = Gathered(later, rows, device)

    gains = [vectors[1 + 4 * layer : 5 + 4 * layer] for layer in range(LAYERS)]
    mixed, stem_state = stem(device, pieces + more, stem_all, vectors, each * per_tok)
    middle_zero, before_zero = token_forward(stem_state, gains[0], tok_turn[0, 0], tok_all[0, 1])
    first_state, inner_zero = channel_forward(middle_zero, gains[0], source_zero)
    middle_one, before_one = token_forward(first_state, gains[1], tok_turn[1, 0], tok_all[1, 1])
    second_state, inner_one = channel_forward(middle_one, gains[1], source_one)
    gradient, last_part, head_grads, bias_part, loss_local = head_step(
        device, second_state, vectors[NV - 2 :], head_all, bias, numbers, *image_rows, all_patches
    )

    head_chain = Chain(reduce_cores(head_grads))
    send, partial, _ = channel_backward(gradient, middle_one, gains[1], inner_one, source_one)
    got = swap(send, "tok", 1)
    keep, gradient, second_one = channel_backward(gradient, middle_one, gains[1], inner_one, source_one, partial)
    chains_one = [Chain(reduce_rows(keep[0], got[0])), Chain(reduce_columns(keep[1], got[1]))]
    (gradient,) = advance([head_chain] + chains_one, gradient)
    gradient, first_one, *token_one = token_backward(
        gradient, first_state, gains[1], before_one, tok_all[1, 0], tok_turn[1, 1]
    )
    send, partial, _ = channel_backward(gradient, middle_zero, gains[0], inner_zero, source_zero)
    send, partial, gradient = advance([head_chain] + chains_one, send, partial, gradient)
    got = swap(send, "tok", 1)
    keep, gradient, second_zero = channel_backward(gradient, middle_zero, gains[0], inner_zero, source_zero, partial)
    chains_zero = [Chain(reduce_rows(keep[0], got[0])), Chain(reduce_columns(keep[1], got[1]))]
    (gradient,) = advance([head_chain] + chains_one + chains_zero, gradient)
    gradient, first_zero, *token_zero = token_backward(
        gradient, stem_state, gains[0], before_zero, tok_all[0, 0], tok_turn[0, 1]
    )
    stem_grads, stem_bias = stem_backward(device, gradient, mixed)
    small = gather_small(
        column_source,
        [stem_bias, first_zero, second_zero, first_one, second_one, last_part],
        bias_part,
        loss_local,
    )
    token_part = jnp.stack([jnp.stack(token_zero), jnp.stack(token_one)])[:, :, :all_patches].astype(low)
    dp_steps = [("dp", mask) for mask in [1] + dp_masks()[::-1]]
    stem_chain = Chain(reduce_cores(stem_grads))
    token_chain = Chain(reduce_tokens(token_part))
    small_chain = Chain(sum_over(small, [("tok", 1), ("tok", 2)] + dp_steps))
    everything = [head_chain] + chains_one + chains_zero + [stem_chain, token_chain, small_chain]
    earlier = []
    while any(chain.state is not None for chain in everything):
        if not earlier and all(chain.result is not None for chain in chains_one):
            *earlier, squares_one = channel_step(
                1, device, chan_w, chan_m, chan_v, *[chain.result for chain in chains_one], []
            )
            earlier = list(advance(everything, *earlier))
        else:
            advance(everything)
    chan_first, chan_second, chan_update, squares_zero = channel_step(
        0, device, chan_w, chan_m, chan_v, *[chain.result for chain in chains_zero], earlier
    )
    token_grad = token_chain.result.astype(jnp.float32)
    small = small_chain.result
    vector_grad = small[:NV, :width]
    bias_grad = small[NV, :classes_all]
    loss_total = small[NV + 1, 0]
    placed = lambda parts: [parts[0], parts[2], parts[1], parts[3]]
    head_grad = ordered(placed(head_chain.result), 1)[:, :classes_all].astype(jnp.float32)
    stem_grad = ordered(placed(stem_chain.result), 1).astype(jnp.float32).T
    stem_first, stem_second, stem_update = moments(stem_w, stem_grad, stem_m, stem_v, weight_decay)
    tok_first, tok_second, tok_update = moments(tok_w, token_grad, tok_m, tok_v, weight_decay)
    head_first, head_second, head_update = moments(head_w, head_grad, head_m, head_v, weight_decay)
    vec_first, vec_second, vec_update = moments(vec_w, vector_grad, vec_m, vec_v, 0.0)
    hb_first, hb_second, hb_update = moments(hb_w, bias_grad, hb_m, hb_v, 0.0)
    matrix_groups = 2 * LAYERS
    squares = jnp.stack([squares_zero, squares_one])
    weight_squares = jnp.concatenate(
        [
            row_squares(stem_w, 1) / count_tok,
            row_squares(tok_w, matrix_groups) / count_dp,
            squares[:, :, 0].reshape(-1) / count_tok,
            row_squares(head_w, 1) / count_tok,
        ]
    )
    update_squares = jnp.concatenate(
        [
            row_squares(stem_update, 1) / count_tok,
            row_squares(tok_update, matrix_groups) / count_dp,
            squares[:, :, 1].reshape(-1) / count_tok,
            row_squares(head_update, 1) / count_tok,
        ]
    )
    norm_chain = Chain(
        sum_over(jnp.stack([weight_squares, update_squares]), [("tok", 1), ("tok", 2)] + dp_steps)
    )
    while norm_chain.state is not None:
        advance([norm_chain])
    weight_total, update_total = norm_chain.result
    weight_norms = jnp.sqrt(weight_total)
    update_norms = jnp.sqrt(update_total)
    stem_end = 1
    tok_end = 1 + matrix_groups
    chan_end = 1 + 2 * matrix_groups
    stem_new = renew(stem_w, stem_update, weight_norms[0:stem_end], update_norms[0:stem_end], 1)
    tok_new = renew(
        tok_w,
        tok_update,
        weight_norms[stem_end:tok_end],
        update_norms[stem_end:tok_end],
        matrix_groups,
    )
    chan_trust = weight_norms[tok_end:chan_end] / (update_norms[tok_end:chan_end] + epsilon)
    chan_new, chan_new_low = channel_renew(chan_trust.reshape(LAYERS, 2), chan_w, chan_update)
    head_new = renew(head_w, head_update, weight_norms[chan_end:], update_norms[chan_end:], 1)
    vec_weight_norm = jnp.sqrt(row_squares(vec_w, NV))
    vec_update_norm = jnp.sqrt(row_squares(vec_update, NV))
    hb_weight_norm = jnp.sqrt(row_squares(hb_w, 1))
    hb_update_norm = jnp.sqrt(row_squares(hb_update, 1))
    vec_new = renew(vec_w, vec_update, vec_weight_norm, vec_update_norm, NV)
    hb_new = renew(hb_w, hb_update, hb_weight_norm, hb_update_norm, 1)
    norms = jnp.stack(
        [
            jnp.concatenate([weight_norms, vec_weight_norm, hb_weight_norm]),
            jnp.concatenate([update_norms, vec_update_norm, hb_update_norm]),
        ],
        1,
    )
    loss_parts = jnp.stack([loss_total, total])
    return (
        stem_new,
        stem_first,
        stem_second,
        tok_new,
        tok_first,
        tok_second,
        chan_new,
        chan_first,
        chan_second,
        head_new,
        head_first,
        head_second,
        vec_new,
        vec_first,
        vec_second,
        hb_new,
        hb_first,
        hb_second,
        stem_new.astype(jnp.bfloat16),
        tok_new.astype(jnp.bfloat16),
        chan_new_low,
        head_new.astype(jnp.bfloat16),
        norms,
        loss_parts,
    )


def solution(mesh):
    in_specs = (
        P("tok", "dp", None),
        P(),
        P(),
        P(),
        P(),
        P(),
        P(None, "dp"),
        P(None, "dp"),
        P(None, "dp"),
        P(None, None, None, "tok"),
        P(None, None, None, "tok"),
        P(None, None, None, "tok"),
        P(None, None, "dp", None),
        P(None, None, "dp", None),
        P(None, None, "dp", None),
        P("dp", None),
        P("dp", None),
        P("dp", None),
        P(),
        P(),
        P(),
        P(),
        P(),
        P(),
    )
    out_specs = (
        P(None, "dp"),
        P(None, "dp"),
        P(None, "dp"),
        P(None, None, None, "tok"),
        P(None, None, None, "tok"),
        P(None, None, None, "tok"),
        P(None, None, "dp", None),
        P(None, None, "dp", None),
        P(None, None, "dp", None),
        P("dp", None),
        P("dp", None),
        P("dp", None),
        P(),
        P(),
        P(),
        P(),
        P(),
        P(),
        P(None, "dp"),
        P(None, None, None, "tok"),
        P(None, None, "dp", None),
        P("dp", None),
        P(),
        P(),
    )
    return jax.shard_map(body, mesh=mesh, in_specs=in_specs, out_specs=out_specs, check_vma=False)
```

time: 810 us -> 608 us (0.75)
  matrix products: 200 us -> 0 us
  Pallas kernels: 0 us -> 173 us
  other arithmetic: 109 us -> 31.5 us
  waiting for transfers between devices: 286 us -> 209 us
  local copies, waits for them, and re-layouts: 54.8 us -> 96.8 us
  blocking collectives: 39.4 us -> 0 us
  starting transfers between devices: 86.2 us -> 66.9 us
    dot_general x30 -> x0, matrix products: 200 us -> none  [the longest x2 68.4 us: layer_backward(): jnp.einsum('bsc,cf->bsf', grad_out, channel_out, preferred_element_type=j...]
    pallas_call x0 -> x33, Pallas kernels: none -> 173 us  [the longest x4 68.4 us: channel_backward(): pl.pallas_call(functools.partial(channel_backward_kernel, source, last),...]
    psum x1 -> x0, waiting for transfers between devices: 59.7 us -> none  [body(): token_grad = lax.psum(token_part, 'dp')]
    psum x1 -> x0, blocking collectives: 39.4 us -> none  [body(): lax.psum((weight_squares, update_squares), ('dp', 'tok'))]
    unnamed x420 -> x212, local copies, waits for them, and re-layouts: 18.6 us -> 54.1 us
    add x28 -> x1, other arithmetic: 29.3 us -> 0.07 us  [body(): rows[:, None] * shard + jnp.arange(shard, dtype=jnp.int32)[None, :]]
    squeeze x1 -> x11, local copies, waits for them, and re-layouts: 0.04 us -> 23.5 us  [the longest x2 9.96 us: body(): got[1]]
    ppermute x111 -> x77, starting transfers between devices: 86.2 us -> 66.8 us  [swap(): return lax.ppermute(array, axis, [(i, i ^ mask) for i in range(count)])]
  transfers between devices with their start and end apart: 112 -> 79, of which waited for: 42 -> 29; matrix products, arithmetic and copies ran while one was open for 19% -> 12% of each run, Pallas kernels for 0% -> 19%
where the time goes in v2:
time: 608 us; the launch traced here: 600 us
  waiting for transfers between devices  209 us (34%)
  Pallas kernels  173 us (28%)
  local copies, waits for them, and re-layouts  96.8 us (16%)
  starting transfers between devices  66.9 us (11%)
  other arithmetic  31.5 us (5%)
  between operations  22.1 us (4%)
    ppermute x77, waiting for transfers between devices, swap(): return lax.ppermute(array, axis, [(i, i ^ mask) for i in range(count)])  209 us
    pallas_call x4, Pallas kernels, channel_backward(): pl.pallas_call(functools.partial(channel_backward_kernel, source, last),...  68.4 us
    ppermute x77, starting transfers between devices, swap(): return lax.ppermute(array, axis, [(i, i ^ mask) for i in range(count)])  66.8 us
    unnamed x212, local copies, waits for them, and re-layouts  54.1 us
    pallas_call x2, Pallas kernels, channel_forward(): pl.pallas_call(functools.partial(channel_forward_kernel, source), grid=(4...  28.1 us
    pallas_call x2, Pallas kernels, channel_step(): pl.pallas_call(step_kernel, grid=(2,), in_specs=[scalars, block, block, b...  18 us
    pallas_call x13, Pallas kernels, fold_all(): pl.pallas_call(functools.partial(fold_kernel, kinds), out_shape=flat, com...  17 us
    pallas_call x2, Pallas kernels, token_backward(): pl.pallas_call(token_backward_kernel, grid=(count,), in_specs=[one, one,...  16 us
  transfers between devices with their start and end apart: 79, of which 29 were waited for; matrix products, arithmetic and copies ran while one was open for 12% of the time, Pallas kernels for 19%

profile of v2, /device:TPU:0, one launch (start us, length us, event | category | flops | bytes accessed | tf_op | source)
XLA Modules:
  0.0 599.8 jit_solution(6358261206004565259)
XLA Ops:
  13.1 4.0 collective-permute-start
  24.1 31.5 %collective-permute-done = bf16[192,768]{1,0:T(8,128)(2,1)} collective-permute-done((bf16[192,768]{1,0:T(8,128)(2,1)}, bf16[192,768]{1,0:T(8,128)(2,1)}, u32[]{:S(2)}, u32[]{:S(2)}) %collective-permute-start) | collective-permute-done | bytes 294944 | tf_op jit(solution)/shard_map/ppermute | solution.py:624
  60.1 14.5 %collective-permute-done.4.incoming = bf16[49,8,768]{2,1,0:T(8,128)(2,1)S(1)} collective-permute-done((bf16[49,8,768]{2,1,0:T(8,128)(2,1)S(1)}, bf16[49,8,768]{2,1,0:T(8,128)(2,1)S(1)}, u32[]{:S(2)}, u32[]{:S(2)}) %collective-permute-start.4) | collective-permute-done | bytes 602144 | tf_op jit(solution)/shard_map/ppermute | solution.py:624
  74.7 27.7 %collective-permute-done.2 = bf16[384,768]{1,0:T(8,128)(2,1)} collective-permute-done((bf16[384,768]{1,0:T(8,128)(2,1)}, bf16[384,768]{1,0:T(8,128)(2,1)}, u32[]{:S(2)}, u32[]{:S(2)}) %collective-permute-start.2) | collective-permute-done | bytes 589856 | tf_op jit(solution)/shard_map/ppermute | solution.py:624
  106.8 14.2 %collective-permute-done.6 = bf16[384,768]{1,0:T(8,128)(2,1)S(1)} collective-permute-done((bf16[384,768]{1,0:T(8,128)(2,1)S(1)}, bf16[384,768]{1,0:T(8,128)(2,1)S(1)}, u32[]{:S(2)}, u32[]{:S(2)}) %collective-permute-start.6) | collective-permute-done | bytes 589856 | tf_op jit(solution)/shard_map/ppermute | solution.py:624
  127.7 2.1 mix.2
  131.3 30.3 %collective-permute-done.9.incoming = bf16[49,8,768]{2,1,0:T(8,128)(2,1)} collective-permute-done((bf16[49,8,768]{2,1,0:T(8,128)(2,1)S(1)}, bf16[49,8,768]{2,1,0:T(8,128)(2,1)}, u32[]{:S(2)}, u32[]{:S(2)}) %collective-permute-start.9) | collective-permute-done | bytes 602144 | tf_op jit(solution)/shard_map/ppermute | solution.py:624
  162.1 2.2 fusion.4
  164.7 2.3 fusion.53
  168.1 2.5 mix.3
  178.5 4.0 gather_fusion.2
  182.5 3.1 collective-permute-done.14.rest_6_
  186.1 2.1 bitcast_select_fusion
  188.6 6.9 %collective-permute-done.15.rest_7_ = bf16[98,768]{1,0:T(8,128)(2,1)S(1)} collective-permute-done((bf16[98,768]{1,0:T(8,128)(2,1)}, bf16[98,768]{1,0:T(8,128)(2,1)S(1)}, u32[]{:S(2)}, u32[]{:S(2)}) %collective-permute-start.15) | collective-permute-done | bytes 150560 | tf_op jit(solution)/shard_map/ppermute | solution.py:624
  198.2 4.0 token_forward.2
  206.5 15.1 %channel_forward.2 = (f32[800,768]{1,0:T(8,128)}, bf16[800,3072]{1,0:T(8,128)(2,1)}) custom-call(f32[800,768]{1,0:T(8,128)} %copy-done.63, f32[4,768]{1,0:T(4,128)S(1)} %get-tuple-element.728.gains, bf16[2,384,768]{2,1,0:T(8,128)(2,1)} %pad_maximum_fusion.rest_0_.rest_1_, bf16[2,384,768]{2,1,0:T(8,128)(2,1)} %collective-permute-done.7.rest_1_.rest_2_, ...), custom_call_target="tpu_custom_call" | custom-call | flops 7549747200 | bytes 14352384 | tf_op jit(solution)/shard_map/channel_forward/pallas_call | solution.py:177
  223.3 4.0 token_forward.3
  231.8 13.0 %channel_forward.3 = (f32[800,768]{1,0:T(8,128)S(1)}, bf16[800,3072]{1,0:T(8,128)(2,1)S(1)}) custom-call(f32[800,768]{1,0:T(8,128)S(1)} %copy-done.65, f32[4,768]{1,0:T(4,128)S(1)} %get-tuple-element.727.gains, s32[8]{0:T(128)S(1)} %get-tuple-element.740.rest_0_.rest_1_, s32[1]{0:T(128)} %bitcast.1.device.rest_1_.rest_2_, bf16[8,4,192,768]{3,2,1,0:T(8,128)(2,1)} %bitcast.116), custom_call_target="tpu_custom_call" | custom-call | flops 7549747200 | bytes 14352384 | tf_op jit(solution)/shard_map/channel_forward/pallas_call | solution.py:177
  244.9 2.2 copy-done.67
  247.1 3.6 head_step.1
  250.7 15.8 %channel_backward.4 = (bf16[2,2,768,768]{3,2,1,0:T(8,128)(2,1)}, f32[800,768]{1,0:T(8,128)S(1)}, f32[2,768]{1,0:T(2,128)}) custom-call(f32[800,768]{1,0:T(8,128)S(1)} %get-tuple-element.337.gradient, f32[800,768]{1,0:T(8,128)S(1)} %copy-done.66, f32[4,768]{1,0:T(4,128)S(1)} %get-tuple-element.727.gains, bf16[800,3072]{1,0:T(8,128)(2,1)} %copy-done.67, ...), custom_call_target="tpu_custom_call" | custom-call | flops 7549747200 | bytes 11894784 | tf_op jit(solution)/shard_map/channel_backward/pallas_call | solution.py:247
  267.2 16.1 %channel_backward.5 = (bf16[2,2,768,768]{3,2,1,0:T(8,128)(2,1)}, f32[800,768]{1,0:T(8,128)S(1)}, f32[2,768]{1,0:T(2,128)S(1)}) custom-call(f32[800,768]{1,0:T(8,128)S(1)} %get-tuple-element.337.gradient, f32[800,768]{1,0:T(8,128)S(1)} %copy-done.66, f32[4,768]{1,0:T(4,128)S(1)} %get-tuple-element.727.gains, bf16[800,3072]{1,0:T(8,128)(2,1)} %copy-done.67, ...), custom_call_target="tpu_custom_call" | custom-call | flops 7549747200 | bytes 11894784 | tf_op jit(solution)/shard_map/channel_backward/pallas_call | solution.py:247
  283.4 4.1 slice_bitcast_fusion.6
  287.5 4.9 slice_bitcast_fusion.2
  292.3 4.9 fold_all.13
  303.9 8.0 %token_backward.2 = (f32[800,768]{1,0:T(8,128)S(1)}, f32[2,768]{1,0:T(2,128)S(1)}, f32[200,384]{1,0:T(8,128)S(1)}, f32[200,384]{1,0:T(8,128)S(1)}) custom-call(f32[800,768]{1,0:T(8,128)S(1)} %get-tuple-element.355.gradient, f32[800,768]{1,0:T(8,128)} %get-tuple-element.328.state, f32[4,768]{1,0:T(4,128)S(1)} %get-tuple-element.727.gains, ...), custom_call_target="tpu_custom_call" | custom-call | flops 1887436800 | bytes 9830400 | tf_op jit(solution)/shard_map/token_backward/pallas_call | solution.py:382
  314.3 17.1 %channel_backward.6 = (bf16[2,2,768,768]{3,2,1,0:T(8,128)(2,1)}, f32[800,768]{1,0:T(8,128)}, f32[2,768]{1,0:T(2,128)}) custom-call(f32[800,768]{1,0:T(8,128)} %copy-done.44, f32[800,768]{1,0:T(8,128)} %copy-done.63, f32[4,768]{1,0:T(4,128)S(1)} %get-tuple-element.728.gains, bf16[800,3072]{1,0:T(8,128)(2,1)} %get-tuple-element.358.inner, ...), custom_call_target="tpu_custom_call" | custom-call | flops 7549747200 | bytes 11894784 | tf_op jit(solution)/shard_map/channel_backward/pallas_call | solution.py:247
  331.4 5.3 collective-permute-done.22.refs_1_
  341.4 2.3 fold_all.14
  345.4 19.3 %channel_backward.7 = (bf16[2,2,768,768]{3,2,1,0:T(8,128)(2,1)}, f32[800,768]{1,0:T(8,128)}, f32[2,768]{1,0:T(2,128)S(1)}) custom-call(f32[800,768]{1,0:T(8,128)} %copy-done.44, f32[800,768]{1,0:T(8,128)} %copy-done.63, f32[4,768]{1,0:T(4,128)S(1)} %get-tuple-element.728.gains, bf16[800,3072]{1,0:T(8,128)(2,1)} %get-tuple-element.358.inner, ...), custom_call_target="tpu_custom_call" | custom-call | flops 7549747200 | bytes 11894784 | tf_op jit(solution)/shard_map/channel_backward/pallas_call | solution.py:247
  364.7 4.9 slice_bitcast_fusion.4
  370.1 5.1 slice_bitcast_fusion
  376.7 8.0 %token_backward.3 = (f32[800,768]{1,0:T(8,128)S(1)}, f32[2,768]{1,0:T(2,128)S(1)}, f32[200,384]{1,0:T(8,128)S(1)}, f32[200,384]{1,0:T(8,128)S(1)}) custom-call(f32[800,768]{1,0:T(8,128)S(1)} %copy-done.7, f32[800,768]{1,0:T(8,128)} %copy-done.5, f32[4,768]{1,0:T(4,128)S(1)} %get-tuple-element.728.gains, bf16[4,384,768]{2,1,0:T(8,128)(2,1)S(1)} %copy-done.9, ...), custom_call_target="tpu_custom_call" | custom-call | flops 1887436800 | bytes 9830400 | tf_op jit(solution)/shard_map/token_backward/pallas_call | solution.py:382
  388.2 5.7 fold_all.15
  396.6 2.2 copy.118
  398.9 3.1 collective-permute-start.30
  404.3 7.1 %collective-permute-done.29.refs_1_ = bf16[192,256]{1,0:T(8,128)(2,1)S(1)} collective-permute-done((bf16[192,256]{1,0:T(8,128)(2,1)}, bf16[192,256]{1,0:T(8,128)(2,1)S(1)}, u32[]{:S(2)}, u32[]{:S(2)}) %collective-permute-start.29) | collective-permute-done | bytes 98336 | tf_op jit(solution)/shard_map/ppermute | solution.py:624
  411.4 4.8 collective-permute-done.30.refs_3_
  416.9 8.8 %collective-permute-done.31.refs_5_ = bf16[192,768]{1,0:T(8,128)(2,1)S(1)} collective-permute-done((bf16[192,768]{1,0:T(8,128)(2,1)S(1)}, bf16[192,768]{1,0:T(8,128)(2,1)S(1)}, u32[]{:S(2)}, u32[]{:S(2)}) %collective-permute-start.31) | collective-permute-done | bytes 294944 | tf_op jit(solution)/shard_map/ppermute | solution.py:624
  435.0 2.9 fold_all.16
  440.6 2.5 collective-permute-start.37
  444.0 7.5 %collective-permute-done.37.refs_1_ = bf16[96,256]{1,0:T(8,128)(2,1)S(1)} collective-permute-done((bf16[96,256]{1,0:T(8,128)(2,1)S(1)}, bf16[96,256]{1,0:T(8,128)(2,1)S(1)}, u32[]{:S(2)}, u32[]{:S(2)}) %collective-permute-start.37) | collective-permute-done | bytes 49184 | tf_op jit(solution)/shard_map/ppermute | solution.py:624
  452.6 3.4 collective-permute-start.39
  456.1 3.5 collective-permute-done.39.refs_5_
  460.5 4.7 collective-permute-done.43.refs_13_
  470.1 2.2 collective-permute-done.46
  473.4 2.6 collective-permute-start.52
  478.7 5.9 collective-permute-done.51.rest_3_
  484.7 5.4 collective-permute-done.52.refs_1_
  499.9 2.0 copy.121
  501.9 9.1 %channel_step.2 = (f32[2,2,96,3072]{3,2,1,0:T(8,128)}, f32[2,2,96,3072]{3,2,1,0:T(8,128)}, f32[2,2,96,3072]{3,2,1,0:T(8,128)S(1)}, f32[2,2]{1,0:T(2,128)S(1)}) custom-call(s32[1]{0:T(128)} %bitcast.1.device.rest_1_.rest_2_, f32[2,2,96,3072]{3,2,1,0:T(8,128)} %weight.5, f32[2,2,96,3072]{3,2,1,0:T(8,128)} %mean.3, f32[2,2,96,3072]{3,2,1,0:T(8,128)} %power.3, ...), custom_call_target="tpu_custom_call" | custom-call | flops 5898240 | bytes 15335424 | tf_op jit(solution)/shard_map/channel_step/pallas_call | solution.py:311
  511.0 2.2 copy-done.1
  513.5 2.0 collective-permute-start.68
  518.4 4.0 collective-permute-done.66.refs_1_
  528.3 6.7 %collective-permute-done.67.refs_3_ = bf16[2,2,196,96]{3,2,1,0:T(8,128)(2,1)S(1)} collective-permute-done((bf16[2,2,196,96]{3,2,1,0:T(8,128)(2,1)S(1)}, bf16[2,2,196,96]{3,2,1,0:T(8,128)(2,1)S(1)}, u32[]{:S(2)}, u32[]{:S(2)}) %collective-permute-start.67) | collective-permute-done | bytes 150560 | tf_op jit(solution)/shard_map/ppermute | solution.py:624
  540.2 2.3 copy-done.2
  542.5 8.9 %channel_step.3 = (f32[2,2,96,3072]{3,2,1,0:T(8,128)}, f32[2,2,96,3072]{3,2,1,0:T(8,128)}, f32[2,2,96,3072]{3,2,1,0:T(8,128)S(1)}, f32[2,2]{1,0:T(2,128)S(1)}) custom-call(s32[1]{0:T(128)} %bitcast.1.device.rest_1_.rest_2_, f32[2,2,96,3072]{3,2,1,0:T(8,128)} %weight.5, ...), custom_call_target="tpu_custom_call", output_to_operand_aliasing={{0}: (10, {}), {1}: (11, {}), {2}: (12, {})} | custom-call | flops 5898240 | bytes 15335424 | tf_op jit(solution)/shard_map/channel_step/pallas_call | solution.py:311
  551.4 2.2 copy-done.3
  561.6 2.1 collective-permute-done.73.refs_1_
  568.3 2.6 collective-permute-done.75.refs_1_
  573.0 2.4 collective-permute-done.76.refs_1_
  581.5 2.3 copy-done
  583.9 2.3 copy-done.4
  586.2 3.9 channel_renew.1
  (459 shorter events, 145.1 us)
Async XLA Ops:
  7.2 171.3 %all-gather.6.cloned.1.call-start = ((), (), s32[]{:S(2)}) async-start(), calls=%async_computation.1 | async-start | bytes 3096576 | tf_op jit(solution)/shard_map/all_gather | solution.py:886
  10.1 220.0 %all-gather.4.cloned.1.call-start = ((), (), s32[]{:S(2)}) async-start(), calls=%async_computation | async-start | bytes 9732096 | tf_op jit(solution)/shard_map/all_gather | solution.py:887
  13.1 42.5 %collective-permute-start = (bf16[192,768]{1,0:T(8,128)(2,1)}, bf16[192,768]{1,0:T(8,128)(2,1)}, u32[]{:S(2)}, u32[]{:S(2)}) collective-permute-start(bf16[192,768]{1,0:T(8,128)(2,1)} %pad_maximum_fusion.7), channel_id=1, source_target_pairs={{0,16},{4,20},{8,24},{12,28},{16,0},{20,4},{24,8},{28,12},{1,17},{... | collective-permute-start | bytes 884744 | tf_op jit(solution)/shard_map/ppermute | solution.py:624
  17.3 6.8 %collective-permute-start.1 = (bf16[2,2,196,96]{2,3,1,0:T(8,128)(2,1)S(1)}, bf16[2,2,196,96]{2,3,1,0:T(8,128)(2,1)S(1)}, u32[]{:S(2)}, u32[]{:S(2)}) collective-permute-start(bf16[2,2,196,96]{2,3,1,0:T(8,128)(2,1)S(1)} %get-tuple-element.716), channel_id=1, source_target_pairs={{0,2},{1,3},{2,0},{3,1},{4,6},{5,7},{6,4},{7,5},{8,10},{9,11},{10,... | collective-permute-start | bytes 451592 | tf_op jit(solution)/shard_map/ppermute | solution.py:624
  18.9 55.8 %collective-permute-start.4 = (bf16[49,8,768]{2,1,0:T(8,128)(2,1)S(1)}, bf16[49,8,768]{2,1,0:T(8,128)(2,1)S(1)}, u32[]{:S(2)}, u32[]{:S(2)}) collective-permute-start(bf16[49,8,768]{2,1,0:T(8,128)(2,1)S(1)} %get-tuple-element.697.own), channel_id=1, source_target_pairs={{0,16},{4,20},{8,24},{12,28},{16,0},{20,4},{24,8},{28,12},{1,17},{... | collective-permute-start | bytes 1806344 | tf_op jit(solution)/shard_map/ppermute | solution.py:624
  57.4 45.0 %collective-permute-start.2 = (bf16[384,768]{1,0:T(8,128)(2,1)}, bf16[384,768]{1,0:T(8,128)(2,1)}, u32[]{:S(2)}, u32[]{:S(2)}) collective-permute-start(bf16[384,768]{1,0:T(8,128)(2,1)} %pad_maximum_fusion.2), channel_id=1, source_target_pairs={{0,8},{4,12},{8,0},{12,4},{16,24},{20,28},{24,16},{28,20},{1,9},{5... | collective-permute-start | bytes 1769480 | tf_op jit(solution)/shard_map/ppermute | solution.py:624
  103.5 17.5 %collective-permute-start.6 = (bf16[384,768]{1,0:T(8,128)(2,1)S(1)}, bf16[384,768]{1,0:T(8,128)(2,1)S(1)}, u32[]{:S(2)}, u32[]{:S(2)}) collective-permute-start(bf16[384,768]{1,0:T(8,128)(2,1)S(1)} %pad_maximum_fusion.4), channel_id=1, source_target_pairs={{0,2},{1,3},{2,0},{3,1},{4,6},{5,7},{6,4},{7,5},{8,10},{9,11},{10,... | collective-permute-start | bytes 1769480 | tf_op jit(solution)/shard_map/ppermute | solution.py:624
  105.2 17.2 %collective-permute-start.5 = (bf16[384,768]{1,0:T(8,128)(2,1)S(1)}, bf16[384,768]{1,0:T(8,128)(2,1)S(1)}, u32[]{:S(2)}, u32[]{:S(2)}) collective-permute-start(bf16[384,768]{1,0:T(8,128)(2,1)S(1)} %pad_maximum_fusion.3), channel_id=1, source_target_pairs={{0,4},{4,0},{8,12},{12,8},{16,20},{20,16},{24,28},{28,24},{1,5},{5... | collective-permute-start | bytes 1769480 | tf_op jit(solution)/shard_map/ppermute | solution.py:624
  122.5 45.6 %collective-permute-start.8 = (bf16[2,384,768]{2,1,0:T(8,128)(2,1)S(1)}, bf16[2,384,768]{2,1,0:T(8,128)(2,1)}, u32[]{:S(2)}, u32[]{:S(2)}) collective-permute-start(bf16[2,384,768]{2,1,0:T(8,128)(2,1)S(1)} %pad_maximum_fusion.1.rest_4_.rest_5_), channel_id=1, source_target_pairs={{0,4},{4,0},{8,12},{12,8},{16,20},{20,16},{24,28},{28,24},{1,5},{5... | collective-permute-start | bytes 3538952 | tf_op jit(solution)/shard_map/ppermute | solution.py:624
  125.2 42.9 %collective-permute-start.7 = (bf16[2,384,768]{2,1,0:T(8,128)(2,1)}, bf16[2,384,768]{2,1,0:T(8,128)(2,1)}, u32[]{:S(2)}, u32[]{:S(2)}) collective-permute-start(bf16[2,384,768]{2,1,0:T(8,128)(2,1)} %pad_maximum_fusion.rest_0_.rest_1_), channel_id=1, source_target_pairs={{0,2},{1,3},{2,0},{3,1},{4,6},{5,7},{6,4},{7,5},{8,10},{9,11},{10,... | collective-permute-start | bytes 3538952 | tf_op jit(solution)/shard_map/ppermute | solution.py:624
  125.8 35.8 %collective-permute-start.9 = (bf16[49,8,768]{2,1,0:T(8,128)(2,1)S(1)}, bf16[49,8,768]{2,1,0:T(8,128)(2,1)}, u32[]{:S(2)}, u32[]{:S(2)}) collective-permute-start(bf16[49,8,768]{2,1,0:T(8,128)(2,1)S(1)} %get-tuple-element.303.own), channel_id=1, source_target_pairs={{0,16},{4,20},{8,24},{12,28},{16,0},{20,4},{24,8},{28,12},{1,17},{... | collective-permute-start | bytes 1806344 | tf_op jit(solution)/shard_map/ppermute | solution.py:624
  129.8 37.3 %collective-permute-start.10 = (bf16[98,768]{1,0:T(8,128)(2,1)}, bf16[98,768]{1,0:T(8,128)(2,1)S(1)}, u32[]{:S(2)}, u32[]{:S(2)}) collective-permute-start(bf16[98,768]{1,0:T(8,128)(2,1)} %get-tuple-element.306), channel_id=1, source_target_pairs={{0,1},{1,0},{2,3},{3,2},{4,5},{5,4},{6,7},{7,6},{8,9},{9,8},{10,11... | collective-permute-start | bytes 451592 | tf_op jit(solution)/shard_map/ppermute | solution.py:624
  129.8 37.3 %collective-permute-start.11 = (bf16[98,768]{1,0:T(8,128)(2,1)}, bf16[98,768]{1,0:T(8,128)(2,1)S(1)}, u32[]{:S(2)}, u32[]{:S(2)}) collective-permute-start(bf16[98,768]{1,0:T(8,128)(2,1)} %get-tuple-element.307), channel_id=1, source_target_pairs={{0,2},{1,3},{2,0},{3,1},{4,6},{5,7},{6,4},{7,5},{8,10},{9,11},{10,... | collective-permute-start | bytes 451592 | tf_op jit(solution)/shard_map/ppermute | solution.py:624
  161.5 6.6 %collective-permute-start.12 = (bf16[98,768]{1,0:T(8,128)(2,1)}, bf16[98,768]{1,0:T(8,128)(2,1)S(1)}, u32[]{:S(2)}, u32[]{:S(2)}) collective-permute-start(bf16[98,768]{1,0:T(8,128)(2,1)} %get-tuple-element.308), channel_id=1, source_target_pairs={{0,3},{1,2},{2,1},{3,0},{4,7},{5,6},{6,5},{7,4},{8,11},{9,10},{10,... | collective-permute-start | bytes 451592 | tf_op jit(solution)/shard_map/ppermute | solution.py:624
  171.5 35.0 %collective-permute-start.16 = (bf16[2,384,768]{2,1,0:T(8,128)(2,1)}, bf16[2,384,768]{2,1,0:T(8,128)(2,1)}, u32[]{:S(2)}, u32[]{:S(2)}) collective-permute-start(bf16[2,384,768]{2,1,0:T(8,128)(2,1)} %pad_maximum_fusion.rest_0_.rest_1_), channel_id=1, source_target_pairs={{0,1},{1,0},{2,3},{3,2},{4,5},{5,4},{6,7},{7,6},{8,9},{9,8},{10,11... | collective-permute-start | bytes 3538952 | tf_op jit(solution)/shard_map/ppermute | solution.py:624
  171.8 34.7 %collective-permute-start.17 = (bf16[2,384,768]{2,1,0:T(8,128)(2,1)}, bf16[2,384,768]{2,1,0:T(8,128)(2,1)}, u32[]{:S(2)}, u32[]{:S(2)}) collective-permute-start(bf16[2,384,768]{2,1,0:T(8,128)(2,1)} %collective-permute-done.7.rest_1_.rest_2_), channel_id=1, source_target_pairs={{0,1},{1,0},{2,3},{3,2},{4,5},{5,4},{6,7},{7,6},{8,9},{9,8},{10,11... | collective-permute-start | bytes 3538952 | tf_op jit(solution)/shard_map/ppermute | solution.py:624
  172.0 34.5 %collective-permute-start.18 = (bf16[2,384,768]{2,1,0:T(8,128)(2,1)S(1)}, bf16[2,384,768]{2,1,0:T(8,128)(2,1)}, u32[]{:S(2)}, u32[]{:S(2)}) collective-permute-start(bf16[2,384,768]{2,1,0:T(8,128)(2,1)S(1)} %pad_maximum_fusion.1.rest_4_.rest_5_), channel_id=1, source_target_pairs={{0,1},{1,0},{2,3},{3,2},{4,5},{5,4},{6,7},{7,6},{8,9},{9,8},{10,11... | collective-permute-start | bytes 3538952 | tf_op jit(solution)/shard_map/ppermute | solution.py:624
  172.3 34.2 %collective-permute-start.19 = (bf16[2,384,768]{2,1,0:T(8,128)(2,1)}, bf16[2,384,768]{2,1,0:T(8,128)(2,1)}, u32[]{:S(2)}, u32[]{:S(2)}) collective-permute-start(bf16[2,384,768]{2,1,0:T(8,128)(2,1)} %collective-permute-done.8.rest_5_.rest_6_), channel_id=1, source_target_pairs={{0,1},{1,0},{2,3},{3,2},{4,5},{5,4},{6,7},{7,6},{8,9},{9,8},{10,11... | collective-permute-start | bytes 3538952 | tf_op jit(solution)/shard_map/ppermute | solution.py:624
  175.6 10.1 %collective-permute-start.14 = (bf16[98,768]{1,0:T(8,128)(2,1)S(1)}, bf16[98,768]{1,0:T(8,128)(2,1)S(1)}, u32[]{:S(2)}, u32[]{:S(2)}) collective-permute-start(bf16[98,768]{1,0:T(8,128)(2,1)S(1)} %get-tuple-element.317), channel_id=1, source_target_pairs={{0,2},{1,3},{2,0},{3,1},{4,6},{5,7},{6,4},{7,5},{8,10},{9,11},{10,... | collective-permute-start | bytes 451592 | tf_op jit(solution)/shard_map/ppermute | solution.py:624
  185.6 9.9 %collective-permute-start.15 = (bf16[98,768]{1,0:T(8,128)(2,1)}, bf16[98,768]{1,0:T(8,128)(2,1)S(1)}, u32[]{:S(2)}, u32[]{:S(2)}) collective-permute-start(bf16[98,768]{1,0:T(8,128)(2,1)} %get-tuple-element.318), channel_id=1, source_target_pairs={{0,3},{1,2},{2,1},{3,0},{4,7},{5,6},{6,5},{7,4},{8,11},{9,10},{10,... | collective-permute-start | bytes 451592 | tf_op jit(solution)/shard_map/ppermute | solution.py:624
  266.5 21.0 %collective-permute-start.21 = (bf16[2,2,768,768]{3,2,1,0:T(8,128)(2,1)}, bf16[2,2,768,768]{3,2,1,0:T(8,128)(2,1)}, u32[]{:S(2)}, u32[]{:S(2)}) collective-permute-start(bf16[2,2,768,768]{3,2,1,0:T(8,128)(2,1)} %get-tuple-element.341), channel_id=1, source_target_pairs={{0,1},{1,0},{2,3},{3,2},{4,5},{5,4},{6,7},{7,6},{8,9},{9,8},{10,11... | collective-permute-start | bytes 14155784 | tf_op jit(solution)/shard_map/ppermute | solution.py:624
  266.7 25.7 %collective-permute-start.20 = (bf16[2,768,256]{2,1,0:T(8,128)(2,1)S(1)}, bf16[2,768,256]{2,1,0:T(8,128)(2,1)S(1)}, u32[]{:S(2)}, u32[]{:S(2)}) collective-permute-start(bf16[2,768,256]{2,1,0:T(8,128)(2,1)S(1)} %get-tuple-element.695), channel_id=1, source_target_pairs={{0,1},{1,0},{2,3},{3,2},{4,5},{5,4},{6,7},{7,6},{8,9},{9,8},{10,11... | collective-permute-start | bytes 2359304 | tf_op jit(solution)/shard_map/ppermute | solution.py:624
  300.0 37.5 %collective-permute-start.23 = (bf16[2,384,768]{2,1,0:T(8,128)(2,1)}, bf16[2,384,768]{2,1,0:T(8,128)(2,1)}, u32[]{:S(2)}, u32[]{:S(2)}) collective-permute-start(bf16[2,384,768]{2,1,0:T(8,128)(2,1)} %get-tuple-element.352), channel_id=1, source_target_pairs={{0,4},{4,0},{8,12},{12,8},{16,20},{20,16},{24,28},{28,24},{1,5},{5... | collective-permute-start | bytes 3538952 | tf_op jit(solution)/shard_map/ppermute | solution.py:624
  300.0 37.5 %collective-permute-start.24 = (bf16[768,768]{1,0:T(8,128)(2,1)}, bf16[768,768]{1,0:T(8,128)(2,1)}, u32[]{:S(2)}, u32[]{:S(2)}) collective-permute-start(bf16[768,768]{1,0:T(8,128)(2,1)} %get-tuple-element.354), channel_id=1, source_target_pairs={{0,2},{1,3},{2,0},{3,1},{4,6},{5,7},{6,4},{7,5},{8,10},{9,11},{10,... | collective-permute-start | bytes 3538952 | tf_op jit(solution)/shard_map/ppermute | solution.py:624
  301.4 35.4 %collective-permute-start.22 = (bf16[768,256]{1,0:T(8,128)(2,1)}, bf16[768,256]{1,0:T(8,128)(2,1)S(1)}, u32[]{:S(2)}, u32[]{:S(2)}) collective-permute-start(bf16[768,256]{1,0:T(8,128)(2,1)} %copy-done.45), channel_id=1, source_target_pairs={{0,2},{1,3},{2,0},{3,1},{4,6},{5,7},{6,4},{7,5},{8,10},{9,11},{10,... | collective-permute-start | bytes 1179656 | tf_op jit(solution)/shard_map/ppermute | solution.py:624
  337.5 32.6 %collective-permute-start.28 = (bf16[2,2,768,768]{3,2,1,0:T(8,128)(2,1)}, bf16[2,2,768,768]{3,2,1,0:T(8,128)(2,1)}, u32[]{:S(2)}, u32[]{:S(2)}) collective-permute-start(bf16[2,2,768,768]{3,2,1,0:T(8,128)(2,1)} %get-tuple-element.376), channel_id=1, source_target_pairs={{0,1},{1,0},{2,3},{3,2},{4,5},{5,4},{6,7},{7,6},{8,9},{9,8},{10,11... | collective-permute-start | bytes 14155784 | tf_op jit(solution)/shard_map/ppermute | solution.py:624
  343.7 32.9 %collective-permute-start.26 = (bf16[2,192,768]{2,1,0:T(8,128)(2,1)S(1)}, bf16[2,192,768]{2,1,0:T(8,128)(2,1)S(1)}, u32[]{:S(2)}, u32[]{:S(2)}) collective-permute-start(bf16[2,192,768]{2,1,0:T(8,128)(2,1)S(1)} %get-tuple-element.370), channel_id=1, source_target_pairs={{0,8},{4,12},{8,0},{12,4},{16,24},{20,28},{24,16},{28,20},{1,9},{5... | collective-permute-start | bytes 1769480 | tf_op jit(solution)/shard_map/ppermute | solution.py:624
  343.8 32.8 %collective-permute-start.27 = (bf16[384,768]{1,0:T(8,128)(2,1)S(1)}, bf16[384,768]{1,0:T(8,128)(2,1)S(1)}, u32[]{:S(2)}, u32[]{:S(2)}) collective-permute-start(bf16[384,768]{1,0:T(8,128)(2,1)S(1)} %get-tuple-element.372), channel_id=1, source_target_pairs={{0,4},{4,0},{8,12},{12,8},{16,20},{20,16},{24,28},{28,24},{1,5},{5... | collective-permute-start | bytes 1769480 | tf_op jit(solution)/shard_map/ppermute | solution.py:624
  369.6 7.0 %collective-permute-start.25 = (bf16[384,256]{1,0:T(8,128)(2,1)S(1)}, bf16[384,256]{1,0:T(8,128)(2,1)S(1)}, u32[]{:S(2)}, u32[]{:S(2)}) collective-permute-start(bf16[384,256]{1,0:T(8,128)(2,1)S(1)} %get-tuple-element.368), channel_id=1, source_target_pairs={{0,4},{4,0},{8,12},{12,8},{16,20},{20,16},{24,28},{28,24},{1,5},{5... | collective-permute-start | bytes 589832 | tf_op jit(solution)/shard_map/ppermute | solution.py:624
  388.2 13.9 %collective-permute-start.36 = (f32[16,1024]{1,0:T(8,128)S(1)}, f32[16,1024]{1,0:T(8,128)S(1)}, u32[]{:S(2)}, u32[]{:S(2)}) collective-permute-start(f32[16,1024]{1,0:T(8,128)S(1)} %gather_small.1.refs_14_), channel_id=1, source_target_pairs={{0,1},{1,0},{2,3},{3,2},{4,5},{5,4},{6,7},{7,6},{8,9},{9,8},{10,11... | collective-permute-start | bytes 196616 | tf_op jit(solution)/shard_map/ppermute | solution.py:624
  394.0 33.2 %collective-permute-start.32 = (bf16[2,384,768]{2,1,0:T(8,128)(2,1)}, bf16[2,384,768]{2,1,0:T(8,128)(2,1)}, u32[]{:S(2)}, u32[]{:S(2)}) collective-permute-start(bf16[2,384,768]{2,1,0:T(8,128)(2,1)} %get-tuple-element.395), channel_id=1, source_target_pairs={{0,4},{4,0},{8,12},{12,8},{16,20},{20,16},{24,28},{28,24},{1,5},{5... | collective-permute-start | bytes 3538952 | tf_op jit(solution)/shard_map/ppermute | solution.py:624
  394.5 32.7 %collective-permute-start.33 = (bf16[768,768]{1,0:T(8,128)(2,1)}, bf16[768,768]{1,0:T(8,128)(2,1)}, u32[]{:S(2)}, u32[]{:S(2)}) collective-permute-start(bf16[768,768]{1,0:T(8,128)(2,1)} %get-tuple-element.397), channel_id=1, source_target_pairs={{0,2},{1,3},{2,0},{3,1},{4,6},{5,7},{6,4},{7,5},{8,10},{9,11},{10,... | collective-permute-start | bytes 3538952 | tf_op jit(solution)/shard_map/ppermute | solution.py:624
  398.9 28.3 %collective-permute-start.34 = (bf16[2,768,192]{1,2,0:T(8,128)(2,1)}, bf16[2,768,192]{1,2,0:T(8,128)(2,1)S(1)}, u32[]{:S(2)}, u32[]{:S(2)}) collective-permute-start(bf16[2,768,192]{1,2,0:T(8,128)(2,1)} %copy.118), channel_id=1, source_target_pairs={{0,1},{1,0},{2,3},{3,2},{4,5},{5,4},{6,7},{7,6},{8,9},{9,8},{10,11... | collective-permute-start | bytes 1769480 | tf_op jit(solution)/shard_map/ppermute | solution.py:624
  398.9 17.3 %collective-permute-start.30 = (bf16[2,96,768]{2,1,0:T(8,128)(2,1)}, bf16[2,96,768]{2,1,0:T(8,128)(2,1)S(1)}, u32[]{:S(2)}, u32[]{:S(2)}) collective-permute-start(bf16[2,96,768]{2,1,0:T(8,128)(2,1)} %copy-done.48), channel_id=1, source_target_pairs={{0,16},{4,20},{8,24},{12,28},{16,0},{20,4},{24,8},{28,12},{1,17},{... | collective-permute-start | bytes 884744 | tf_op jit(solution)/shard_map/ppermute | solution.py:624
  402.7 8.7 %collective-permute-start.29 = (bf16[192,256]{1,0:T(8,128)(2,1)}, bf16[192,256]{1,0:T(8,128)(2,1)S(1)}, u32[]{:S(2)}, u32[]{:S(2)}) collective-permute-start(bf16[192,256]{1,0:T(8,128)(2,1)} %get-tuple-element.389), channel_id=1, source_target_pairs={{0,8},{4,12},{8,0},{12,4},{16,24},{20,28},{24,16},{28,20},{1,9},{5... | collective-permute-start | bytes 294920 | tf_op jit(solution)/shard_map/ppermute | solution.py:624
  411.4 15.1 %collective-permute-start.35 = (bf16[2,2,196,192]{3,2,1,0:T(8,128)(2,1)S(1)}, bf16[2,2,196,192]{3,2,1,0:T(8,128)(2,1)S(1)}, u32[]{:S(2)}, u32[]{:S(2)}) collective-permute-start(bf16[2,2,196,192]{3,2,1,0:T(8,128)(2,1)S(1)} %get-tuple-element.707), channel_id=1, source_target_pairs={{0,1},{1,0},{2,3},{3,2},{4,5},{5,4},{6,7},{7,6},{8,9},{9,8},{10,11... | collective-permute-start | bytes 903176 | tf_op jit(solution)/shard_map/ppermute | solution.py:624
  416.9 8.8 %collective-permute-start.31 = (bf16[192,768]{1,0:T(8,128)(2,1)S(1)}, bf16[192,768]{1,0:T(8,128)(2,1)S(1)}, u32[]{:S(2)}, u32[]{:S(2)}) collective-permute-start(bf16[192,768]{1,0:T(8,128)(2,1)S(1)} %copy-done.47), channel_id=1, source_target_pairs={{0,8},{4,12},{8,0},{12,4},{16,24},{20,28},{24,16},{28,20},{1,9},{5... | collective-permute-start | bytes 884744 | tf_op jit(solution)/shard_map/ppermute | solution.py:624
  438.0 27.3 %collective-permute-start.40 = (bf16[2,192,768]{2,1,0:T(8,128)(2,1)S(1)}, bf16[2,192,768]{2,1,0:T(8,128)(2,1)S(1)}, u32[]{:S(2)}, u32[]{:S(2)}) collective-permute-start(bf16[2,192,768]{2,1,0:T(8,128)(2,1)S(1)} %get-tuple-element.437), channel_id=1, source_target_pairs={{0,8},{4,12},{8,0},{12,4},{16,24},{20,28},{24,16},{28,20},{1,9},{5... | collective-permute-start | bytes 1769480 | tf_op jit(solution)/shard_map/ppermute | solution.py:624
  438.3 27.0 %collective-permute-start.41 = (bf16[384,768]{1,0:T(8,128)(2,1)S(1)}, bf16[384,768]{1,0:T(8,128)(2,1)S(1)}, u32[]{:S(2)}, u32[]{:S(2)}) collective-permute-start(bf16[384,768]{1,0:T(8,128)(2,1)S(1)} %get-tuple-element.439), channel_id=1, source_target_pairs={{0,4},{4,0},{8,12},{12,8},{16,20},{20,16},{24,28},{28,24},{1,5},{5... | collective-permute-start | bytes 1769480 | tf_op jit(solution)/shard_map/ppermute | solution.py:624
  439.4 13.2 %collective-permute-start.44 = (f32[16,1024]{1,0:T(8,128)S(1)}, f32[16,1024]{1,0:T(8,128)S(1)}, u32[]{:S(2)}, u32[]{:S(2)}) collective-permute-start(f32[16,1024]{1,0:T(8,128)S(1)} %get-tuple-element.458.refs_14_), channel_id=1, source_target_pairs={{0,2},{1,3},{2,0},{3,1},{4,6},{5,7},{6,4},{7,5},{8,10},{9,11},{10,... | collective-permute-start | bytes 196616 | tf_op jit(solution)/shard_map/ppermute | solution.py:624
  440.6 11.0 %collective-permute-start.37 = (bf16[96,256]{1,0:T(8,128)(2,1)S(1)}, bf16[96,256]{1,0:T(8,128)(2,1)S(1)}, u32[]{:S(2)}, u32[]{:S(2)}) collective-permute-start(bf16[96,256]{1,0:T(8,128)(2,1)S(1)} %get-tuple-element.432), channel_id=1, source_target_pairs={{0,16},{4,20},{8,24},{12,28},{16,0},{20,4},{24,8},{28,12},{1,17},{... | collective-permute-start | bytes 147464 | tf_op jit(solution)/shard_map/ppermute | solution.py:624
  443.1 22.2 %collective-permute-start.42 = (bf16[768,192]{1,0:T(8,128)(2,1)S(1)}, bf16[768,192]{1,0:T(8,128)(2,1)S(1)}, u32[]{:S(2)}, u32[]{:S(2)}) collective-permute-start(bf16[768,192]{1,0:T(8,128)(2,1)S(1)} %get-tuple-element.441), channel_id=1, source_target_pairs={{0,2},{1,3},{2,0},{3,1},{4,6},{5,7},{6,4},{7,5},{8,10},{9,11},{10,... | collective-permute-start | bytes 884744 | tf_op jit(solution)/shard_map/ppermute | solution.py:624
  451.5 13.7 %collective-permute-start.38 = (bf16[2,96,768]{2,1,0:T(8,128)(2,1)S(1)}, bf16[2,96,768]{2,1,0:T(8,128)(2,1)S(1)}, u32[]{:S(2)}, u32[]{:S(2)}) collective-permute-start(bf16[2,96,768]{2,1,0:T(8,128)(2,1)S(1)} %get-tuple-element.446.refs_2_), channel_id=1, source_target_pairs={{0,2},{1,3},{2,0},{3,1},{4,6},{5,7},{6,4},{7,5},{8,10},{9,11},{10,... | collective-permute-start | bytes 884744 | tf_op jit(solution)/shard_map/ppermute | solution.py:624
  452.6 7.0 %collective-permute-start.39 = (bf16[96,768]{1,0:T(8,128)(2,1)S(1)}, bf16[96,768]{1,0:T(8,128)(2,1)S(1)}, u32[]{:S(2)}, u32[]{:S(2)}) collective-permute-start(bf16[96,768]{1,0:T(8,128)(2,1)S(1)} %get-tuple-element.435), channel_id=1, source_target_pairs={{0,16},{4,20},{8,24},{12,28},{16,0},{20,4},{24,8},{28,12},{1,17},{... | collective-permute-start | bytes 442376 | tf_op jit(solution)/shard_map/ppermute | solution.py:624
  465.8 10.1 %collective-permute-start.54 = (bf16[384,192]{1,0:T(8,128)(2,1)S(1)}, bf16[384,192]{1,0:T(8,128)(2,1)S(1)}, u32[]{:S(2)}, u32[]{:S(2)}) collective-permute-start(bf16[384,192]{1,0:T(8,128)(2,1)S(1)} %get-tuple-element.468), channel_id=1, source_target_pairs={{0,4},{4,0},{8,12},{12,8},{16,20},{20,16},{24,28},{28,24},{1,5},{5... | collective-permute-start | bytes 442376 | tf_op jit(solution)/shard_map/ppermute | solution.py:624
  469.8 7.0 %collective-permute-start.49 = (bf16[96,768]{1,0:T(8,128)(2,1)S(1)}, bf16[96,768]{1,0:T(8,128)(2,1)S(1)}, u32[]{:S(2)}, u32[]{:S(2)}) collective-permute-start(bf16[96,768]{1,0:T(8,128)(2,1)S(1)} %get-tuple-element.490.rest_0_), channel_id=1, source_target_pairs={{0,1},{1,0},{2,3},{3,2},{4,5},{5,4},{6,7},{7,6},{8,9},{9,8},{10,11... | collective-permute-start | bytes 442376 | tf_op jit(solution)/shard_map/ppermute | solution.py:624
  473.4 11.3 %collective-permute-start.48 = (bf16[2,96,768]{2,1,0:T(8,128)(2,1)S(1)}, bf16[2,96,768]{2,1,0:T(8,128)(2,1)S(1)}, u32[]{:S(2)}, u32[]{:S(2)}) collective-permute-start(bf16[2,96,768]{2,1,0:T(8,128)(2,1)S(1)} %get-tuple-element.488.near), channel_id=1, source_target_pairs={{0,1},{1,0},{2,3},{3,2},{4,5},{5,4},{6,7},{7,6},{8,9},{9,8},{10,11... | collective-permute-start | bytes 884744 | tf_op jit(solution)/shard_map/ppermute | solution.py:624
  473.4 16.6 %collective-permute-start.52 = (bf16[2,96,768]{2,1,0:T(8,128)(2,1)S(1)}, bf16[2,96,768]{2,1,0:T(8,128)(2,1)S(1)}, u32[]{:S(2)}, u32[]{:S(2)}) collective-permute-start(bf16[2,96,768]{2,1,0:T(8,128)(2,1)S(1)} %get-tuple-element.464), channel_id=1, source_target_pairs={{0,16},{4,20},{8,24},{12,28},{16,0},{20,4},{24,8},{28,12},{1,17},{... | collective-permute-start | bytes 884744 | tf_op jit(solution)/shard_map/ppermute | solution.py:624
  476.0 14.0 %collective-permute-start.53 = (bf16[192,768]{1,0:T(8,128)(2,1)S(1)}, bf16[192,768]{1,0:T(8,128)(2,1)S(1)}, u32[]{:S(2)}, u32[]{:S(2)}) collective-permute-start(bf16[192,768]{1,0:T(8,128)(2,1)S(1)} %get-tuple-element.466), channel_id=1, source_target_pairs={{0,8},{4,12},{8,0},{12,4},{16,24},{20,28},{24,16},{28,20},{1,9},{5... | collective-permute-start | bytes 884744 | tf_op jit(solution)/shard_map/ppermute | solution.py:624
  476.8 7.9 %collective-permute-start.55 = (bf16[2,2,196,96]{3,2,1,0:T(8,128)(2,1)S(1)}, bf16[2,2,196,96]{3,2,1,0:T(8,128)(2,1)S(1)}, u32[]{:S(2)}, u32[]{:S(2)}) collective-permute-start(bf16[2,2,196,96]{3,2,1,0:T(8,128)(2,1)S(1)} %get-tuple-element.477.refs_6_), channel_id=1, source_target_pairs={{0,4},{4,0},{8,12},{12,8},{16,20},{20,16},{24,28},{28,24},{1,5},{5... | collective-permute-start | bytes 451592 | tf_op jit(solution)/shard_map/ppermute | solution.py:624
  490.3 22.9 %collective-permute-start.57 = (bf16[2,96,768]{2,1,0:T(8,128)(2,1)S(1)}, bf16[2,96,768]{2,1,0:T(8,128)(2,1)S(1)}, u32[]{:S(2)}, u32[]{:S(2)}) collective-permute-start(bf16[2,96,768]{2,1,0:T(8,128)(2,1)S(1)} %get-tuple-element.497.refs_0_), channel_id=1, source_target_pairs={{0,2},{1,3},{2,0},{3,1},{4,6},{5,7},{6,4},{7,5},{8,10},{9,11},{10,... | collective-permute-start | bytes 884744 | tf_op jit(solution)/shard_map/ppermute | solution.py:624
  491.3 21.9 %collective-permute-start.60 = (bf16[2,2,196,96]{3,2,1,0:T(8,128)(2,1)S(1)}, bf16[2,2,196,96]{3,2,1,0:T(8,128)(2,1)S(1)}, u32[]{:S(2)}, u32[]{:S(2)}) collective-permute-start(bf16[2,2,196,96]{3,2,1,0:T(8,128)(2,1)S(1)} %get-tuple-element.503.refs_6_), channel_id=1, source_target_pairs={{0,8},{4,12},{8,0},{12,4},{16,24},{20,28},{24,16},{28,20},{1,9},{5... | collective-permute-start | bytes 451592 | tf_op jit(solution)/shard_map/ppermute | solution.py:624
  493.0 20.2 %collective-permute-start.58 = (bf16[96,768]{1,0:T(8,128)(2,1)S(1)}, bf16[96,768]{1,0:T(8,128)(2,1)S(1)}, u32[]{:S(2)}, u32[]{:S(2)}) collective-permute-start(bf16[96,768]{1,0:T(8,128)(2,1)S(1)} %get-tuple-element.483), channel_id=1, source_target_pairs={{0,16},{4,20},{8,24},{12,28},{16,0},{20,4},{24,8},{28,12},{1,17},{... | collective-permute-start | bytes 442376 | tf_op jit(solution)/shard_map/ppermute | solution.py:624
  493.9 19.2 %collective-permute-start.59 = (bf16[192,192]{1,0:T(8,128)(2,1)S(1)}, bf16[192,192]{1,0:T(8,128)(2,1)S(1)}, u32[]{:S(2)}, u32[]{:S(2)}) collective-permute-start(bf16[192,192]{1,0:T(8,128)(2,1)S(1)} %get-tuple-element.485), channel_id=1, source_target_pairs={{0,8},{4,12},{8,0},{12,4},{16,24},{20,28},{24,16},{28,20},{1,9},{5... | collective-permute-start | bytes 221192 | tf_op jit(solution)/shard_map/ppermute | solution.py:624
  495.6 17.6 %collective-permute-start.61 = (f32[16,1024]{1,0:T(8,128)S(1)}, f32[16,1024]{1,0:T(8,128)S(1)}, u32[]{:S(2)}, u32[]{:S(2)}) collective-permute-start(f32[16,1024]{1,0:T(8,128)S(1)} %get-tuple-element.505.refs_8_), channel_id=1, source_target_pairs={{0,8},{4,12},{8,0},{12,4},{16,24},{20,28},{24,16},{28,20},{1,9},{5... | collective-permute-start | bytes 196616 | tf_op jit(solution)/shard_map/ppermute | solution.py:624
  513.4 21.6 %collective-permute-start.62 = (bf16[2,96,768]{2,1,0:T(8,128)(2,1)S(1)}, bf16[2,96,768]{2,1,0:T(8,128)(2,1)S(1)}, u32[]{:S(2)}, u32[]{:S(2)}) collective-permute-start(bf16[2,96,768]{2,1,0:T(8,128)(2,1)S(1)} %get-tuple-element.513.near), channel_id=1, source_target_pairs={{0,1},{1,0},{2,3},{3,2},{4,5},{5,4},{6,7},{7,6},{8,9},{9,8},{10,11... | collective-permute-start | bytes 884744 | tf_op jit(solution)/shard_map/ppermute | solution.py:624
  513.5 10.0 %collective-permute-start.68 = (f32[16,1024]{1,0:T(8,128)S(1)}, f32[16,1024]{1,0:T(8,128)S(1)}, u32[]{:S(2)}, u32[]{:S(2)}) collective-permute-start(f32[16,1024]{1,0:T(8,128)S(1)} %get-tuple-element.528.refs_4_), channel_id=1, source_target_pairs={{0,16},{4,20},{8,24},{12,28},{16,0},{20,4},{24,8},{28,12},{1,17},{... | collective-permute-start | bytes 196616 | tf_op jit(solution)/shard_map/ppermute | solution.py:624
  515.6 6.9 %collective-permute-start.66 = (bf16[96,192]{1,0:T(8,128)(2,1)S(1)}, bf16[96,192]{1,0:T(8,128)(2,1)S(1)}, u32[]{:S(2)}, u32[]{:S(2)}) collective-permute-start(bf16[96,192]{1,0:T(8,128)(2,1)S(1)} %get-tuple-element.510), channel_id=1, source_target_pairs={{0,16},{4,20},{8,24},{12,28},{16,0},{20,4},{24,8},{28,12},{1,17},{... | collective-permute-start | bytes 110600 | tf_op jit(solution)/shard_map/ppermute | solution.py:624
  516.5 10.1 %collective-permute-start.63 = (bf16[96,768]{1,0:T(8,128)(2,1)S(1)}, bf16[96,768]{1,0:T(8,128)(2,1)S(1)}, u32[]{:S(2)}, u32[]{:S(2)}) collective-permute-start(bf16[96,768]{1,0:T(8,128)(2,1)S(1)} %get-tuple-element.515.rest_0_), channel_id=1, source_target_pairs={{0,1},{1,0},{2,3},{3,2},{4,5},{5,4},{6,7},{7,6},{8,9},{9,8},{10,11... | collective-permute-start | bytes 442376 | tf_op jit(solution)/shard_map/ppermute | solution.py:624
  516.6 10.0 %collective-permute-start.64 = (bf16[96,768]{1,0:T(8,128)(2,1)S(1)}, bf16[96,768]{1,0:T(8,128)(2,1)S(1)}, u32[]{:S(2)}, u32[]{:S(2)}) collective-permute-start(bf16[96,768]{1,0:T(8,128)(2,1)S(1)} %get-tuple-element.515.rest_0_), channel_id=1, source_target_pairs={{0,2},{1,3},{2,0},{3,1},{4,6},{5,7},{6,4},{7,5},{8,10},{9,11},{10,... | collective-permute-start | bytes 442376 | tf_op jit(solution)/shard_map/ppermute | solution.py:624
  523.5 11.5 %collective-permute-start.67 = (bf16[2,2,196,96]{3,2,1,0:T(8,128)(2,1)S(1)}, bf16[2,2,196,96]{3,2,1,0:T(8,128)(2,1)S(1)}, u32[]{:S(2)}, u32[]{:S(2)}) collective-permute-start(bf16[2,2,196,96]{3,2,1,0:T(8,128)(2,1)S(1)} %get-tuple-element.526.refs_2_), channel_id=1, source_target_pairs={{0,16},{4,20},{8,24},{12,28},{16,0},{20,4},{24,8},{28,12},{1,17},{... | collective-permute-start | bytes 451592 | tf_op jit(solution)/shard_map/ppermute | solution.py:624
  535.1 20.3 %collective-permute-start.69 = (bf16[96,192]{1,0:T(8,128)(2,1)S(1)}, bf16[96,192]{1,0:T(8,128)(2,1)S(1)}, u32[]{:S(2)}, u32[]{:S(2)}) collective-permute-start(bf16[96,192]{1,0:T(8,128)(2,1)S(1)} %get-tuple-element.534), channel_id=1, source_target_pairs={{0,1},{1,0},{2,3},{3,2},{4,5},{5,4},{6,7},{7,6},{8,9},{9,8},{10,11... | collective-permute-start | bytes 110600 | tf_op jit(solution)/shard_map/ppermute | solution.py:624
  535.2 20.2 %collective-permute-start.70 = (bf16[96,192]{1,0:T(8,128)(2,1)S(1)}, bf16[96,192]{1,0:T(8,128)(2,1)S(1)}, u32[]{:S(2)}, u32[]{:S(2)}) collective-permute-start(bf16[96,192]{1,0:T(8,128)(2,1)S(1)} %get-tuple-element.534), channel_id=1, source_target_pairs={{0,2},{1,3},{2,0},{3,1},{4,6},{5,7},{6,4},{7,5},{8,10},{9,11},{10,... | collective-permute-start | bytes 110600 | tf_op jit(solution)/shard_map/ppermute | solution.py:624
  536.2 19.3 %collective-permute-start.71 = (bf16[96,192]{1,0:T(8,128)(2,1)S(1)}, bf16[96,192]{1,0:T(8,128)(2,1)S(1)}, u32[]{:S(2)}, u32[]{:S(2)}) collective-permute-start(bf16[96,192]{1,0:T(8,128)(2,1)S(1)} %get-tuple-element.534), channel_id=1, source_target_pairs={{0,3},{1,2},{2,1},{3,0},{4,7},{5,6},{6,5},{7,4},{8,11},{9,10},{10,... | collective-permute-start | bytes 110600 | tf_op jit(solution)/shard_map/ppermute | solution.py:624
  (117 other events, 1182.4 us)
Sparse Core Ops, SparseCore 0:
  10.8 90.4 all-gather.5
  104.7 108.9 all-gather.3

commit v3 on v2

--- a/solution.py
+++ b/solution.py
@@ -14,6 +14,8 @@
 LANES = 128
 SUBLANES = 8
 FOLD_MAX = 1200000
+MISC = 256
+SMALL = 64
 
 low = jnp.bfloat16
 beta_one = 0.9
@@ -25,6 +27,7 @@
 cubic = 0.044715
 room = pltpu.CompilerParams(vmem_limit_bytes=44 * 1024 * 1024)
 places = (0, 2, 1, 3)
+large = pltpu.CompilerParams(vmem_limit_bytes=60 * 1024 * 1024)
 
 
 def dot(left, right, contract=(1, 0)):
@@ -93,6 +96,14 @@
     )(state, gains, token_in, token_out)
 
 
+def block_copies(spots, blocks, lanes, held, sems):
+    rows = blocks.shape[1]
+    return [
+        pltpu.make_async_copy(blocks.at[spots[i], :, lanes], held.at[pl.ds(i * rows, rows)], sems.at[i])
+        for i in range(blocks.shape[0])
+    ]
+
+
 def hbm(arrays):
     return [pl.BlockSpec(memory_space=pl.ANY)] * len(arrays)
 
@@ -121,10 +132,10 @@
 
 
 class Gathered:
-    def __init__(self, array, shards, device):
+    def __init__(self, array, shards, device, rows):
         self.arrays = [shards, device, array]
         self.specs = [scalars, scalars] + hbm([array])
-        self.blocks, self.rows, self.size = array.shape[0], array.shape[2] // 2, array.shape[3]
+        self.blocks, self.rows, self.size = array.shape[0], rows, array.shape[3]
         self.width = self.blocks * self.rows
         self.sems = 2 * self.blocks
 
@@ -296,28 +307,37 @@
         mean_new[0, 0, :, lanes] = mean_next
         power_new[0, 0, :, lanes] = power_next
         update[0, 0, :, lanes] = change
-        weight_part += jnp.sum(value * value)
-        update_part += jnp.sum(change * change)
-    sums[way, 0] = weight_part
-    sums[way, 1] = update_part
+        weight_part += jnp.sum(jnp.sum(value * value, 0, keepdims=True))
+        update_part += jnp.sum(jnp.sum(change * change, 0, keepdims=True))
+
+    @pl.when(pl.program_id(1) == 0)
+    def _():
+        sums[way, 0] = weight_part
+        sums[way, 1] = update_part
+
+    @pl.when(pl.program_id(1) > 0)
+    def _():
+        sums[way, 0] += weight_part
+        sums[way, 1] += update_part
 
 
 def channel_step(layer, device, weight, mean, power, chain_in, chain_out, earlier):
     near, far = chain_in
-    rows = near.shape[1]
+    rows, size = near.shape[1:]
     columns = weight.shape[3]
-    block = pl.BlockSpec((1, 1, rows, columns), lambda w: (layer, w, 0, 0))
+    chunk = 32 if rows % 32 == 0 else rows
+    block = pl.BlockSpec((1, 1, chunk, columns), lambda w, i: (layer, w, i, 0))
+    two = pl.BlockSpec((2, chunk, size), lambda w, i: (0, i, 0))
+    one = pl.BlockSpec((chunk, size), lambda w, i: (i, 0))
     shape = jax.ShapeDtypeStruct(weight.shape, jnp.float32)
     return pl.pallas_call(
         step_kernel,
-        grid=(2,),
-        in_specs=[scalars, block, block, block]
-        + [whole(array) for array in (near, far, *chain_out)]
-        + hbm(earlier),
+        grid=(2, rows // chunk),
+        in_specs=[scalars, block, block, block, two, two, one, one, one, one] + hbm(earlier),
         out_specs=[block, block, block, scalars],
         out_shape=[shape, shape, shape, jax.ShapeDtypeStruct((2, 2), jnp.float32)],
         input_output_aliases={10 + i: i for i in range(len(earlier))},
-        compiler_params=room,
+        compiler_params=large,
         cost_estimate=cost(40 * near.size, 104 * near.size),
         name="channel_step",
     )(device, weight, mean, power, near, far, *chain_out, *earlier)
@@ -338,7 +358,7 @@
         in_specs=[pl.BlockSpec(memory_space=pltpu.SMEM), block, block],
         out_specs=[block, block],
         out_shape=[jax.ShapeDtypeStruct(weight.shape, jnp.float32), jax.ShapeDtypeStruct(weight.shape, low)],
-        compiler_params=room,
+        compiler_params=large,
         cost_estimate=cost(3 * weight.size, 14 * weight.size),
         name="channel_renew",
     )(trust, weight, update)
@@ -352,8 +372,8 @@
     normed = (hat * gains[0:1] + gains[1:2]).astype(low)
     hidden, slope = gelu_both(before[0].astype(jnp.float32))
     grad_before = (slope * dot(token_out_turn[...], token_grad)).astype(low)
-    part_out = dot(token_grad, hidden.astype(low), (1, 1))
-    part_in = dot(normed, grad_before, (1, 1))
+    part_out = dot(hidden.astype(low), token_grad, (1, 1))
+    part_in = dot(grad_before, normed, (1, 1))
     upstream = dot(token_in[...], grad_before)
     grad_state[...] = gradient[...] + centred_back(upstream * gains[0:1], hat, inverse)
     part_gain = jnp.sum(upstream * hat, 0, keepdims=True)
@@ -386,12 +406,12 @@
             one, one, whole(gains), pl.BlockSpec((1, hidden, width), lambda i: (i, 0, 0)),
             whole(token_in), whole(token_out_turn),
         ] + [pl.BlockSpec(memory_space=pl.ANY)] * len(after),
-        out_specs=[one, still((2, width)), still((rows, hidden)), still((rows, hidden))],
+        out_specs=[one, still((2, width)), still((hidden, rows)), still((hidden, rows))],
         out_shape=[
             jax.ShapeDtypeStruct(state.shape, jnp.float32),
             jax.ShapeDtypeStruct((2, width), jnp.float32),
-            jax.ShapeDtypeStruct((rows, hidden), jnp.float32),
-            jax.ShapeDtypeStruct((rows, hidden), jnp.float32),
+            jax.ShapeDtypeStruct((hidden, rows), jnp.float32),
+            jax.ShapeDtypeStruct((hidden, rows), jnp.float32),
         ],
         compiler_params=room,
         cost_estimate=cost(8 * count * rows * hidden * width, 16 * state.size, 0),
@@ -437,8 +457,11 @@
     )(place, share, device, own, incoming)
 
 
-def stem_kernel(device, *rest):
-    pieces, (weights, gains, mixed, state, joint, spare) = rest[:-6], rest[-6:]
+def stem_kernel(device, spots, *rest):
+    pieces, (blocks, gains, mixed, state, joint, spare, weights, sems) = rest[:-8], rest[-8:]
+    copies = block_copies(spots, blocks, pl.ds(0, weights.shape[1]), weights, sems)
+    for copy in copies:
+        copy.start()
     count = len(pieces) // 2
     odd, upper = (device[0] & 1) == 1, (device[0] & 2) == 2
     patches = pieces[0].shape[0] // 2
@@ -453,15 +476,16 @@
                 at = (side * 2 + i) * rows + k * patches
                 joint[at : at + patches, :] = spare[i * patches : (i + 1) * patches, :]
     mixed[...] = joint[...].astype(low)
+    for copy in copies:
+        copy.wait()
     state[...] = dot(mixed[...], weights[...], (1, 1)) + gains[0:1]
 
 
-def stem(device, pieces, weights, gains, rows, after=()):
-    width, pixels = weights.shape
-    scalar = pl.BlockSpec(memory_space=pltpu.SMEM)
+def stem(device, spots, pieces, blocks, gains, rows):
+    width, pixels = blocks.shape[0] * blocks.shape[1], pieces[0].shape[1]
     return pl.pallas_call(
         stem_kernel,
-        in_specs=[scalar] + [pl.BlockSpec()] * (len(pieces) + 2),
+        in_specs=[scalars, scalars] + [pl.BlockSpec()] * len(pieces) + hbm([blocks]) + [pl.BlockSpec()],
         out_shape=[
             jax.ShapeDtypeStruct((rows, pixels), low),
             jax.ShapeDtypeStruct((rows, width), jnp.float32),
@@ -469,17 +493,22 @@
         scratch_shapes=[
             pltpu.VMEM((rows, pixels), jnp.float32),
             pltpu.VMEM(pieces[0].shape, jnp.float32),
+            pltpu.VMEM((width, pixels), low),
+            pltpu.SemaphoreType.DMA((blocks.shape[0],)),
         ],
         compiler_params=room,
         cost_estimate=cost(2 * rows * width * pixels, 12 * rows * width),
         name="stem",
-    )(device, *pieces, weights, gains)
+    )(device, spots, *pieces, blocks, gains)
 
 
 def head_kernel(
-    patches, device, state, gains, head, bias, numbers, labels, others, lam, weight, scale,
-    gradient, grad_vectors, grads, grad_bias, loss, pooled, upstream,
+    patches, pixels, device, spots, state, gains, blocks, bias, numbers, labels, others, lam, weight, scale,
+    gradient, grad_vectors, grads, grad_bias, loss, pooled, upstream, head, sems,
 ):
+    copies = block_copies(spots, blocks, pl.ds(pixels, head.shape[1]), head, sems)
+    for copy in copies:
+        copy.start()
     rows, width = state.shape
     count = lam.shape[0]
     each = rows // count
@@ -491,6 +520,8 @@
         sums.append(jnp.sum(jnp.where(live, hat[i * each : (i + 1) * each], 0.0), 0, keepdims=True))
         pooled[i : i + 1] = sums[i] / patches * gains[0:1] + gains[1:2]
     pooled_low = pooled[...].astype(low)
+    for copy in copies:
+        copy.wait()
     logits = dot(pooled_low, head[...])[:count] + bias[...]
     logits = jnp.where(numbers[...] >= 0, logits, -jnp.inf)
     peak = jnp.max(logits, -1, keepdims=True)
@@ -526,12 +557,12 @@
     gradient[...] = centred_back(upstream[...] * gains[0:1], hat, inverse)
 
 
-def head_step(device, state, gains, weights, bias, numbers, labels, others, lam, weight, scale, patches):
+def head_step(device, spots, state, gains, blocks, bias, numbers, labels, others, lam, weight, scale, patches, pixels):
     rows, width = state.shape
-    columns = weights.shape[1]
+    columns = bias.shape[1]
     return pl.pallas_call(
-        functools.partial(head_kernel, patches),
-        in_specs=[scalars] + [pl.BlockSpec()] * 10,
+        functools.partial(head_kernel, patches, pixels),
+        in_specs=[scalars, scalars] + [pl.BlockSpec()] * 2 + hbm([blocks]) + [pl.BlockSpec()] * 7,
         out_shape=[
             jax.ShapeDtypeStruct(state.shape, jnp.float32),
             jax.ShapeDtypeStruct((2, width), jnp.float32),
@@ -542,11 +573,13 @@
         scratch_shapes=[
             pltpu.VMEM((16, width), jnp.float32),
             pltpu.VMEM(state.shape, jnp.float32),
+            pltpu.VMEM((width, columns), low),
+            pltpu.SemaphoreType.DMA((blocks.shape[0],)),
         ],
         compiler_params=room,
         cost_estimate=cost(64 * width * columns, 8 * rows * width),
         name="head_step",
-    )(device, state, gains, weights, bias, numbers, labels, others, lam, weight, scale)
+    )(device, spots, state, gains, blocks, bias, numbers, labels, others, lam, weight, scale)
 
 
 def stem_backward_kernel(device, gradient, mixed, grads, shift):
@@ -554,9 +587,10 @@
     shift[...] = jnp.sum(rounded.astype(jnp.float32), 0, keepdims=True)
     whole_grad = dot(gradient[...].T.astype(low), mixed[...]).astype(low)
     size = whole_grad.shape[1] // 4
+    grads[...] = jnp.zeros_like(grads)
     for a in range(4):
         rel = device[0] ^ a
-        grads[(rel & 1) * 2 + (rel >> 1)] = whole_grad[:, a * size : (a + 1) * size]
+        grads[(rel & 1) * 2 + (rel >> 1), :, :size] = whole_grad[:, a * size : (a + 1) * size]
 
 
 def stem_backward(device, gradient, mixed):
@@ -565,7 +599,7 @@
         stem_backward_kernel,
         in_specs=[scalars] + [pl.BlockSpec()] * 2,
         out_shape=[
-            jax.ShapeDtypeStruct((4, width, pixels // 4), low),
+            jax.ShapeDtypeStruct((4, width, MISC), low),
             jax.ShapeDtypeStruct((1, width), jnp.float32),
         ],
         compiler_params=room,
@@ -596,27 +630,52 @@
     )(vectors, source)
 
 
-def gather_small_kernel(source, *rest):
-    parts, (bias, loss, out, joint) = rest[:-4], rest[-4:]
+def gather_misc_kernel(count, source, stem_grads, *rest):
+    tokens, parts, (bias, loss), outs, (joint, small) = (
+        rest[:4],
+        rest[4:count],
+        rest[count : count + 2],
+        rest[count + 2 : count + 6],
+        rest[count + 6 :],
+    )
     joint[...] = jnp.zeros_like(joint)
     at = 0
     for part in parts:
         joint[at : at + part.shape[0]] = part[...]
         at += part.shape[0]
-    out[...] = jnp.zeros_like(out)
-    out[:, : joint.shape[1]] = moved(joint[...], source[...], 1)
-    out[at : at + 1] = bias[...]
-    out[at + 1 : at + 2, 0:1] = loss[...]
-
-
-def gather_small(source, parts, bias, loss):
+    true = moved(joint[...], source[...], 1)
+    small[...] = jnp.zeros_like(small)
+    for j in range(joint.shape[1] // MISC):
+        small[j * 16 : (j + 1) * 16] = true[:, j * MISC : (j + 1) * MISC]
+    at = joint.shape[1] // MISC * 16
+    for j in range(bias.shape[1] // MISC):
+        small[at + j : at + j + 1] = bias[:, j * MISC : (j + 1) * MISC]
+    at += bias.shape[1] // MISC
+    small[at : at + 1, 0:1] = loss[...]
+    stem_rows = stem_grads.shape[1]
+    rows = tokens[0].shape[0] // 4
+    patches = tokens[0].shape[1]
+    for place, out in enumerate(outs):
+        out[:stem_rows] = stem_grads[place]
+        for j, token in enumerate(tokens):
+            at = stem_rows + j * rows
+            out[at : at + rows] = jnp.zeros((rows, MISC), low)
+            out[at : at + rows, :patches] = token[place * rows : (place + 1) * rows].astype(low)
+        out[stem_rows + 4 * rows :] = small[...].astype(low)
+
+
+def gather_misc(source, stem_grads, tokens, parts, bias, loss):
+    rows = stem_grads.shape[1] + tokens[0].shape[0] + SMALL
     return pl.pallas_call(
-        gather_small_kernel,
-        out_shape=jax.ShapeDtypeStruct((16, bias.shape[1]), jnp.float32),
-        scratch_shapes=[pltpu.VMEM((16, parts[0].shape[1]), jnp.float32)],
+        functools.partial(gather_misc_kernel, 4 + len(parts)),
+        out_shape=[jax.ShapeDtypeStruct((rows, MISC), low)] * 4,
+        scratch_shapes=[
+            pltpu.VMEM((16, parts[0].shape[1]), jnp.float32),
+            pltpu.VMEM((SMALL, MISC), jnp.float32),
+        ],
         compiler_params=room,
-        name="gather_small",
-    )(source, *parts, bias, loss)
+        name="gather_misc",
+    )(source, stem_grads, *tokens, *parts, bias, loss)
 
 
 def swap(array, axis, mask):
@@ -665,6 +724,11 @@
     return (keep.astype(jnp.float32) + got.astype(jnp.float32)).astype(keep.dtype)
 
 
+def added_four(keep, second, first, both):
+    wide = lambda array: array.astype(jnp.float32)
+    return ((wide(keep) + wide(first)) + (wide(second) + wide(both))).astype(keep.dtype)
+
+
 def cut_rows(array, half):
     middle = array.shape[-2] // 2
     return array[..., half * middle : (half + 1) * middle, :]
@@ -675,25 +739,32 @@
         return [added(cut_rows(keep, half), cut_rows(got, half)) for half in range(2)]
     if kind == "blocks":
         return [added(keep[0], got[0]), added(keep[1], got[1])]
+    if isinstance(kind, int):
+        total = added(keep, got) if not isinstance(got, (list, tuple)) else added_four(keep, *got)
+        return [
+            jnp.concatenate([total[: kind // 2], total[kind:]]),
+            jnp.concatenate([total[kind // 2 : kind], total[kind:]]),
+        ]
     if kind == "turned":
         return [jnp.stack([added(keep[0], got[1]), added(keep[1], got[0])])]
     return [added(keep, got)]
 
 
-def fold_kernel(kinds, *refs):
-    outs = list(refs[2 * len(kinds) :])
-    for i, kind in enumerate(kinds):
-        for value in folded(refs[2 * i][...], refs[2 * i + 1][...], kind):
-            outs.pop(0)[...] = value
+def fold_kernel(jobs, *refs):
+    refs = list(refs)
+    values = [jax.tree.map(lambda _: refs.pop(0)[...], job[:2]) for job in jobs]
+    for (keep, got), (_, _, kind) in zip(values, jobs, strict=True):
+        for value in folded(keep, got, kind):
+            refs.pop(0)[...] = value
 
 
 def fold_all(jobs):
-    kinds = [kind for _, _, kind in jobs]
-    arrays = [array for keep, got, _ in jobs for array in (keep, got)]
+    arrays = jax.tree.leaves([job[:2] for job in jobs])
     shapes = [jax.eval_shape(functools.partial(folded, kind=kind), keep, got) for keep, got, kind in jobs]
     flat = [shape for group in shapes for shape in group]
+    blank = [(*jax.tree.map(lambda _: 0, job[:2]), job[2]) for job in jobs]
     outs = pl.pallas_call(
-        functools.partial(fold_kernel, kinds),
+        functools.partial(fold_kernel, blank),
         out_shape=flat,
         compiler_params=room,
         cost_estimate=cost(sum(a.size for a in arrays), sum(4 * a.size for a in arrays)),
@@ -706,8 +777,44 @@
     return out
 
 
-def reduce_rows(keep, got):
-    keep, send = yield keep, got, "rows"
+def split_kernel(*refs):
+    further = len(refs) > 10
+    keep_low, keep_high, keep_out, got_low, got_high, got_out = refs[:6]
+    in_keep, in_send, out_keep, out_send = refs[-4:]
+    columns = keep_out.shape[3]
+    in_keep[...] = added(keep_low[0], got_low[0])
+    in_send[...] = added(keep_high[0], got_high[0])
+    for half, out in enumerate((out_keep, out_send)):
+        out[:, :columns] = added(keep_out[0, half], got_out[0, half])
+        if further:
+            out[:, columns:] = added(refs[6][half], refs[7][half])
+
+
+def split_cores(keep, got, further=(), steps=4):
+    rows, columns = keep.shape[2:]
+    few, many = rows // 2 // steps, rows // steps
+    low_rows = pl.BlockSpec((1, 2, few, columns), lambda i: (0, 0, i, 0))
+    high_rows = pl.BlockSpec((1, 2, few, columns), lambda i: (0, 0, i + steps, 0))
+    out_rows = pl.BlockSpec((1, 2, many, columns), lambda i: (1, 0, i, 0))
+    total = columns + (further[0].shape[2] if further else 0)
+    two = pl.BlockSpec((2, few, columns), lambda i: (0, i, 0))
+    one = pl.BlockSpec((many, total), lambda i: (i, 0))
+    pair = jax.ShapeDtypeStruct((2, rows // 2, columns), keep.dtype)
+    single = jax.ShapeDtypeStruct((rows, total), keep.dtype)
+    return pl.pallas_call(
+        split_kernel,
+        grid=(steps,),
+        in_specs=[low_rows, high_rows, out_rows] * 2
+        + [pl.BlockSpec((2, many, total - columns), lambda i: (0, i, 0))] * len(further),
+        out_specs=[two, two, one, one],
+        out_shape=[pair, pair, single, single],
+        compiler_params=large,
+        cost_estimate=cost(keep.size, 6 * keep.size),
+        name="split_cores",
+    )(keep, keep, keep, got, got, got, *further)
+
+
+def reduce_rows(keep, send):
     steps = [1] + dp_masks()[::-1]
     for mask in steps[:-1]:
         keep, send = yield keep, swap(send, "dp", mask), "rows"
@@ -717,8 +824,7 @@
     return near, far
 
 
-def reduce_columns(keep, got):
-    keep, send = yield keep, got, "blocks"
+def reduce_columns(keep, send):
     keep, send = yield keep, swap(send, "tok", 2), "rows"
     steps = [1] + dp_masks()[::-1]
     for mask in steps[:-1]:
@@ -728,21 +834,17 @@
     return [keep, *others]
 
 
-def reduce_cores(grads):
-    keep, got = grads[:2], swap(grads[2:], "tok", 1)
-    return (yield from reduce_columns(keep, got))
-
-
-def reduce_tokens(array):
-    axis = array.ndim - 1
-    for mask in (1, 2):
-        middle = array.shape[axis] // 2
-        keep = lax.slice_in_dim(array, 0, middle, axis=axis)
-        send = lax.slice_in_dim(array, middle, 2 * middle, axis=axis)
-        (array,) = yield keep, swap(send, "tok", mask), "sum"
-    for mask in [1] + dp_masks()[::-1]:
-        (array,) = yield array, swap(array, "dp", mask), "sum"
-    return array
+def reduce_misc(stem_rows, keep, far, near, both):
+    arrived = [swap(array, "tok", mask) for mask, array in ((2, far), (1, near), (3, both))]
+    keep, send = yield keep, arrived, stem_rows
+    steps = [1] + dp_masks()[::-1]
+    for mask in steps[:-1]:
+        stem_rows //= 2
+        keep, send = yield keep, swap(send, "dp", mask), stem_rows
+    (keep,) = yield keep, swap(send, "dp", steps[-1]), "sum"
+    block = keep[: stem_rows // 2]
+    rest, others = yield keep, [swap(block, "tok", q) for q in range(1, 4)], "none"
+    return [block, *others], rest[stem_rows // 2 :]
 
 
 def sum_over(array, steps):
@@ -769,14 +871,16 @@
     jobs = []
     for chain, (keep, got) in zip(chains, states, strict=True):
         kind = chain.state[2]
-        small = keep.size <= FOLD_MAX if kind != "none" else False
-        if kind in ("rows",) and keep.shape[-2] % 32:
+        small = keep.size <= FOLD_MAX and kind != "none"
+        if (kind == "rows" and keep.shape[-2] % 32) or (isinstance(kind, int) and kind % 32):
             small = False
         if small:
             jobs.append((chain, keep, got, kind))
     results = dict(
         zip([id(job[0]) for job in jobs], fold_all([job[1:] for job in jobs]) if jobs else [], strict=True)
     )
+    others, fenced = fence(others, results)
+    results = fenced
     for chain, (keep, got) in zip(chains, states, strict=True):
         kind = chain.state[2]
         if id(chain) in results:
@@ -806,10 +910,8 @@
 def moments(weight, gradient, first, second, decay_rate):
     first_new = beta_one * first + (1 - beta_one) * gradient
     second_new = beta_two * second + (1 - beta_two) * gradient * gradient
-    update = (
-        first_new / (1 - beta_one**STEP) / (jnp.sqrt(second_new / (1 - beta_two**STEP)) + epsilon)
-        + decay_rate * weight
-    )
+    scale_one, scale_two = 1 / (1 - beta_one**STEP), 1 / (1 - beta_two**STEP)
+    update = scale_one * first_new / (jnp.sqrt(scale_two * second_new) + epsilon) + decay_rate * weight
     return (first_new, second_new, update)
 
 
@@ -883,9 +985,11 @@
     rows = jnp.asarray(order, jnp.int32) ^ device_row
     column_source = (rows[:, None] * shard + jnp.arange(shard, dtype=jnp.int32)[None, :]).reshape(1, width)
     ends = jnp.concatenate([stem_w.astype(low).T, jnp.pad(head_w.astype(low), ((0, 0), (0, class_pad)))], 1)
-    ends = lax.all_gather(ends, "dp")
-    later = lax.all_gather(chan_low[1].reshape(2 * shard, size), ("dp", "tok"))
-    later = later.reshape(count_dp, count_tok, 2 * shard, size)
+    ends = lax.all_gather(quarter(ends, 0), ("dp", "tok"))
+    pixels = stem_w.shape[0]
+    later = chan_low[1].reshape(2 * shard, size)
+
+    later = lax.all_gather(later, ("dp", "tok")).reshape(count_dp, count_tok, -1, size)
 
     vectors = relative_vectors(vec_w, column_source)
     numbers = jnp.arange(classes_all + class_pad, dtype=jnp.int32)
@@ -915,91 +1019,103 @@
     image_rows = [row_of(array) for array in (labels, other_labels, lam, weights, weights / total)]
 
     blocks = [chan_low[0, 0], chan_low[0, 1]]
-    tok_low = tok_w.astype(low)
+    tok_low = jnp.swapaxes(tok_w, 2, 3).astype(low)
     partner_mask = count_dp // 2
-    incoming_one = swap(own_parts[0], "dp", partner_mask)
+    incoming = swap(own_parts[0], "dp", partner_mask)
     for step, mask in enumerate(masks):
         got = swap(packed(blocks), "dp", mask)
         if step == 0:
-            blocks, got, tok_far, own_parts[1] = fence(blocks, got, swap(tok_low, "tok", 2), own_parts[1])
-            tok_half = jnp.concatenate([tok_low, tok_far], 3)
+            blocks, got, tok_far, own_parts[1], incoming = fence(
+                blocks, got, swap(tok_low, "tok", 2), own_parts[1], incoming
+            )
+            pieces = mixed_pieces(0, incoming)
+            tok_half = jnp.concatenate([tok_low, tok_far], 2)
             tok_near = swap(tok_half, "tok", 1)
         elif step == 1:
-            blocks, got, tok_near, incoming_one, own_parts[1], vectors, image_rows = fence(
-                blocks, got, tok_near, incoming_one, own_parts[1], vectors, image_rows
+            blocks, got, tok_near, own_parts[1], vectors, image_rows, pieces = fence(
+                blocks, got, tok_near, own_parts[1], vectors, image_rows, pieces
             )
         else:
             blocks, got = fence(blocks, got)
         blocks = doubled(blocks, got)
-    tok_all = jnp.concatenate([tok_half, tok_near], 3)
-    tok_all = jnp.pad(tok_all, ((0, 0), (0, 0), (0, each - all_patches), (0, 0)))
-    tok_turn = jnp.swapaxes(tok_all, 2, 3)
+    tok_turn = jnp.concatenate([tok_half, tok_near], 2)
+    tok_turn = jnp.pad(tok_turn, ((0, 0), (0, 0), (0, 0), (0, each - all_patches)))
+    tok_all = jnp.swapaxes(tok_turn, 2, 3)
 
     incoming_two = swap(own_parts[1], "dp", partner_mask)
     first, second = blocks
     first_low, second_far = swap(first, "dp", 1), swap(second, "tok", 2)
-    first, second, first_low, second_far, incoming_one = fence(first, second, first_low, second_far, incoming_one)
-    pieces = mixed_pieces(0, incoming_one)
+    first, second, first_low, second_far, incoming_two, tok_all, tok_turn = fence(
+        first, second, first_low, second_far, incoming_two, tok_all, tok_turn
+    )
+    more = mixed_pieces(1, incoming_two)
     firsts, seconds = jnp.stack([first, first_low]), jnp.stack([second, second_far])
     firsts_far, seconds_low = swap(firsts, "tok", 2), swap(seconds, "dp", 1)
-    firsts, seconds, firsts_far, seconds_low, incoming_two, pieces, tok_all, tok_turn = fence(
-        firsts, seconds, firsts_far, seconds_low, incoming_two, pieces, tok_all, tok_turn
-    )
-    more = mixed_pieces(1, incoming_two)
+    firsts, seconds, firsts_far, seconds_low, pieces, more = fence(
+        firsts, seconds, firsts_far, seconds_low, pieces, more
+    )
     source_zero = Pieces(
         [firsts, firsts_far, swap(firsts, "tok", 1), swap(firsts_far, "tok", 1)],
         [seconds, seconds_low, swap(seconds, "tok", 1), swap(seconds_low, "tok", 1)],
     )
-    ends = jnp.take(ends, rows, axis=0).reshape(width, -1)
-    stem_all, head_all = ends[:, : stem_w.shape[0]], ends[:, stem_w.shape[0] :]
     if shard % 16:
-        later = jnp.take(later, rows, axis=0).reshape(width // 96, 96 // shard, count_tok, 2, shard, size)
-        later = later.transpose(0, 2, 3, 1, 4, 5).reshape(width // 96, count_tok, 2 * 96, size)
-        source_one = Gathered(later, jnp.arange(width // 96, dtype=jnp.int32), device)
+        many = 96 // shard
+        groups = count_dp // many
+        later = jnp.take(later, rows, axis=0).reshape(groups, many, count_tok, 2, shard, size)
+        later = later.transpose(0, 2, 3, 1, 4, 5).reshape(groups, count_tok, 2 * many * shard, size)
+        ends = jnp.take(ends.reshape(count_dp, shard, -1), rows, axis=0).reshape(groups, many * shard, -1)
+        spots = jnp.arange(groups, dtype=jnp.int32)
+        source_one = Gathered(later, spots, device, many * shard)
     else:
-        source_one = Gathered(later, rows, device)
+        spots = rows
+        ends = ends.reshape(count_dp, shard, -1)
+        source_one = Gathered(later, spots, device, shard)
 
     gains = [vectors[1 + 4 * layer : 5 + 4 * layer] for layer in range(LAYERS)]
-    mixed, stem_state = stem(device, pieces + more, stem_all, vectors, each * per_tok)
+    mixed, stem_state = stem(device, spots, pieces + more, ends, vectors, each * per_tok)
     middle_zero, before_zero = token_forward(stem_state, gains[0], tok_turn[0, 0], tok_all[0, 1])
     first_state, inner_zero = channel_forward(middle_zero, gains[0], source_zero)
     middle_one, before_one = token_forward(first_state, gains[1], tok_turn[1, 0], tok_all[1, 1])
     second_state, inner_one = channel_forward(middle_one, gains[1], source_one)
     gradient, last_part, head_grads, bias_part, loss_local = head_step(
-        device, second_state, vectors[NV - 2 :], head_all, bias, numbers, *image_rows, all_patches
-    )
-
-    head_chain = Chain(reduce_cores(head_grads))
+        device, spots, second_state, vectors[NV - 2 :], ends, bias, numbers, *image_rows, all_patches, pixels
+    )
+
+    head_got = swap(head_grads[2:], "tok", 1)
     send, partial, _ = channel_backward(gradient, middle_one, gains[1], inner_one, source_one)
     got = swap(send, "tok", 1)
     keep, gradient, second_one = channel_backward(gradient, middle_one, gains[1], inner_one, source_one, partial)
-    chains_one = [Chain(reduce_rows(keep[0], got[0])), Chain(reduce_columns(keep[1], got[1]))]
-    (gradient,) = advance([head_chain] + chains_one, gradient)
+    in_keep, in_send, out_keep, out_send = split_cores(keep, got, (head_grads[:2], head_got))
+    in_keep, in_send, out_keep, out_send, gradient = fence(in_keep, in_send, out_keep, out_send, gradient)
+    chains_one = [Chain(reduce_rows(in_keep, in_send)), Chain(reduce_columns(out_keep, out_send))]
     gradient, first_one, *token_one = token_backward(
         gradient, first_state, gains[1], before_one, tok_all[1, 0], tok_turn[1, 1]
     )
     send, partial, _ = channel_backward(gradient, middle_zero, gains[0], inner_zero, source_zero)
-    send, partial, gradient = advance([head_chain] + chains_one, send, partial, gradient)
+    send, partial, gradient = advance(chains_one, send, partial, gradient)
     got = swap(send, "tok", 1)
     keep, gradient, second_zero = channel_backward(gradient, middle_zero, gains[0], inner_zero, source_zero, partial)
-    chains_zero = [Chain(reduce_rows(keep[0], got[0])), Chain(reduce_columns(keep[1], got[1]))]
-    (gradient,) = advance([head_chain] + chains_one + chains_zero, gradient)
+    in_keep, in_send, out_keep, out_send = split_cores(keep, got)
+    in_keep, in_send, out_keep, out_send, gradient = advance(
+        chains_one, in_keep, in_send, out_keep, out_send, gradient
+    )
+    chains_zero = [Chain(reduce_rows(in_keep, in_send)), Chain(reduce_columns(out_keep, out_send))]
     gradient, first_zero, *token_zero = token_backward(
         gradient, stem_state, gains[0], before_zero, tok_all[0, 0], tok_turn[0, 1]
     )
     stem_grads, stem_bias = stem_backward(device, gradient, mixed)
-    small = gather_small(
+    misc = gather_misc(
         column_source,
+        stem_grads,
+        token_zero + token_one,
         [stem_bias, first_zero, second_zero, first_one, second_one, last_part],
         bias_part,
         loss_local,
     )
-    token_part = jnp.stack([jnp.stack(token_zero), jnp.stack(token_one)])[:, :, :all_patches].astype(low)
+    misc = advance(chains_one + chains_zero, *misc)
+    misc_chain = Chain(reduce_misc(width, *misc))
     dp_steps = [("dp", mask) for mask in [1] + dp_masks()[::-1]]
-    stem_chain = Chain(reduce_cores(stem_grads))
-    token_chain = Chain(reduce_tokens(token_part))
-    small_chain = Chain(sum_over(small, [("tok", 1), ("tok", 2)] + dp_steps))
-    everything = [head_chain] + chains_one + chains_zero + [stem_chain, token_chain, small_chain]
+    everything = chains_one + chains_zero + [misc_chain]
     earlier = []
     while any(chain.state is not None for chain in everything):
         if not earlier and all(chain.result is not None for chain in chains_one):
@@ -1012,14 +1128,21 @@
     chan_first, chan_second, chan_update, squares_zero = channel_step(
         0, device, chan_w, chan_m, chan_v, *[chain.result for chain in chains_zero], earlier
     )
-    token_grad = token_chain.result.astype(jnp.float32)
-    small = small_chain.result
-    vector_grad = small[:NV, :width]
-    bias_grad = small[NV, :classes_all]
-    loss_total = small[NV + 1, 0]
+    stem_parts, misc = misc_chain.result
+    hidden = tok_w.shape[3]
+    token_grad = misc[: 4 * hidden].reshape(LAYERS, 2, hidden, MISC)[..., :all_patches].astype(jnp.float32)
+    small = misc[4 * hidden :].astype(jnp.float32)
+    blocks = width // MISC
+    vector_grad = jnp.concatenate([small[16 * j : 16 * j + NV] for j in range(blocks)], 1)
+    bias_grad = small[16 * blocks : 16 * blocks + numbers.shape[1] // MISC].reshape(-1)[:classes_all]
+    loss_total = small[16 * blocks + numbers.shape[1] // MISC, 0]
+    turned = lambda array: jnp.swapaxes(array, -1, -2)
+    tok_w, tok_m, tok_v, stem_w, stem_m, stem_v = [turned(a) for a in (tok_w, tok_m, tok_v, stem_w, stem_m, stem_v)]
     placed = lambda parts: [parts[0], parts[2], parts[1], parts[3]]
-    head_grad = ordered(placed(head_chain.result), 1)[:, :classes_all].astype(jnp.float32)
-    stem_grad = ordered(placed(stem_chain.result), 1).astype(jnp.float32).T
+    head_parts = [part[:, size:] for part in chains_one[1].result]
+    head_grad = ordered(placed(head_parts), 1)[:, :classes_all].astype(jnp.float32)
+    stem_parts = [part[:, : pixels // count_tok] for part in stem_parts]
+    stem_grad = ordered(placed(stem_parts), 1).astype(jnp.float32)
     stem_first, stem_second, stem_update = moments(stem_w, stem_grad, stem_m, stem_v, weight_decay)
     tok_first, tok_second, tok_update = moments(tok_w, token_grad, tok_m, tok_v, weight_decay)
     head_first, head_second, head_update = moments(head_w, head_grad, head_m, head_v, weight_decay)
@@ -1027,28 +1150,24 @@
     hb_first, hb_second, hb_update = moments(hb_w, bias_grad, hb_m, hb_v, 0.0)
     matrix_groups = 2 * LAYERS
     squares = jnp.stack([squares_zero, squares_one])
-    weight_squares = jnp.concatenate(
+    pair_of = lambda array, other, groups: jnp.stack([row_squares(array, groups), row_squares(other, groups)])
+    token_squares = Chain(sum_over(pair_of(tok_w, tok_update, matrix_groups), [("tok", 1), ("tok", 2)]))
+    while token_squares.state is not None:
+        advance([token_squares])
+    shard_squares = jnp.concatenate(
         [
-            row_squares(stem_w, 1) / count_tok,
-            row_squares(tok_w, matrix_groups) / count_dp,
-            squares[:, :, 0].reshape(-1) / count_tok,
-            row_squares(head_w, 1) / count_tok,
-        ]
-    )
-    update_squares = jnp.concatenate(
-        [
-            row_squares(stem_update, 1) / count_tok,
-            row_squares(tok_update, matrix_groups) / count_dp,
-            squares[:, :, 1].reshape(-1) / count_tok,
-            row_squares(head_update, 1) / count_tok,
-        ]
-    )
-    norm_chain = Chain(
-        sum_over(jnp.stack([weight_squares, update_squares]), [("tok", 1), ("tok", 2)] + dp_steps)
-    )
+            pair_of(stem_w, stem_update, 1),
+            squares.transpose(2, 0, 1).reshape(2, matrix_groups),
+            pair_of(head_w, head_update, 1),
+        ],
+        1,
+    )
+    norm_chain = Chain(sum_over(shard_squares, dp_steps))
     while norm_chain.state is not None:
         advance([norm_chain])
-    weight_total, update_total = norm_chain.result
+    weight_total, update_total = jnp.concatenate(
+        [norm_chain.result[:, :1], token_squares.result, norm_chain.result[:, 1:]], 1
+    )
     weight_norms = jnp.sqrt(weight_total)
     update_norms = jnp.sqrt(update_total)
     stem_end = 1
@@ -1071,6 +1190,9 @@
     hb_update_norm = jnp.sqrt(row_squares(hb_update, 1))
     vec_new = renew(vec_w, vec_update, vec_weight_norm, vec_update_norm, NV)
     hb_new = renew(hb_w, hb_update, hb_weight_norm, hb_update_norm, 1)
+    stem_new, stem_first, stem_second, tok_new, tok_first, tok_second = [
+        turned(a) for a in (stem_new, stem_first, stem_second, tok_new, tok_first, tok_second)
+    ]
     norms = jnp.stack(
         [
             jnp.concatenate([weight_norms, vec_weight_norm, hb_weight_norm]),

time: 608 us -> 525 us (0.86)
  local copies, waits for them, and re-layouts: 96.8 us -> 46.2 us
  waiting for transfers between devices: 209 us -> 181 us
  starting transfers between devices: 66.9 us -> 55.7 us
  Pallas kernels: 173 us -> 183 us
    ppermute x77 -> x61, waiting for transfers between devices: 209 us -> 179 us  [swap(): return lax.ppermute(array, axis, [(i, i ^ mask) for i in range(count)])]
    unnamed x212 -> x209, local copies, waits for them, and re-layouts: 54.1 us -> 30.6 us
    squeeze x4 -> x0, local copies, waits for them, and re-layouts: 18.9 us -> none  [the longest x2 9.96 us: body(): got[1]]
    ppermute x77 -> x61, starting transfers between devices: 66.8 us -> 55.6 us  [swap(): return lax.ppermute(array, axis, [(i, i ^ mask) for i in range(count)])]
    pallas_call x18 -> x19, Pallas kernels: 41.7 us -> 50.7 us  [the longest x2 18.9 us: channel_step(): pl.pallas_call(step_kernel, grid=(2, rows // chunk), in_specs=[scalars, b...]
  transfers between devices with their start and end apart: 79 -> 63, of which waited for: 29 -> 28; matrix products, arithmetic and copies ran while one was open for 12% -> 6% of each run, Pallas kernels for 19% -> 25%
where the time goes in v3:
time: 525 us; the launch traced here: 516 us
  Pallas kernels  183 us (35%)
  waiting for transfers between devices  181 us (34%)
  starting transfers between devices  55.7 us (11%)
  local copies, waits for them, and re-layouts  46.2 us (9%)
  other arithmetic  29.9 us (6%)
  between operations  19.9 us (4%)
    ppermute x61, waiting for transfers between devices, swap(): return lax.ppermute(array, axis, [(i, i ^ mask) for i in range(count)])  179 us
    pallas_call x4, Pallas kernels, channel_backward(): pl.pallas_call(functools.partial(channel_backward_kernel, source, last),...  67.7 us
    ppermute x61, starting transfers between devices, swap(): return lax.ppermute(array, axis, [(i, i ^ mask) for i in range(count)])  55.6 us
    unnamed x209, local copies, waits for them, and re-layouts  30.6 us
    pallas_call x2, Pallas kernels, channel_forward(): pl.pallas_call(functools.partial(channel_forward_kernel, source), grid=(4...  28 us
    pallas_call x2, Pallas kernels, channel_step(): pl.pallas_call(step_kernel, grid=(2, rows // chunk), in_specs=[scalars, b...  18.9 us
    pallas_call x2, Pallas kernels, token_backward(): pl.pallas_call(token_backward_kernel, grid=(count,), in_specs=[one, one,...  16.8 us
    pallas_call x2, Pallas kernels, split_cores(): pl.pallas_call(split_kernel, grid=(steps,), in_specs=[low_rows, high_rows...  13.8 us
  transfers between devices with their start and end apart: 63, of which 28 were waited for; matrix products, arithmetic and copies ran while one was open for 6% of the time, Pallas kernels for 25%

profile of v3, /device:TPU:0, one launch (start us, length us, event | category | flops | bytes accessed | tf_op | source)
XLA Modules:
  0.0 515.9 jit_solution(3999406345290909556)
XLA Ops:
  12.2 3.0 collective-permute-start.1
  15.3 2.7 collective-permute-start
  25.1 21.9 %collective-permute-done = bf16[192,768]{1,0:T(8,128)(2,1)S(1)} collective-permute-done((bf16[192,768]{1,0:T(8,128)(2,1)S(1)}, bf16[192,768]{1,0:T(8,128)(2,1)S(1)}, u32[]{:S(2)}, u32[]{:S(2)}) %collective-permute-start) | collective-permute-done | bytes 294944 | tf_op jit(solution)/shard_map/ppermute | solution.py:683
  47.0 11.7 %collective-permute-done.2.incoming = bf16[49,8,768]{2,1,0:T(8,128)(2,1)S(1)} collective-permute-done((bf16[49,8,768]{2,1,0:T(8,128)(2,1)S(1)}, bf16[49,8,768]{2,1,0:T(8,128)(2,1)S(1)}, u32[]{:S(2)}, u32[]{:S(2)}) %collective-permute-start.2) | collective-permute-done | bytes 602144 | tf_op jit(solution)/shard_map/ppermute | solution.py:683
  67.1 5.7 %collective-permute-done.6.rest_2_ = bf16[98,768]{1,0:T(8,128)(2,1)S(1)} collective-permute-done((bf16[98,768]{1,0:T(8,128)(2,1)S(1)}, bf16[98,768]{1,0:T(8,128)(2,1)S(1)}, u32[]{:S(2)}, u32[]{:S(2)}) %collective-permute-start.6) | collective-permute-done | bytes 150560 | tf_op jit(solution)/shard_map/ppermute | solution.py:683
  72.9 2.4 collective-permute-done.7.rest_3_
  75.3 2.4 collective-permute-done.3
  80.3 3.7 collective-permute-start.10
  87.1 10.5 %collective-permute-done.8 = bf16[384,768]{1,0:T(8,128)(2,1)S(1)} collective-permute-done((bf16[384,768]{1,0:T(8,128)(2,1)S(1)}, bf16[384,768]{1,0:T(8,128)(2,1)S(1)}, u32[]{:S(2)}, u32[]{:S(2)}) %collective-permute-start.8) | collective-permute-done | bytes 589856 | tf_op jit(solution)/shard_map/ppermute | solution.py:683
  97.5 5.6 %collective-permute-done.9 = bf16[384,768]{1,0:T(8,128)(2,1)S(1)} collective-permute-done((bf16[384,768]{1,0:T(8,128)(2,1)S(1)}, bf16[384,768]{1,0:T(8,128)(2,1)S(1)}, u32[]{:S(2)}, u32[]{:S(2)}) %collective-permute-start.9) | collective-permute-done | bytes 589856 | tf_op jit(solution)/shard_map/ppermute | solution.py:683
  103.1 14.1 %collective-permute-done.10.incoming = bf16[49,8,768]{2,1,0:T(8,128)(2,1)S(1)} collective-permute-done((bf16[49,8,768]{2,1,0:T(8,128)(2,1)S(1)}, bf16[49,8,768]{2,1,0:T(8,128)(2,1)S(1)}, u32[]{:S(2)}, u32[]{:S(2)}) %collective-permute-start.10) | collective-permute-done | bytes 602144 | tf_op jit(solution)/shard_map/ppermute | solution.py:683
  123.8 32.4 %collective-permute-done.14.rest_6_ = bf16[98,768]{1,0:T(8,128)(2,1)S(1)} collective-permute-done((bf16[98,768]{1,0:T(8,128)(2,1)S(1)}, bf16[98,768]{1,0:T(8,128)(2,1)S(1)}, u32[]{:S(2)}, u32[]{:S(2)}) %collective-permute-start.14) | collective-permute-done | bytes 150560 | tf_op jit(solution)/shard_map/ppermute | solution.py:683
  156.2 3.4 collective-permute-done.15.rest_7_
  159.6 2.0 collective-permute-start.16
  165.2 1.8 copy-done
  174.9 2.7 stem.1
  178.7 4.0 token_forward.2
  185.6 15.0 %channel_forward.2 = (f32[800,768]{1,0:T(8,128)}, bf16[800,3072]{1,0:T(8,128)(2,1)}) custom-call(f32[800,768]{1,0:T(8,128)} %copy-done.56, f32[4,768]{1,0:T(4,128)S(1)} %get-tuple-element.620.gains, bf16[2,384,768]{2,1,0:T(8,128)(2,1)} %pad_maximum_fusion.rest_0_.rest_1_, bf16[2,384,768]{2,1,0:T(8,128)(2,1)} %collective-permute-done.11.rest_1_.rest_2_, ...), custom_call_target="tpu_custom_call" | custom-call | flops 7549747200 | bytes 14352384 | tf_op jit(solution)/shard_map/channel_forward/pallas_call | solution.py:188
  200.6 1.7 copy-done.3
  202.3 4.0 token_forward.3
  207.7 2.5 all-gather.4.cloned.1.call-done
  210.2 13.0 %channel_forward.3 = (f32[800,768]{1,0:T(8,128)S(1)}, bf16[800,3072]{1,0:T(8,128)(2,1)S(1)}) custom-call(f32[800,768]{1,0:T(8,128)S(1)} %get-tuple-element.337.middle, f32[4,768]{1,0:T(4,128)S(1)} %get-tuple-element.619.gains, s32[8]{0:T(128)S(1)} %copy-done.52, s32[1]{0:T(128)} %bitcast.3.device.rest_1_.rest_2_, bf16[8,4,192,768]{3,2,1,0:T(8,128)(2,1)} %bitcast.153), custom_call_target="tpu_custom_call" | custom-call | flops 7549747200 | bytes 14352384 | tf_op jit(solution)/shard_map/channel_forward/pallas_call | solution.py:188
  223.2 2.2 copy-done.59
  225.4 4.3 head_step.1
  229.8 15.8 %channel_backward.4 = (bf16[2,2,768,768]{3,2,1,0:T(8,128)(2,1)}, f32[800,768]{1,0:T(8,128)S(1)}, f32[2,768]{1,0:T(2,128)}) custom-call(f32[800,768]{1,0:T(8,128)S(1)} %get-tuple-element.344.gradient, f32[800,768]{1,0:T(8,128)S(1)} %get-tuple-element.337.middle, f32[4,768]{1,0:T(4,128)S(1)} %get-tuple-element.619.gains, bf16[800,3072]{1,0:T(8,128)(2,1)} %copy-done.59, ...), custom_call_target="tpu_custom_call" | custom-call | flops 7549747200 | bytes 11894784 | tf_op jit(solution)/shard_map/channel_backward/pallas_call | solution.py:258
  247.9 16.0 %channel_backward.5 = (bf16[2,2,768,768]{3,2,1,0:T(8,128)(2,1)}, f32[800,768]{1,0:T(8,128)S(1)}, f32[2,768]{1,0:T(2,128)S(1)}) custom-call(f32[800,768]{1,0:T(8,128)S(1)} %get-tuple-element.344.gradient, f32[800,768]{1,0:T(8,128)S(1)} %copy-done.58, f32[4,768]{1,0:T(4,128)S(1)} %get-tuple-element.619.gains, bf16[800,3072]{1,0:T(8,128)(2,1)} %copy-done.59, ...), custom_call_target="tpu_custom_call" | custom-call | flops 7549747200 | bytes 11894784 | tf_op jit(solution)/shard_map/channel_backward/pallas_call | solution.py:258
  264.9 7.1 %split_cores.2 = (bf16[2,384,768]{2,1,0:T(8,128)(2,1)}, bf16[2,384,768]{2,1,0:T(8,128)(2,1)}, bf16[768,1024]{1,0:T(8,128)(2,1)}, bf16[768,1024]{1,0:T(8,128)(2,1)}) custom-call(bf16[2,2,768,768]{3,2,1,0:T(8,128)(2,1)} %get-tuple-element.347.refs_0_.refs_1_.refs_2_, bf16[2,2,768,768]{3,2,1,0:T(8,128)(2,1)} %get-tuple-element.347.refs_0_.refs_1_.refs_2_, ...), custom_call_target="tpu_custom_call" | custom-call | flops 2359296 | bytes 14155776 | tf_op jit(solution)/shard_map/split_cores/pallas_call | solution.py:804
  274.3 1.7 copy-done.8
  276.0 8.6 %token_backward.2 = (f32[800,768]{1,0:T(8,128)S(1)}, f32[2,768]{1,0:T(2,128)S(1)}, f32[384,200]{1,0:T(8,128)S(1)}, f32[384,200]{1,0:T(8,128)S(1)}) custom-call(f32[800,768]{1,0:T(8,128)S(1)} %get-tuple-element.359.gradient, f32[800,768]{1,0:T(8,128)} %get-tuple-element.336.state, f32[4,768]{1,0:T(4,128)S(1)} %get-tuple-element.619.gains, ...), custom_call_target="tpu_custom_call" | custom-call | flops 1887436800 | bytes 9830400 | tf_op jit(solution)/shard_map/token_backward/pallas_call | solution.py:402
  286.7 17.4 %channel_backward.6 = (bf16[2,2,768,768]{3,2,1,0:T(8,128)(2,1)}, f32[800,768]{1,0:T(8,128)}, f32[2,768]{1,0:T(2,128)}) custom-call(f32[800,768]{1,0:T(8,128)} %copy-done.55, f32[800,768]{1,0:T(8,128)} %copy-done.56, f32[4,768]{1,0:T(4,128)S(1)} %get-tuple-element.620.gains, bf16[800,3072]{1,0:T(8,128)(2,1)} %get-tuple-element.362.inner, ...), custom_call_target="tpu_custom_call" | custom-call | flops 7549747200 | bytes 11894784 | tf_op jit(solution)/shard_map/channel_backward/pallas_call | solution.py:258
  304.1 4.8 collective-permute-done.23.refs_3_
  308.9 3.1 fold_all.12
  315.8 18.5 %channel_backward.7 = (bf16[2,2,768,768]{3,2,1,0:T(8,128)(2,1)}, f32[800,768]{1,0:T(8,128)}, f32[2,768]{1,0:T(2,128)S(1)}) custom-call(f32[800,768]{1,0:T(8,128)} %copy-done.55, f32[800,768]{1,0:T(8,128)} %copy-done.56, f32[4,768]{1,0:T(4,128)S(1)} %get-tuple-element.620.gains, bf16[800,3072]{1,0:T(8,128)(2,1)} %get-tuple-element.362.inner, ...), custom_call_target="tpu_custom_call" | custom-call | flops 7549747200 | bytes 11894784 | tf_op jit(solution)/shard_map/channel_backward/pallas_call | solution.py:258
  334.3 6.6 %split_cores.3 = (bf16[2,384,768]{2,1,0:T(8,128)(2,1)}, bf16[2,384,768]{2,1,0:T(8,128)(2,1)}, bf16[768,768]{1,0:T(8,128)(2,1)}, bf16[768,768]{1,0:T(8,128)(2,1)}) custom-call(bf16[2,2,768,768]{3,2,1,0:T(8,128)(2,1)} %get-tuple-element.382.refs_0_.refs_1_.refs_2_, bf16[2,2,768,768]{3,2,1,0:T(8,128)(2,1)} %get-tuple-element.382.refs_0_.refs_1_.refs_2_, ...), custom_call_target="tpu_custom_call" | custom-call | flops 2359296 | bytes 14155776 | tf_op jit(solution)/shard_map/split_cores/pallas_call | solution.py:804
  342.2 2.2 fold_all.13
  348.5 1.9 collective-permute-start.27
  351.5 1.7 copy-done.6
  353.1 8.2 %token_backward.3 = (f32[800,768]{1,0:T(8,128)S(1)}, f32[2,768]{1,0:T(2,128)S(1)}, f32[384,200]{1,0:T(8,128)S(1)}, f32[384,200]{1,0:T(8,128)S(1)}) custom-call(f32[800,768]{1,0:T(8,128)S(1)} %copy-done.4, f32[800,768]{1,0:T(8,128)} %copy-done.2, f32[4,768]{1,0:T(4,128)S(1)} %get-tuple-element.620.gains, bf16[4,384,768]{2,1,0:T(8,128)(2,1)S(1)} %copy-done.6, ...), custom_call_target="tpu_custom_call" | custom-call | flops 1887436800 | bytes 9830400 | tf_op jit(solution)/shard_map/token_backward/pallas_call | solution.py:402
  361.4 1.8 stem_backward.1
  363.3 2.0 gather_misc.1
  365.4 8.6 %collective-permute-done.29.refs_5_ = bf16[2,384,768]{2,1,0:T(8,128)(2,1)} collective-permute-done((bf16[2,384,768]{2,1,0:T(8,128)(2,1)}, bf16[2,384,768]{2,1,0:T(8,128)(2,1)}, u32[]{:S(2)}, u32[]{:S(2)}) %collective-permute-start.29) | collective-permute-done | bytes 1179680 | tf_op jit(solution)/shard_map/ppermute | solution.py:683
  374.3 2.4 fold_all.14
  381.5 7.2 %collective-permute-done.32.refs_3_ = bf16[96,1024]{1,0:T(8,128)(2,1)S(1)} collective-permute-done((bf16[96,1024]{1,0:T(8,128)(2,1)S(1)}, bf16[96,1024]{1,0:T(8,128)(2,1)S(1)}, u32[]{:S(2)}, u32[]{:S(2)}) %collective-permute-start.32) | collective-permute-done | bytes 196640 | tf_op jit(solution)/shard_map/ppermute | solution.py:683
  389.3 14.3 %collective-permute-done.33.refs_5_ = bf16[2,192,768]{2,1,0:T(8,128)(2,1)S(1)} collective-permute-done((bf16[2,192,768]{2,1,0:T(8,128)(2,1)S(1)}, bf16[2,192,768]{2,1,0:T(8,128)(2,1)S(1)}, u32[]{:S(2)}, u32[]{:S(2)}) %collective-permute-start.33) | collective-permute-done | bytes 589856 | tf_op jit(solution)/shard_map/ppermute | solution.py:683
  403.6 6.6 %collective-permute-done.37.refs_11_ = bf16[1216,256]{1,0:T(8,128)(2,1)S(1)} collective-permute-done((bf16[1216,256]{1,0:T(8,128)(2,1)S(1)}, bf16[1216,256]{1,0:T(8,128)(2,1)S(1)}, u32[]{:S(2)}, u32[]{:S(2)}) %collective-permute-start.37) | collective-permute-done | bytes 622624 | tf_op jit(solution)/shard_map/ppermute | solution.py:683
  410.8 2.0 collective-permute-start.41
  414.9 1.9 collective-permute-start.42
  419.3 3.2 collective-permute-done.40.rest_2_
  423.9 5.7 %collective-permute-done.42.refs_1_ = bf16[2,96,768]{2,1,0:T(8,128)(2,1)S(1)} collective-permute-done((bf16[2,96,768]{2,1,0:T(8,128)(2,1)S(1)}, bf16[2,96,768]{2,1,0:T(8,128)(2,1)S(1)}, u32[]{:S(2)}, u32[]{:S(2)}) %collective-permute-start.42) | collective-permute-done | bytes 294944 | tf_op jit(solution)/shard_map/ppermute | solution.py:683
  430.8 1.5 collective-permute-start.45
  433.8 9.3 %channel_step.2 = (f32[2,2,96,3072]{3,2,1,0:T(8,128)}, f32[2,2,96,3072]{3,2,1,0:T(8,128)}, f32[2,2,96,3072]{3,2,1,0:T(8,128)}, f32[2,2]{1,0:T(2,128)}) custom-call(s32[1]{0:T(128)} %bitcast.3.device.rest_1_.rest_2_, f32[2,2,96,3072]{3,2,1,0:T(8,128)} %weight.5, f32[2,2,96,3072]{3,2,1,0:T(8,128)} %mean.3, f32[2,2,96,3072]{3,2,1,0:T(8,128)} %power.3, ...), custom_call_target="tpu_custom_call" | custom-call | flops 5898240 | bytes 15335424 | tf_op jit(solution)/shard_map/channel_step/pallas_call | solution.py:333
  443.4 1.6 collective-permute-start.52
  449.1 2.3 collective-permute-done.51.rest_3_
  451.4 3.8 collective-permute-done.50.rest_2_
  455.2 1.9 collective-permute-done.52.refs_1_
  459.2 9.6 %channel_step.3 = (f32[2,2,96,3072]{3,2,1,0:T(8,128)}, f32[2,2,96,3072]{3,2,1,0:T(8,128)}, f32[2,2,96,3072]{3,2,1,0:T(8,128)}, f32[2,2]{1,0:T(2,128)}) custom-call(s32[1]{0:T(128)} %bitcast.3.device.rest_1_.rest_2_, f32[2,2,96,3072]{3,2,1,0:T(8,128)} %weight.5, ...), custom_call_target="tpu_custom_call", output_to_operand_aliasing={{0}: (10, {}), {1}: (11, {}), {2}: (12, {})} | custom-call | flops 5898240 | bytes 15335424 | tf_op jit(solution)/shard_map/channel_step/pallas_call | solution.py:333
  472.3 1.7 multiply_reduce_fusion.3
  474.0 2.7 maximum_maximum_fusion.refs_0_
  476.7 1.7 collective-permute-start.56
  478.5 2.3 multiply_reduce_fusion
  481.0 1.9 pad_maximum_fusion.18
  485.5 2.6 collective-permute-done.60.refs_1_
  489.5 4.0 collective-permute-done.58.refs_1_
  500.8 6.8 %channel_renew.1 = (f32[2,2,96,3072]{3,2,1,0:T(8,128)}, bf16[2,2,96,3072]{3,2,1,0:T(8,128)(2,1)}) custom-call(f32[2,2]{1,0:T(2,128)} %div.62.trust, f32[2,2,96,3072]{3,2,1,0:T(8,128)} %weight.5, f32[2,2,96,3072]{3,2,1,0:T(8,128)} %get-tuple-element.553.update), custom_call_target="tpu_custom_call" | custom-call | flops 3538944 | bytes 16515072 | tf_op jit(solution)/shard_map/channel_renew/pallas_call | solution.py:355
  (404 shorter events, 100.5 us)
Async XLA Ops:
  7.2 158.0 %all-gather.6.cloned.1.call-start = ((), (), s32[]{:S(2)}) async-start(), calls=%async_computation.1 | async-start | bytes 2838528 | tf_op jit(solution)/shard_map/all_gather | solution.py:988
  10.0 200.2 %all-gather.4.cloned.1.call-start = ((), (), s32[]{:S(2)}) async-start(), calls=%async_computation | async-start | bytes 9732096 | tf_op jit(solution)/shard_map/all_gather | solution.py:992
  12.2 12.9 %collective-permute-start.1 = (bf16[2,2,96,196]{3,2,1,0:T(8,128)(2,1)S(1)}, bf16[2,2,96,196]{3,2,1,0:T(8,128)(2,1)S(1)}, u32[]{:S(2)}, u32[]{:S(2)}) collective-permute-start(bf16[2,2,96,196]{3,2,1,0:T(8,128)(2,1)S(1)} %bitcast_convert_fusion), channel_id=1, source_target_pairs={{0,2},{1,3},{2,0},{3,1},{4,6},{5,7},{6,4},{7,5},{8,10},{9,11},{10,... | collective-permute-start | bytes 451592 | tf_op jit(solution)/shard_map/ppermute | solution.py:683
  15.3 31.7 %collective-permute-start = (bf16[192,768]{1,0:T(8,128)(2,1)S(1)}, bf16[192,768]{1,0:T(8,128)(2,1)S(1)}, u32[]{:S(2)}, u32[]{:S(2)}) collective-permute-start(bf16[192,768]{1,0:T(8,128)(2,1)S(1)} %pad_maximum_fusion.6), channel_id=1, source_target_pairs={{0,16},{4,20},{8,24},{12,28},{16,0},{20,4},{24,8},{28,12},{1,17},{... | collective-permute-start | bytes 884744 | tf_op jit(solution)/shard_map/ppermute | solution.py:683
  19.3 39.5 %collective-permute-start.2 = (bf16[49,8,768]{2,1,0:T(8,128)(2,1)S(1)}, bf16[49,8,768]{2,1,0:T(8,128)(2,1)S(1)}, u32[]{:S(2)}, u32[]{:S(2)}) collective-permute-start(bf16[49,8,768]{2,1,0:T(8,128)(2,1)S(1)} %get-tuple-element.586.own), channel_id=1, source_target_pairs={{0,16},{4,20},{8,24},{12,28},{16,0},{20,4},{24,8},{28,12},{1,17},{... | collective-permute-start | bytes 1806344 | tf_op jit(solution)/shard_map/ppermute | solution.py:683
  59.7 17.9 %collective-permute-start.3 = (bf16[384,768]{1,0:T(8,128)(2,1)}, bf16[384,768]{1,0:T(8,128)(2,1)}, u32[]{:S(2)}, u32[]{:S(2)}) collective-permute-start(bf16[384,768]{1,0:T(8,128)(2,1)} %pad_maximum_fusion.2), channel_id=1, source_target_pairs={{0,8},{4,12},{8,0},{12,4},{16,24},{20,28},{24,16},{28,20},{1,9},{5... | collective-permute-start | bytes 1769480 | tf_op jit(solution)/shard_map/ppermute | solution.py:683
  61.3 14.0 %collective-permute-start.4 = (bf16[2,2,192,196]{3,2,1,0:T(8,128)(2,1)}, bf16[2,2,192,196]{3,2,1,0:T(8,128)(2,1)}, u32[]{:S(2)}, u32[]{:S(2)}) collective-permute-start(bf16[2,2,192,196]{3,2,1,0:T(8,128)(2,1)} %pad_maximum_fusion.5), channel_id=1, source_target_pairs={{0,1},{1,0},{2,3},{3,2},{4,5},{5,4},{6,7},{7,6},{8,9},{9,8},{10,11... | collective-permute-start | bytes 903176 | tf_op jit(solution)/shard_map/ppermute | solution.py:683
  63.4 3.8 collective-permute-start.5
  63.9 9.0 %collective-permute-start.6 = (bf16[98,768]{1,0:T(8,128)(2,1)S(1)}, bf16[98,768]{1,0:T(8,128)(2,1)S(1)}, u32[]{:S(2)}, u32[]{:S(2)}) collective-permute-start(bf16[98,768]{1,0:T(8,128)(2,1)S(1)} %get-tuple-element.299), channel_id=1, source_target_pairs={{0,2},{1,3},{2,0},{3,1},{4,6},{5,7},{6,4},{7,5},{8,10},{9,11},{10,... | collective-permute-start | bytes 451592 | tf_op jit(solution)/shard_map/ppermute | solution.py:683
  64.4 10.9 %collective-permute-start.7 = (bf16[98,768]{1,0:T(8,128)(2,1)S(1)}, bf16[98,768]{1,0:T(8,128)(2,1)S(1)}, u32[]{:S(2)}, u32[]{:S(2)}) collective-permute-start(bf16[98,768]{1,0:T(8,128)(2,1)S(1)} %get-tuple-element.300), channel_id=1, source_target_pairs={{0,3},{1,2},{2,1},{3,0},{4,7},{5,6},{6,5},{7,4},{8,11},{9,10},{10,... | collective-permute-start | bytes 451592 | tf_op jit(solution)/shard_map/ppermute | solution.py:683
  78.8 18.7 %collective-permute-start.8 = (bf16[384,768]{1,0:T(8,128)(2,1)S(1)}, bf16[384,768]{1,0:T(8,128)(2,1)S(1)}, u32[]{:S(2)}, u32[]{:S(2)}) collective-permute-start(bf16[384,768]{1,0:T(8,128)(2,1)S(1)} %pad_maximum_fusion.3), channel_id=1, source_target_pairs={{0,4},{4,0},{8,12},{12,8},{16,20},{20,16},{24,28},{28,24},{1,5},{5... | collective-permute-start | bytes 1769480 | tf_op jit(solution)/shard_map/ppermute | solution.py:683
  80.3 36.9 %collective-permute-start.10 = (bf16[49,8,768]{2,1,0:T(8,128)(2,1)S(1)}, bf16[49,8,768]{2,1,0:T(8,128)(2,1)S(1)}, u32[]{:S(2)}, u32[]{:S(2)}) collective-permute-start(bf16[49,8,768]{2,1,0:T(8,128)(2,1)S(1)} %get-tuple-element.304.own), channel_id=1, source_target_pairs={{0,16},{4,20},{8,24},{12,28},{16,0},{20,4},{24,8},{28,12},{1,17},{... | collective-permute-start | bytes 1806344 | tf_op jit(solution)/shard_map/ppermute | solution.py:683
  84.1 19.1 %collective-permute-start.9 = (bf16[384,768]{1,0:T(8,128)(2,1)S(1)}, bf16[384,768]{1,0:T(8,128)(2,1)S(1)}, u32[]{:S(2)}, u32[]{:S(2)}) collective-permute-start(bf16[384,768]{1,0:T(8,128)(2,1)S(1)} %pad_maximum_fusion.4), channel_id=1, source_target_pairs={{0,2},{1,3},{2,0},{3,1},{4,6},{5,7},{6,4},{7,5},{8,10},{9,11},{10,... | collective-permute-start | bytes 1769480 | tf_op jit(solution)/shard_map/ppermute | solution.py:683
  118.3 41.3 %collective-permute-start.12 = (bf16[2,384,768]{2,1,0:T(8,128)(2,1)}, bf16[2,384,768]{2,1,0:T(8,128)(2,1)}, u32[]{:S(2)}, u32[]{:S(2)}) collective-permute-start(bf16[2,384,768]{2,1,0:T(8,128)(2,1)} %pad_maximum_fusion.1.rest_4_.rest_5_), channel_id=1, source_target_pairs={{0,4},{4,0},{8,12},{12,8},{16,20},{20,16},{24,28},{28,24},{1,5},{5... | collective-permute-start | bytes 3538952 | tf_op jit(solution)/shard_map/ppermute | solution.py:683
  120.0 39.6 %collective-permute-start.11 = (bf16[2,384,768]{2,1,0:T(8,128)(2,1)}, bf16[2,384,768]{2,1,0:T(8,128)(2,1)}, u32[]{:S(2)}, u32[]{:S(2)}) collective-permute-start(bf16[2,384,768]{2,1,0:T(8,128)(2,1)} %pad_maximum_fusion.rest_0_.rest_1_), channel_id=1, source_target_pairs={{0,2},{1,3},{2,0},{3,1},{4,6},{5,7},{6,4},{7,5},{8,10},{9,11},{10,... | collective-permute-start | bytes 3538952 | tf_op jit(solution)/shard_map/ppermute | solution.py:683
  121.8 1.9 collective-permute-start.13
  121.9 34.3 %collective-permute-start.14 = (bf16[98,768]{1,0:T(8,128)(2,1)S(1)}, bf16[98,768]{1,0:T(8,128)(2,1)S(1)}, u32[]{:S(2)}, u32[]{:S(2)}) collective-permute-start(bf16[98,768]{1,0:T(8,128)(2,1)S(1)} %get-tuple-element.317), channel_id=1, source_target_pairs={{0,2},{1,3},{2,0},{3,1},{4,6},{5,7},{6,4},{7,5},{8,10},{9,11},{10,... | collective-permute-start | bytes 451592 | tf_op jit(solution)/shard_map/ppermute | solution.py:683
  123.5 36.1 %collective-permute-start.15 = (bf16[98,768]{1,0:T(8,128)(2,1)S(1)}, bf16[98,768]{1,0:T(8,128)(2,1)S(1)}, u32[]{:S(2)}, u32[]{:S(2)}) collective-permute-start(bf16[98,768]{1,0:T(8,128)(2,1)S(1)} %get-tuple-element.318), channel_id=1, source_target_pairs={{0,3},{1,2},{2,1},{3,0},{4,7},{5,6},{6,5},{7,4},{8,11},{9,10},{10,... | collective-permute-start | bytes 451592 | tf_op jit(solution)/shard_map/ppermute | solution.py:683
  159.6 26.0 %collective-permute-start.16 = (bf16[2,384,768]{2,1,0:T(8,128)(2,1)}, bf16[2,384,768]{2,1,0:T(8,128)(2,1)}, u32[]{:S(2)}, u32[]{:S(2)}) collective-permute-start(bf16[2,384,768]{2,1,0:T(8,128)(2,1)} %pad_maximum_fusion.rest_0_.rest_1_), channel_id=1, source_target_pairs={{0,1},{1,0},{2,3},{3,2},{4,5},{5,4},{6,7},{7,6},{8,9},{9,8},{10,11... | collective-permute-start | bytes 3538952 | tf_op jit(solution)/shard_map/ppermute | solution.py:683
  161.6 24.0 %collective-permute-start.17 = (bf16[2,384,768]{2,1,0:T(8,128)(2,1)}, bf16[2,384,768]{2,1,0:T(8,128)(2,1)}, u32[]{:S(2)}, u32[]{:S(2)}) collective-permute-start(bf16[2,384,768]{2,1,0:T(8,128)(2,1)} %collective-permute-done.11.rest_1_.rest_2_), channel_id=1, source_target_pairs={{0,1},{1,0},{2,3},{3,2},{4,5},{5,4},{6,7},{7,6},{8,9},{9,8},{10,11... | collective-permute-start | bytes 3538952 | tf_op jit(solution)/shard_map/ppermute | solution.py:683
  161.7 23.9 %collective-permute-start.18 = (bf16[2,384,768]{2,1,0:T(8,128)(2,1)}, bf16[2,384,768]{2,1,0:T(8,128)(2,1)}, u32[]{:S(2)}, u32[]{:S(2)}) collective-permute-start(bf16[2,384,768]{2,1,0:T(8,128)(2,1)} %pad_maximum_fusion.1.rest_4_.rest_5_), channel_id=1, source_target_pairs={{0,1},{1,0},{2,3},{3,2},{4,5},{5,4},{6,7},{7,6},{8,9},{9,8},{10,11... | collective-permute-start | bytes 3538952 | tf_op jit(solution)/shard_map/ppermute | solution.py:683
  162.1 23.5 %collective-permute-start.19 = (bf16[2,384,768]{2,1,0:T(8,128)(2,1)}, bf16[2,384,768]{2,1,0:T(8,128)(2,1)}, u32[]{:S(2)}, u32[]{:S(2)}) collective-permute-start(bf16[2,384,768]{2,1,0:T(8,128)(2,1)} %collective-permute-done.12.rest_5_.rest_6_), channel_id=1, source_target_pairs={{0,1},{1,0},{2,3},{3,2},{4,5},{5,4},{6,7},{7,6},{8,9},{9,8},{10,11... | collective-permute-start | bytes 3538952 | tf_op jit(solution)/shard_map/ppermute | solution.py:683
  245.6 18.3 %collective-permute-start.20 = (bf16[2,2,768,768]{3,2,1,0:T(8,128)(2,1)}, bf16[2,2,768,768]{3,2,1,0:T(8,128)(2,1)}, u32[]{:S(2)}, u32[]{:S(2)}) collective-permute-start(bf16[2,2,768,768]{3,2,1,0:T(8,128)(2,1)} %get-tuple-element.348), channel_id=1, source_target_pairs={{0,1},{1,0},{2,3},{3,2},{4,5},{5,4},{6,7},{7,6},{8,9},{9,8},{10,11... | collective-permute-start | bytes 14155784 | tf_op jit(solution)/shard_map/ppermute | solution.py:683
  247.0 17.0 %collective-permute-start.21 = (bf16[2,768,256]{2,1,0:T(8,128)(2,1)S(1)}, bf16[2,768,256]{2,1,0:T(8,128)(2,1)S(1)}, u32[]{:S(2)}, u32[]{:S(2)}) collective-permute-start(bf16[2,768,256]{2,1,0:T(8,128)(2,1)S(1)} %get-tuple-element.584), channel_id=1, source_target_pairs={{0,1},{1,0},{2,3},{3,2},{4,5},{5,4},{6,7},{7,6},{8,9},{9,8},{10,11... | collective-permute-start | bytes 2359304 | tf_op jit(solution)/shard_map/ppermute | solution.py:683
  272.0 36.9 %collective-permute-start.23 = (bf16[768,1024]{1,0:T(8,128)(2,1)}, bf16[768,1024]{1,0:T(8,128)(2,1)}, u32[]{:S(2)}, u32[]{:S(2)}) collective-permute-start(bf16[768,1024]{1,0:T(8,128)(2,1)} %get-tuple-element.358), channel_id=1, source_target_pairs={{0,2},{1,3},{2,0},{3,1},{4,6},{5,7},{6,4},{7,5},{8,10},{9,11},{10,... | collective-permute-start | bytes 4718600 | tf_op jit(solution)/shard_map/ppermute | solution.py:683
  273.5 30.6 %collective-permute-start.22 = (bf16[2,384,768]{2,1,0:T(8,128)(2,1)}, bf16[2,384,768]{2,1,0:T(8,128)(2,1)}, u32[]{:S(2)}, u32[]{:S(2)}) collective-permute-start(bf16[2,384,768]{2,1,0:T(8,128)(2,1)} %get-tuple-element.356), channel_id=1, source_target_pairs={{0,4},{4,0},{8,12},{12,8},{16,20},{20,16},{24,28},{28,24},{1,5},{5... | collective-permute-start | bytes 3538952 | tf_op jit(solution)/shard_map/ppermute | solution.py:683
  312.9 21.4 %collective-permute-start.26 = (bf16[2,2,768,768]{3,2,1,0:T(8,128)(2,1)S(1)}, bf16[2,2,768,768]{3,2,1,0:T(8,128)(2,1)}, u32[]{:S(2)}, u32[]{:S(2)}) collective-permute-start(bf16[2,2,768,768]{3,2,1,0:T(8,128)(2,1)S(1)} %copy-done.102), channel_id=1, source_target_pairs={{0,1},{1,0},{2,3},{3,2},{4,5},{5,4},{6,7},{7,6},{8,9},{9,8},{10,11... | collective-permute-start | bytes 14155784 | tf_op jit(solution)/shard_map/ppermute | solution.py:683
  312.9 28.1 %collective-permute-start.25 = (bf16[384,1024]{1,0:T(8,128)(2,1)}, bf16[384,1024]{1,0:T(8,128)(2,1)}, u32[]{:S(2)}, u32[]{:S(2)}) collective-permute-start(bf16[384,1024]{1,0:T(8,128)(2,1)} %get-tuple-element.379), channel_id=1, source_target_pairs={{0,4},{4,0},{8,12},{12,8},{16,20},{20,16},{24,28},{28,24},{1,5},{5... | collective-permute-start | bytes 2359304 | tf_op jit(solution)/shard_map/ppermute | solution.py:683
  314.4 26.6 %collective-permute-start.24 = (bf16[2,192,768]{2,1,0:T(8,128)(2,1)}, bf16[2,192,768]{2,1,0:T(8,128)(2,1)}, u32[]{:S(2)}, u32[]{:S(2)}) collective-permute-start(bf16[2,192,768]{2,1,0:T(8,128)(2,1)} %get-tuple-element.377), channel_id=1, source_target_pairs={{0,8},{4,12},{8,0},{12,4},{16,24},{20,28},{24,16},{28,20},{1,9},{5... | collective-permute-start | bytes 1769480 | tf_op jit(solution)/shard_map/ppermute | solution.py:683
  345.9 28.1 %collective-permute-start.29 = (bf16[2,384,768]{2,1,0:T(8,128)(2,1)}, bf16[2,384,768]{2,1,0:T(8,128)(2,1)}, u32[]{:S(2)}, u32[]{:S(2)}) collective-permute-start(bf16[2,384,768]{2,1,0:T(8,128)(2,1)} %get-tuple-element.407), channel_id=1, source_target_pairs={{0,4},{4,0},{8,12},{12,8},{16,20},{20,16},{24,28},{28,24},{1,5},{5... | collective-permute-start | bytes 3538952 | tf_op jit(solution)/shard_map/ppermute | solution.py:683
  346.5 27.9 %collective-permute-start.30 = (bf16[768,768]{1,0:T(8,128)(2,1)}, bf16[768,768]{1,0:T(8,128)(2,1)}, u32[]{:S(2)}, u32[]{:S(2)}) collective-permute-start(bf16[768,768]{1,0:T(8,128)(2,1)} %get-tuple-element.409), channel_id=1, source_target_pairs={{0,2},{1,3},{2,0},{3,1},{4,6},{5,7},{6,4},{7,5},{8,10},{9,11},{10,... | collective-permute-start | bytes 3538952 | tf_op jit(solution)/shard_map/ppermute | solution.py:683
  347.9 17.5 %collective-permute-start.28 = (bf16[192,1024]{1,0:T(8,128)(2,1)}, bf16[192,1024]{1,0:T(8,128)(2,1)S(1)}, u32[]{:S(2)}, u32[]{:S(2)}) collective-permute-start(bf16[192,1024]{1,0:T(8,128)(2,1)} %get-tuple-element.405), channel_id=1, source_target_pairs={{0,8},{4,12},{8,0},{12,4},{16,24},{20,28},{24,16},{28,20},{1,9},{5... | collective-permute-start | bytes 1179656 | tf_op jit(solution)/shard_map/ppermute | solution.py:683
  348.5 16.9 %collective-permute-start.27 = (bf16[2,96,768]{2,1,0:T(8,128)(2,1)}, bf16[2,96,768]{2,1,0:T(8,128)(2,1)}, u32[]{:S(2)}, u32[]{:S(2)}) collective-permute-start(bf16[2,96,768]{2,1,0:T(8,128)(2,1)} %get-tuple-element.403), channel_id=1, source_target_pairs={{0,16},{4,20},{8,24},{12,28},{16,0},{20,4},{24,8},{28,12},{1,17},{... | collective-permute-start | bytes 884744 | tf_op jit(solution)/shard_map/ppermute | solution.py:683
  376.7 11.9 %collective-permute-start.31 = (bf16[2,96,768]{2,1,0:T(8,128)(2,1)S(1)}, bf16[2,96,768]{2,1,0:T(8,128)(2,1)S(1)}, u32[]{:S(2)}, u32[]{:S(2)}) collective-permute-start(bf16[2,96,768]{2,1,0:T(8,128)(2,1)S(1)} %get-tuple-element.461.refs_0_), channel_id=1, source_target_pairs={{0,2},{1,3},{2,0},{3,1},{4,6},{5,7},{6,4},{7,5},{8,10},{9,11},{10,... | collective-permute-start | bytes 884744 | tf_op jit(solution)/shard_map/ppermute | solution.py:683
  378.2 10.4 %collective-permute-start.32 = (bf16[96,1024]{1,0:T(8,128)(2,1)S(1)}, bf16[96,1024]{1,0:T(8,128)(2,1)S(1)}, u32[]{:S(2)}, u32[]{:S(2)}) collective-permute-start(bf16[96,1024]{1,0:T(8,128)(2,1)S(1)} %get-tuple-element.452), channel_id=1, source_target_pairs={{0,16},{4,20},{8,24},{12,28},{16,0},{20,4},{24,8},{28,12},{1,17},{... | collective-permute-start | bytes 589832 | tf_op jit(solution)/shard_map/ppermute | solution.py:683
  379.3 24.2 %collective-permute-start.35 = (bf16[1216,256]{1,0:T(8,128)(2,1)S(1)}, bf16[1216,256]{1,0:T(8,128)(2,1)S(1)}, u32[]{:S(2)}, u32[]{:S(2)}) collective-permute-start(bf16[1216,256]{1,0:T(8,128)(2,1)S(1)} %get-tuple-element.458), channel_id=1, source_target_pairs={{0,2},{1,3},{2,0},{3,1},{4,6},{5,7},{6,4},{7,5},{8,10},{9,11},{10,... | collective-permute-start | bytes 1867784 | tf_op jit(solution)/shard_map/ppermute | solution.py:683
  380.7 22.9 %collective-permute-start.36 = (bf16[1216,256]{1,0:T(8,128)(2,1)S(1)}, bf16[1216,256]{1,0:T(8,128)(2,1)S(1)}, u32[]{:S(2)}, u32[]{:S(2)}) collective-permute-start(bf16[1216,256]{1,0:T(8,128)(2,1)S(1)} %get-tuple-element.459), channel_id=1, source_target_pairs={{0,1},{1,0},{2,3},{3,2},{4,5},{5,4},{6,7},{7,6},{8,9},{9,8},{10,11... | collective-permute-start | bytes 1867784 | tf_op jit(solution)/shard_map/ppermute | solution.py:683
  380.7 29.4 %collective-permute-start.37 = (bf16[1216,256]{1,0:T(8,128)(2,1)S(1)}, bf16[1216,256]{1,0:T(8,128)(2,1)S(1)}, u32[]{:S(2)}, u32[]{:S(2)}) collective-permute-start(bf16[1216,256]{1,0:T(8,128)(2,1)S(1)} %get-tuple-element.460), channel_id=1, source_target_pairs={{0,3},{1,2},{2,1},{3,0},{4,7},{5,6},{6,5},{7,4},{8,11},{9,10},{10,... | collective-permute-start | bytes 1867784 | tf_op jit(solution)/shard_map/ppermute | solution.py:683
  388.6 14.9 %collective-permute-start.33 = (bf16[2,192,768]{2,1,0:T(8,128)(2,1)S(1)}, bf16[2,192,768]{2,1,0:T(8,128)(2,1)S(1)}, u32[]{:S(2)}, u32[]{:S(2)}) collective-permute-start(bf16[2,192,768]{2,1,0:T(8,128)(2,1)S(1)} %get-tuple-element.454), channel_id=1, source_target_pairs={{0,8},{4,12},{8,0},{12,4},{16,24},{20,28},{24,16},{28,20},{1,9},{5... | collective-permute-start | bytes 1769480 | tf_op jit(solution)/shard_map/ppermute | solution.py:683
  388.6 14.9 %collective-permute-start.34 = (bf16[384,768]{1,0:T(8,128)(2,1)S(1)}, bf16[384,768]{1,0:T(8,128)(2,1)S(1)}, u32[]{:S(2)}, u32[]{:S(2)}) collective-permute-start(bf16[384,768]{1,0:T(8,128)(2,1)S(1)} %get-tuple-element.456), channel_id=1, source_target_pairs={{0,4},{4,0},{8,12},{12,8},{16,20},{20,16},{24,28},{28,24},{1,5},{5... | collective-permute-start | bytes 1769480 | tf_op jit(solution)/shard_map/ppermute | solution.py:683
  410.8 7.3 %collective-permute-start.41 = (bf16[96,1024]{1,0:T(8,128)(2,1)S(1)}, bf16[96,1024]{1,0:T(8,128)(2,1)S(1)}, u32[]{:S(2)}, u32[]{:S(2)}) collective-permute-start(bf16[96,1024]{1,0:T(8,128)(2,1)S(1)} %get-tuple-element.502.rest_0_), channel_id=1, source_target_pairs={{0,3},{1,2},{2,1},{3,0},{4,7},{5,6},{6,5},{7,4},{8,11},{9,10},{10,... | collective-permute-start | bytes 589832 | tf_op jit(solution)/shard_map/ppermute | solution.py:683
  412.8 17.2 %collective-permute-start.44 = (bf16[832,256]{1,0:T(8,128)(2,1)S(1)}, bf16[832,256]{1,0:T(8,128)(2,1)S(1)}, u32[]{:S(2)}, u32[]{:S(2)}) collective-permute-start(bf16[832,256]{1,0:T(8,128)(2,1)S(1)} %get-tuple-element.488), channel_id=1, source_target_pairs={{0,4},{4,0},{8,12},{12,8},{16,20},{20,16},{24,28},{28,24},{1,5},{5... | collective-permute-start | bytes 1277960 | tf_op jit(solution)/shard_map/ppermute | solution.py:683
  413.4 9.0 %collective-permute-start.40 = (bf16[96,1024]{1,0:T(8,128)(2,1)S(1)}, bf16[96,1024]{1,0:T(8,128)(2,1)S(1)}, u32[]{:S(2)}, u32[]{:S(2)}) collective-permute-start(bf16[96,1024]{1,0:T(8,128)(2,1)S(1)} %get-tuple-element.502.rest_0_), channel_id=1, source_target_pairs={{0,2},{1,3},{2,0},{3,1},{4,6},{5,7},{6,4},{7,5},{8,10},{9,11},{10,... | collective-permute-start | bytes 589832 | tf_op jit(solution)/shard_map/ppermute | solution.py:683
  414.9 14.7 %collective-permute-start.42 = (bf16[2,96,768]{2,1,0:T(8,128)(2,1)S(1)}, bf16[2,96,768]{2,1,0:T(8,128)(2,1)S(1)}, u32[]{:S(2)}, u32[]{:S(2)}) collective-permute-start(bf16[2,96,768]{2,1,0:T(8,128)(2,1)S(1)} %get-tuple-element.484), channel_id=1, source_target_pairs={{0,16},{4,20},{8,24},{12,28},{16,0},{20,4},{24,8},{28,12},{1,17},{... | collective-permute-start | bytes 884744 | tf_op jit(solution)/shard_map/ppermute | solution.py:683
  416.8 13.2 %collective-permute-start.43 = (bf16[192,768]{1,0:T(8,128)(2,1)S(1)}, bf16[192,768]{1,0:T(8,128)(2,1)S(1)}, u32[]{:S(2)}, u32[]{:S(2)}) collective-permute-start(bf16[192,768]{1,0:T(8,128)(2,1)S(1)} %get-tuple-element.486), channel_id=1, source_target_pairs={{0,8},{4,12},{8,0},{12,4},{16,24},{20,28},{24,16},{28,20},{1,9},{5... | collective-permute-start | bytes 884744 | tf_op jit(solution)/shard_map/ppermute | solution.py:683
  418.2 11.8 %collective-permute-start.38 = (bf16[2,96,768]{2,1,0:T(8,128)(2,1)S(1)}, bf16[2,96,768]{2,1,0:T(8,128)(2,1)S(1)}, u32[]{:S(2)}, u32[]{:S(2)}) collective-permute-start(bf16[2,96,768]{2,1,0:T(8,128)(2,1)S(1)} %get-tuple-element.500.near), channel_id=1, source_target_pairs={{0,1},{1,0},{2,3},{3,2},{4,5},{5,4},{6,7},{7,6},{8,9},{9,8},{10,11... | collective-permute-start | bytes 884744 | tf_op jit(solution)/shard_map/ppermute | solution.py:683
  422.5 1.4 collective-permute-start.39
  430.2 12.9 %collective-permute-start.47 = (bf16[640,256]{1,0:T(8,128)(2,1)S(1)}, bf16[640,256]{1,0:T(8,128)(2,1)S(1)}, u32[]{:S(2)}, u32[]{:S(2)}) collective-permute-start(bf16[640,256]{1,0:T(8,128)(2,1)S(1)} %get-tuple-element.499), channel_id=1, source_target_pairs={{0,8},{4,12},{8,0},{12,4},{16,24},{20,28},{24,16},{28,20},{1,9},{5... | collective-permute-start | bytes 983048 | tf_op jit(solution)/shard_map/ppermute | solution.py:683
  430.8 12.4 %collective-permute-start.45 = (bf16[2,96,768]{2,1,0:T(8,128)(2,1)S(1)}, bf16[2,96,768]{2,1,0:T(8,128)(2,1)S(1)}, u32[]{:S(2)}, u32[]{:S(2)}) collective-permute-start(bf16[2,96,768]{2,1,0:T(8,128)(2,1)S(1)} %get-tuple-element.512.refs_0_), channel_id=1, source_target_pairs={{0,2},{1,3},{2,0},{3,1},{4,6},{5,7},{6,4},{7,5},{8,10},{9,11},{10,... | collective-permute-start | bytes 884744 | tf_op jit(solution)/shard_map/ppermute | solution.py:683
  432.3 10.8 %collective-permute-start.46 = (bf16[96,768]{1,0:T(8,128)(2,1)S(1)}, bf16[96,768]{1,0:T(8,128)(2,1)S(1)}, u32[]{:S(2)}, u32[]{:S(2)}) collective-permute-start(bf16[96,768]{1,0:T(8,128)(2,1)S(1)} %get-tuple-element.497), channel_id=1, source_target_pairs={{0,16},{4,20},{8,24},{12,28},{16,0},{20,4},{24,8},{28,12},{1,17},{... | collective-permute-start | bytes 442376 | tf_op jit(solution)/shard_map/ppermute | solution.py:683
  443.4 13.7 %collective-permute-start.52 = (bf16[544,256]{1,0:T(8,128)(2,1)S(1)}, bf16[544,256]{1,0:T(8,128)(2,1)S(1)}, u32[]{:S(2)}, u32[]{:S(2)}) collective-permute-start(bf16[544,256]{1,0:T(8,128)(2,1)S(1)} %get-tuple-element.525), channel_id=1, source_target_pairs={{0,16},{4,20},{8,24},{12,28},{16,0},{20,4},{24,8},{28,12},{1,17},{... | collective-permute-start | bytes 835592 | tf_op jit(solution)/shard_map/ppermute | solution.py:683
  444.9 12.1 %collective-permute-start.48 = (bf16[2,96,768]{2,1,0:T(8,128)(2,1)S(1)}, bf16[2,96,768]{2,1,0:T(8,128)(2,1)S(1)}, u32[]{:S(2)}, u32[]{:S(2)}) collective-permute-start(bf16[2,96,768]{2,1,0:T(8,128)(2,1)S(1)} %get-tuple-element.531.near), channel_id=1, source_target_pairs={{0,1},{1,0},{2,3},{3,2},{4,5},{5,4},{6,7},{7,6},{8,9},{9,8},{10,11... | collective-permute-start | bytes 884744 | tf_op jit(solution)/shard_map/ppermute | solution.py:683
  445.8 5.6 %collective-permute-start.51 = (bf16[96,768]{1,0:T(8,128)(2,1)S(1)}, bf16[96,768]{1,0:T(8,128)(2,1)S(1)}, u32[]{:S(2)}, u32[]{:S(2)}) collective-permute-start(bf16[96,768]{1,0:T(8,128)(2,1)S(1)} %get-tuple-element.533.rest_0_), channel_id=1, source_target_pairs={{0,3},{1,2},{2,1},{3,0},{4,7},{5,6},{6,5},{7,4},{8,11},{9,10},{10,... | collective-permute-start | bytes 442376 | tf_op jit(solution)/shard_map/ppermute | solution.py:683
  446.6 8.6 %collective-permute-start.50 = (bf16[96,768]{1,0:T(8,128)(2,1)S(1)}, bf16[96,768]{1,0:T(8,128)(2,1)S(1)}, u32[]{:S(2)}, u32[]{:S(2)}) collective-permute-start(bf16[96,768]{1,0:T(8,128)(2,1)S(1)} %get-tuple-element.533.rest_0_), channel_id=1, source_target_pairs={{0,2},{1,3},{2,0},{3,1},{4,6},{5,7},{6,4},{7,5},{8,10},{9,11},{10,... | collective-permute-start | bytes 442376 | tf_op jit(solution)/shard_map/ppermute | solution.py:683
  448.0 7.2 %collective-permute-start.49 = (bf16[96,768]{1,0:T(8,128)(2,1)S(1)}, bf16[96,768]{1,0:T(8,128)(2,1)S(1)}, u32[]{:S(2)}, u32[]{:S(2)}) collective-permute-start(bf16[96,768]{1,0:T(8,128)(2,1)S(1)} %get-tuple-element.533.rest_0_), channel_id=1, source_target_pairs={{0,1},{1,0},{2,3},{3,2},{4,5},{5,4},{6,7},{7,6},{8,9},{9,8},{10,11... | collective-permute-start | bytes 442376 | tf_op jit(solution)/shard_map/ppermute | solution.py:683
  449.1 58.5 %copy-start.69 = (f32[96,1000]{1,0:T(8,128)}, f32[96,1000]{1,0:T(8,128)S(1)}, u32[]{:S(2)}) copy-start(f32[96,1000]{1,0:T(8,128)S(1)} %get-tuple-element.581) | copy-start | bytes 1152004
  457.3 12.4 %collective-permute-start.55 = (bf16[96,256]{1,0:T(8,128)(2,1)S(1)}, bf16[96,256]{1,0:T(8,128)(2,1)S(1)}, u32[]{:S(2)}, u32[]{:S(2)}) collective-permute-start(bf16[96,256]{1,0:T(8,128)(2,1)S(1)} %slice.223), channel_id=1, source_target_pairs={{0,3},{1,2},{2,1},{3,0},{4,7},{5,6},{6,5},{7,4},{8,11},{9,10},{10,... | collective-permute-start | bytes 147464 | tf_op jit(solution)/shard_map/ppermute | solution.py:683
  457.8 11.9 %collective-permute-start.54 = (bf16[96,256]{1,0:T(8,128)(2,1)S(1)}, bf16[96,256]{1,0:T(8,128)(2,1)S(1)}, u32[]{:S(2)}, u32[]{:S(2)}) collective-permute-start(bf16[96,256]{1,0:T(8,128)(2,1)S(1)} %slice.223), channel_id=1, source_target_pairs={{0,2},{1,3},{2,0},{3,1},{4,6},{5,7},{6,4},{7,5},{8,10},{9,11},{10,... | collective-permute-start | bytes 147464 | tf_op jit(solution)/shard_map/ppermute | solution.py:683
  458.7 11.0 %collective-permute-start.53 = (bf16[96,256]{1,0:T(8,128)(2,1)S(1)}, bf16[96,256]{1,0:T(8,128)(2,1)S(1)}, u32[]{:S(2)}, u32[]{:S(2)}) collective-permute-start(bf16[96,256]{1,0:T(8,128)(2,1)S(1)} %slice.223), channel_id=1, source_target_pairs={{0,1},{1,0},{2,3},{3,2},{4,5},{5,4},{6,7},{7,6},{8,9},{9,8},{10,11... | collective-permute-start | bytes 147464 | tf_op jit(solution)/shard_map/ppermute | solution.py:683
  476.7 8.8 %collective-permute-start.56 = (f32[2,6]{1,0:T(2,128)S(1)}, f32[2,6]{1,0:T(2,128)S(1)}, u32[]{:S(2)}, u32[]{:S(2)}) collective-permute-start(f32[2,6]{1,0:T(2,128)S(1)} %maximum_maximum_fusion.refs_0_), channel_id=1, source_target_pairs={{0,4},{4,0},{8,12},{12,8},{16,20},{20,16},{24,28},{28,24},{1,5},{5... | collective-permute-start | bytes 152 | tf_op jit(solution)/shard_map/ppermute | solution.py:683
  480.9 3.6 collective-permute-start.59
  484.5 3.6 collective-permute-start.60
  485.5 3.6 collective-permute-start.57
  489.1 4.5 collective-permute-start.58
  (103 other events, 1017.2 us)
Sparse Core Ops, SparseCore 0:
  11.5 107.5 all-gather.5
  122.6 87.5 all-gather.3

commit v4 on v3

--- a/solution.py
+++ b/solution.py
@@ -28,6 +28,8 @@
 room = pltpu.CompilerParams(vmem_limit_bytes=44 * 1024 * 1024)
 places = (0, 2, 1, 3)
 large = pltpu.CompilerParams(vmem_limit_bytes=60 * 1024 * 1024)
+slim = pltpu.CompilerParams(vmem_limit_bytes=36 * 1024 * 1024)
+lean = pltpu.CompilerParams(vmem_limit_bytes=24 * 1024 * 1024)
 
 
 def dot(left, right, contract=(1, 0)):
@@ -90,7 +92,7 @@
             jax.ShapeDtypeStruct(state.shape, jnp.float32),
             jax.ShapeDtypeStruct((count, hidden, width), low),
         ],
-        compiler_params=room,
+        compiler_params=lean,
         cost_estimate=cost(4 * count * rows * hidden * width, 10 * state.size, 0),
         name="token_forward",
     )(state, gains, token_in, token_out)
@@ -105,7 +107,7 @@
 
 
 def hbm(arrays):
-    return [pl.BlockSpec(memory_space=pl.ANY)] * len(arrays)
+    return [pl.BlockSpec(memory_space=pltpu.HBM)] * len(arrays)
 
 
 scalars = pl.BlockSpec(memory_space=pltpu.SMEM)
@@ -200,7 +202,7 @@
             pltpu.VMEM((4, width, size), low),
             pltpu.SemaphoreType.DMA((4, source.sems)),
         ],
-        compiler_params=room,
+        compiler_params=slim,
         cost_estimate=cost(4 * rows * width * total, 4 * width * total + 2 * rows * total),
         name="channel_forward",
     )(middle, gains, *source.arrays)
@@ -343,25 +345,77 @@
     )(device, weight, mean, power, near, far, *chain_out, *earlier)
 
 
-def renew_kernel(trust, weight, update, fresh, fresh_low):
-    value = weight[...] - learn_rate * (trust[pl.program_id(0), pl.program_id(1)] * update[...])
-    fresh[...] = value
-    fresh_low[...] = value.astype(low)
-
-
-def channel_renew(trust, weight, update):
+def ends_kernel(
+    device, squares_zero, squares_one, stem_w, stem_m, stem_v, head_w, head_m, head_v, *rest
+):
+    stem_grads, head_grads, outs, sums = rest[:4], rest[4:8], rest[8:14], rest[14]
+
+    def step(sources, grads, first, results):
+        weight, mean, power = sources
+        mean_new, power_new, update = results
+        parts = [grad[:, first:].astype(jnp.float32) for grad in grads]
+        size = -(-weight.shape[1] // (4 * 64)) * 64
+        weight_part, update_part = 0.0, 0.0
+        for a in range(4):
+            rel = device[0] ^ a
+            lanes = slice(a * size, min((a + 1) * size, weight.shape[1]))
+            cut = [part[:, : lanes.stop - lanes.start] for part in parts]
+            grad = jnp.where(rel < 2, jnp.where(rel == 0, cut[0], cut[1]), jnp.where(rel == 2, cut[2], cut[3]))
+            value = weight[:, lanes]
+            mean_new[:, lanes], power_new[:, lanes], change = moments(
+                value, grad, mean[:, lanes], power[:, lanes], weight_decay
+            )
+            update[:, lanes] = change
+            weight_part += jnp.sum(jnp.sum(value * value, 0, keepdims=True), 1, keepdims=True)
+            update_part += jnp.sum(jnp.sum(change * change, 0, keepdims=True), 1, keepdims=True)
+        return weight_part, update_part
+
+    stem_part = step((stem_w, stem_m, stem_v), stem_grads, 0, outs[:3])
+    head_part = step((head_w, head_m, head_v), head_grads, head_grads[0].shape[1] - MISC, outs[3:])
+    lane = lax.broadcasted_iota(jnp.int32, (1, LANES), 1)
+    sums[...] = jnp.zeros_like(sums)
+    for kind in range(2):
+        values = [stem_part[kind]]
+        values += [squares[way, kind] for squares in (squares_zero, squares_one) for way in range(2)]
+        values += [head_part[kind]]
+        sums[kind : kind + 1] = sum(jnp.where(lane == k, value, 0.0) for k, value in enumerate(values))
+
+
+def ends_step(device, squares, stem, head, stem_grads, head_grads):
+    shapes = [jax.ShapeDtypeStruct(arrays[0].shape, jnp.float32) for arrays in (stem, head) for _ in range(3)]
+    return pl.pallas_call(
+        ends_kernel,
+        in_specs=[scalars] * 3 + [pl.BlockSpec()] * 14,
+        out_shape=shapes + [jax.ShapeDtypeStruct((SUBLANES, LANES), jnp.float32)],
+        compiler_params=lean,
+        name="ends_step",
+    )(device, *squares, *stem, *head, *stem_grads, *head_grads)
+
+
+def renew_kernel(squares, weight, update, fresh, fresh_low):
+    norms = jnp.sqrt(squares[0:2])
+    trust = norms[0:1] / (norms[1:2] + epsilon)
+    spot = 1 + pl.program_id(0) * pl.num_programs(1) + pl.program_id(1)
+    lane = lax.broadcasted_iota(jnp.int32, trust.shape, 1)
+    trust = jnp.sum(jnp.where(lane == spot, trust, 0.0), 1, keepdims=True)
+    value = weight[0, 0] - learn_rate * (trust * update[0, 0])
+    fresh[0, 0] = value
+    fresh_low[0, 0] = value.astype(low)
+
+
+def channel_renew(squares, weight, update):
     layers, ways, rows, columns = weight.shape
     block = pl.BlockSpec((1, 1, rows, columns), lambda i, j: (i, j, 0, 0))
     return pl.pallas_call(
         renew_kernel,
         grid=(layers, ways),
-        in_specs=[pl.BlockSpec(memory_space=pltpu.SMEM), block, block],
+        in_specs=[whole(squares), block, block],
         out_specs=[block, block],
         out_shape=[jax.ShapeDtypeStruct(weight.shape, jnp.float32), jax.ShapeDtypeStruct(weight.shape, low)],
         compiler_params=large,
         cost_estimate=cost(3 * weight.size, 14 * weight.size),
         name="channel_renew",
-    )(trust, weight, update)
+    )(squares, weight, update)
 
 
 def token_backward_kernel(gradient, state, gains, before, token_in, token_out_turn, *rest):
@@ -413,7 +467,7 @@
             jax.ShapeDtypeStruct((hidden, rows), jnp.float32),
             jax.ShapeDtypeStruct((hidden, rows), jnp.float32),
         ],
-        compiler_params=room,
+        compiler_params=lean,
         cost_estimate=cost(8 * count * rows * hidden * width, 16 * state.size, 0),
         name="token_backward",
     )(gradient, state, gains, before, token_in, token_out_turn, *after)
@@ -451,24 +505,29 @@
             pltpu.VMEM((patches * images, LANES), jnp.float32),
             pltpu.VMEM((rows, LANES), jnp.float32),
         ],
-        compiler_params=room,
+        compiler_params=lean,
         cost_estimate=cost(4 * own.size, 6 * own.size),
         name="mix",
     )(place, share, device, own, incoming)
 
 
 def stem_kernel(device, spots, *rest):
-    pieces, (blocks, gains, mixed, state, joint, spare, weights, sems) = rest[:-8], rest[-8:]
+    sources, (blocks, gains, mixed, state, joint, spare, pieces, weights, piece_sems, sems) = rest[:-10], rest[-10:]
+    piece_copies = [
+        pltpu.make_async_copy(source, pieces.at[k], piece_sems.at[k]) for k, source in enumerate(sources)
+    ]
     copies = block_copies(spots, blocks, pl.ds(0, weights.shape[1]), weights, sems)
-    for copy in copies:
+    for copy in piece_copies + copies:
         copy.start()
-    count = len(pieces) // 2
+    count = len(sources) // 2
     odd, upper = (device[0] & 1) == 1, (device[0] & 2) == 2
-    patches = pieces[0].shape[0] // 2
+    patches = pieces.shape[1] // 2
     rows = joint.shape[0] // (2 * 2)
     joint[...] = jnp.zeros_like(joint)
+    for copy in piece_copies:
+        copy.wait()
     for side in range(2):
-        arrived = [ref[...].astype(jnp.float32) for ref in pieces[side * count : (side + 1) * count]]
+        arrived = [pieces[side * count + k].astype(jnp.float32) for k in range(count)]
         arrived = [jnp.where(odd, arrived[k ^ 1], arrived[k]) for k in range(count)]
         for k in range(count):
             spare[...] = jnp.where(upper, arrived[k ^ 2], arrived[k])
@@ -485,7 +544,7 @@
     width, pixels = blocks.shape[0] * blocks.shape[1], pieces[0].shape[1]
     return pl.pallas_call(
         stem_kernel,
-        in_specs=[scalars, scalars] + [pl.BlockSpec()] * len(pieces) + hbm([blocks]) + [pl.BlockSpec()],
+        in_specs=[scalars, scalars] + hbm(pieces) + hbm([blocks]) + [pl.BlockSpec()],
         out_shape=[
             jax.ShapeDtypeStruct((rows, pixels), low),
             jax.ShapeDtypeStruct((rows, width), jnp.float32),
@@ -493,10 +552,12 @@
         scratch_shapes=[
             pltpu.VMEM((rows, pixels), jnp.float32),
             pltpu.VMEM(pieces[0].shape, jnp.float32),
+            pltpu.VMEM((len(pieces), *pieces[0].shape), low),
             pltpu.VMEM((width, pixels), low),
+            pltpu.SemaphoreType.DMA((len(pieces),)),
             pltpu.SemaphoreType.DMA((blocks.shape[0],)),
         ],
-        compiler_params=room,
+        compiler_params=large,
         cost_estimate=cost(2 * rows * width * pixels, 12 * rows * width),
         name="stem",
     )(device, spots, *pieces, blocks, gains)
@@ -576,7 +637,7 @@
             pltpu.VMEM((width, columns), low),
             pltpu.SemaphoreType.DMA((blocks.shape[0],)),
         ],
-        compiler_params=room,
+        compiler_params=lean,
         cost_estimate=cost(64 * width * columns, 8 * rows * width),
         name="head_step",
     )(device, spots, state, gains, blocks, bias, numbers, labels, others, lam, weight, scale)
@@ -602,7 +663,7 @@
             jax.ShapeDtypeStruct((4, width, MISC), low),
             jax.ShapeDtypeStruct((1, width), jnp.float32),
         ],
-        compiler_params=room,
+        compiler_params=lean,
         cost_estimate=cost(2 * gradient.size * pixels, 8 * gradient.size),
         name="stem_backward",
     )(device, gradient, mixed)
@@ -625,7 +686,7 @@
     return pl.pallas_call(
         vectors_kernel,
         out_shape=jax.ShapeDtypeStruct(vectors.shape, jnp.float32),
-        compiler_params=room,
+        compiler_params=lean,
         name="relative_vectors",
     )(vectors, source)
 
@@ -635,8 +696,8 @@
         rest[:4],
         rest[4:count],
         rest[count : count + 2],
-        rest[count + 2 : count + 6],
-        rest[count + 6 :],
+        [rest[count + 2 + place // 2].at[place % 2] for place in range(4)],
+        rest[count + 4 :],
     )
     joint[...] = jnp.zeros_like(joint)
     at = 0
@@ -668,12 +729,12 @@
     rows = stem_grads.shape[1] + tokens[0].shape[0] + SMALL
     return pl.pallas_call(
         functools.partial(gather_misc_kernel, 4 + len(parts)),
-        out_shape=[jax.ShapeDtypeStruct((rows, MISC), low)] * 4,
+        out_shape=[jax.ShapeDtypeStruct((2, rows, MISC), low)] * 2,
         scratch_shapes=[
             pltpu.VMEM((16, parts[0].shape[1]), jnp.float32),
             pltpu.VMEM((SMALL, MISC), jnp.float32),
         ],
-        compiler_params=room,
+        compiler_params=lean,
         name="gather_misc",
     )(source, stem_grads, *tokens, *parts, bias, loss)
 
@@ -724,11 +785,6 @@
     return (keep.astype(jnp.float32) + got.astype(jnp.float32)).astype(keep.dtype)
 
 
-def added_four(keep, second, first, both):
-    wide = lambda array: array.astype(jnp.float32)
-    return ((wide(keep) + wide(first)) + (wide(second) + wide(both))).astype(keep.dtype)
-
-
 def cut_rows(array, half):
     middle = array.shape[-2] // 2
     return array[..., half * middle : (half + 1) * middle, :]
@@ -740,7 +796,7 @@
     if kind == "blocks":
         return [added(keep[0], got[0]), added(keep[1], got[1])]
     if isinstance(kind, int):
-        total = added(keep, got) if not isinstance(got, (list, tuple)) else added_four(keep, *got)
+        total = added(keep, got)
         return [
             jnp.concatenate([total[: kind // 2], total[kind:]]),
             jnp.concatenate([total[kind // 2 : kind], total[kind:]]),
@@ -766,7 +822,7 @@
     outs = pl.pallas_call(
         functools.partial(fold_kernel, blank),
         out_shape=flat,
-        compiler_params=room,
+        compiler_params=lean,
         cost_estimate=cost(sum(a.size for a in arrays), sum(4 * a.size for a in arrays)),
         name="fold_all",
     )(*arrays)
@@ -834,9 +890,8 @@
     return [keep, *others]
 
 
-def reduce_misc(stem_rows, keep, far, near, both):
-    arrived = [swap(array, "tok", mask) for mask, array in ((2, far), (1, near), (3, both))]
-    keep, send = yield keep, arrived, stem_rows
+def reduce_misc(stem_rows, keep, send):
+    keep, send = yield keep, swap(send, "tok", 2), stem_rows
     steps = [1] + dp_masks()[::-1]
     for mask in steps[:-1]:
         stem_rows //= 2
@@ -1025,35 +1080,32 @@
     for step, mask in enumerate(masks):
         got = swap(packed(blocks), "dp", mask)
         if step == 0:
-            blocks, got, tok_far, own_parts[1], incoming = fence(
-                blocks, got, swap(tok_low, "tok", 2), own_parts[1], incoming
-            )
+            blocks, got, tok_low, own_parts[1], incoming = fence(blocks, got, tok_low, own_parts[1], incoming)
             pieces = mixed_pieces(0, incoming)
-            tok_half = jnp.concatenate([tok_low, tok_far], 2)
-            tok_near = swap(tok_half, "tok", 1)
+            incoming_two = swap(own_parts[1], "dp", partner_mask)
+            tok_far = swap(tok_low, "tok", 2)
         elif step == 1:
-            blocks, got, tok_near, own_parts[1], vectors, image_rows, pieces = fence(
-                blocks, got, tok_near, own_parts[1], vectors, image_rows, pieces
+            blocks, got, vectors, image_rows, pieces, tok_low, tok_far = fence(
+                blocks, got, vectors, image_rows, pieces, tok_low, tok_far
             )
         else:
             blocks, got = fence(blocks, got)
         blocks = doubled(blocks, got)
-    tok_turn = jnp.concatenate([tok_half, tok_near], 2)
+    tok_half = jnp.concatenate([tok_low, tok_far], 2)
+    tok_turn = jnp.concatenate([tok_half, swap(tok_half, "tok", 1)], 2)
     tok_turn = jnp.pad(tok_turn, ((0, 0), (0, 0), (0, 0), (0, each - all_patches)))
-    tok_all = jnp.swapaxes(tok_turn, 2, 3)
-
-    incoming_two = swap(own_parts[1], "dp", partner_mask)
+    token_turn = [[tok_turn[layer, way] for way in range(2)] for layer in range(LAYERS)]
+    token_all = [[array.T for array in pair] for pair in token_turn]
+
     first, second = blocks
     first_low, second_far = swap(first, "dp", 1), swap(second, "tok", 2)
-    first, second, first_low, second_far, incoming_two, tok_all, tok_turn = fence(
-        first, second, first_low, second_far, incoming_two, tok_all, tok_turn
+    first, second, first_low, second_far, incoming_two, token_all, token_turn = fence(
+        first, second, first_low, second_far, incoming_two, token_all, token_turn
     )
     more = mixed_pieces(1, incoming_two)
     firsts, seconds = jnp.stack([first, first_low]), jnp.stack([second, second_far])
     firsts_far, seconds_low = swap(firsts, "tok", 2), swap(seconds, "dp", 1)
-    firsts, seconds, firsts_far, seconds_low, pieces, more = fence(
-        firsts, seconds, firsts_far, seconds_low, pieces, more
-    )
+    firsts, seconds, firsts_far, seconds_low, more = fence(firsts, seconds, firsts_far, seconds_low, more)
     source_zero = Pieces(
         [firsts, firsts_far, swap(firsts, "tok", 1), swap(firsts_far, "tok", 1)],
         [seconds, seconds_low, swap(seconds, "tok", 1), swap(seconds_low, "tok", 1)],
@@ -1073,9 +1125,9 @@
 
     gains = [vectors[1 + 4 * layer : 5 + 4 * layer] for layer in range(LAYERS)]
     mixed, stem_state = stem(device, spots, pieces + more, ends, vectors, each * per_tok)
-    middle_zero, before_zero = token_forward(stem_state, gains[0], tok_turn[0, 0], tok_all[0, 1])
+    middle_zero, before_zero = token_forward(stem_state, gains[0], token_turn[0][0], token_all[0][1])
     first_state, inner_zero = channel_forward(middle_zero, gains[0], source_zero)
-    middle_one, before_one = token_forward(first_state, gains[1], tok_turn[1, 0], tok_all[1, 1])
+    middle_one, before_one = token_forward(first_state, gains[1], token_turn[1][0], token_all[1][1])
     second_state, inner_one = channel_forward(middle_one, gains[1], source_one)
     gradient, last_part, head_grads, bias_part, loss_local = head_step(
         device, spots, second_state, vectors[NV - 2 :], ends, bias, numbers, *image_rows, all_patches, pixels
@@ -1089,7 +1141,7 @@
     in_keep, in_send, out_keep, out_send, gradient = fence(in_keep, in_send, out_keep, out_send, gradient)
     chains_one = [Chain(reduce_rows(in_keep, in_send)), Chain(reduce_columns(out_keep, out_send))]
     gradient, first_one, *token_one = token_backward(
-        gradient, first_state, gains[1], before_one, tok_all[1, 0], tok_turn[1, 1]
+        gradient, first_state, gains[1], before_one, token_all[1][0], token_turn[1][1]
     )
     send, partial, _ = channel_backward(gradient, middle_zero, gains[0], inner_zero, source_zero)
     send, partial, gradient = advance(chains_one, send, partial, gradient)
@@ -1101,7 +1153,7 @@
     )
     chains_zero = [Chain(reduce_rows(in_keep, in_send)), Chain(reduce_columns(out_keep, out_send))]
     gradient, first_zero, *token_zero = token_backward(
-        gradient, stem_state, gains[0], before_zero, tok_all[0, 0], tok_turn[0, 1]
+        gradient, stem_state, gains[0], before_zero, token_all[0][0], token_turn[0][1]
     )
     stem_grads, stem_bias = stem_backward(device, gradient, mixed)
     misc = gather_misc(
@@ -1113,7 +1165,8 @@
         loss_local,
     )
     misc = advance(chains_one + chains_zero, *misc)
-    misc_chain = Chain(reduce_misc(width, *misc))
+    ((misc_keep, misc_send),) = fold_all([(misc[0], swap(misc[1], "tok", 1), "blocks")])
+    misc_chain = Chain(reduce_misc(width, misc_keep, misc_send))
     dp_steps = [("dp", mask) for mask in [1] + dp_masks()[::-1]]
     everything = chains_one + chains_zero + [misc_chain]
     earlier = []
@@ -1138,35 +1191,35 @@
     loss_total = small[16 * blocks + numbers.shape[1] // MISC, 0]
     turned = lambda array: jnp.swapaxes(array, -1, -2)
     tok_w, tok_m, tok_v, stem_w, stem_m, stem_v = [turned(a) for a in (tok_w, tok_m, tok_v, stem_w, stem_m, stem_v)]
-    placed = lambda parts: [parts[0], parts[2], parts[1], parts[3]]
-    head_parts = [part[:, size:] for part in chains_one[1].result]
-    head_grad = ordered(placed(head_parts), 1)[:, :classes_all].astype(jnp.float32)
-    stem_parts = [part[:, : pixels // count_tok] for part in stem_parts]
-    stem_grad = ordered(placed(stem_parts), 1).astype(jnp.float32)
-    stem_first, stem_second, stem_update = moments(stem_w, stem_grad, stem_m, stem_v, weight_decay)
+    stem_first, stem_second, stem_update, head_first, head_second, head_update, shard_squares = ends_step(
+        device,
+        (squares_zero, squares_one),
+        (stem_w, stem_m, stem_v),
+        (head_w, head_m, head_v),
+        stem_parts,
+        chains_one[1].result,
+    )
     tok_first, tok_second, tok_update = moments(tok_w, token_grad, tok_m, tok_v, weight_decay)
-    head_first, head_second, head_update = moments(head_w, head_grad, head_m, head_v, weight_decay)
     vec_first, vec_second, vec_update = moments(vec_w, vector_grad, vec_m, vec_v, 0.0)
     hb_first, hb_second, hb_update = moments(hb_w, bias_grad, hb_m, hb_v, 0.0)
     matrix_groups = 2 * LAYERS
-    squares = jnp.stack([squares_zero, squares_one])
     pair_of = lambda array, other, groups: jnp.stack([row_squares(array, groups), row_squares(other, groups)])
-    token_squares = Chain(sum_over(pair_of(tok_w, tok_update, matrix_groups), [("tok", 1), ("tok", 2)]))
-    while token_squares.state is not None:
-        advance([token_squares])
-    shard_squares = jnp.concatenate(
-        [
-            pair_of(stem_w, stem_update, 1),
-            squares.transpose(2, 0, 1).reshape(2, matrix_groups),
-            pair_of(head_w, head_update, 1),
-        ],
-        1,
-    )
-    norm_chain = Chain(sum_over(shard_squares, dp_steps))
-    while norm_chain.state is not None:
-        advance([norm_chain])
+    token_squares = pair_of(tok_w, tok_update, matrix_groups)
+    token_squares = token_squares + swap(token_squares, "tok", 1)
+    at = 1
+    while at < count_dp:
+        if 4 * at <= count_dp:
+            one, two, three = [swap(shard_squares, "dp", k * at) for k in (1, 2, 3)]
+            shard_squares = (shard_squares + one) + (two + three)
+            at *= 4
+        else:
+            shard_squares = shard_squares + swap(shard_squares, "dp", at)
+            at *= 2
+    last = 2 + matrix_groups
+    token_squares, shard_squares = fence(token_squares, shard_squares)
+    token_squares = token_squares + swap(token_squares, "tok", 2)
     weight_total, update_total = jnp.concatenate(
-        [norm_chain.result[:, :1], token_squares.result, norm_chain.result[:, 1:]], 1
+        [shard_squares[:2, :1], token_squares, shard_squares[:2, 1:last]], 1
     )
     weight_norms = jnp.sqrt(weight_total)
     update_norms = jnp.sqrt(update_total)
@@ -1181,8 +1234,7 @@
         update_norms[stem_end:tok_end],
         matrix_groups,
     )
-    chan_trust = weight_norms[tok_end:chan_end] / (update_norms[tok_end:chan_end] + epsilon)
-    chan_new, chan_new_low = channel_renew(chan_trust.reshape(LAYERS, 2), chan_w, chan_update)
+    chan_new, chan_new_low = channel_renew(shard_squares, chan_w, chan_update)
     head_new = renew(head_w, head_update, weight_norms[chan_end:], update_norms[chan_end:], 1)
     vec_weight_norm = jnp.sqrt(row_squares(vec_w, NV))
     vec_update_norm = jnp.sqrt(row_squares(vec_update, NV))

time: 525 us -> 502 us (0.956)
  other arithmetic: 29.9 us -> 16.7 us
  waiting for transfers between devices: 181 us -> 173 us
    ppermute x61, waiting for transfers between devices: 179 us -> 163 us  [swap(): return lax.ppermute(array, axis, [(i, i ^ mask) for i in range(count)])]
    all_gather x1, waiting for transfers between devices: 2.5 us -> 10.5 us  [body(): lax.all_gather(later, ('dp', 'tok')).reshape(count_dp, count_tok, -1, size)]
    pallas_call x2 -> x3, Pallas kernels: 9.55 us -> 15.7 us  [the longest x1 7.2 us: channel_renew(): pl.pallas_call(renew_kernel, grid=(layers, ways), in_specs=[whole(squares...]
    unnamed x209 -> x195, local copies, waits for them, and re-layouts: 30.6 us -> 25.5 us
  transfers between devices with their start and end apart: 63 -> 63, of which waited for: 28 -> 26; matrix products, arithmetic and copies ran while one was open for 6% -> 5% of each run, Pallas kernels for 25% -> 27%
where the time goes in v4:
time: 502 us; the launch traced here: 493 us
  Pallas kernels  185 us (37%)
  waiting for transfers between devices  173 us (34%)
  starting transfers between devices  56.7 us (11%)
  local copies, waits for them, and re-layouts  41.8 us (8%)
  between operations  19.9 us (4%)
  other arithmetic  16.7 us (3%)
    ppermute x61, waiting for transfers between devices, swap(): return lax.ppermute(array, axis, [(i, i ^ mask) for i in range(count)])  163 us
    pallas_call x4, Pallas kernels, channel_backward(): pl.pallas_call(functools.partial(channel_backward_kernel, source, last),...  68 us
    ppermute x61, starting transfers between devices, swap(): return lax.ppermute(array, axis, [(i, i ^ mask) for i in range(count)])  56.7 us
    pallas_call x2, Pallas kernels, channel_forward(): pl.pallas_call(functools.partial(channel_forward_kernel, source), grid=(4...  25.7 us
    unnamed x195, local copies, waits for them, and re-layouts  25.5 us
    pallas_call x2, Pallas kernels, channel_step(): pl.pallas_call(step_kernel, grid=(2, rows // chunk), in_specs=[scalars, b...  18.9 us
    pallas_call x2, Pallas kernels, token_backward(): pl.pallas_call(token_backward_kernel, grid=(count,), in_specs=[one, one,...  14.6 us
    pallas_call x2, Pallas kernels, split_cores(): pl.pallas_call(split_kernel, grid=(steps,), in_specs=[low_rows, high_rows...  13.8 us
  transfers between devices with their start and end apart: 63, of which 26 were waited for; matrix products, arithmetic and copies ran while one was open for 5% of the time, Pallas kernels for 27%

profile of v4, /device:TPU:0, one launch (start us, length us, event | category | flops | bytes accessed | tf_op | source)
XLA Modules:
  0.0 493.4 jit_solution(9651598796005833926)
XLA Ops:
  12.2 4.1 collective-permute-start
  23.3 21.9 %collective-permute-done = bf16[192,768]{1,0:T(8,128)(2,1)S(1)} collective-permute-done((bf16[192,768]{1,0:T(8,128)(2,1)S(1)}, bf16[192,768]{1,0:T(8,128)(2,1)S(1)}, u32[]{:S(2)}, u32[]{:S(2)}) %collective-permute-start) | collective-permute-done | bytes 294944 | tf_op jit(solution)/shard_map/ppermute | solution.py:744
  45.2 12.2 %collective-permute-done.1.incoming = bf16[49,8,768]{2,1,0:T(8,128)(2,1)S(1)} collective-permute-done((bf16[49,8,768]{2,1,0:T(8,128)(2,1)S(1)}, bf16[49,8,768]{2,1,0:T(8,128)(2,1)S(1)}, u32[]{:S(2)}, u32[]{:S(2)}) %collective-permute-start.1) | collective-permute-done | bytes 602144 | tf_op jit(solution)/shard_map/ppermute | solution.py:744
  65.3 3.5 collective-permute-start.9
  69.6 3.3 collective-permute-done.5.rest_3_
  72.9 4.2 collective-permute-done.6
  77.1 7.3 %collective-permute-done.2 = bf16[384,768]{1,0:T(8,128)(2,1)} collective-permute-done((bf16[384,768]{1,0:T(8,128)(2,1)}, bf16[384,768]{1,0:T(8,128)(2,1)}, u32[]{:S(2)}, u32[]{:S(2)}) %collective-permute-start.2) | collective-permute-done | bytes 589856 | tf_op jit(solution)/shard_map/ppermute | solution.py:744
  87.1 2.4 collective-permute-start.8
  90.7 14.0 %collective-permute-done.9.incoming = bf16[49,8,768]{2,1,0:T(8,128)(2,1)S(1)} collective-permute-done((bf16[49,8,768]{2,1,0:T(8,128)(2,1)S(1)}, bf16[49,8,768]{2,1,0:T(8,128)(2,1)S(1)}, u32[]{:S(2)}, u32[]{:S(2)}) %collective-permute-start.9) | collective-permute-done | bytes 602144 | tf_op jit(solution)/shard_map/ppermute | solution.py:744
  111.3 32.2 %collective-permute-done.14.rest_6_ = bf16[98,768]{1,0:T(8,128)(2,1)S(1)} collective-permute-done((bf16[98,768]{1,0:T(8,128)(2,1)S(1)}, bf16[98,768]{1,0:T(8,128)(2,1)S(1)}, u32[]{:S(2)}, u32[]{:S(2)}) %collective-permute-start.14) | collective-permute-done | bytes 150560 | tf_op jit(solution)/shard_map/ppermute | solution.py:744
  143.5 4.0 collective-permute-done.15.rest_7_
  147.5 1.9 collective-permute-start.16
  151.6 1.7 copy.84.token_out
  153.3 6.1 %stem.1 = (bf16[800,768]{1,0:T(8,128)(2,1)}, f32[800,768]{1,0:T(8,128)}) custom-call(s32[1]{0:T(128)} %bitcast.3.device.rest_1_.rest_2_, s32[8]{0:T(128)} %get-tuple-element.618.spots.rest_0_.rest_1_, bf16[98,768]{1,0:T(8,128)(2,1)} %copy-done.52, bf16[98,768]{1,0:T(8,128)(2,1)} %copy-done.74, bf16[98,768]{1,0:T(8,128)(2,1)} %copy-done.75, ...), custom_call_target="tpu_custom_call" | custom-call | flops 943718400 | bytes 7372800 | tf_op jit(solution)/shard_map/stem/pallas_call | solution.py:545
  159.4 1.7 copy-done.3
  161.1 4.0 token_forward.2
  166.6 12.6 %channel_forward.2 = (f32[800,768]{1,0:T(8,128)S(1)}, bf16[800,3072]{1,0:T(8,128)(2,1)}) custom-call(f32[800,768]{1,0:T(8,128)S(1)} %get-tuple-element.322.middle, f32[4,768]{1,0:T(4,128)S(1)} %get-tuple-element.591.gains, bf16[2,384,768]{2,1,0:T(8,128)(2,1)S(1)} %copy-done.18, bf16[2,384,768]{2,1,0:T(8,128)(2,1)} %collective-permute-done.11.rest_1_.rest_2_, ...), custom_call_target="tpu_custom_call" | custom-call | flops 7549747200 | bytes 14352384 | tf_op jit(solution)/shard_map/channel_forward/pallas_call | solution.py:190
  179.3 4.0 token_forward.3
  186.1 10.5 %all-gather.4.cloned.1.call-done = bf16[32,192,768]{2,1,0:T(8,128)(2,1)} async-done(((bf16[1,192,768]{2,1,0:T(8,128)(2,1)}), bf16[32,192,768]{2,1,0:T(8,128)(2,1)}) %all-gather.4.cloned.1.call-update) | async-done | bytes 9437200 | tf_op jit(solution)/shard_map/all_gather | solution.py:1047
  196.6 1.7 copy-done.62
  198.3 13.0 %channel_forward.3 = (f32[800,768]{1,0:T(8,128)S(1)}, bf16[800,3072]{1,0:T(8,128)(2,1)S(1)}) custom-call(f32[800,768]{1,0:T(8,128)S(1)} %copy-done.62, f32[4,768]{1,0:T(4,128)S(1)} %get-tuple-element.590.gains, s32[8]{0:T(128)S(1)} %copy-done.56, s32[1]{0:T(128)} %bitcast.3.device.rest_1_.rest_2_, bf16[8,4,192,768]{3,2,1,0:T(8,128)(2,1)} %bitcast.121), custom_call_target="tpu_custom_call" | custom-call | flops 7549747200 | bytes 14352384 | tf_op jit(solution)/shard_map/channel_forward/pallas_call | solution.py:190
  211.4 4.3 head_step.1
  215.8 15.8 %channel_backward.4 = (bf16[2,2,768,768]{3,2,1,0:T(8,128)(2,1)}, f32[800,768]{1,0:T(8,128)S(1)}, f32[2,768]{1,0:T(2,128)}) custom-call(f32[800,768]{1,0:T(8,128)S(1)} %get-tuple-element.337.gradient, f32[800,768]{1,0:T(8,128)S(1)} %copy-done.63, f32[4,768]{1,0:T(4,128)S(1)} %get-tuple-element.590.gains, bf16[800,3072]{1,0:T(8,128)(2,1)} %copy-done.64, ...), custom_call_target="tpu_custom_call" | custom-call | flops 7549747200 | bytes 11894784 | tf_op jit(solution)/shard_map/channel_backward/pallas_call | solution.py:260
  233.2 16.1 %channel_backward.5 = (bf16[2,2,768,768]{3,2,1,0:T(8,128)(2,1)}, f32[800,768]{1,0:T(8,128)S(1)}, f32[2,768]{1,0:T(2,128)S(1)}) custom-call(f32[800,768]{1,0:T(8,128)S(1)} %get-tuple-element.337.gradient, f32[800,768]{1,0:T(8,128)S(1)} %copy-done.63, f32[4,768]{1,0:T(4,128)S(1)} %get-tuple-element.590.gains, bf16[800,3072]{1,0:T(8,128)(2,1)} %copy-done.64, ...), custom_call_target="tpu_custom_call" | custom-call | flops 7549747200 | bytes 11894784 | tf_op jit(solution)/shard_map/channel_backward/pallas_call | solution.py:260
  251.7 7.1 %split_cores.2 = (bf16[2,384,768]{2,1,0:T(8,128)(2,1)}, bf16[2,384,768]{2,1,0:T(8,128)(2,1)}, bf16[768,1024]{1,0:T(8,128)(2,1)}, bf16[768,1024]{1,0:T(8,128)(2,1)}) custom-call(bf16[2,2,768,768]{3,2,1,0:T(8,128)(2,1)} %get-tuple-element.340.refs_0_.refs_1_.refs_2_, bf16[2,2,768,768]{3,2,1,0:T(8,128)(2,1)} %get-tuple-element.340.refs_0_.refs_1_.refs_2_, ...), custom_call_target="tpu_custom_call" | custom-call | flops 2359296 | bytes 14155776 | tf_op jit(solution)/shard_map/split_cores/pallas_call | solution.py:860
  258.8 1.5 collective-permute-start.23
  261.2 1.7 copy-done.7
  262.9 1.7 copy-done.11
  264.5 7.6 %token_backward.2 = (f32[800,768]{1,0:T(8,128)S(1)}, f32[2,768]{1,0:T(2,128)S(1)}, f32[384,200]{1,0:T(8,128)S(1)}, f32[384,200]{1,0:T(8,128)S(1)}) custom-call(f32[800,768]{1,0:T(8,128)S(1)} %copy-done.7, f32[800,768]{1,0:T(8,128)S(1)} %get-tuple-element.327.state, f32[4,768]{1,0:T(4,128)S(1)} %get-tuple-element.590.gains, ...), custom_call_target="tpu_custom_call" | custom-call | flops 1887436800 | bytes 9830400 | tf_op jit(solution)/shard_map/token_backward/pallas_call | solution.py:456
  275.1 17.2 %channel_backward.6 = (bf16[2,2,768,768]{3,2,1,0:T(8,128)(2,1)}, f32[800,768]{1,0:T(8,128)}, f32[2,768]{1,0:T(2,128)}) custom-call(f32[800,768]{1,0:T(8,128)} %copy-done.59, f32[800,768]{1,0:T(8,128)} %copy-done.60, f32[4,768]{1,0:T(4,128)S(1)} %get-tuple-element.591.gains, bf16[800,3072]{1,0:T(8,128)(2,1)} %get-tuple-element.357.inner, ...), custom_call_target="tpu_custom_call" | custom-call | flops 7549747200 | bytes 11894784 | tf_op jit(solution)/shard_map/channel_backward/pallas_call | solution.py:260
  292.3 3.4 collective-permute-done.23.refs_3_
  295.7 3.1 fold_all.8
  299.7 1.5 collective-permute-start.25
  302.6 18.9 %channel_backward.7 = (bf16[2,2,768,768]{3,2,1,0:T(8,128)(2,1)}, f32[800,768]{1,0:T(8,128)}, f32[2,768]{1,0:T(2,128)S(1)}) custom-call(f32[800,768]{1,0:T(8,128)} %copy-done.59, f32[800,768]{1,0:T(8,128)} %copy-done.60, f32[4,768]{1,0:T(4,128)S(1)} %get-tuple-element.591.gains, bf16[800,3072]{1,0:T(8,128)(2,1)} %get-tuple-element.357.inner, ...), custom_call_target="tpu_custom_call" | custom-call | flops 7549747200 | bytes 11894784 | tf_op jit(solution)/shard_map/channel_backward/pallas_call | solution.py:260
  321.5 6.7 %split_cores.3 = (bf16[2,384,768]{2,1,0:T(8,128)(2,1)}, bf16[2,384,768]{2,1,0:T(8,128)(2,1)}, bf16[768,768]{1,0:T(8,128)(2,1)}, bf16[768,768]{1,0:T(8,128)(2,1)}) custom-call(bf16[2,2,768,768]{3,2,1,0:T(8,128)(2,1)} %get-tuple-element.377.refs_0_.refs_1_.refs_2_, bf16[2,2,768,768]{3,2,1,0:T(8,128)(2,1)} %get-tuple-element.377.refs_0_.refs_1_.refs_2_, ...), custom_call_target="tpu_custom_call" | custom-call | flops 2359296 | bytes 14155776 | tf_op jit(solution)/shard_map/split_cores/pallas_call | solution.py:860
  329.4 2.2 fold_all.9
  335.7 1.9 collective-permute-start.27
  338.7 1.7 copy-done.5
  340.3 1.7 copy-done.9
  342.0 7.0 %token_backward.3 = (f32[800,768]{1,0:T(8,128)S(1)}, f32[2,768]{1,0:T(2,128)S(1)}, f32[384,200]{1,0:T(8,128)S(1)}, f32[384,200]{1,0:T(8,128)S(1)}) custom-call(f32[800,768]{1,0:T(8,128)S(1)} %copy-done.5, f32[800,768]{1,0:T(8,128)S(1)} %copy-done.4, f32[4,768]{1,0:T(4,128)S(1)} %get-tuple-element.591.gains, bf16[4,384,768]{2,1,0:T(8,128)(2,1)S(1)} %copy-done.9, ...), custom_call_target="tpu_custom_call" | custom-call | flops 1887436800 | bytes 9830400 | tf_op jit(solution)/shard_map/token_backward/pallas_call | solution.py:456
  349.1 1.8 stem_backward.1
  351.0 2.0 gather_misc.1
  353.1 8.1 %collective-permute-done.29.refs_5_ = bf16[2,384,768]{2,1,0:T(8,128)(2,1)} collective-permute-done((bf16[2,384,768]{2,1,0:T(8,128)(2,1)}, bf16[2,384,768]{2,1,0:T(8,128)(2,1)}, u32[]{:S(2)}, u32[]{:S(2)}) %collective-permute-start.29) | collective-permute-done | bytes 1179680 | tf_op jit(solution)/shard_map/ppermute | solution.py:744
  361.5 2.4 fold_all.10
  364.0 2.9 collective-permute-done.35.refs_1_
  367.2 1.5 collective-permute-start.36
  371.4 1.9 collective-permute-start.32
  373.3 12.8 %collective-permute-done.32.refs_3_ = bf16[96,1024]{1,0:T(8,128)(2,1)S(1)} collective-permute-done((bf16[96,1024]{1,0:T(8,128)(2,1)S(1)}, bf16[96,1024]{1,0:T(8,128)(2,1)S(1)}, u32[]{:S(2)}, u32[]{:S(2)}) %collective-permute-start.32) | collective-permute-done | bytes 196640 | tf_op jit(solution)/shard_map/ppermute | solution.py:744
  386.1 3.6 collective-permute-done.31.refs_1_
  395.2 2.3 collective-permute-done.40.rest_3_.rest_7_
  397.6 4.1 collective-permute-done.39.rest_2_.rest_6_
  403.2 6.3 %collective-permute-done.41.refs_1_ = bf16[2,96,768]{2,1,0:T(8,128)(2,1)S(1)} collective-permute-done((bf16[2,96,768]{2,1,0:T(8,128)(2,1)S(1)}, bf16[2,96,768]{2,1,0:T(8,128)(2,1)S(1)}, u32[]{:S(2)}, u32[]{:S(2)}) %collective-permute-start.41) | collective-permute-done | bytes 294944 | tf_op jit(solution)/shard_map/ppermute | solution.py:744
  410.7 2.2 collective-permute-start.45
  413.0 9.3 %channel_step.2 = (f32[2,2,96,3072]{3,2,1,0:T(8,128)}, f32[2,2,96,3072]{3,2,1,0:T(8,128)}, f32[2,2,96,3072]{3,2,1,0:T(8,128)}, f32[2,2]{1,0:T(2,128)}) custom-call(s32[1]{0:T(128)} %bitcast.3.device.rest_1_.rest_2_, f32[2,2,96,3072]{3,2,1,0:T(8,128)} %weight.5, f32[2,2,96,3072]{3,2,1,0:T(8,128)} %mean.3, f32[2,2,96,3072]{3,2,1,0:T(8,128)} %power.3, ...), custom_call_target="tpu_custom_call" | custom-call | flops 5898240 | bytes 15335424 | tf_op jit(solution)/shard_map/channel_step/pallas_call | solution.py:335
  426.0 3.9 collective-permute-done.50.rest_3_
  430.0 3.5 collective-permute-done.49.rest_2_
  433.5 5.4 %collective-permute-done.51.refs_1_ = bf16[544,256]{1,0:T(8,128)(2,1)S(1)} collective-permute-done((bf16[544,256]{1,0:T(8,128)(2,1)S(1)}, bf16[544,256]{1,0:T(8,128)(2,1)S(1)}, u32[]{:S(2)}, u32[]{:S(2)}) %collective-permute-start.51) | collective-permute-done | bytes 278560 | tf_op jit(solution)/shard_map/ppermute | solution.py:744
  441.0 9.6 %channel_step.3 = (f32[2,2,96,3072]{3,2,1,0:T(8,128)}, f32[2,2,96,3072]{3,2,1,0:T(8,128)}, f32[2,2,96,3072]{3,2,1,0:T(8,128)}, f32[2,2]{1,0:T(2,128)}) custom-call(s32[1]{0:T(128)} %bitcast.3.device.rest_1_.rest_2_, f32[2,2,96,3072]{3,2,1,0:T(8,128)} %weight.5, ...), custom_call_target="tpu_custom_call", output_to_operand_aliasing={{0}: (10, {}), {1}: (11, {}), {2}: (12, {})} | custom-call | flops 5898240 | bytes 15335424 | tf_op jit(solution)/shard_map/channel_step/pallas_call | solution.py:335
  452.0 2.4 ends_step.1
  454.4 2.2 collective-permute-start.57
  459.9 2.4 multiply_reduce_fusion
  464.1 1.9 pad_maximum_fusion.13
  466.6 4.0 collective-permute-done.59
  471.5 7.2 %channel_renew.1 = (f32[2,2,96,3072]{3,2,1,0:T(8,128)}, bf16[2,2,96,3072]{3,2,1,0:T(8,128)(2,1)}) custom-call(f32[8,128]{1,0:T(8,128)} %copy-done.85, f32[2,2,96,3072]{3,2,1,0:T(8,128)} %weight.5, f32[2,2,96,3072]{3,2,1,0:T(8,128)} %get-tuple-element.540.update), custom_call_target="tpu_custom_call" | custom-call | flops 3538944 | bytes 16515072 | tf_op jit(solution)/shard_map/channel_renew/pallas_call | solution.py:409
  (382 shorter events, 82.1 us)
Async XLA Ops:
  7.2 146.1 %all-gather.6.cloned.1.call-start = ((), (), s32[]{:S(2)}) async-start(), calls=%async_computation.1 | async-start | bytes 2838528 | tf_op jit(solution)/shard_map/all_gather | solution.py:1043
  9.9 186.7 %all-gather.4.cloned.1.call-start = ((), (), s32[]{:S(2)}) async-start(), calls=%async_computation | async-start | bytes 9732096 | tf_op jit(solution)/shard_map/all_gather | solution.py:1047
  12.2 33.0 %collective-permute-start = (bf16[192,768]{1,0:T(8,128)(2,1)S(1)}, bf16[192,768]{1,0:T(8,128)(2,1)S(1)}, u32[]{:S(2)}, u32[]{:S(2)}) collective-permute-start(bf16[192,768]{1,0:T(8,128)(2,1)S(1)} %pad_maximum_fusion.6), channel_id=1, source_target_pairs={{0,16},{4,20},{8,24},{12,28},{16,0},{20,4},{24,8},{28,12},{1,17},{... | collective-permute-start | bytes 884744 | tf_op jit(solution)/shard_map/ppermute | solution.py:744
  17.7 39.7 %collective-permute-start.1 = (bf16[49,8,768]{2,1,0:T(8,128)(2,1)S(1)}, bf16[49,8,768]{2,1,0:T(8,128)(2,1)S(1)}, u32[]{:S(2)}, u32[]{:S(2)}) collective-permute-start(bf16[49,8,768]{2,1,0:T(8,128)(2,1)S(1)} %get-tuple-element.568.own), channel_id=1, source_target_pairs={{0,16},{4,20},{8,24},{12,28},{16,0},{20,4},{24,8},{28,12},{1,17},{... | collective-permute-start | bytes 1806344 | tf_op jit(solution)/shard_map/ppermute | solution.py:744
  58.2 26.2 %collective-permute-start.2 = (bf16[384,768]{1,0:T(8,128)(2,1)}, bf16[384,768]{1,0:T(8,128)(2,1)}, u32[]{:S(2)}, u32[]{:S(2)}) collective-permute-start(bf16[384,768]{1,0:T(8,128)(2,1)} %pad_maximum_fusion.2), channel_id=1, source_target_pairs={{0,8},{4,12},{8,0},{12,4},{16,24},{20,28},{24,16},{28,20},{1,9},{5... | collective-permute-start | bytes 1769480 | tf_op jit(solution)/shard_map/ppermute | solution.py:744
  61.1 4.2 collective-permute-start.3
  61.1 8.5 %collective-permute-start.4 = (bf16[98,768]{1,0:T(8,128)(2,1)S(1)}, bf16[98,768]{1,0:T(8,128)(2,1)S(1)}, u32[]{:S(2)}, u32[]{:S(2)}) collective-permute-start(bf16[98,768]{1,0:T(8,128)(2,1)S(1)} %get-tuple-element.292), channel_id=1, source_target_pairs={{0,2},{1,3},{2,0},{3,1},{4,6},{5,7},{6,4},{7,5},{8,10},{9,11},{10,... | collective-permute-start | bytes 451592 | tf_op jit(solution)/shard_map/ppermute | solution.py:744
  62.6 10.3 %collective-permute-start.5 = (bf16[98,768]{1,0:T(8,128)(2,1)S(1)}, bf16[98,768]{1,0:T(8,128)(2,1)}, u32[]{:S(2)}, u32[]{:S(2)}) collective-permute-start(bf16[98,768]{1,0:T(8,128)(2,1)S(1)} %get-tuple-element.293), channel_id=1, source_target_pairs={{0,3},{1,2},{2,1},{3,0},{4,7},{5,6},{6,5},{7,4},{8,11},{9,10},{10,... | collective-permute-start | bytes 451592 | tf_op jit(solution)/shard_map/ppermute | solution.py:744
  63.0 14.2 %collective-permute-start.6 = (bf16[2,2,96,196]{3,2,1,0:T(8,128)(2,1)S(1)}, bf16[2,2,96,196]{3,2,1,0:T(8,128)(2,1)S(1)}, u32[]{:S(2)}, u32[]{:S(2)}) collective-permute-start(bf16[2,2,96,196]{3,2,1,0:T(8,128)(2,1)S(1)} %bitcast_convert_fusion), channel_id=1, source_target_pairs={{0,2},{1,3},{2,0},{3,1},{4,6},{5,7},{6,4},{7,5},{8,10},{9,11},{10,... | collective-permute-start | bytes 451592 | tf_op jit(solution)/shard_map/ppermute | solution.py:744
  65.2 85.3 %copy-start.43 = (f32[11,768]{1,0:T(8,128)}, f32[11,768]{1,0:T(8,128)S(1)}, u32[]{:S(2)}) copy-start(f32[11,768]{1,0:T(8,128)S(1)} %relative_vectors.1.rest_9_) | copy-start | bytes 101380
  65.3 39.4 %collective-permute-start.9 = (bf16[49,8,768]{2,1,0:T(8,128)(2,1)S(1)}, bf16[49,8,768]{2,1,0:T(8,128)(2,1)S(1)}, u32[]{:S(2)}, u32[]{:S(2)}) collective-permute-start(bf16[49,8,768]{2,1,0:T(8,128)(2,1)S(1)} %get-tuple-element.302.own), channel_id=1, source_target_pairs={{0,16},{4,20},{8,24},{12,28},{16,0},{20,4},{24,8},{28,12},{1,17},{... | collective-permute-start | bytes 1806344 | tf_op jit(solution)/shard_map/ppermute | solution.py:744
  84.5 5.0 %collective-permute-start.10 = (bf16[2,2,192,196]{3,2,1,0:T(8,128)(2,1)S(1)}, bf16[2,2,192,196]{3,2,1,0:T(8,128)(2,1)S(1)}, u32[]{:S(2)}, u32[]{:S(2)}) collective-permute-start(bf16[2,2,192,196]{3,2,1,0:T(8,128)(2,1)S(1)} %pad_maximum_fusion.5), channel_id=1, source_target_pairs={{0,1},{1,0},{2,3},{3,2},{4,5},{5,4},{6,7},{7,6},{8,9},{9,8},{10,11... | collective-permute-start | bytes 903176 | tf_op jit(solution)/shard_map/ppermute | solution.py:744
  85.8 19.3 %collective-permute-start.7 = (bf16[384,768]{1,0:T(8,128)(2,1)S(1)}, bf16[384,768]{1,0:T(8,128)(2,1)S(1)}, u32[]{:S(2)}, u32[]{:S(2)}) collective-permute-start(bf16[384,768]{1,0:T(8,128)(2,1)S(1)} %pad_maximum_fusion.3), channel_id=1, source_target_pairs={{0,4},{4,0},{8,12},{12,8},{16,20},{20,16},{24,28},{28,24},{1,5},{5... | collective-permute-start | bytes 1769480 | tf_op jit(solution)/shard_map/ppermute | solution.py:744
  87.1 18.0 %collective-permute-start.8 = (bf16[384,768]{1,0:T(8,128)(2,1)S(1)}, bf16[384,768]{1,0:T(8,128)(2,1)S(1)}, u32[]{:S(2)}, u32[]{:S(2)}) collective-permute-start(bf16[384,768]{1,0:T(8,128)(2,1)S(1)} %pad_maximum_fusion.4), channel_id=1, source_target_pairs={{0,2},{1,3},{2,0},{3,1},{4,6},{5,7},{6,4},{7,5},{8,10},{9,11},{10,... | collective-permute-start | bytes 1769480 | tf_op jit(solution)/shard_map/ppermute | solution.py:744
  105.3 42.2 %collective-permute-start.12 = (bf16[2,384,768]{2,1,0:T(8,128)(2,1)S(1)}, bf16[2,384,768]{2,1,0:T(8,128)(2,1)}, u32[]{:S(2)}, u32[]{:S(2)}) collective-permute-start(bf16[2,384,768]{2,1,0:T(8,128)(2,1)S(1)} %pad_maximum_fusion.1.rest_4_.rest_5_), channel_id=1, source_target_pairs={{0,4},{4,0},{8,12},{12,8},{16,20},{20,16},{24,28},{28,24},{1,5},{5... | collective-permute-start | bytes 3538952 | tf_op jit(solution)/shard_map/ppermute | solution.py:744
  106.9 40.6 %collective-permute-start.11 = (bf16[2,384,768]{2,1,0:T(8,128)(2,1)S(1)}, bf16[2,384,768]{2,1,0:T(8,128)(2,1)}, u32[]{:S(2)}, u32[]{:S(2)}) collective-permute-start(bf16[2,384,768]{2,1,0:T(8,128)(2,1)S(1)} %pad_maximum_fusion.rest_0_.rest_1_), channel_id=1, source_target_pairs={{0,2},{1,3},{2,0},{3,1},{4,6},{5,7},{6,4},{7,5},{8,10},{9,11},{10,... | collective-permute-start | bytes 3538952 | tf_op jit(solution)/shard_map/ppermute | solution.py:744
  109.5 1.9 collective-permute-start.13
  109.5 34.1 %collective-permute-start.14 = (bf16[98,768]{1,0:T(8,128)(2,1)S(1)}, bf16[98,768]{1,0:T(8,128)(2,1)S(1)}, u32[]{:S(2)}, u32[]{:S(2)}) collective-permute-start(bf16[98,768]{1,0:T(8,128)(2,1)S(1)} %get-tuple-element.312), channel_id=1, source_target_pairs={{0,2},{1,3},{2,0},{3,1},{4,6},{5,7},{6,4},{7,5},{8,10},{9,11},{10,... | collective-permute-start | bytes 451592 | tf_op jit(solution)/shard_map/ppermute | solution.py:744
  110.9 36.6 %collective-permute-start.15 = (bf16[98,768]{1,0:T(8,128)(2,1)S(1)}, bf16[98,768]{1,0:T(8,128)(2,1)S(1)}, u32[]{:S(2)}, u32[]{:S(2)}) collective-permute-start(bf16[98,768]{1,0:T(8,128)(2,1)S(1)} %get-tuple-element.313), channel_id=1, source_target_pairs={{0,3},{1,2},{2,1},{3,0},{4,7},{5,6},{6,5},{7,4},{8,11},{9,10},{10,... | collective-permute-start | bytes 451592 | tf_op jit(solution)/shard_map/ppermute | solution.py:744
  147.5 19.0 %collective-permute-start.16 = (bf16[2,384,768]{2,1,0:T(8,128)(2,1)S(1)}, bf16[2,384,768]{2,1,0:T(8,128)(2,1)}, u32[]{:S(2)}, u32[]{:S(2)}) collective-permute-start(bf16[2,384,768]{2,1,0:T(8,128)(2,1)S(1)} %pad_maximum_fusion.rest_0_.rest_1_), channel_id=1, source_target_pairs={{0,1},{1,0},{2,3},{3,2},{4,5},{5,4},{6,7},{7,6},{8,9},{9,8},{10,11... | collective-permute-start | bytes 3538952 | tf_op jit(solution)/shard_map/ppermute | solution.py:744
  149.4 17.1 %collective-permute-start.17 = (bf16[2,384,768]{2,1,0:T(8,128)(2,1)}, bf16[2,384,768]{2,1,0:T(8,128)(2,1)}, u32[]{:S(2)}, u32[]{:S(2)}) collective-permute-start(bf16[2,384,768]{2,1,0:T(8,128)(2,1)} %collective-permute-done.11.rest_1_.rest_2_), channel_id=1, source_target_pairs={{0,1},{1,0},{2,3},{3,2},{4,5},{5,4},{6,7},{7,6},{8,9},{9,8},{10,11... | collective-permute-start | bytes 3538952 | tf_op jit(solution)/shard_map/ppermute | solution.py:744
  149.5 17.0 %collective-permute-start.18 = (bf16[2,384,768]{2,1,0:T(8,128)(2,1)S(1)}, bf16[2,384,768]{2,1,0:T(8,128)(2,1)}, u32[]{:S(2)}, u32[]{:S(2)}) collective-permute-start(bf16[2,384,768]{2,1,0:T(8,128)(2,1)S(1)} %pad_maximum_fusion.1.rest_4_.rest_5_), channel_id=1, source_target_pairs={{0,1},{1,0},{2,3},{3,2},{4,5},{5,4},{6,7},{7,6},{8,9},{9,8},{10,11... | collective-permute-start | bytes 3538952 | tf_op jit(solution)/shard_map/ppermute | solution.py:744
  149.9 16.6 %collective-permute-start.19 = (bf16[2,384,768]{2,1,0:T(8,128)(2,1)}, bf16[2,384,768]{2,1,0:T(8,128)(2,1)}, u32[]{:S(2)}, u32[]{:S(2)}) collective-permute-start(bf16[2,384,768]{2,1,0:T(8,128)(2,1)} %collective-permute-done.12.rest_5_.rest_6_), channel_id=1, source_target_pairs={{0,1},{1,0},{2,3},{3,2},{4,5},{5,4},{6,7},{7,6},{8,9},{9,8},{10,11... | collective-permute-start | bytes 3538952 | tf_op jit(solution)/shard_map/ppermute | solution.py:744
  231.6 19.1 %collective-permute-start.20 = (bf16[2,2,768,768]{3,2,1,0:T(8,128)(2,1)}, bf16[2,2,768,768]{3,2,1,0:T(8,128)(2,1)}, u32[]{:S(2)}, u32[]{:S(2)}) collective-permute-start(bf16[2,2,768,768]{3,2,1,0:T(8,128)(2,1)} %get-tuple-element.341), channel_id=1, source_target_pairs={{0,1},{1,0},{2,3},{3,2},{4,5},{5,4},{6,7},{7,6},{8,9},{9,8},{10,11... | collective-permute-start | bytes 14155784 | tf_op jit(solution)/shard_map/ppermute | solution.py:744
  232.9 17.8 %collective-permute-start.21 = (bf16[2,768,256]{2,1,0:T(8,128)(2,1)S(1)}, bf16[2,768,256]{2,1,0:T(8,128)(2,1)S(1)}, u32[]{:S(2)}, u32[]{:S(2)}) collective-permute-start(bf16[2,768,256]{2,1,0:T(8,128)(2,1)S(1)} %get-tuple-element.566), channel_id=1, source_target_pairs={{0,1},{1,0},{2,3},{3,2},{4,5},{5,4},{6,7},{7,6},{8,9},{9,8},{10,11... | collective-permute-start | bytes 2359304 | tf_op jit(solution)/shard_map/ppermute | solution.py:744
  258.8 36.9 %collective-permute-start.23 = (bf16[768,1024]{1,0:T(8,128)(2,1)}, bf16[768,1024]{1,0:T(8,128)(2,1)}, u32[]{:S(2)}, u32[]{:S(2)}) collective-permute-start(bf16[768,1024]{1,0:T(8,128)(2,1)} %get-tuple-element.351), channel_id=1, source_target_pairs={{0,2},{1,3},{2,0},{3,1},{4,6},{5,7},{6,4},{7,5},{8,10},{9,11},{10,... | collective-permute-start | bytes 4718600 | tf_op jit(solution)/shard_map/ppermute | solution.py:744
  260.3 32.0 %collective-permute-start.22 = (bf16[2,384,768]{2,1,0:T(8,128)(2,1)}, bf16[2,384,768]{2,1,0:T(8,128)(2,1)}, u32[]{:S(2)}, u32[]{:S(2)}) collective-permute-start(bf16[2,384,768]{2,1,0:T(8,128)(2,1)} %get-tuple-element.349), channel_id=1, source_target_pairs={{0,4},{4,0},{8,12},{12,8},{16,20},{20,16},{24,28},{28,24},{1,5},{5... | collective-permute-start | bytes 3538952 | tf_op jit(solution)/shard_map/ppermute | solution.py:744
  299.7 21.8 %collective-permute-start.26 = (bf16[2,2,768,768]{3,2,1,0:T(8,128)(2,1)S(1)}, bf16[2,2,768,768]{3,2,1,0:T(8,128)(2,1)}, u32[]{:S(2)}, u32[]{:S(2)}) collective-permute-start(bf16[2,2,768,768]{3,2,1,0:T(8,128)(2,1)S(1)} %copy-done.95), channel_id=1, source_target_pairs={{0,1},{1,0},{2,3},{3,2},{4,5},{5,4},{6,7},{7,6},{8,9},{9,8},{10,11... | collective-permute-start | bytes 14155784 | tf_op jit(solution)/shard_map/ppermute | solution.py:744
  299.7 28.5 %collective-permute-start.25 = (bf16[384,1024]{1,0:T(8,128)(2,1)}, bf16[384,1024]{1,0:T(8,128)(2,1)}, u32[]{:S(2)}, u32[]{:S(2)}) collective-permute-start(bf16[384,1024]{1,0:T(8,128)(2,1)} %get-tuple-element.374), channel_id=1, source_target_pairs={{0,4},{4,0},{8,12},{12,8},{16,20},{20,16},{24,28},{28,24},{1,5},{5... | collective-permute-start | bytes 2359304 | tf_op jit(solution)/shard_map/ppermute | solution.py:744
  301.2 27.0 %collective-permute-start.24 = (bf16[2,192,768]{2,1,0:T(8,128)(2,1)}, bf16[2,192,768]{2,1,0:T(8,128)(2,1)}, u32[]{:S(2)}, u32[]{:S(2)}) collective-permute-start(bf16[2,192,768]{2,1,0:T(8,128)(2,1)} %get-tuple-element.372), channel_id=1, source_target_pairs={{0,8},{4,12},{8,0},{12,4},{16,24},{20,28},{24,16},{28,20},{1,9},{5... | collective-permute-start | bytes 1769480 | tf_op jit(solution)/shard_map/ppermute | solution.py:744
  333.1 28.1 %collective-permute-start.29 = (bf16[2,384,768]{2,1,0:T(8,128)(2,1)}, bf16[2,384,768]{2,1,0:T(8,128)(2,1)}, u32[]{:S(2)}, u32[]{:S(2)}) collective-permute-start(bf16[2,384,768]{2,1,0:T(8,128)(2,1)} %get-tuple-element.402), channel_id=1, source_target_pairs={{0,4},{4,0},{8,12},{12,8},{16,20},{20,16},{24,28},{28,24},{1,5},{5... | collective-permute-start | bytes 3538952 | tf_op jit(solution)/shard_map/ppermute | solution.py:744
  333.7 27.9 %collective-permute-start.30 = (bf16[768,768]{1,0:T(8,128)(2,1)}, bf16[768,768]{1,0:T(8,128)(2,1)}, u32[]{:S(2)}, u32[]{:S(2)}) collective-permute-start(bf16[768,768]{1,0:T(8,128)(2,1)} %get-tuple-element.404), channel_id=1, source_target_pairs={{0,2},{1,3},{2,0},{3,1},{4,6},{5,7},{6,4},{7,5},{8,10},{9,11},{10,... | collective-permute-start | bytes 3538952 | tf_op jit(solution)/shard_map/ppermute | solution.py:744
  335.1 18.0 %collective-permute-start.28 = (bf16[192,1024]{1,0:T(8,128)(2,1)}, bf16[192,1024]{1,0:T(8,128)(2,1)S(1)}, u32[]{:S(2)}, u32[]{:S(2)}) collective-permute-start(bf16[192,1024]{1,0:T(8,128)(2,1)} %get-tuple-element.400), channel_id=1, source_target_pairs={{0,8},{4,12},{8,0},{12,4},{16,24},{20,28},{24,16},{28,20},{1,9},{5... | collective-permute-start | bytes 1179656 | tf_op jit(solution)/shard_map/ppermute | solution.py:744
  335.7 17.4 %collective-permute-start.27 = (bf16[2,96,768]{2,1,0:T(8,128)(2,1)}, bf16[2,96,768]{2,1,0:T(8,128)(2,1)}, u32[]{:S(2)}, u32[]{:S(2)}) collective-permute-start(bf16[2,96,768]{2,1,0:T(8,128)(2,1)} %get-tuple-element.398), channel_id=1, source_target_pairs={{0,16},{4,20},{8,24},{12,28},{16,0},{20,4},{24,8},{28,12},{1,17},{... | collective-permute-start | bytes 884744 | tf_op jit(solution)/shard_map/ppermute | solution.py:744
  363.9 3.0 collective-permute-start.35
  367.2 22.5 %collective-permute-start.36 = (bf16[1216,256]{1,0:T(8,128)(2,1)S(1)}, bf16[1216,256]{1,0:T(8,128)(2,1)S(1)}, u32[]{:S(2)}, u32[]{:S(2)}) collective-permute-start(bf16[1216,256]{1,0:T(8,128)(2,1)S(1)} %get-tuple-element.453), channel_id=1, source_target_pairs={{0,2},{1,3},{2,0},{3,1},{4,6},{5,7},{6,4},{7,5},{8,10},{9,11},{10,... | collective-permute-start | bytes 1867784 | tf_op jit(solution)/shard_map/ppermute | solution.py:744
  368.7 21.0 %collective-permute-start.33 = (bf16[2,192,768]{2,1,0:T(8,128)(2,1)S(1)}, bf16[2,192,768]{2,1,0:T(8,128)(2,1)S(1)}, u32[]{:S(2)}, u32[]{:S(2)}) collective-permute-start(bf16[2,192,768]{2,1,0:T(8,128)(2,1)S(1)} %get-tuple-element.447), channel_id=1, source_target_pairs={{0,8},{4,12},{8,0},{12,4},{16,24},{20,28},{24,16},{28,20},{1,9},{5... | collective-permute-start | bytes 1769480 | tf_op jit(solution)/shard_map/ppermute | solution.py:744
  369.3 20.4 %collective-permute-start.34 = (bf16[384,768]{1,0:T(8,128)(2,1)S(1)}, bf16[384,768]{1,0:T(8,128)(2,1)S(1)}, u32[]{:S(2)}, u32[]{:S(2)}) collective-permute-start(bf16[384,768]{1,0:T(8,128)(2,1)S(1)} %get-tuple-element.449), channel_id=1, source_target_pairs={{0,4},{4,0},{8,12},{12,8},{16,20},{20,16},{24,28},{28,24},{1,5},{5... | collective-permute-start | bytes 1769480 | tf_op jit(solution)/shard_map/ppermute | solution.py:744
  370.0 19.6 %collective-permute-start.31 = (bf16[2,96,768]{2,1,0:T(8,128)(2,1)S(1)}, bf16[2,96,768]{2,1,0:T(8,128)(2,1)S(1)}, u32[]{:S(2)}, u32[]{:S(2)}) collective-permute-start(bf16[2,96,768]{2,1,0:T(8,128)(2,1)S(1)} %get-tuple-element.454.refs_0_), channel_id=1, source_target_pairs={{0,2},{1,3},{2,0},{3,1},{4,6},{5,7},{6,4},{7,5},{8,10},{9,11},{10,... | collective-permute-start | bytes 884744 | tf_op jit(solution)/shard_map/ppermute | solution.py:744
  371.4 14.7 %collective-permute-start.32 = (bf16[96,1024]{1,0:T(8,128)(2,1)S(1)}, bf16[96,1024]{1,0:T(8,128)(2,1)S(1)}, u32[]{:S(2)}, u32[]{:S(2)}) collective-permute-start(bf16[96,1024]{1,0:T(8,128)(2,1)S(1)} %get-tuple-element.445), channel_id=1, source_target_pairs={{0,16},{4,20},{8,24},{12,28},{16,0},{20,4},{24,8},{28,12},{1,17},{... | collective-permute-start | bytes 589832 | tf_op jit(solution)/shard_map/ppermute | solution.py:744
  390.3 7.3 %collective-permute-start.40 = (bf16[96,1024]{1,0:T(8,128)(2,1)S(1)}, bf16[96,1024]{1,0:T(8,128)(2,1)S(1)}, u32[]{:S(2)}, u32[]{:S(2)}) collective-permute-start(bf16[96,1024]{1,0:T(8,128)(2,1)S(1)} %get-tuple-element.493.rest_0_.rest_4_), channel_id=1, source_target_pairs={{0,3},{1,2},{2,1},{3,0},{4,7},{5,6},{6,5},{7,4},{8,11},{9,10},{10,... | collective-permute-start | bytes 589832 | tf_op jit(solution)/shard_map/ppermute | solution.py:744
  390.7 18.8 %collective-permute-start.43 = (bf16[832,256]{1,0:T(8,128)(2,1)S(1)}, bf16[832,256]{1,0:T(8,128)(2,1)S(1)}, u32[]{:S(2)}, u32[]{:S(2)}) collective-permute-start(bf16[832,256]{1,0:T(8,128)(2,1)S(1)} %get-tuple-element.479), channel_id=1, source_target_pairs={{0,4},{4,0},{8,12},{12,8},{16,20},{20,16},{24,28},{28,24},{1,5},{5... | collective-permute-start | bytes 1277960 | tf_op jit(solution)/shard_map/ppermute | solution.py:744
  391.9 9.9 %collective-permute-start.39 = (bf16[96,1024]{1,0:T(8,128)(2,1)S(1)}, bf16[96,1024]{1,0:T(8,128)(2,1)S(1)}, u32[]{:S(2)}, u32[]{:S(2)}) collective-permute-start(bf16[96,1024]{1,0:T(8,128)(2,1)S(1)} %get-tuple-element.493.rest_0_.rest_4_), channel_id=1, source_target_pairs={{0,2},{1,3},{2,0},{3,1},{4,6},{5,7},{6,4},{7,5},{8,10},{9,11},{10,... | collective-permute-start | bytes 589832 | tf_op jit(solution)/shard_map/ppermute | solution.py:744
  392.7 16.8 %collective-permute-start.41 = (bf16[2,96,768]{2,1,0:T(8,128)(2,1)S(1)}, bf16[2,96,768]{2,1,0:T(8,128)(2,1)S(1)}, u32[]{:S(2)}, u32[]{:S(2)}) collective-permute-start(bf16[2,96,768]{2,1,0:T(8,128)(2,1)S(1)} %get-tuple-element.475), channel_id=1, source_target_pairs={{0,16},{4,20},{8,24},{12,28},{16,0},{20,4},{24,8},{28,12},{1,17},{... | collective-permute-start | bytes 884744 | tf_op jit(solution)/shard_map/ppermute | solution.py:744
  393.8 15.7 %collective-permute-start.42 = (bf16[192,768]{1,0:T(8,128)(2,1)S(1)}, bf16[192,768]{1,0:T(8,128)(2,1)S(1)}, u32[]{:S(2)}, u32[]{:S(2)}) collective-permute-start(bf16[192,768]{1,0:T(8,128)(2,1)S(1)} %get-tuple-element.477), channel_id=1, source_target_pairs={{0,8},{4,12},{8,0},{12,4},{16,24},{20,28},{24,16},{28,20},{1,9},{5... | collective-permute-start | bytes 884744 | tf_op jit(solution)/shard_map/ppermute | solution.py:744
  397.5 12.0 %collective-permute-start.37 = (bf16[2,96,768]{2,1,0:T(8,128)(2,1)S(1)}, bf16[2,96,768]{2,1,0:T(8,128)(2,1)S(1)}, u32[]{:S(2)}, u32[]{:S(2)}) collective-permute-start(bf16[2,96,768]{2,1,0:T(8,128)(2,1)S(1)} %get-tuple-element.491.near), channel_id=1, source_target_pairs={{0,1},{1,0},{2,3},{3,2},{4,5},{5,4},{6,7},{7,6},{8,9},{9,8},{10,11... | collective-permute-start | bytes 884744 | tf_op jit(solution)/shard_map/ppermute | solution.py:744
  401.7 1.4 collective-permute-start.38
  409.8 12.8 %collective-permute-start.46 = (bf16[640,256]{1,0:T(8,128)(2,1)S(1)}, bf16[640,256]{1,0:T(8,128)(2,1)S(1)}, u32[]{:S(2)}, u32[]{:S(2)}) collective-permute-start(bf16[640,256]{1,0:T(8,128)(2,1)S(1)} %get-tuple-element.490), channel_id=1, source_target_pairs={{0,8},{4,12},{8,0},{12,4},{16,24},{20,28},{24,16},{28,20},{1,9},{5... | collective-permute-start | bytes 983048 | tf_op jit(solution)/shard_map/ppermute | solution.py:744
  410.0 12.3 %collective-permute-start.44 = (bf16[2,96,768]{2,1,0:T(8,128)(2,1)S(1)}, bf16[2,96,768]{2,1,0:T(8,128)(2,1)S(1)}, u32[]{:S(2)}, u32[]{:S(2)}) collective-permute-start(bf16[2,96,768]{2,1,0:T(8,128)(2,1)S(1)} %get-tuple-element.503.refs_0_), channel_id=1, source_target_pairs={{0,2},{1,3},{2,0},{3,1},{4,6},{5,7},{6,4},{7,5},{8,10},{9,11},{10,... | collective-permute-start | bytes 884744 | tf_op jit(solution)/shard_map/ppermute | solution.py:744
  410.7 11.6 %collective-permute-start.45 = (bf16[96,768]{1,0:T(8,128)(2,1)S(1)}, bf16[96,768]{1,0:T(8,128)(2,1)S(1)}, u32[]{:S(2)}, u32[]{:S(2)}) collective-permute-start(bf16[96,768]{1,0:T(8,128)(2,1)S(1)} %get-tuple-element.488), channel_id=1, source_target_pairs={{0,16},{4,20},{8,24},{12,28},{16,0},{20,4},{24,8},{28,12},{1,17},{... | collective-permute-start | bytes 442376 | tf_op jit(solution)/shard_map/ppermute | solution.py:744
  422.8 16.0 %collective-permute-start.47 = (bf16[2,96,768]{2,1,0:T(8,128)(2,1)S(1)}, bf16[2,96,768]{2,1,0:T(8,128)(2,1)S(1)}, u32[]{:S(2)}, u32[]{:S(2)}) collective-permute-start(bf16[2,96,768]{2,1,0:T(8,128)(2,1)S(1)} %get-tuple-element.520.near), channel_id=1, source_target_pairs={{0,1},{1,0},{2,3},{3,2},{4,5},{5,4},{6,7},{7,6},{8,9},{9,8},{10,11... | collective-permute-start | bytes 884744 | tf_op jit(solution)/shard_map/ppermute | solution.py:744
  422.9 15.9 %collective-permute-start.51 = (bf16[544,256]{1,0:T(8,128)(2,1)S(1)}, bf16[544,256]{1,0:T(8,128)(2,1)S(1)}, u32[]{:S(2)}, u32[]{:S(2)}) collective-permute-start(bf16[544,256]{1,0:T(8,128)(2,1)S(1)} %get-tuple-element.516), channel_id=1, source_target_pairs={{0,16},{4,20},{8,24},{12,28},{16,0},{20,4},{24,8},{28,12},{1,17},{... | collective-permute-start | bytes 835592 | tf_op jit(solution)/shard_map/ppermute | solution.py:744
  424.1 5.8 %collective-permute-start.50 = (bf16[96,768]{1,0:T(8,128)(2,1)S(1)}, bf16[96,768]{1,0:T(8,128)(2,1)S(1)}, u32[]{:S(2)}, u32[]{:S(2)}) collective-permute-start(bf16[96,768]{1,0:T(8,128)(2,1)S(1)} %get-tuple-element.522.rest_0_), channel_id=1, source_target_pairs={{0,3},{1,2},{2,1},{3,0},{4,7},{5,6},{6,5},{7,4},{8,11},{9,10},{10,... | collective-permute-start | bytes 442376 | tf_op jit(solution)/shard_map/ppermute | solution.py:744
  424.5 9.0 %collective-permute-start.49 = (bf16[96,768]{1,0:T(8,128)(2,1)S(1)}, bf16[96,768]{1,0:T(8,128)(2,1)S(1)}, u32[]{:S(2)}, u32[]{:S(2)}) collective-permute-start(bf16[96,768]{1,0:T(8,128)(2,1)S(1)} %get-tuple-element.522.rest_0_), channel_id=1, source_target_pairs={{0,2},{1,3},{2,0},{3,1},{4,6},{5,7},{6,4},{7,5},{8,10},{9,11},{10,... | collective-permute-start | bytes 442376 | tf_op jit(solution)/shard_map/ppermute | solution.py:744
  425.9 7.5 %collective-permute-start.48 = (bf16[96,768]{1,0:T(8,128)(2,1)S(1)}, bf16[96,768]{1,0:T(8,128)(2,1)S(1)}, u32[]{:S(2)}, u32[]{:S(2)}) collective-permute-start(bf16[96,768]{1,0:T(8,128)(2,1)S(1)} %get-tuple-element.522.rest_0_), channel_id=1, source_target_pairs={{0,1},{1,0},{2,3},{3,2},{4,5},{5,4},{6,7},{7,6},{8,9},{9,8},{10,11... | collective-permute-start | bytes 442376 | tf_op jit(solution)/shard_map/ppermute | solution.py:744
  439.1 11.5 %collective-permute-start.54 = (bf16[96,256]{1,0:T(8,128)(2,1)S(1)}, bf16[96,256]{1,0:T(8,128)(2,1)S(1)}, u32[]{:S(2)}, u32[]{:S(2)}) collective-permute-start(bf16[96,256]{1,0:T(8,128)(2,1)S(1)} %slice.164.rest_0_), channel_id=1, source_target_pairs={{0,3},{1,2},{2,1},{3,0},{4,7},{5,6},{6,5},{7,4},{8,11},{9,10},{10,... | collective-permute-start | bytes 147464 | tf_op jit(solution)/shard_map/ppermute | solution.py:744
  439.6 11.0 %collective-permute-start.53 = (bf16[96,256]{1,0:T(8,128)(2,1)S(1)}, bf16[96,256]{1,0:T(8,128)(2,1)S(1)}, u32[]{:S(2)}, u32[]{:S(2)}) collective-permute-start(bf16[96,256]{1,0:T(8,128)(2,1)S(1)} %slice.164.rest_0_), channel_id=1, source_target_pairs={{0,2},{1,3},{2,0},{3,1},{4,6},{5,7},{6,4},{7,5},{8,10},{9,11},{10,... | collective-permute-start | bytes 147464 | tf_op jit(solution)/shard_map/ppermute | solution.py:744
  440.6 10.0 %collective-permute-start.52 = (bf16[96,256]{1,0:T(8,128)(2,1)S(1)}, bf16[96,256]{1,0:T(8,128)(2,1)S(1)}, u32[]{:S(2)}, u32[]{:S(2)}) collective-permute-start(bf16[96,256]{1,0:T(8,128)(2,1)S(1)} %slice.164.rest_0_), channel_id=1, source_target_pairs={{0,1},{1,0},{2,3},{3,2},{4,5},{5,4},{6,7},{7,6},{8,9},{9,8},{10,11... | collective-permute-start | bytes 147464 | tf_op jit(solution)/shard_map/ppermute | solution.py:744
  454.4 11.7 %collective-permute-start.58 = (f32[8,128]{1,0:T(8,128)S(1)}, f32[8,128]{1,0:T(8,128)S(1)}, u32[]{:S(2)}, u32[]{:S(2)}) collective-permute-start(f32[8,128]{1,0:T(8,128)S(1)} %get-tuple-element.534), channel_id=1, source_target_pairs={{0,12},{4,8},{8,4},{12,0},{16,28},{20,24},{24,20},{28,16},{1,13},{... | collective-permute-start | bytes 12296 | tf_op jit(solution)/shard_map/ppermute | solution.py:744
  454.4 11.7 %collective-permute-start.57 = (f32[8,128]{1,0:T(8,128)S(1)}, f32[8,128]{1,0:T(8,128)S(1)}, u32[]{:S(2)}, u32[]{:S(2)}) collective-permute-start(f32[8,128]{1,0:T(8,128)S(1)} %get-tuple-element.534), channel_id=1, source_target_pairs={{0,8},{4,12},{8,0},{12,4},{16,24},{20,28},{24,16},{28,20},{1,9},{5... | collective-permute-start | bytes 12296 | tf_op jit(solution)/shard_map/ppermute | solution.py:744
  456.6 9.4 %collective-permute-start.56 = (f32[8,128]{1,0:T(8,128)S(1)}, f32[8,128]{1,0:T(8,128)S(1)}, u32[]{:S(2)}, u32[]{:S(2)}) collective-permute-start(f32[8,128]{1,0:T(8,128)S(1)} %get-tuple-element.534), channel_id=1, source_target_pairs={{0,4},{4,0},{8,12},{12,8},{16,20},{20,16},{24,28},{28,24},{1,5},{5... | collective-permute-start | bytes 12296 | tf_op jit(solution)/shard_map/ppermute | solution.py:744
  462.5 4.1 collective-permute-start.55
  466.0 4.6 collective-permute-start.59
  470.7 8.0 %collective-permute-start.60 = (f32[2,4]{1,0:T(2,128)S(1)}, f32[2,4]{1,0:T(2,128)S(1)}, u32[]{:S(2)}, u32[]{:S(2)}) collective-permute-start(f32[2,4]{1,0:T(2,128)S(1)} %fusion.21), channel_id=1, source_target_pairs={{0,2},{1,3},{2,0},{3,1},{4,6},{5,7},{6,4},{7,5},{8,10},{9,11},{10,... | collective-permute-start | bytes 104 | tf_op jit(solution)/shard_map/ppermute | solution.py:744
  (96 other events, 976.6 us)
Sparse Core Ops, SparseCore 0:
  11.5 94.7 all-gather.5
  109.8 86.8 all-gather.3

commit v5 on v4

--- a/solution.py
+++ b/solution.py
@@ -479,8 +479,9 @@
     group = images // len(outs)
     for at in range(0, width, LANES):
         lanes = slice(at, at + LANES)
-        own_wide[...] = own[:, :, lanes].astype(jnp.float32).reshape(own_wide.shape)
-        incoming_wide[...] = incoming[:, :, lanes].astype(jnp.float32).reshape(own_wide.shape)
+        held = slice(0, patches * images)
+        own_wide[held] = own[:, :, lanes].astype(jnp.float32).reshape(-1, LANES)
+        incoming_wide[held] = incoming[:, :, lanes].astype(jnp.float32).reshape(-1, LANES)
         for q, out in enumerate(outs):
             for i in range(group):
                 image = (device[0] ^ q) * group + i
@@ -489,7 +490,7 @@
                 joint[i * patches : (i + 1) * patches, :] = (
                     share[image] * first + (1 - share[image]) * second
                 )
-            out[:, lanes] = joint[...].astype(low)
+            out[:, lanes] = joint[: group * patches].astype(low)
 
 
 def mix(place, share, device, own, incoming, groups):
@@ -501,9 +502,9 @@
         in_specs=[scalar, scalar, scalar, pl.BlockSpec(), pl.BlockSpec()],
         out_shape=[jax.ShapeDtypeStruct((rows, width), low)] * groups,
         scratch_shapes=[
-            pltpu.VMEM((patches * images, LANES), jnp.float32),
-            pltpu.VMEM((patches * images, LANES), jnp.float32),
-            pltpu.VMEM((rows, LANES), jnp.float32),
+            pltpu.VMEM(((patches + SUBLANES) * images, LANES), jnp.float32),
+            pltpu.VMEM(((patches + SUBLANES) * images, LANES), jnp.float32),
+            pltpu.VMEM((rows + 2 * SUBLANES, LANES), jnp.float32),
         ],
         compiler_params=lean,
         cost_estimate=cost(4 * own.size, 6 * own.size),
@@ -522,7 +523,7 @@
     count = len(sources) // 2
     odd, upper = (device[0] & 1) == 1, (device[0] & 2) == 2
     patches = pieces.shape[1] // 2
-    rows = joint.shape[0] // (2 * 2)
+    rows = mixed.shape[0] // (2 * 2)
     joint[...] = jnp.zeros_like(joint)
     for copy in piece_copies:
         copy.wait()
@@ -530,11 +531,11 @@
         arrived = [pieces[side * count + k].astype(jnp.float32) for k in range(count)]
         arrived = [jnp.where(odd, arrived[k ^ 1], arrived[k]) for k in range(count)]
         for k in range(count):
-            spare[...] = jnp.where(upper, arrived[k ^ 2], arrived[k])
+            spare[: 2 * patches] = jnp.where(upper, arrived[k ^ 2], arrived[k])
             for i in range(2):
                 at = (side * 2 + i) * rows + k * patches
                 joint[at : at + patches, :] = spare[i * patches : (i + 1) * patches, :]
-    mixed[...] = joint[...].astype(low)
+    mixed[...] = joint[: mixed.shape[0]].astype(low)
     for copy in copies:
         copy.wait()
     state[...] = dot(mixed[...], weights[...], (1, 1)) + gains[0:1]
@@ -550,8 +551,8 @@
             jax.ShapeDtypeStruct((rows, width), jnp.float32),
         ],
         scratch_shapes=[
-            pltpu.VMEM((rows, pixels), jnp.float32),
-            pltpu.VMEM(pieces[0].shape, jnp.float32),
+            pltpu.VMEM((rows + 2 * SUBLANES, pixels), jnp.float32),
+            pltpu.VMEM((pieces[0].shape[0] + 2 * SUBLANES, pixels), jnp.float32),
             pltpu.VMEM((len(pieces), *pieces[0].shape), low),
             pltpu.VMEM((width, pixels), low),
             pltpu.SemaphoreType.DMA((len(pieces),)),
@@ -704,7 +705,7 @@
     for part in parts:
         joint[at : at + part.shape[0]] = part[...]
         at += part.shape[0]
-    true = moved(joint[...], source[...], 1)
+    true = moved(joint[:16], source[...], 1)
     small[...] = jnp.zeros_like(small)
     for j in range(joint.shape[1] // MISC):
         small[j * 16 : (j + 1) * 16] = true[:, j * MISC : (j + 1) * MISC]
@@ -731,7 +732,7 @@
         functools.partial(gather_misc_kernel, 4 + len(parts)),
         out_shape=[jax.ShapeDtypeStruct((2, rows, MISC), low)] * 2,
         scratch_shapes=[
-            pltpu.VMEM((16, parts[0].shape[1]), jnp.float32),
+            pltpu.VMEM((32, parts[0].shape[1]), jnp.float32),
             pltpu.VMEM((SMALL, MISC), jnp.float32),
         ],
         compiler_params=lean,
@@ -1076,31 +1077,33 @@
     blocks = [chan_low[0, 0], chan_low[0, 1]]
     tok_low = jnp.swapaxes(tok_w, 2, 3).astype(low)
     partner_mask = count_dp // 2
-    incoming = swap(own_parts[0], "dp", partner_mask)
     for step, mask in enumerate(masks):
         got = swap(packed(blocks), "dp", mask)
         if step == 0:
-            blocks, got, tok_low, own_parts[1], incoming = fence(blocks, got, tok_low, own_parts[1], incoming)
+            blocks, got, tok_low, tok_far, own_parts = fence(
+                blocks, got, tok_low, swap(tok_low, "tok", 2), own_parts
+            )
+            incoming = swap(own_parts[0], "dp", partner_mask)
+            tok_half = jnp.concatenate([tok_low, tok_far], 2)
+            tok_near = swap(tok_half, "tok", 1)
+        elif step == 1:
+            blocks, got, vectors, image_rows, own_parts, incoming, tok_half, tok_near = fence(
+                blocks, got, vectors, image_rows, own_parts, incoming, tok_half, tok_near
+            )
+            incoming_two = swap(own_parts[1], "dp", partner_mask)
             pieces = mixed_pieces(0, incoming)
-            incoming_two = swap(own_parts[1], "dp", partner_mask)
-            tok_far = swap(tok_low, "tok", 2)
-        elif step == 1:
-            blocks, got, vectors, image_rows, pieces, tok_low, tok_far = fence(
-                blocks, got, vectors, image_rows, pieces, tok_low, tok_far
-            )
         else:
             blocks, got = fence(blocks, got)
         blocks = doubled(blocks, got)
-    tok_half = jnp.concatenate([tok_low, tok_far], 2)
-    tok_turn = jnp.concatenate([tok_half, swap(tok_half, "tok", 1)], 2)
+    tok_turn = jnp.concatenate([tok_half, tok_near], 2)
     tok_turn = jnp.pad(tok_turn, ((0, 0), (0, 0), (0, 0), (0, each - all_patches)))
     token_turn = [[tok_turn[layer, way] for way in range(2)] for layer in range(LAYERS)]
     token_all = [[array.T for array in pair] for pair in token_turn]
 
     first, second = blocks
     first_low, second_far = swap(first, "dp", 1), swap(second, "tok", 2)
-    first, second, first_low, second_far, incoming_two, token_all, token_turn = fence(
-        first, second, first_low, second_far, incoming_two, token_all, token_turn
+    first, second, first_low, second_far, incoming_two, pieces, token_all, token_turn = fence(
+        first, second, first_low, second_far, incoming_two, pieces, token_all, token_turn
     )
     more = mixed_pieces(1, incoming_two)
     firsts, seconds = jnp.stack([first, first_low]), jnp.stack([second, second_far])

time: 502 us -> 500 us (level)
    all_gather x1, waiting for transfers between devices: 10.5 us -> 20.6 us  [body(): lax.all_gather(later, ('dp', 'tok')).reshape(count_dp, count_tok, -1, size)]
    ppermute x61, waiting for transfers between devices: 163 us -> 154 us  [swap(): return lax.ppermute(array, axis, [(i, i ^ mask) for i in range(count)])]
    unnamed x195 -> x198, local copies, waits for them, and re-layouts: 25.5 us -> 24.9 us
  transfers between devices with their start and end apart: 63 -> 63, of which waited for: 26 -> 24; matrix products, arithmetic and copies ran while one was open for 5% -> 5% of each run, Pallas kernels for 27% -> 27%
where the time goes in v5:
time: 500 us; the launch traced here: 492 us
  Pallas kernels  185 us (37%)
  waiting for transfers between devices  174 us (35%)
  starting transfers between devices  54.3 us (11%)
  local copies, waits for them, and re-layouts  41 us (8%)
  between operations  20 us (4%)
  other arithmetic  16.7 us (3%)
    ppermute x61, waiting for transfers between devices, swap(): return lax.ppermute(array, axis, [(i, i ^ mask) for i in range(count)])  154 us
    pallas_call x4, Pallas kernels, channel_backward(): pl.pallas_call(functools.partial(channel_backward_kernel, source, last),...  68 us
    ppermute x61, starting transfers between devices, swap(): return lax.ppermute(array, axis, [(i, i ^ mask) for i in range(count)])  54.2 us
    pallas_call x2, Pallas kernels, channel_forward(): pl.pallas_call(functools.partial(channel_forward_kernel, source), grid=(4...  25.7 us
    unnamed x198, local copies, waits for them, and re-layouts  24.9 us
    all_gather x1, waiting for transfers between devices, body(): lax.all_gather(later, ('dp', 'tok')).reshape(count_dp, count_tok, -1, size)  20.6 us
    pallas_call x2, Pallas kernels, channel_step(): pl.pallas_call(step_kernel, grid=(2, rows // chunk), in_specs=[scalars, b...  18.9 us
    pallas_call x2, Pallas kernels, token_backward(): pl.pallas_call(token_backward_kernel, grid=(count,), in_specs=[one, one,...  14.6 us
  transfers between devices with their start and end apart: 63, of which 24 were waited for; matrix products, arithmetic and copies ran while one was open for 5% of the time, Pallas kernels for 27%

profile of v5, /device:TPU:0, one launch (start us, length us, event | category | flops | bytes accessed | tf_op | source)
XLA Modules:
  0.0 491.6 jit_solution(15039226996642264790)
XLA Ops:
  12.2 3.0 collective-permute-start.1
  15.3 2.7 collective-permute-start
  24.7 7.6 %collective-permute-done = bf16[192,768]{1,0:T(8,128)(2,1)S(1)} collective-permute-done((bf16[192,768]{1,0:T(8,128)(2,1)S(1)}, bf16[192,768]{1,0:T(8,128)(2,1)S(1)}, u32[]{:S(2)}, u32[]{:S(2)}) %collective-permute-start) | collective-permute-done | bytes 294944 | tf_op jit(solution)/shard_map/ppermute | solution.py:745
  34.0 3.4 collective-permute-start.3
  38.6 1.5 collective-permute-done.4
  40.1 24.0 %collective-permute-done.2 = bf16[384,768]{1,0:T(8,128)(2,1)} collective-permute-done((bf16[384,768]{1,0:T(8,128)(2,1)}, bf16[384,768]{1,0:T(8,128)(2,1)}, u32[]{:S(2)}, u32[]{:S(2)}) %collective-permute-start.2) | collective-permute-done | bytes 589856 | tf_op jit(solution)/shard_map/ppermute | solution.py:745
  64.0 3.2 collective-permute-done.3.incoming
  68.4 1.6 collective-permute-start.5
  72.0 1.7 collective-permute-start.9
  75.8 14.8 %collective-permute-done.9.rest_2_ = bf16[98,768]{1,0:T(8,128)(2,1)S(1)} collective-permute-done((bf16[98,768]{1,0:T(8,128)(2,1)S(1)}, bf16[98,768]{1,0:T(8,128)(2,1)S(1)}, u32[]{:S(2)}, u32[]{:S(2)}) %collective-permute-start.9) | collective-permute-done | bytes 150560 | tf_op jit(solution)/shard_map/ppermute | solution.py:745
  90.6 12.2 %collective-permute-done.7.incoming = bf16[49,8,768]{2,1,0:T(8,128)(2,1)S(1)} collective-permute-done((bf16[49,8,768]{2,1,0:T(8,128)(2,1)S(1)}, bf16[49,8,768]{2,1,0:T(8,128)(2,1)S(1)}, u32[]{:S(2)}, u32[]{:S(2)}) %collective-permute-start.7) | collective-permute-done | bytes 602144 | tf_op jit(solution)/shard_map/ppermute | solution.py:745
  103.7 1.7 collective-permute-start.11
  109.2 26.1 %collective-permute-done.14.rest_6_ = bf16[98,768]{1,0:T(8,128)(2,1)S(1)} collective-permute-done((bf16[98,768]{1,0:T(8,128)(2,1)S(1)}, bf16[98,768]{1,0:T(8,128)(2,1)S(1)}, u32[]{:S(2)}, u32[]{:S(2)}) %collective-permute-start.14) | collective-permute-done | bytes 150560 | tf_op jit(solution)/shard_map/ppermute | solution.py:745
  135.4 1.5 collective-permute-done.15.rest_7_
  139.6 1.7 copy.84.token_out
  141.3 6.1 %stem.1 = (bf16[800,768]{1,0:T(8,128)(2,1)}, f32[800,768]{1,0:T(8,128)}) custom-call(s32[1]{0:T(128)} %bitcast.3.device.rest_1_.rest_2_, s32[8]{0:T(128)} %get-tuple-element.626.spots.rest_0_.rest_1_, bf16[98,768]{1,0:T(8,128)(2,1)} %copy-done.52, bf16[98,768]{1,0:T(8,128)(2,1)} %copy-done.74, bf16[98,768]{1,0:T(8,128)(2,1)} %copy-done.75, ...), custom_call_target="tpu_custom_call" | custom-call | flops 943718400 | bytes 7372800 | tf_op jit(solution)/shard_map/stem/pallas_call | solution.py:546
  147.4 1.7 copy-done.3
  149.1 4.0 token_forward.2
  154.6 12.7 %channel_forward.2 = (f32[800,768]{1,0:T(8,128)S(1)}, bf16[800,3072]{1,0:T(8,128)(2,1)}) custom-call(f32[800,768]{1,0:T(8,128)S(1)} %get-tuple-element.330.middle, f32[4,768]{1,0:T(4,128)S(1)} %get-tuple-element.599.gains, bf16[2,384,768]{2,1,0:T(8,128)(2,1)S(1)} %copy-done.18, bf16[2,384,768]{2,1,0:T(8,128)(2,1)} %collective-permute-done.11.rest_1_.rest_2_, ...), custom_call_target="tpu_custom_call" | custom-call | flops 7549747200 | bytes 14352384 | tf_op jit(solution)/shard_map/channel_forward/pallas_call | solution.py:190
  167.3 4.0 token_forward.3
  174.1 20.6 %all-gather.4.cloned.1.call-done = bf16[32,192,768]{2,1,0:T(8,128)(2,1)} async-done(((bf16[1,192,768]{2,1,0:T(8,128)(2,1)}), bf16[32,192,768]{2,1,0:T(8,128)(2,1)}) %all-gather.4.cloned.1.call-update) | async-done | bytes 9437200 | tf_op jit(solution)/shard_map/all_gather | solution.py:1048
  194.8 1.7 copy-done.62
  196.5 13.0 %channel_forward.3 = (f32[800,768]{1,0:T(8,128)S(1)}, bf16[800,3072]{1,0:T(8,128)(2,1)S(1)}) custom-call(f32[800,768]{1,0:T(8,128)S(1)} %copy-done.62, f32[4,768]{1,0:T(4,128)S(1)} %get-tuple-element.598.gains, s32[8]{0:T(128)S(1)} %copy-done.56, s32[1]{0:T(128)} %bitcast.3.device.rest_1_.rest_2_, bf16[8,4,192,768]{3,2,1,0:T(8,128)(2,1)} %bitcast.121), custom_call_target="tpu_custom_call" | custom-call | flops 7549747200 | bytes 14352384 | tf_op jit(solution)/shard_map/channel_forward/pallas_call | solution.py:190
  209.6 4.3 head_step.1
  213.9 15.8 %channel_backward.4 = (bf16[2,2,768,768]{3,2,1,0:T(8,128)(2,1)}, f32[800,768]{1,0:T(8,128)S(1)}, f32[2,768]{1,0:T(2,128)}) custom-call(f32[800,768]{1,0:T(8,128)S(1)} %get-tuple-element.345.gradient, f32[800,768]{1,0:T(8,128)S(1)} %copy-done.63, f32[4,768]{1,0:T(4,128)S(1)} %get-tuple-element.598.gains, bf16[800,3072]{1,0:T(8,128)(2,1)} %copy-done.64, ...), custom_call_target="tpu_custom_call" | custom-call | flops 7549747200 | bytes 11894784 | tf_op jit(solution)/shard_map/channel_backward/pallas_call | solution.py:260
  231.3 16.1 %channel_backward.5 = (bf16[2,2,768,768]{3,2,1,0:T(8,128)(2,1)}, f32[800,768]{1,0:T(8,128)S(1)}, f32[2,768]{1,0:T(2,128)S(1)}) custom-call(f32[800,768]{1,0:T(8,128)S(1)} %get-tuple-element.345.gradient, f32[800,768]{1,0:T(8,128)S(1)} %copy-done.63, f32[4,768]{1,0:T(4,128)S(1)} %get-tuple-element.598.gains, bf16[800,3072]{1,0:T(8,128)(2,1)} %copy-done.64, ...), custom_call_target="tpu_custom_call" | custom-call | flops 7549747200 | bytes 11894784 | tf_op jit(solution)/shard_map/channel_backward/pallas_call | solution.py:260
  249.8 7.1 %split_cores.2 = (bf16[2,384,768]{2,1,0:T(8,128)(2,1)}, bf16[2,384,768]{2,1,0:T(8,128)(2,1)}, bf16[768,1024]{1,0:T(8,128)(2,1)}, bf16[768,1024]{1,0:T(8,128)(2,1)}) custom-call(bf16[2,2,768,768]{3,2,1,0:T(8,128)(2,1)} %get-tuple-element.348.refs_0_.refs_1_.refs_2_, bf16[2,2,768,768]{3,2,1,0:T(8,128)(2,1)} %get-tuple-element.348.refs_0_.refs_1_.refs_2_, ...), custom_call_target="tpu_custom_call" | custom-call | flops 2359296 | bytes 14155776 | tf_op jit(solution)/shard_map/split_cores/pallas_call | solution.py:861
  259.2 1.7 copy-done.7
  260.9 1.7 copy-done.11
  262.5 7.6 %token_backward.2 = (f32[800,768]{1,0:T(8,128)S(1)}, f32[2,768]{1,0:T(2,128)S(1)}, f32[384,200]{1,0:T(8,128)S(1)}, f32[384,200]{1,0:T(8,128)S(1)}) custom-call(f32[800,768]{1,0:T(8,128)S(1)} %copy-done.7, f32[800,768]{1,0:T(8,128)S(1)} %get-tuple-element.335.state, f32[4,768]{1,0:T(4,128)S(1)} %get-tuple-element.598.gains, ...), custom_call_target="tpu_custom_call" | custom-call | flops 1887436800 | bytes 9830400 | tf_op jit(solution)/shard_map/token_backward/pallas_call | solution.py:456
  273.1 17.2 %channel_backward.6 = (bf16[2,2,768,768]{3,2,1,0:T(8,128)(2,1)}, f32[800,768]{1,0:T(8,128)}, f32[2,768]{1,0:T(2,128)}) custom-call(f32[800,768]{1,0:T(8,128)} %copy-done.59, f32[800,768]{1,0:T(8,128)} %copy-done.60, f32[4,768]{1,0:T(4,128)S(1)} %get-tuple-element.599.gains, bf16[800,3072]{1,0:T(8,128)(2,1)} %get-tuple-element.365.inner, ...), custom_call_target="tpu_custom_call" | custom-call | flops 7549747200 | bytes 11894784 | tf_op jit(solution)/shard_map/channel_backward/pallas_call | solution.py:260
  290.3 3.5 collective-permute-done.23.refs_3_
  293.9 3.1 fold_all.8
  300.8 18.9 %channel_backward.7 = (bf16[2,2,768,768]{3,2,1,0:T(8,128)(2,1)}, f32[800,768]{1,0:T(8,128)}, f32[2,768]{1,0:T(2,128)S(1)}) custom-call(f32[800,768]{1,0:T(8,128)} %copy-done.59, f32[800,768]{1,0:T(8,128)} %copy-done.60, f32[4,768]{1,0:T(4,128)S(1)} %get-tuple-element.599.gains, bf16[800,3072]{1,0:T(8,128)(2,1)} %get-tuple-element.365.inner, ...), custom_call_target="tpu_custom_call" | custom-call | flops 7549747200 | bytes 11894784 | tf_op jit(solution)/shard_map/channel_backward/pallas_call | solution.py:260
  319.7 6.6 %split_cores.3 = (bf16[2,384,768]{2,1,0:T(8,128)(2,1)}, bf16[2,384,768]{2,1,0:T(8,128)(2,1)}, bf16[768,768]{1,0:T(8,128)(2,1)}, bf16[768,768]{1,0:T(8,128)(2,1)}) custom-call(bf16[2,2,768,768]{3,2,1,0:T(8,128)(2,1)} %get-tuple-element.385.refs_0_.refs_1_.refs_2_, bf16[2,2,768,768]{3,2,1,0:T(8,128)(2,1)} %get-tuple-element.385.refs_0_.refs_1_.refs_2_, ...), custom_call_target="tpu_custom_call" | custom-call | flops 2359296 | bytes 14155776 | tf_op jit(solution)/shard_map/split_cores/pallas_call | solution.py:861
  327.6 2.2 fold_all.9
  333.8 2.0 collective-permute-start.27
  336.8 1.7 copy-done.5
  338.5 1.7 copy-done.9
  340.2 7.0 %token_backward.3 = (f32[800,768]{1,0:T(8,128)S(1)}, f32[2,768]{1,0:T(2,128)S(1)}, f32[384,200]{1,0:T(8,128)S(1)}, f32[384,200]{1,0:T(8,128)S(1)}) custom-call(f32[800,768]{1,0:T(8,128)S(1)} %copy-done.5, f32[800,768]{1,0:T(8,128)S(1)} %copy-done.4, f32[4,768]{1,0:T(4,128)S(1)} %get-tuple-element.599.gains, bf16[4,384,768]{2,1,0:T(8,128)(2,1)S(1)} %copy-done.9, ...), custom_call_target="tpu_custom_call" | custom-call | flops 1887436800 | bytes 9830400 | tf_op jit(solution)/shard_map/token_backward/pallas_call | solution.py:456
  347.2 1.8 stem_backward.1
  349.2 2.0 gather_misc.1
  351.2 8.1 %collective-permute-done.29.refs_5_ = bf16[2,384,768]{2,1,0:T(8,128)(2,1)} collective-permute-done((bf16[2,384,768]{2,1,0:T(8,128)(2,1)}, bf16[2,384,768]{2,1,0:T(8,128)(2,1)}, u32[]{:S(2)}, u32[]{:S(2)}) %collective-permute-start.29) | collective-permute-done | bytes 1179680 | tf_op jit(solution)/shard_map/ppermute | solution.py:745
  359.7 2.4 fold_all.10
  362.2 2.9 collective-permute-done.35.refs_1_
  369.5 1.9 collective-permute-start.32
  371.4 12.8 %collective-permute-done.32.refs_3_ = bf16[96,1024]{1,0:T(8,128)(2,1)S(1)} collective-permute-done((bf16[96,1024]{1,0:T(8,128)(2,1)S(1)}, bf16[96,1024]{1,0:T(8,128)(2,1)S(1)}, u32[]{:S(2)}, u32[]{:S(2)}) %collective-permute-start.32) | collective-permute-done | bytes 196640 | tf_op jit(solution)/shard_map/ppermute | solution.py:745
  384.2 3.6 collective-permute-done.31.refs_1_
  393.4 2.3 collective-permute-done.40.rest_3_.rest_7_
  395.7 4.1 collective-permute-done.39.rest_2_.rest_6_
  401.3 6.3 %collective-permute-done.41.refs_1_ = bf16[2,96,768]{2,1,0:T(8,128)(2,1)S(1)} collective-permute-done((bf16[2,96,768]{2,1,0:T(8,128)(2,1)S(1)}, bf16[2,96,768]{2,1,0:T(8,128)(2,1)S(1)}, u32[]{:S(2)}, u32[]{:S(2)}) %collective-permute-start.41) | collective-permute-done | bytes 294944 | tf_op jit(solution)/shard_map/ppermute | solution.py:745
  408.7 2.3 collective-permute-start.45
  411.0 9.3 %channel_step.2 = (f32[2,2,96,3072]{3,2,1,0:T(8,128)}, f32[2,2,96,3072]{3,2,1,0:T(8,128)}, f32[2,2,96,3072]{3,2,1,0:T(8,128)}, f32[2,2]{1,0:T(2,128)}) custom-call(s32[1]{0:T(128)} %bitcast.3.device.rest_1_.rest_2_, f32[2,2,96,3072]{3,2,1,0:T(8,128)} %weight.5, f32[2,2,96,3072]{3,2,1,0:T(8,128)} %mean.3, f32[2,2,96,3072]{3,2,1,0:T(8,128)} %power.3, ...), custom_call_target="tpu_custom_call" | custom-call | flops 5898240 | bytes 15335424 | tf_op jit(solution)/shard_map/channel_step/pallas_call | solution.py:335
  422.6 1.5 collective-permute-start.49
  424.2 3.9 collective-permute-done.50.rest_3_
  428.2 3.5 collective-permute-done.49.rest_2_
  431.7 5.4 %collective-permute-done.51.refs_1_ = bf16[544,256]{1,0:T(8,128)(2,1)S(1)} collective-permute-done((bf16[544,256]{1,0:T(8,128)(2,1)S(1)}, bf16[544,256]{1,0:T(8,128)(2,1)S(1)}, u32[]{:S(2)}, u32[]{:S(2)}) %collective-permute-start.51) | collective-permute-done | bytes 278560 | tf_op jit(solution)/shard_map/ppermute | solution.py:745
  439.2 9.6 %channel_step.3 = (f32[2,2,96,3072]{3,2,1,0:T(8,128)}, f32[2,2,96,3072]{3,2,1,0:T(8,128)}, f32[2,2,96,3072]{3,2,1,0:T(8,128)}, f32[2,2]{1,0:T(2,128)}) custom-call(s32[1]{0:T(128)} %bitcast.3.device.rest_1_.rest_2_, f32[2,2,96,3072]{3,2,1,0:T(8,128)} %weight.5, ...), custom_call_target="tpu_custom_call", output_to_operand_aliasing={{0}: (10, {}), {1}: (11, {}), {2}: (12, {})} | custom-call | flops 5898240 | bytes 15335424 | tf_op jit(solution)/shard_map/channel_step/pallas_call | solution.py:335
  450.2 2.4 ends_step.1
  452.6 2.1 collective-permute-start.57
  458.1 2.4 multiply_reduce_fusion
  462.4 1.9 pad_maximum_fusion.12
  464.8 4.0 collective-permute-done.59
  469.7 7.2 %channel_renew.1 = (f32[2,2,96,3072]{3,2,1,0:T(8,128)}, bf16[2,2,96,3072]{3,2,1,0:T(8,128)(2,1)}) custom-call(f32[8,128]{1,0:T(8,128)} %copy-done.86, f32[2,2,96,3072]{3,2,1,0:T(8,128)} %weight.5, f32[2,2,96,3072]{3,2,1,0:T(8,128)} %get-tuple-element.548.update), custom_call_target="tpu_custom_call" | custom-call | flops 3538944 | bytes 16515072 | tf_op jit(solution)/shard_map/channel_renew/pallas_call | solution.py:409
  (385 shorter events, 78.7 us)
Async XLA Ops:
  7.2 134.1 %all-gather.6.cloned.1.call-start = ((), (), s32[]{:S(2)}) async-start(), calls=%async_computation.1 | async-start | bytes 2838528 | tf_op jit(solution)/shard_map/all_gather | solution.py:1044
  10.0 184.8 %all-gather.4.cloned.1.call-start = ((), (), s32[]{:S(2)}) async-start(), calls=%async_computation | async-start | bytes 9732096 | tf_op jit(solution)/shard_map/all_gather | solution.py:1048
  12.2 12.5 %collective-permute-start.1 = (bf16[2,2,96,196]{3,2,1,0:T(8,128)(2,1)S(1)}, bf16[2,2,96,196]{3,2,1,0:T(8,128)(2,1)S(1)}, u32[]{:S(2)}, u32[]{:S(2)}) collective-permute-start(bf16[2,2,96,196]{3,2,1,0:T(8,128)(2,1)S(1)} %bitcast_convert_fusion), channel_id=1, source_target_pairs={{0,2},{1,3},{2,0},{3,1},{4,6},{5,7},{6,4},{7,5},{8,10},{9,11},{10,... | collective-permute-start | bytes 451592 | tf_op jit(solution)/shard_map/ppermute | solution.py:745
  15.3 17.1 %collective-permute-start = (bf16[192,768]{1,0:T(8,128)(2,1)S(1)}, bf16[192,768]{1,0:T(8,128)(2,1)S(1)}, u32[]{:S(2)}, u32[]{:S(2)}) collective-permute-start(bf16[192,768]{1,0:T(8,128)(2,1)S(1)} %pad_maximum_fusion.5), channel_id=1, source_target_pairs={{0,16},{4,20},{8,24},{12,28},{16,0},{20,4},{24,8},{28,12},{1,17},{... | collective-permute-start | bytes 884744 | tf_op jit(solution)/shard_map/ppermute | solution.py:745
  33.2 30.8 %collective-permute-start.2 = (bf16[384,768]{1,0:T(8,128)(2,1)}, bf16[384,768]{1,0:T(8,128)(2,1)}, u32[]{:S(2)}, u32[]{:S(2)}) collective-permute-start(bf16[384,768]{1,0:T(8,128)(2,1)} %pad_maximum_fusion.2), channel_id=1, source_target_pairs={{0,8},{4,12},{8,0},{12,4},{16,24},{20,28},{24,16},{28,20},{1,9},{5... | collective-permute-start | bytes 1769480 | tf_op jit(solution)/shard_map/ppermute | solution.py:745
  34.0 33.2 %collective-permute-start.3 = (bf16[49,8,768]{2,1,0:T(8,128)(2,1)S(1)}, bf16[49,8,768]{2,1,0:T(8,128)(2,1)S(1)}, u32[]{:S(2)}, u32[]{:S(2)}) collective-permute-start(bf16[49,8,768]{2,1,0:T(8,128)(2,1)S(1)} %get-tuple-element.301.own), channel_id=1, source_target_pairs={{0,16},{4,20},{8,24},{12,28},{16,0},{20,4},{24,8},{28,12},{1,17},{... | collective-permute-start | bytes 1806344 | tf_op jit(solution)/shard_map/ppermute | solution.py:745
  38.2 100.3 %copy-start.43 = (f32[11,768]{1,0:T(8,128)}, f32[11,768]{1,0:T(8,128)S(1)}, u32[]{:S(2)}) copy-start(f32[11,768]{1,0:T(8,128)S(1)} %relative_vectors.1.rest_9_) | copy-start | bytes 101380
  38.3 1.8 collective-permute-start.4
  68.4 22.2 %collective-permute-start.5 = (bf16[384,768]{1,0:T(8,128)(2,1)S(1)}, bf16[384,768]{1,0:T(8,128)(2,1)S(1)}, u32[]{:S(2)}, u32[]{:S(2)}) collective-permute-start(bf16[384,768]{1,0:T(8,128)(2,1)S(1)} %pad_maximum_fusion.3), channel_id=1, source_target_pairs={{0,4},{4,0},{8,12},{12,8},{16,20},{20,16},{24,28},{28,24},{1,5},{5... | collective-permute-start | bytes 1769480 | tf_op jit(solution)/shard_map/ppermute | solution.py:745
  70.0 20.6 %collective-permute-start.6 = (bf16[384,768]{1,0:T(8,128)(2,1)S(1)}, bf16[384,768]{1,0:T(8,128)(2,1)S(1)}, u32[]{:S(2)}, u32[]{:S(2)}) collective-permute-start(bf16[384,768]{1,0:T(8,128)(2,1)S(1)} %pad_maximum_fusion.4), channel_id=1, source_target_pairs={{0,2},{1,3},{2,0},{3,1},{4,6},{5,7},{6,4},{7,5},{8,10},{9,11},{10,... | collective-permute-start | bytes 1769480 | tf_op jit(solution)/shard_map/ppermute | solution.py:745
  70.5 32.3 %collective-permute-start.7 = (bf16[49,8,768]{2,1,0:T(8,128)(2,1)S(1)}, bf16[49,8,768]{2,1,0:T(8,128)(2,1)S(1)}, u32[]{:S(2)}, u32[]{:S(2)}) collective-permute-start(bf16[49,8,768]{2,1,0:T(8,128)(2,1)S(1)} %get-tuple-element.300.own), channel_id=1, source_target_pairs={{0,16},{4,20},{8,24},{12,28},{16,0},{20,4},{24,8},{28,12},{1,17},{... | collective-permute-start | bytes 1806344 | tf_op jit(solution)/shard_map/ppermute | solution.py:745
  72.0 1.9 collective-permute-start.8
  72.0 18.6 %collective-permute-start.9 = (bf16[98,768]{1,0:T(8,128)(2,1)S(1)}, bf16[98,768]{1,0:T(8,128)(2,1)S(1)}, u32[]{:S(2)}, u32[]{:S(2)}) collective-permute-start(bf16[98,768]{1,0:T(8,128)(2,1)S(1)} %get-tuple-element.305), channel_id=1, source_target_pairs={{0,2},{1,3},{2,0},{3,1},{4,6},{5,7},{6,4},{7,5},{8,10},{9,11},{10,... | collective-permute-start | bytes 451592 | tf_op jit(solution)/shard_map/ppermute | solution.py:745
  73.9 16.7 %collective-permute-start.10 = (bf16[98,768]{1,0:T(8,128)(2,1)S(1)}, bf16[98,768]{1,0:T(8,128)(2,1)S(1)}, u32[]{:S(2)}, u32[]{:S(2)}) collective-permute-start(bf16[98,768]{1,0:T(8,128)(2,1)S(1)} %get-tuple-element.306), channel_id=1, source_target_pairs={{0,3},{1,2},{2,1},{3,0},{4,7},{5,6},{6,5},{7,4},{8,11},{9,10},{10,... | collective-permute-start | bytes 451592 | tf_op jit(solution)/shard_map/ppermute | solution.py:745
  102.9 34.0 %collective-permute-start.12 = (bf16[2,384,768]{2,1,0:T(8,128)(2,1)S(1)}, bf16[2,384,768]{2,1,0:T(8,128)(2,1)}, u32[]{:S(2)}, u32[]{:S(2)}) collective-permute-start(bf16[2,384,768]{2,1,0:T(8,128)(2,1)S(1)} %pad_maximum_fusion.1.rest_4_.rest_5_), channel_id=1, source_target_pairs={{0,4},{4,0},{8,12},{12,8},{16,20},{20,16},{24,28},{28,24},{1,5},{5... | collective-permute-start | bytes 3538952 | tf_op jit(solution)/shard_map/ppermute | solution.py:745
  103.7 33.2 %collective-permute-start.11 = (bf16[2,384,768]{2,1,0:T(8,128)(2,1)S(1)}, bf16[2,384,768]{2,1,0:T(8,128)(2,1)}, u32[]{:S(2)}, u32[]{:S(2)}) collective-permute-start(bf16[2,384,768]{2,1,0:T(8,128)(2,1)S(1)} %pad_maximum_fusion.rest_0_.rest_1_), channel_id=1, source_target_pairs={{0,2},{1,3},{2,0},{3,1},{4,6},{5,7},{6,4},{7,5},{8,10},{9,11},{10,... | collective-permute-start | bytes 3538952 | tf_op jit(solution)/shard_map/ppermute | solution.py:745
  107.4 1.9 collective-permute-start.13
  107.4 28.0 %collective-permute-start.14 = (bf16[98,768]{1,0:T(8,128)(2,1)S(1)}, bf16[98,768]{1,0:T(8,128)(2,1)S(1)}, u32[]{:S(2)}, u32[]{:S(2)}) collective-permute-start(bf16[98,768]{1,0:T(8,128)(2,1)S(1)} %get-tuple-element.320), channel_id=1, source_target_pairs={{0,2},{1,3},{2,0},{3,1},{4,6},{5,7},{6,4},{7,5},{8,10},{9,11},{10,... | collective-permute-start | bytes 451592 | tf_op jit(solution)/shard_map/ppermute | solution.py:745
  107.7 29.2 %collective-permute-start.15 = (bf16[98,768]{1,0:T(8,128)(2,1)S(1)}, bf16[98,768]{1,0:T(8,128)(2,1)S(1)}, u32[]{:S(2)}, u32[]{:S(2)}) collective-permute-start(bf16[98,768]{1,0:T(8,128)(2,1)S(1)} %get-tuple-element.321), channel_id=1, source_target_pairs={{0,3},{1,2},{2,1},{3,0},{4,7},{5,6},{6,5},{7,4},{8,11},{9,10},{10,... | collective-permute-start | bytes 451592 | tf_op jit(solution)/shard_map/ppermute | solution.py:745
  136.9 17.6 %collective-permute-start.16 = (bf16[2,384,768]{2,1,0:T(8,128)(2,1)S(1)}, bf16[2,384,768]{2,1,0:T(8,128)(2,1)}, u32[]{:S(2)}, u32[]{:S(2)}) collective-permute-start(bf16[2,384,768]{2,1,0:T(8,128)(2,1)S(1)} %pad_maximum_fusion.rest_0_.rest_1_), channel_id=1, source_target_pairs={{0,1},{1,0},{2,3},{3,2},{4,5},{5,4},{6,7},{7,6},{8,9},{9,8},{10,11... | collective-permute-start | bytes 3538952 | tf_op jit(solution)/shard_map/ppermute | solution.py:745
  137.0 17.5 %collective-permute-start.17 = (bf16[2,384,768]{2,1,0:T(8,128)(2,1)}, bf16[2,384,768]{2,1,0:T(8,128)(2,1)}, u32[]{:S(2)}, u32[]{:S(2)}) collective-permute-start(bf16[2,384,768]{2,1,0:T(8,128)(2,1)} %collective-permute-done.11.rest_1_.rest_2_), channel_id=1, source_target_pairs={{0,1},{1,0},{2,3},{3,2},{4,5},{5,4},{6,7},{7,6},{8,9},{9,8},{10,11... | collective-permute-start | bytes 3538952 | tf_op jit(solution)/shard_map/ppermute | solution.py:745
  137.5 17.0 %collective-permute-start.18 = (bf16[2,384,768]{2,1,0:T(8,128)(2,1)S(1)}, bf16[2,384,768]{2,1,0:T(8,128)(2,1)}, u32[]{:S(2)}, u32[]{:S(2)}) collective-permute-start(bf16[2,384,768]{2,1,0:T(8,128)(2,1)S(1)} %pad_maximum_fusion.1.rest_4_.rest_5_), channel_id=1, source_target_pairs={{0,1},{1,0},{2,3},{3,2},{4,5},{5,4},{6,7},{7,6},{8,9},{9,8},{10,11... | collective-permute-start | bytes 3538952 | tf_op jit(solution)/shard_map/ppermute | solution.py:745
  137.6 17.0 %collective-permute-start.19 = (bf16[2,384,768]{2,1,0:T(8,128)(2,1)}, bf16[2,384,768]{2,1,0:T(8,128)(2,1)}, u32[]{:S(2)}, u32[]{:S(2)}) collective-permute-start(bf16[2,384,768]{2,1,0:T(8,128)(2,1)} %collective-permute-done.12.rest_5_.rest_6_), channel_id=1, source_target_pairs={{0,1},{1,0},{2,3},{3,2},{4,5},{5,4},{6,7},{7,6},{8,9},{9,8},{10,11... | collective-permute-start | bytes 3538952 | tf_op jit(solution)/shard_map/ppermute | solution.py:745
  229.8 19.1 %collective-permute-start.20 = (bf16[2,2,768,768]{3,2,1,0:T(8,128)(2,1)}, bf16[2,2,768,768]{3,2,1,0:T(8,128)(2,1)}, u32[]{:S(2)}, u32[]{:S(2)}) collective-permute-start(bf16[2,2,768,768]{3,2,1,0:T(8,128)(2,1)} %get-tuple-element.349), channel_id=1, source_target_pairs={{0,1},{1,0},{2,3},{3,2},{4,5},{5,4},{6,7},{7,6},{8,9},{9,8},{10,11... | collective-permute-start | bytes 14155784 | tf_op jit(solution)/shard_map/ppermute | solution.py:745
  231.1 17.8 %collective-permute-start.21 = (bf16[2,768,256]{2,1,0:T(8,128)(2,1)S(1)}, bf16[2,768,256]{2,1,0:T(8,128)(2,1)S(1)}, u32[]{:S(2)}, u32[]{:S(2)}) collective-permute-start(bf16[2,768,256]{2,1,0:T(8,128)(2,1)S(1)} %get-tuple-element.574), channel_id=1, source_target_pairs={{0,1},{1,0},{2,3},{3,2},{4,5},{5,4},{6,7},{7,6},{8,9},{9,8},{10,11... | collective-permute-start | bytes 2359304 | tf_op jit(solution)/shard_map/ppermute | solution.py:745
  256.9 36.9 %collective-permute-start.23 = (bf16[768,1024]{1,0:T(8,128)(2,1)}, bf16[768,1024]{1,0:T(8,128)(2,1)}, u32[]{:S(2)}, u32[]{:S(2)}) collective-permute-start(bf16[768,1024]{1,0:T(8,128)(2,1)} %get-tuple-element.359), channel_id=1, source_target_pairs={{0,2},{1,3},{2,0},{3,1},{4,6},{5,7},{6,4},{7,5},{8,10},{9,11},{10,... | collective-permute-start | bytes 4718600 | tf_op jit(solution)/shard_map/ppermute | solution.py:745
  258.4 31.9 %collective-permute-start.22 = (bf16[2,384,768]{2,1,0:T(8,128)(2,1)}, bf16[2,384,768]{2,1,0:T(8,128)(2,1)}, u32[]{:S(2)}, u32[]{:S(2)}) collective-permute-start(bf16[2,384,768]{2,1,0:T(8,128)(2,1)} %get-tuple-element.357), channel_id=1, source_target_pairs={{0,4},{4,0},{8,12},{12,8},{16,20},{20,16},{24,28},{28,24},{1,5},{5... | collective-permute-start | bytes 3538952 | tf_op jit(solution)/shard_map/ppermute | solution.py:745
  297.8 21.8 %collective-permute-start.26 = (bf16[2,2,768,768]{3,2,1,0:T(8,128)(2,1)S(1)}, bf16[2,2,768,768]{3,2,1,0:T(8,128)(2,1)}, u32[]{:S(2)}, u32[]{:S(2)}) collective-permute-start(bf16[2,2,768,768]{3,2,1,0:T(8,128)(2,1)S(1)} %copy-done.96), channel_id=1, source_target_pairs={{0,1},{1,0},{2,3},{3,2},{4,5},{5,4},{6,7},{7,6},{8,9},{9,8},{10,11... | collective-permute-start | bytes 14155784 | tf_op jit(solution)/shard_map/ppermute | solution.py:745
  297.8 28.5 %collective-permute-start.25 = (bf16[384,1024]{1,0:T(8,128)(2,1)}, bf16[384,1024]{1,0:T(8,128)(2,1)}, u32[]{:S(2)}, u32[]{:S(2)}) collective-permute-start(bf16[384,1024]{1,0:T(8,128)(2,1)} %get-tuple-element.382), channel_id=1, source_target_pairs={{0,4},{4,0},{8,12},{12,8},{16,20},{20,16},{24,28},{28,24},{1,5},{5... | collective-permute-start | bytes 2359304 | tf_op jit(solution)/shard_map/ppermute | solution.py:745
  299.3 27.0 %collective-permute-start.24 = (bf16[2,192,768]{2,1,0:T(8,128)(2,1)}, bf16[2,192,768]{2,1,0:T(8,128)(2,1)}, u32[]{:S(2)}, u32[]{:S(2)}) collective-permute-start(bf16[2,192,768]{2,1,0:T(8,128)(2,1)} %get-tuple-element.380), channel_id=1, source_target_pairs={{0,8},{4,12},{8,0},{12,4},{16,24},{20,28},{24,16},{28,20},{1,9},{5... | collective-permute-start | bytes 1769480 | tf_op jit(solution)/shard_map/ppermute | solution.py:745
  331.2 28.1 %collective-permute-start.29 = (bf16[2,384,768]{2,1,0:T(8,128)(2,1)}, bf16[2,384,768]{2,1,0:T(8,128)(2,1)}, u32[]{:S(2)}, u32[]{:S(2)}) collective-permute-start(bf16[2,384,768]{2,1,0:T(8,128)(2,1)} %get-tuple-element.410), channel_id=1, source_target_pairs={{0,4},{4,0},{8,12},{12,8},{16,20},{20,16},{24,28},{28,24},{1,5},{5... | collective-permute-start | bytes 3538952 | tf_op jit(solution)/shard_map/ppermute | solution.py:745
  331.8 27.9 %collective-permute-start.30 = (bf16[768,768]{1,0:T(8,128)(2,1)}, bf16[768,768]{1,0:T(8,128)(2,1)}, u32[]{:S(2)}, u32[]{:S(2)}) collective-permute-start(bf16[768,768]{1,0:T(8,128)(2,1)} %get-tuple-element.412), channel_id=1, source_target_pairs={{0,2},{1,3},{2,0},{3,1},{4,6},{5,7},{6,4},{7,5},{8,10},{9,11},{10,... | collective-permute-start | bytes 3538952 | tf_op jit(solution)/shard_map/ppermute | solution.py:745
  333.2 18.0 %collective-permute-start.28 = (bf16[192,1024]{1,0:T(8,128)(2,1)}, bf16[192,1024]{1,0:T(8,128)(2,1)S(1)}, u32[]{:S(2)}, u32[]{:S(2)}) collective-permute-start(bf16[192,1024]{1,0:T(8,128)(2,1)} %get-tuple-element.408), channel_id=1, source_target_pairs={{0,8},{4,12},{8,0},{12,4},{16,24},{20,28},{24,16},{28,20},{1,9},{5... | collective-permute-start | bytes 1179656 | tf_op jit(solution)/shard_map/ppermute | solution.py:745
  333.8 17.4 %collective-permute-start.27 = (bf16[2,96,768]{2,1,0:T(8,128)(2,1)}, bf16[2,96,768]{2,1,0:T(8,128)(2,1)}, u32[]{:S(2)}, u32[]{:S(2)}) collective-permute-start(bf16[2,96,768]{2,1,0:T(8,128)(2,1)} %get-tuple-element.406), channel_id=1, source_target_pairs={{0,16},{4,20},{8,24},{12,28},{16,0},{20,4},{24,8},{28,12},{1,17},{... | collective-permute-start | bytes 884744 | tf_op jit(solution)/shard_map/ppermute | solution.py:745
  362.1 3.0 collective-permute-start.35
  365.4 22.5 %collective-permute-start.36 = (bf16[1216,256]{1,0:T(8,128)(2,1)S(1)}, bf16[1216,256]{1,0:T(8,128)(2,1)S(1)}, u32[]{:S(2)}, u32[]{:S(2)}) collective-permute-start(bf16[1216,256]{1,0:T(8,128)(2,1)S(1)} %get-tuple-element.461), channel_id=1, source_target_pairs={{0,2},{1,3},{2,0},{3,1},{4,6},{5,7},{6,4},{7,5},{8,10},{9,11},{10,... | collective-permute-start | bytes 1867784 | tf_op jit(solution)/shard_map/ppermute | solution.py:745
  366.9 21.0 %collective-permute-start.33 = (bf16[2,192,768]{2,1,0:T(8,128)(2,1)S(1)}, bf16[2,192,768]{2,1,0:T(8,128)(2,1)S(1)}, u32[]{:S(2)}, u32[]{:S(2)}) collective-permute-start(bf16[2,192,768]{2,1,0:T(8,128)(2,1)S(1)} %get-tuple-element.455), channel_id=1, source_target_pairs={{0,8},{4,12},{8,0},{12,4},{16,24},{20,28},{24,16},{28,20},{1,9},{5... | collective-permute-start | bytes 1769480 | tf_op jit(solution)/shard_map/ppermute | solution.py:745
  367.4 20.4 %collective-permute-start.34 = (bf16[384,768]{1,0:T(8,128)(2,1)S(1)}, bf16[384,768]{1,0:T(8,128)(2,1)S(1)}, u32[]{:S(2)}, u32[]{:S(2)}) collective-permute-start(bf16[384,768]{1,0:T(8,128)(2,1)S(1)} %get-tuple-element.457), channel_id=1, source_target_pairs={{0,4},{4,0},{8,12},{12,8},{16,20},{20,16},{24,28},{28,24},{1,5},{5... | collective-permute-start | bytes 1769480 | tf_op jit(solution)/shard_map/ppermute | solution.py:745
  368.0 19.8 %collective-permute-start.31 = (bf16[2,96,768]{2,1,0:T(8,128)(2,1)S(1)}, bf16[2,96,768]{2,1,0:T(8,128)(2,1)S(1)}, u32[]{:S(2)}, u32[]{:S(2)}) collective-permute-start(bf16[2,96,768]{2,1,0:T(8,128)(2,1)S(1)} %get-tuple-element.462.refs_0_), channel_id=1, source_target_pairs={{0,2},{1,3},{2,0},{3,1},{4,6},{5,7},{6,4},{7,5},{8,10},{9,11},{10,... | collective-permute-start | bytes 884744 | tf_op jit(solution)/shard_map/ppermute | solution.py:745
  369.5 14.8 %collective-permute-start.32 = (bf16[96,1024]{1,0:T(8,128)(2,1)S(1)}, bf16[96,1024]{1,0:T(8,128)(2,1)S(1)}, u32[]{:S(2)}, u32[]{:S(2)}) collective-permute-start(bf16[96,1024]{1,0:T(8,128)(2,1)S(1)} %get-tuple-element.453), channel_id=1, source_target_pairs={{0,16},{4,20},{8,24},{12,28},{16,0},{20,4},{24,8},{28,12},{1,17},{... | collective-permute-start | bytes 589832 | tf_op jit(solution)/shard_map/ppermute | solution.py:745
  388.4 7.3 %collective-permute-start.40 = (bf16[96,1024]{1,0:T(8,128)(2,1)S(1)}, bf16[96,1024]{1,0:T(8,128)(2,1)S(1)}, u32[]{:S(2)}, u32[]{:S(2)}) collective-permute-start(bf16[96,1024]{1,0:T(8,128)(2,1)S(1)} %get-tuple-element.501.rest_0_.rest_4_), channel_id=1, source_target_pairs={{0,3},{1,2},{2,1},{3,0},{4,7},{5,6},{6,5},{7,4},{8,11},{9,10},{10,... | collective-permute-start | bytes 589832 | tf_op jit(solution)/shard_map/ppermute | solution.py:745
  388.8 18.8 %collective-permute-start.43 = (bf16[832,256]{1,0:T(8,128)(2,1)S(1)}, bf16[832,256]{1,0:T(8,128)(2,1)S(1)}, u32[]{:S(2)}, u32[]{:S(2)}) collective-permute-start(bf16[832,256]{1,0:T(8,128)(2,1)S(1)} %get-tuple-element.487), channel_id=1, source_target_pairs={{0,4},{4,0},{8,12},{12,8},{16,20},{20,16},{24,28},{28,24},{1,5},{5... | collective-permute-start | bytes 1277960 | tf_op jit(solution)/shard_map/ppermute | solution.py:745
  390.0 9.8 %collective-permute-start.39 = (bf16[96,1024]{1,0:T(8,128)(2,1)S(1)}, bf16[96,1024]{1,0:T(8,128)(2,1)S(1)}, u32[]{:S(2)}, u32[]{:S(2)}) collective-permute-start(bf16[96,1024]{1,0:T(8,128)(2,1)S(1)} %get-tuple-element.501.rest_0_.rest_4_), channel_id=1, source_target_pairs={{0,2},{1,3},{2,0},{3,1},{4,6},{5,7},{6,4},{7,5},{8,10},{9,11},{10,... | collective-permute-start | bytes 589832 | tf_op jit(solution)/shard_map/ppermute | solution.py:745
  390.9 16.8 %collective-permute-start.41 = (bf16[2,96,768]{2,1,0:T(8,128)(2,1)S(1)}, bf16[2,96,768]{2,1,0:T(8,128)(2,1)S(1)}, u32[]{:S(2)}, u32[]{:S(2)}) collective-permute-start(bf16[2,96,768]{2,1,0:T(8,128)(2,1)S(1)} %get-tuple-element.483), channel_id=1, source_target_pairs={{0,16},{4,20},{8,24},{12,28},{16,0},{20,4},{24,8},{28,12},{1,17},{... | collective-permute-start | bytes 884744 | tf_op jit(solution)/shard_map/ppermute | solution.py:745
  391.9 15.8 %collective-permute-start.42 = (bf16[192,768]{1,0:T(8,128)(2,1)S(1)}, bf16[192,768]{1,0:T(8,128)(2,1)S(1)}, u32[]{:S(2)}, u32[]{:S(2)}) collective-permute-start(bf16[192,768]{1,0:T(8,128)(2,1)S(1)} %get-tuple-element.485), channel_id=1, source_target_pairs={{0,8},{4,12},{8,0},{12,4},{16,24},{20,28},{24,16},{28,20},{1,9},{5... | collective-permute-start | bytes 884744 | tf_op jit(solution)/shard_map/ppermute | solution.py:745
  395.7 12.0 %collective-permute-start.37 = (bf16[2,96,768]{2,1,0:T(8,128)(2,1)S(1)}, bf16[2,96,768]{2,1,0:T(8,128)(2,1)S(1)}, u32[]{:S(2)}, u32[]{:S(2)}) collective-permute-start(bf16[2,96,768]{2,1,0:T(8,128)(2,1)S(1)} %get-tuple-element.499.near), channel_id=1, source_target_pairs={{0,1},{1,0},{2,3},{3,2},{4,5},{5,4},{6,7},{7,6},{8,9},{9,8},{10,11... | collective-permute-start | bytes 884744 | tf_op jit(solution)/shard_map/ppermute | solution.py:745
  399.8 1.4 collective-permute-start.38
  407.9 12.9 %collective-permute-start.46 = (bf16[640,256]{1,0:T(8,128)(2,1)S(1)}, bf16[640,256]{1,0:T(8,128)(2,1)S(1)}, u32[]{:S(2)}, u32[]{:S(2)}) collective-permute-start(bf16[640,256]{1,0:T(8,128)(2,1)S(1)} %get-tuple-element.498), channel_id=1, source_target_pairs={{0,8},{4,12},{8,0},{12,4},{16,24},{20,28},{24,16},{28,20},{1,9},{5... | collective-permute-start | bytes 983048 | tf_op jit(solution)/shard_map/ppermute | solution.py:745
  408.1 12.3 %collective-permute-start.44 = (bf16[2,96,768]{2,1,0:T(8,128)(2,1)S(1)}, bf16[2,96,768]{2,1,0:T(8,128)(2,1)S(1)}, u32[]{:S(2)}, u32[]{:S(2)}) collective-permute-start(bf16[2,96,768]{2,1,0:T(8,128)(2,1)S(1)} %get-tuple-element.511.refs_0_), channel_id=1, source_target_pairs={{0,2},{1,3},{2,0},{3,1},{4,6},{5,7},{6,4},{7,5},{8,10},{9,11},{10,... | collective-permute-start | bytes 884744 | tf_op jit(solution)/shard_map/ppermute | solution.py:745
  408.7 11.7 %collective-permute-start.45 = (bf16[96,768]{1,0:T(8,128)(2,1)S(1)}, bf16[96,768]{1,0:T(8,128)(2,1)S(1)}, u32[]{:S(2)}, u32[]{:S(2)}) collective-permute-start(bf16[96,768]{1,0:T(8,128)(2,1)S(1)} %get-tuple-element.496), channel_id=1, source_target_pairs={{0,16},{4,20},{8,24},{12,28},{16,0},{20,4},{24,8},{28,12},{1,17},{... | collective-permute-start | bytes 442376 | tf_op jit(solution)/shard_map/ppermute | solution.py:745
  421.0 16.0 %collective-permute-start.47 = (bf16[2,96,768]{2,1,0:T(8,128)(2,1)S(1)}, bf16[2,96,768]{2,1,0:T(8,128)(2,1)S(1)}, u32[]{:S(2)}, u32[]{:S(2)}) collective-permute-start(bf16[2,96,768]{2,1,0:T(8,128)(2,1)S(1)} %get-tuple-element.528.near), channel_id=1, source_target_pairs={{0,1},{1,0},{2,3},{3,2},{4,5},{5,4},{6,7},{7,6},{8,9},{9,8},{10,11... | collective-permute-start | bytes 884744 | tf_op jit(solution)/shard_map/ppermute | solution.py:745
  421.1 15.9 %collective-permute-start.51 = (bf16[544,256]{1,0:T(8,128)(2,1)S(1)}, bf16[544,256]{1,0:T(8,128)(2,1)S(1)}, u32[]{:S(2)}, u32[]{:S(2)}) collective-permute-start(bf16[544,256]{1,0:T(8,128)(2,1)S(1)} %get-tuple-element.524), channel_id=1, source_target_pairs={{0,16},{4,20},{8,24},{12,28},{16,0},{20,4},{24,8},{28,12},{1,17},{... | collective-permute-start | bytes 835592 | tf_op jit(solution)/shard_map/ppermute | solution.py:745
  422.4 5.8 %collective-permute-start.50 = (bf16[96,768]{1,0:T(8,128)(2,1)S(1)}, bf16[96,768]{1,0:T(8,128)(2,1)S(1)}, u32[]{:S(2)}, u32[]{:S(2)}) collective-permute-start(bf16[96,768]{1,0:T(8,128)(2,1)S(1)} %get-tuple-element.530.rest_0_), channel_id=1, source_target_pairs={{0,3},{1,2},{2,1},{3,0},{4,7},{5,6},{6,5},{7,4},{8,11},{9,10},{10,... | collective-permute-start | bytes 442376 | tf_op jit(solution)/shard_map/ppermute | solution.py:745
  422.6 9.0 %collective-permute-start.49 = (bf16[96,768]{1,0:T(8,128)(2,1)S(1)}, bf16[96,768]{1,0:T(8,128)(2,1)S(1)}, u32[]{:S(2)}, u32[]{:S(2)}) collective-permute-start(bf16[96,768]{1,0:T(8,128)(2,1)S(1)} %get-tuple-element.530.rest_0_), channel_id=1, source_target_pairs={{0,2},{1,3},{2,0},{3,1},{4,6},{5,7},{6,4},{7,5},{8,10},{9,11},{10,... | collective-permute-start | bytes 442376 | tf_op jit(solution)/shard_map/ppermute | solution.py:745
  424.2 7.5 %collective-permute-start.48 = (bf16[96,768]{1,0:T(8,128)(2,1)S(1)}, bf16[96,768]{1,0:T(8,128)(2,1)S(1)}, u32[]{:S(2)}, u32[]{:S(2)}) collective-permute-start(bf16[96,768]{1,0:T(8,128)(2,1)S(1)} %get-tuple-element.530.rest_0_), channel_id=1, source_target_pairs={{0,1},{1,0},{2,3},{3,2},{4,5},{5,4},{6,7},{7,6},{8,9},{9,8},{10,11... | collective-permute-start | bytes 442376 | tf_op jit(solution)/shard_map/ppermute | solution.py:745
  437.3 11.5 %collective-permute-start.54 = (bf16[96,256]{1,0:T(8,128)(2,1)S(1)}, bf16[96,256]{1,0:T(8,128)(2,1)S(1)}, u32[]{:S(2)}, u32[]{:S(2)}) collective-permute-start(bf16[96,256]{1,0:T(8,128)(2,1)S(1)} %slice.164.rest_0_), channel_id=1, source_target_pairs={{0,3},{1,2},{2,1},{3,0},{4,7},{5,6},{6,5},{7,4},{8,11},{9,10},{10,... | collective-permute-start | bytes 147464 | tf_op jit(solution)/shard_map/ppermute | solution.py:745
  437.7 11.1 %collective-permute-start.53 = (bf16[96,256]{1,0:T(8,128)(2,1)S(1)}, bf16[96,256]{1,0:T(8,128)(2,1)S(1)}, u32[]{:S(2)}, u32[]{:S(2)}) collective-permute-start(bf16[96,256]{1,0:T(8,128)(2,1)S(1)} %slice.164.rest_0_), channel_id=1, source_target_pairs={{0,2},{1,3},{2,0},{3,1},{4,6},{5,7},{6,4},{7,5},{8,10},{9,11},{10,... | collective-permute-start | bytes 147464 | tf_op jit(solution)/shard_map/ppermute | solution.py:745
  438.8 10.0 %collective-permute-start.52 = (bf16[96,256]{1,0:T(8,128)(2,1)S(1)}, bf16[96,256]{1,0:T(8,128)(2,1)S(1)}, u32[]{:S(2)}, u32[]{:S(2)}) collective-permute-start(bf16[96,256]{1,0:T(8,128)(2,1)S(1)} %slice.164.rest_0_), channel_id=1, source_target_pairs={{0,1},{1,0},{2,3},{3,2},{4,5},{5,4},{6,7},{7,6},{8,9},{9,8},{10,11... | collective-permute-start | bytes 147464 | tf_op jit(solution)/shard_map/ppermute | solution.py:745
  452.6 11.7 %collective-permute-start.58 = (f32[8,128]{1,0:T(8,128)S(1)}, f32[8,128]{1,0:T(8,128)S(1)}, u32[]{:S(2)}, u32[]{:S(2)}) collective-permute-start(f32[8,128]{1,0:T(8,128)S(1)} %get-tuple-element.542), channel_id=1, source_target_pairs={{0,12},{4,8},{8,4},{12,0},{16,28},{20,24},{24,20},{28,16},{1,13},{... | collective-permute-start | bytes 12296 | tf_op jit(solution)/shard_map/ppermute | solution.py:745
  452.6 11.7 %collective-permute-start.57 = (f32[8,128]{1,0:T(8,128)S(1)}, f32[8,128]{1,0:T(8,128)S(1)}, u32[]{:S(2)}, u32[]{:S(2)}) collective-permute-start(f32[8,128]{1,0:T(8,128)S(1)} %get-tuple-element.542), channel_id=1, source_target_pairs={{0,8},{4,12},{8,0},{12,4},{16,24},{20,28},{24,16},{28,20},{1,9},{5... | collective-permute-start | bytes 12296 | tf_op jit(solution)/shard_map/ppermute | solution.py:745
  454.7 9.6 %collective-permute-start.56 = (f32[8,128]{1,0:T(8,128)S(1)}, f32[8,128]{1,0:T(8,128)S(1)}, u32[]{:S(2)}, u32[]{:S(2)}) collective-permute-start(f32[8,128]{1,0:T(8,128)S(1)} %get-tuple-element.542), channel_id=1, source_target_pairs={{0,4},{4,0},{8,12},{12,8},{16,20},{20,16},{24,28},{28,24},{1,5},{5... | collective-permute-start | bytes 12296 | tf_op jit(solution)/shard_map/ppermute | solution.py:745
  460.7 4.1 collective-permute-start.55
  464.3 4.6 collective-permute-start.59
  468.9 7.9 %collective-permute-start.60 = (f32[2,4]{1,0:T(2,128)S(1)}, f32[2,4]{1,0:T(2,128)S(1)}, u32[]{:S(2)}, u32[]{:S(2)}) collective-permute-start(f32[2,4]{1,0:T(2,128)S(1)} %fusion.19), channel_id=1, source_target_pairs={{0,2},{1,3},{2,0},{3,1},{4,6},{5,7},{6,4},{7,5},{8,10},{9,11},{10,... | collective-permute-start | bytes 104 | tf_op jit(solution)/shard_map/ppermute | solution.py:745
  (97 other events, 932.9 us)
Sparse Core Ops, SparseCore 0:
  11.5 87.0 all-gather.5
  102.1 92.6 all-gather.3
